TPU v7x, 32 devices: a whole 2x2x4 slice. The times are simulated.
32 devices in a mesh: cfg: 2 (over core), seq: 4 (over z), blk: 4 (over y, x).
Axes of the slice: x: 2, y: 2, z: 4, core: 2. Of those that a mesh axis runs over, the one named last changes fastest.
Arguments:
- queries: bfloat16 [2, 1536, 1536], P('cfg', 'seq', 'blk'), may hold values from -20 to 20
- keys: bfloat16 [2, 1536, 1536], P('cfg', 'seq', 'blk'), may hold values from -20 to 20
- values: bfloat16 [2, 1536, 1536], P('cfg', 'seq', 'blk'), may hold values from -6 to 6
- residual: bfloat16 [2, 1536, 1536], P('cfg', 'seq'), may hold values from -6 to 6
- w_out: bfloat16 [1536, 1536], P('blk'), may hold values from -0.15625 to 0.15625
- w_up: bfloat16 [1536, 6144], P(None, 'blk'), may hold values from -0.15625 to 0.15625
- w_down: bfloat16 [6144, 1536], P('blk'), may hold values from -0.078125 to 0.078125
- modulation: float32 [3, 4, 1536], replicated, may hold values from -3 to 3
- guide_scale: float32 [3], replicated, may hold values from 1.5 to 4
- slot_clip: int32 [1536], P('seq'), may hold values from 0 to 3, as said below
- owner: int32 [1536, 1], P('seq'), may hold values from 0 to 3; in each aligned block of 192 rows (0 to 191, 192 to 383, ...) at most 96 rows name the same one
Outputs:
- returned: bfloat16 [2, 1536, 1536], P('cfg', 'seq', 'blk')
Inputs may be any that keep to these rules, and one draw needn't show every extreme that they name: `slot_clip`: each device's block of 384 slots holds its live slots first and its padding slots, marked 3, last; live slots, counted block after block, are dealt to the clips in turn (the t-th live slot belongs to clip t mod 3), so each clip has 448 live slots. In each aligned half-block of 192 slots no owner is named more than 96 times.
All inputs are finite; a program needn't handle non-finite values.
Results may differ from a plain program's by a relative error of at most 0.017.
Values may be sent and summed in bfloat16 or wider, within the bound.
No kernel may reach another device: no remote copies, remote signals or barrier semaphores. Data moves between devices by JAX's collectives and lax.ppermute only.
A program may use at most 128 MiB of HBM per device.

v0:
```python
import math

import jax
import jax.numpy as jnp
from jax import lax
from jax.sharding import PartitionSpec as P

D = 1536
HEAD_DIM = 128
CLIPS = 3


NEG_FILL = -1e30


def swapped(value, axis, bit):
    mask = 2**bit
    pairs = [(source, source ^ mask) for source in range(lax.axis_size(axis))]
    return lax.ppermute(value, axis, pairs)


def shards(
    queries, keys, values, residual, w_out, w_up, w_down, modulation, guide_scale, slot_clip, owner
):
    query_here = queries[0]
    slots, width = query_here.shape
    heads_here = width // HEAD_DIM
    factor = 1.0 / math.sqrt(HEAD_DIM)
    live = slot_clip < CLIPS
    query_heads = query_here.reshape(slots, heads_here, HEAD_DIM)

    def absorb_block(carry, key_block, value_block, clip_block):
        count = key_block.shape[0]
        kept = (clip_block[None, :] == slot_clip[:, None]) & live[:, None]
        best, total, accum = carry
        key_heads = key_block.reshape(count, heads_here, HEAD_DIM)
        value_heads = value_block.reshape(count, heads_here, HEAD_DIM)
        scores = (
            jnp.einsum("qhd,khd->hqk", query_heads, key_heads, preferred_element_type=jnp.float32)
            * factor
        )
        scores = jnp.where(kept[None], scores, NEG_FILL)
        new_best = jnp.maximum(best, jnp.max(scores, axis=-1))
        fade = jnp.exp(best - new_best)
        probs = jnp.exp(scores - new_best[..., None])
        total = total * fade + jnp.sum(probs, axis=-1)
        added = jnp.einsum(
            "hqk,khd->qhd",
            probs.astype(jnp.bfloat16),
            value_heads,
            preferred_element_type=jnp.float32,
        )
        accum = accum * jnp.transpose(fade)[:, :, None] + added
        return (new_best, total, accum)

    def absorb(carry, piece):
        key_piece, value_piece, clip_piece = piece
        count = key_piece.shape[0]
        step_rows = next(
            (size_b for size_b in (512, 384, 256, 128) if count % size_b == 0 and count > size_b),
            count,
        )
        if step_rows == count:
            return absorb_block(carry, key_piece, value_piece, clip_piece)
        blocks = count // step_rows

        def scan_step(state, block_items):
            return (absorb_block(state, block_items[0], block_items[1], block_items[2]), None)

        stacked = (
            key_piece.reshape(blocks, step_rows, width),
            value_piece.reshape(blocks, step_rows, width),
            clip_piece.reshape(blocks, step_rows),
        )
        carry_out, unused = lax.scan(scan_step, carry, stacked)
        return carry_out

    start_state = (
        jnp.full((heads_here, slots), NEG_FILL, jnp.float32),
        jnp.zeros((heads_here, slots), jnp.float32),
        jnp.zeros((slots, heads_here, HEAD_DIM), jnp.float32),
    )
    best, total, accum = absorb(
        start_state,
        (
            lax.all_gather(keys[0], "seq", axis=0, tiled=True),
            lax.all_gather(values[0], "seq", axis=0, tiled=True),
            lax.all_gather(slot_clip, "seq", axis=0, tiled=True),
        ),
    )
    attended = (accum / jnp.transpose(total)[:, :, None]).reshape(slots, width)
    attended = jnp.where(live[:, None], attended, 0.0).astype(jnp.bfloat16)
    partial_out = jnp.dot(attended, w_out, preferred_element_type=jnp.float32)
    selector = (slot_clip[:, None] == jnp.arange(CLIPS, dtype=jnp.int32)[None, :]).astype(
        jnp.float32
    )
    row_mod = jnp.dot(
        selector, modulation.reshape(CLIPS, 4 * D), precision=lax.Precision.HIGHEST
    ).reshape(slots, 4, D)
    columns = D // lax.axis_size("blk")
    col_start = lax.axis_index("blk") * columns
    mod_cols = lax.dynamic_slice_in_dim(row_mod, col_start, columns, 2)
    projected = lax.psum(partial_out.astype(jnp.bfloat16), "blk").astype(jnp.float32)
    mixed = residual[0].astype(jnp.float32) + row_mod[:, 0] * projected
    centre = mixed - jnp.mean(mixed, axis=-1, keepdims=True)
    spread = jnp.mean(centre * centre, axis=-1, keepdims=True)
    normed = (centre * lax.rsqrt(spread + 1e-06) * (1.0 + row_mod[:, 2]) + row_mod[:, 1]).astype(
        jnp.bfloat16
    )
    mixed_cols = lax.dynamic_slice_in_dim(mixed, col_start, columns, 1)
    hidden = jax.nn.gelu(
        jnp.dot(normed, w_up, preferred_element_type=jnp.float32), approximate=True
    ).astype(jnp.bfloat16)
    terms = jnp.dot(hidden, w_down, preferred_element_type=jnp.float32)
    summed = lax.psum_scatter(
        terms.astype(jnp.bfloat16), "blk", scatter_dimension=1, tiled=True
    ).astype(jnp.float32)
    block_out = (mixed_cols + mod_cols[:, 3] * summed).astype(jnp.bfloat16)
    half_len = slots // 2
    side = lax.axis_index("cfg")
    partner = swapped(block_out, "cfg", 0)
    cond_all = jnp.where(side == 0, block_out, partner)
    uncond_all = jnp.where(side == 0, partner, block_out)
    cond_rows = lax.dynamic_slice_in_dim(cond_all, side * half_len, half_len, 0)
    uncond_rows = lax.dynamic_slice_in_dim(uncond_all, side * half_len, half_len, 0)
    clip_half = lax.dynamic_slice_in_dim(slot_clip, side * half_len, half_len, 0)
    clip_pick = (clip_half[:, None] == jnp.arange(CLIPS, dtype=jnp.int32)[None, :]).astype(
        jnp.float32
    )
    strength = jnp.sum(clip_pick * guide_scale[None, :], axis=1)
    cond_float = cond_rows.astype(jnp.float32)
    uncond_float = uncond_rows.astype(jnp.float32)
    guided = uncond_float + strength[:, None] * (cond_float - uncond_float)
    guided = jnp.where((clip_half < CLIPS)[:, None], guided, 0.0).astype(jnp.bfloat16)
    seq_count = lax.axis_size("seq")
    capacity = max(2, slots // seq_count)
    owner_half = lax.dynamic_slice_in_dim(owner[:, 0], side * half_len, half_len, 0)
    owner_hot = (owner_half[:, None] == jnp.arange(seq_count, dtype=jnp.int32)[None, :]).astype(
        jnp.int32
    )
    rank = jnp.sum((jnp.cumsum(owner_hot, axis=0) - owner_hot) * owner_hot, axis=1)
    target = owner_half * capacity + rank
    placing = (
        jnp.arange(seq_count * capacity, dtype=jnp.int32)[:, None] == target[None, :]
    ).astype(jnp.bfloat16)
    outgoing = jnp.dot(placing, guided, preferred_element_type=jnp.float32).astype(jnp.bfloat16)
    outgoing = outgoing.reshape(seq_count, capacity, columns)
    arrived = lax.all_to_all(outgoing, "seq", split_axis=0, concat_axis=0, tiled=True)
    return arrived.reshape(1, seq_count * capacity, columns)


def solution(mesh):
    placed = (
        P("cfg", "seq", "blk"),
        P("cfg", "seq", "blk"),
        P("cfg", "seq", "blk"),
        P("cfg", "seq", None),
        P("blk", None),
        P(None, "blk"),
        P("blk", None),
        P(),
        P(),
        P("seq"),
        P("seq", None),
    )
    return jax.shard_map(
        shards, mesh=mesh, in_specs=placed, out_specs=P("cfg", "seq", "blk"), check_vma=False
    )
```

profile of v0, /device:TPU:0, one launch (start us, length us, event | category | flops | bytes accessed | tf_op | source)
XLA Modules:
  0.0 247.1 jit_solution(1570301492339026289)
XLA Ops:
  6.5 0.7 all-gather.8.cloned.1.call-update
  8.1 1.2 copy.42
  9.3 0.9 copy.44
  10.8 13.6 %all-gather.2 = s32[4,1,384]{2,1,0:T(1,128)S(1)} all-gather(s32[1,1,384]{2,1,0:T(1,128)S(1)} %reshape.132), channel_id=1, replica_groups=mesh['cfg'=2,'seq'=4,'blk'=4] {'seq'}, dimensions={0}, use_global_device_ids=true | all-gather | bytes 7680 | tf_op jit(solution)/shard_map/all_gather | solution.py:88
  25.1 1.2 broadcast_compare_fusion
  26.3 15.8 %all-gather.8.cloned.1.call-done = bf16[1,1536,384]{2,1,0:T(8,128)(2,1)} async-done(((bf16[1,384,384]{2,1,0:T(8,128)(2,1)}), bf16[1,1536,384]{2,1,0:T(8,128)(2,1)}) %all-gather.8.cloned.1.call-update) | async-done | bytes 1179664 | tf_op jit(solution)/shard_map/all_gather | solution.py:87
  42.1 31.2 %all-gather.6.cloned.1.call-done = bf16[1,1536,384]{2,1,0:T(8,128)(2,1)} async-done(((bf16[1,384,384]{2,1,0:T(8,128)(2,1)}), bf16[1,1536,384]{2,1,0:T(8,128)(2,1)}) %all-gather.6.cloned.1.call-update) | async-done | bytes 1179664 | tf_op jit(solution)/shard_map/all_gather | solution.py:86
  73.3 44.7 %while.15 = (s32[]{:T(128)}, f32[3,384]{1,0:T(4,128)S(1)}, f32[3,384]{1,0:T(4,128)}, f32[384,3,128]{0,2,1:T(8,128)}, s32[3,512]{1,0:T(4,128)}, /*index=5*/s32[38...) while((s32[]{:T(128)}, f32[3,384]{1,0:T(4,128)S(1)}, ...), condition=%wide.region_6.7_spmd.clone, body=%wide.region_3.6_spmd.clone.sunk | while | flops 309320448 | bytes 14176349 | solution.py:75
  73.3 0.7 constant_dynamic-slice_fusion.6
  74.0 1.6 compare_and_fusion.2
  75.5 2.0 constant_dynamic-slice_fusion.7
  77.5 0.9 copy.62
  78.4 2.4 fusion.90
  80.8 1.3 fusion.91
  82.1 1.9 copy.63
  84.0 2.7 %fusion.94 = f32[384,3,128]{0,2,1:T(8,128)} fusion(bf16[512,3,128]{0,2,1:T(8,128)(2,1)} %bitcast.122, f32[3,512,384]{2,1,0:T(8,128)S(1)} %get-tuple-element.233, f32[3,384]{1,0:T(4,128)S(1)} %get-tuple-element.261, pred[384,512]{0,1:T(8,128)(4,1)} %compare_and_fusion.2, f32[384,3,128]{0,2,1:T(8,128)} %get-tuple-element.251, ...), kind=kOutput, calls=%fused_computation.6.clone.1 | convolution fusion | flops 153796608 | bytes 4137985 | tf_op jit(solution)/shard_map/while/body/eval_jaxpr/hqk,khd->qhd/dot_general | solution.py:47
  88.7 1.6 compare_and_fusion.2
  90.3 2.0 constant_dynamic-slice_fusion.7
  92.2 0.9 copy.62
  93.2 2.4 fusion.90
  95.6 1.3 fusion.91
  96.9 1.9 copy.63
  98.8 2.9 %fusion.94 = f32[384,3,128]{0,2,1:T(8,128)} fusion(bf16[512,3,128]{0,2,1:T(8,128)(2,1)} %bitcast.122, f32[3,512,384]{2,1,0:T(8,128)S(1)} %get-tuple-element.233, f32[3,384]{1,0:T(4,128)S(1)} %get-tuple-element.261, pred[384,512]{0,1:T(8,128)(4,1)} %compare_and_fusion.2, f32[384,3,128]{0,2,1:T(8,128)} %get-tuple-element.251, ...), kind=kOutput, calls=%fused_computation.6.clone.1 | convolution fusion | flops 153796608 | bytes 4137985 | tf_op jit(solution)/shard_map/while/body/eval_jaxpr/hqk,khd->qhd/dot_general | solution.py:47
  103.7 1.6 compare_and_fusion.2
  105.3 2.0 constant_dynamic-slice_fusion.7
  107.2 0.9 copy.62
  108.2 2.4 fusion.90
  110.6 1.3 fusion.91
  111.9 1.9 copy.63
  113.8 2.9 %fusion.94 = f32[384,3,128]{0,2,1:T(8,128)} fusion(bf16[512,3,128]{0,2,1:T(8,128)(2,1)} %bitcast.122, f32[3,512,384]{2,1,0:T(8,128)S(1)} %get-tuple-element.233, f32[3,384]{1,0:T(4,128)S(1)} %get-tuple-element.261, pred[384,512]{0,1:T(8,128)(4,1)} %compare_and_fusion.2, f32[384,3,128]{0,2,1:T(8,128)} %get-tuple-element.251, ...), kind=kOutput, calls=%fused_computation.6.clone.1 | convolution fusion | flops 153796608 | bytes 4137985 | tf_op jit(solution)/shard_map/while/body/eval_jaxpr/hqk,khd->qhd/dot_general | solution.py:47
  118.0 1.1 broadcast_divide_fusion
  119.8 1.8 convolution_convert_fusion.1
  121.8 6.4 %fusion.54 = f32[384,4,1536]{2,0,1:T(8,128)} fusion(s32[384]{0:T(512)S(1)} %copy-done.4, f32[1,3,4,1536]{3,2,1,0:T(4,128)S(1)} %bitcast.132), kind=kOutput, calls=%fused_computation.73 | convolution fusion | flops 84935808 | bytes 9512448 | tf_op jit(solution)/shard_map/dot_general | solution.py:97
  128.2 47.2 %all-reduce.3.cloned.1.call-done = bf16[384,1536]{1,0:T(8,128)(2,1)} async-done(((bf16[384,1536]{1,0:T(8,128)(2,1)}), bf16[384,1536]{1,0:T(8,128)(2,1)}) %all-reduce.3.cloned.1.call-update) | async-done | bytes 1179664 | tf_op jit(solution)/shard_map/psum | solution.py:103
  175.4 2.8 %fusion.66 = (f32[384]{0:T(512)S(1)}, f32[384,1536]{1,0:T(8,128)S(1)}) fusion(bf16[384,1536]{1,0:T(8,128)(2,1)} %all-reduce.3.cloned.1.call-done, f32[384,4,1536]{2,0,1:T(8,128)} %fusion.54, bf16[1,384,1536]{2,1,0:T(8,128)(2,1)} %param.16), kind=kLoop, calls=%fused_computation.97 | loop fusion | flops 2948736 | bytes 7079424 | tf_op jit(solution)/shard_map/reduce_sum | solution.py:105
  178.6 10.1 %convolution_convert_fusion = bf16[384,1536]{1,0:T(8,128)(2,1)} fusion(bf16[1536,1536]{1,0:T(8,128)(2,1)} %param.19, bf16[1536,1536]{1,0:T(8,128)(2,1)} %param.18, f32[384,4,1536]{2,0,1:T(8,128)} %fusion.54, f32[384,1536]{1,0:T(8,128)S(1)} %get-tuple-element.158, f32[384]{0:T(512)S(1)} %add_rsqrt_fusion, f32[384]{0:T(512)S(1)} %broadcast_multiply_fusion), kind=kOutput, calls=%fused_computation.24 | convolution fusion | flops 3633315840 | bytes 17697792 | tf_op jit(solution)/shard_map/dot_general | solution.py:114
  188.7 2.4 copy.48
  191.2 1.2 reduce-window.6
  193.2 0.7 reduce-window.9
  194.4 0.8 copy.41
  195.9 0.7 select_reduce_fusion
  196.7 23.1 %reduce-scatter.4.cloned.1.call-done = bf16[384,384]{1,0:T(8,128)(2,1)} async-done(((bf16[1536,384]{1,0:T(8,128)(2,1)}), bf16[384,384]{1,0:T(8,128)(2,1)}) %reduce-scatter.4.cloned.1.call-update) | async-done | bytes 294928
  219.8 1.8 copy.49
  221.6 1.2 fusion.38
  223.0 1.5 collective-permute-done
  224.5 1.0 convolution_convert_fusion.2
  225.6 14.3 %all_to_all.5 = bf16[4,96,384]{2,1,0:T(8,128)(2,1)S(1)} all-to-all(bf16[4,96,384]{2,1,0:T(8,128)(2,1)S(1)} %bitcast.129), channel_id=1, replica_groups=mesh['cfg'=2,'seq'=4,'blk'=4] {'seq'}, dimensions={0} | all-to-all | bytes 589824 | tf_op jit(solution)/shard_map/all_to_all | solution.py:148
  239.8 0.7 copy.78
  (67 shorter events, 10.8 us)
Async XLA Ops:
  6.5 113.3 %copy-start = (bf16[384,1536]{1,0:T(8,128)(2,1)S(1)}, bf16[384,1536]{1,0:T(8,128)(2,1)}, u32[]{:S(2)}) copy-start(bf16[384,1536]{1,0:T(8,128)(2,1)} %param.17) | copy-start | bytes 3538948
  6.5 35.6 %all-gather.8.cloned.1.call-start = ((), (), s32[]{:S(2)}) async-start(), calls=%async_computation.4 | async-start | bytes 1474560 | tf_op jit(solution)/shard_map/all_gather | solution.py:87
  7.3 66.0 %all-gather.6.cloned.1.call-start = ((), (), s32[]{:S(2)}) async-start(), calls=%async_computation.3 | async-start | bytes 1474560 | tf_op jit(solution)/shard_map/all_gather | solution.py:86
  8.0 167.4 %all-reduce.3.cloned.1.call-start = ((), (), s32[]{:S(2)}) async-start(), calls=%async_computation.2 | async-start | bytes 2359296 | tf_op jit(solution)/shard_map/psum | solution.py:103
  84.0 2.7 %copy-start.1 = (pred[384,512]{0,1:T(8,128)(4,1)S(1)}, pred[384,512]{0,1:T(8,128)(4,1)}, u32[]{:S(2)}) copy-start(pred[384,512]{0,1:T(8,128)(4,1)} %compare_and_fusion.2) | copy-start | bytes 589828 | tf_op jit(solution)/shard_map/while
  86.7 0.7 copy-start.2
  87.4 0.6 copy-start.3
  98.8 2.9 %copy-start.1 = (pred[384,512]{0,1:T(8,128)(4,1)S(1)}, pred[384,512]{0,1:T(8,128)(4,1)}, u32[]{:S(2)}) copy-start(pred[384,512]{0,1:T(8,128)(4,1)} %compare_and_fusion.2) | copy-start | bytes 589828 | tf_op jit(solution)/shard_map/while
  101.7 0.7 copy-start.2
  102.4 0.6 copy-start.3
  113.8 2.9 %copy-start.1 = (pred[384,512]{0,1:T(8,128)(4,1)S(1)}, pred[384,512]{0,1:T(8,128)(4,1)}, u32[]{:S(2)}) copy-start(pred[384,512]{0,1:T(8,128)(4,1)} %compare_and_fusion.2) | copy-start | bytes 589828 | tf_op jit(solution)/shard_map/while
  116.7 0.7 copy-start.2
  117.4 0.6 copy-start.3
  119.1 2.6 %copy-start.4 = (s32[384]{0:T(512)S(1)}, s32[384]{0:T(512)}, u32[]{:S(2)}) copy-start(s32[384]{0:T(512)} %get-tuple-element.289) | copy-start | bytes 4612
  119.1 2.6 %copy-start.5 = (f32[3,4,1536]{2,1,0:T(4,128)S(1)}, f32[3,4,1536]{2,1,0:T(4,128)}, u32[]{:S(2)}) copy-start(f32[3,4,1536]{2,1,0:T(4,128)} %param.20) | copy-start | bytes 221188
  121.7 98.1 %reduce-scatter.4.cloned.1.call-start = ((), (), s32[]{:S(2)}) async-start(), calls=%async_computation.5 | async-start | bytes 1474560
  188.7 2.4 copy-start.6
  222.9 1.6 collective-permute-start
Sparse Core Ops, SparseCore 0:
  8.9 33.1 all-gather.7
  43.7 29.5 all-gather.5
  121.8 53.5 all-reduce.2
  191.2 28.5 reduce-scatter.3
where the time goes:
time: 248 us; the launch traced here: 247 us
  waiting for transfers between devices  120 us (48%)
  matrix products  35.1 us (14%)
  local copies, waits for them, and re-layouts  29.2 us (12%)
  blocking collectives  27.9 us (11%)
  other arithmetic  21.2 us (9%)
  between operations  13.3 us (5%)
    psum x1, waiting for transfers between devices, shards(): lax.psum(partial_out.astype(jnp.bfloat16), 'blk').astype(jnp.float32)  47.2 us
    all_gather x1, waiting for transfers between devices, shards(): lax.all_gather(keys[0], 'seq', axis=0, tiled=True)  31.2 us
    unnamed x5, waiting for transfers between devices  24.5 us
    dynamic_slice x12, local copies, waits for them, and re-layouts, absorb(): carry_out, unused = lax.scan(scan_step, carry, stacked)  16.5 us
    all_gather x1, waiting for transfers between devices, shards(): lax.all_gather(values[0], 'seq', axis=0, tiled=True)  15.8 us
    all_to_all x1, blocking collectives, shards(): lax.all_to_all(outgoing, 'seq', split_axis=0, concat_axis=0, tiled=True)  14.3 us
    all_gather x1, blocking collectives, shards(): lax.all_gather(slot_clip, 'seq', axis=0, tiled=True)  13.6 us
    dot_general x1, matrix products, shards(): terms = jnp.dot(hidden, w_down, preferred_element_type=jnp.float32)  10.1 us
  transfers between devices with their start and end apart: 5, of which 5 were waited for; matrix products, arithmetic and copies ran while one was open for 7% of the time, Pallas kernels for 0%

commit v1 on v0

v1 whole, which is shorter than its diff:
```python
import functools
import math

import jax
import jax.numpy as jnp
from jax import lax
from jax.experimental import pallas as pl
from jax.experimental.pallas import tpu as pltpu
from jax.sharding import PartitionSpec as P

D = 1536
HEAD_DIM = 128
CLIPS = 3
NEG_FILL = -1e30
FAR = 2.0**100
VMEM = pl.BlockSpec(memory_space=pltpu.VMEM)
ANY = pl.BlockSpec(memory_space=pl.ANY)
F32 = jnp.float32
BF16 = jnp.bfloat16


def shape_of(extent, dtype=BF16):
    return jax.ShapeDtypeStruct(extent, dtype)


def params(mib):
    return pltpu.CompilerParams(vmem_limit_bytes=mib * 2**20)


def head_at(side, place):
    return jnp.where(side == 0, place, 3 - place)


def works(side, place):
    return place < 3 if side == 0 else place >= 1


def hop(value, step, back=False):
    pairs = []
    for side in range(2):
        for place in range(4):
            target = (place + step) % 4
            if works(side, target):
                pair = (side * 4 + place, side * 4 + target)
                pairs.append(pair[::-1] if back else pair)
    return lax.ppermute(value, ("cfg", "seq"), pairs)


def pack_kernel(q_ref, k_ref, v_ref, clip_ref, *outs):
    side, place = lax.axis_index("cfg"), lax.axis_index("seq")
    slots = q_ref.shape[0]
    for step, out in enumerate(outs):
        head = jnp.clip(head_at(side, lax.rem(place + step, 4)), 0, 2)
        columns = pl.ds(pl.multiple_of(head * HEAD_DIM, HEAD_DIM), HEAD_DIM)
        for part, source in enumerate((q_ref, k_ref, v_ref)):
            out[part * slots : (part + 1) * slots, :] = source[:, columns]
        out[3 * slots :, :] = clip_ref[...]


def attend_kernel(*refs):
    blocks, outs, (q_aug, k_aug, v_aug, clips) = refs[:4], refs[4:8], refs[8:]
    slots = outs[0].shape[0]
    lane = lax.broadcasted_iota(jnp.int32, (128, 128), 1)
    row = lax.broadcasted_iota(jnp.int32, (128, 128), 0)
    eye = (lane == row).astype(BF16)
    for index, block in enumerate(blocks):
        base = index * slots
        here = slice(base, base + slots)
        q_aug[here, :128] = block[:slots, :]
        k_aug[here, :128] = block[slots : 2 * slots, :]
        v_aug[here, :128] = block[2 * slots : 3 * slots, :]
        turned = lax.dot_general(
            eye, block[3 * slots :, :], (((1,), (1,)), ((), ())), preferred_element_type=F32
        )
        for group in range(slots // 128):
            part = slice(base + group * 128, base + (group + 1) * 128)
            clip = jnp.broadcast_to(turned[:, group : group + 1], (128, 128)).astype(jnp.int32)
            clips[part, :] = clip
            same = lane == clip
            kept = same & (clip < CLIPS)
            k_aug[part, 128:] = same.astype(BF16)
            q_aug[part, 128:] = jnp.where(kept | (lane > CLIPS), 0.0, -FAR).astype(BF16)
            v_aug[part, 128:] = (lane == 0).astype(BF16)
    scale = math.log2(math.e) / math.sqrt(HEAD_DIM)
    for index, out in enumerate(outs):
        here = slice(index * slots, (index + 1) * slots)
        scores = lax.dot_general(
            q_aug[here, :], k_aug[...], (((1,), (1,)), ((), ())), preferred_element_type=F32
        )
        peak = jnp.max(scores, axis=1, keepdims=True)
        probs = jnp.exp2((scores - peak) * scale).astype(BF16)
        summed = jnp.dot(probs, v_aug[...], preferred_element_type=F32)
        result = summed[:, :128] / summed[:, 128:129]
        out[...] = jnp.where(clips[here, :] < CLIPS, result, 0.0).astype(BF16)


def regroup_kernel(own, back1, back2, back3, first, second):
    side, place = lax.axis_index("cfg"), lax.axis_index("seq")
    half = first.shape[0]
    for head in range(3):
        home = jnp.where(side == 0, head, 3 - head)
        step = lax.rem(home - place + 4, 4)
        columns = slice(head * HEAD_DIM, (head + 1) * HEAD_DIM)
        for index, source in enumerate((own, back1, back2, back3)):

            @pl.when(step == index)
            def _():
                for out, which in ((first, 1 - side), (second, side)):
                    rows = pl.ds(pl.multiple_of(which * half, half), half)
                    out[:, columns] = source[rows, :]


def attention_by_head(query, key, value, slot_clip):
    slots = query.shape[0]
    clip_rows = jnp.pad(slot_clip.reshape(slots // 128, 128), ((0, 16 - slots // 128), (0, 0)))
    packed = pl.pallas_call(
        pack_kernel,
        out_shape=[shape_of((3 * slots + 16, 128))] * 4,
        in_specs=[VMEM] * 4,
        out_specs=[VMEM] * 4,
        compiler_params=params(16),
        name="pack",
    )(query, key, value, clip_rows.astype(BF16))
    blocks = [packed[0]] + [hop(packed[step], step) for step in (1, 2, 3)]
    results = pl.pallas_call(
        attend_kernel,
        out_shape=[shape_of((slots, 128))] * 4,
        in_specs=[VMEM] * 4,
        out_specs=[VMEM] * 4,
        scratch_shapes=[pltpu.VMEM((4 * slots, 256), BF16)] * 3
        + [pltpu.VMEM((4 * slots, 128), jnp.int32)],
        compiler_params=params(32),
        name="attend",
    )(*blocks)
    backs = [hop(results[step], step, back=True) for step in (1, 2, 3)]
    half = slots // 2
    return pl.pallas_call(
        regroup_kernel,
        out_shape=[shape_of((half, 3 * HEAD_DIM))] * 2,
        in_specs=[VMEM] * 4,
        out_specs=[VMEM] * 2,
        compiler_params=params(16),
        name="regroup",
    )(results[0], *backs)


def attention_by_rows(query, key, value, slot_clip):
    slots, width = query.shape
    heads = width // HEAD_DIM
    live = slot_clip < CLIPS
    factor = 1.0 / math.sqrt(HEAD_DIM)
    query_heads = query.reshape(slots, heads, HEAD_DIM)

    def absorb(carry, piece):
        key_piece, value_piece, clip_piece = piece
        best, total, accum = carry
        kept = (clip_piece[None, :] == slot_clip[:, None]) & live[:, None]
        scores = jnp.einsum("qhd,khd->hqk", query_heads, key_piece, preferred_element_type=F32)
        scores = jnp.where(kept[None], scores * factor, NEG_FILL)
        new_best = jnp.maximum(best, jnp.max(scores, axis=-1))
        fade = jnp.exp(best - new_best)
        probs = jnp.exp(scores - new_best[..., None])
        total = total * fade + jnp.sum(probs, axis=-1)
        added = jnp.einsum(
            "hqk,khd->qhd", probs.astype(BF16), value_piece, preferred_element_type=F32
        )
        accum = accum * jnp.transpose(fade)[:, :, None] + added
        return (new_best, total, accum), None

    start = (
        jnp.full((heads, slots), NEG_FILL, F32),
        jnp.zeros((heads, slots), F32),
        jnp.zeros((slots, heads, HEAD_DIM), F32),
    )
    pieces = (
        lax.all_gather(key, "seq").reshape(-1, slots, heads, HEAD_DIM),
        lax.all_gather(value, "seq").reshape(-1, slots, heads, HEAD_DIM),
        lax.all_gather(slot_clip, "seq"),
    )
    (best, total, accum), _ = lax.scan(absorb, start, pieces)
    attended = (accum / jnp.transpose(total)[:, :, None]).reshape(slots, width)
    attended = jnp.where(live[:, None], attended, 0.0).astype(BF16)
    half = slots // 2
    side = lax.axis_index("cfg")
    return [
        lax.dynamic_slice_in_dim(attended, which * half, half, 0) for which in (1 - side, side)
    ]


def feed_kernel(turn, *refs):
    (att, (w_own, *w_got), (up_hbm, down_hbm, res_hbm, mod, clip_ref)) = (
        refs[:4],
        refs[4:11],
        refs[11:16],
    )
    out = refs[16]
    rows_in, w_out, up, down, res, mixed, total, normed, hidden, sems = refs[17:]
    side, blk = lax.axis_index("cfg"), lax.axis_index("blk")
    half = out.shape[0]
    which = 1 - side if turn == 0 else side
    rows = pl.ds(pl.multiple_of(which * half, half), half)
    width = att[0].shape[1]
    part = width // 2
    first = []
    for step in range(4):
        first.append((att[step], rows_in.at[:, step * width : (step + 1) * width]))
    first.append((w_own, w_out.at[0:width, :]))
    for step in range(1, 4):
        for piece, where in ((w_got[step - 1], side), (w_got[step + 2], 1 - side)):
            offset = pl.multiple_of(step * width + where * part, part)
            first.append((piece, w_out.at[pl.ds(offset, part), :]))
    first.append((res_hbm.at[rows, :], res))
    plan = first + [(up_hbm, up), (down_hbm, down)]
    copies = [
        pltpu.make_async_copy(source, target, sems.at[index])
        for index, (source, target) in enumerate(plan)
    ]
    for copy in copies:
        copy.start()
    clip = clip_ref[rows, :][:, :1]
    tile = 512

    def chosen(kind, columns):
        picked = jnp.zeros((half, tile), F32)
        for index in range(CLIPS):
            line = mod[index * 4 + kind : index * 4 + kind + 1, columns]
            picked = jnp.where(clip == index, line, picked)
        return picked

    for copy in copies[:-2]:
        copy.wait()
    for start in range(0, D, tile):
        columns = slice(start, start + tile)
        projected = jnp.dot(rows_in[...], w_out[:, columns], preferred_element_type=F32)
        mixed[:, columns] = res[:, columns].astype(F32) + chosen(0, columns) * projected
    held = mixed[...]
    centre = held - jnp.mean(held, axis=1, keepdims=True)
    spread = lax.rsqrt(jnp.mean(centre * centre, axis=1, keepdims=True) + 1e-06)
    for start in range(0, D, tile):
        columns = slice(start, start + tile)
        value = centre[:, columns] * spread * (1.0 + chosen(2, columns)) + chosen(1, columns)
        normed[:, columns] = value.astype(BF16)
    copies[-2].wait()
    for start in range(0, D, tile):
        columns = slice(start, start + tile)
        raised = jnp.dot(normed[...], up[:, columns], preferred_element_type=F32)
        hidden[:, columns] = jax.nn.gelu(raised, approximate=True).astype(BF16)
    copies[-1].wait()
    for start in range(0, D, tile):
        columns = slice(start, start + tile)
        lowered = jnp.dot(hidden[...], down[:, columns], preferred_element_type=F32)
        total[:, columns] = chosen(3, columns) * lowered
    own = pl.ds(pl.multiple_of(blk * width, width), width)
    total[:, own] = total[:, own] + mixed[:, own]
    out[...] = total[...].astype(out.dtype)


def feed(turn, att, w_parts, w_up, w_down, residual, mod, clip_wide):
    half, width = att[0].shape
    return pl.pallas_call(
        functools.partial(feed_kernel, turn),
        out_shape=shape_of((half, D), BF16 if turn == 0 else F32),
        in_specs=[ANY] * 14 + [VMEM] * 2,
        out_specs=VMEM,
        scratch_shapes=[
            pltpu.VMEM((half, D), BF16),
            pltpu.VMEM((D, D), BF16),
            pltpu.VMEM((D, D), BF16),
            pltpu.VMEM((D, D), BF16),
            pltpu.VMEM((half, D), BF16),
            pltpu.VMEM((half, D), F32),
            pltpu.VMEM((half, D), F32),
            pltpu.VMEM((half, D), BF16),
            pltpu.VMEM((half, D), BF16),
            pltpu.SemaphoreType.DMA((14,)),
        ],
        compiler_params=params(40),
        name="feed",
    )(*att, *w_parts, w_up, w_down, residual, mod, clip_wide)


def guide_kernel(mine_ref, other_ref, strength_ref, own, *sent):
    side, blk = lax.axis_index("cfg"), lax.axis_index("blk")
    width = own.shape[1]
    strength = strength_ref[:, :1]
    lean = jnp.where(side == 0, strength, 1.0 - strength)
    for step, out in enumerate((own, *sent)):
        target = jnp.bitwise_xor(blk, step)
        columns = pl.ds(pl.multiple_of(target * width, width), width)
        other = other_ref[:, columns].astype(F32)
        guided = other + lean * (mine_ref[:, columns] - other)
        out[...] = guided.astype(out.dtype)


def place_kernel(own, got1, got2, got3, placing, *outs):
    guided = own[...] + got1[...].astype(F32) + got2[...].astype(F32) + got3[...].astype(F32)
    placed = jnp.dot(placing[...], guided.astype(BF16), preferred_element_type=F32).astype(BF16)
    if len(outs) == 1:
        outs[0][...] = placed
    else:
        count = outs[0].shape[0]
        for index, out in enumerate(outs):
            out[...] = placed[index * count : (index + 1) * count, :]


def arrange_kernel(own, got1, got2, got3, out):
    place = lax.axis_index("seq")
    count = own.shape[0]
    for step, source in enumerate((own, got1, got2, got3)):
        origin = lax.rem(place + 4 - step, 4)
        out[pl.ds(pl.multiple_of(origin * count, count), count), :] = source[...]


def exchanged(value, axis, mask):
    pairs = [(index, index ^ mask) for index in range(lax.axis_size(axis))]
    return lax.ppermute(value, axis, pairs)


def shards(
    queries, keys, values, residual, w_out, w_up, w_down, modulation, guide_scale, slot_clip, owner
):
    slots, width = queries.shape[1:]
    half = slots // 2
    seq_count = lax.axis_size("seq")
    capacity = max(2, slots // seq_count)
    side, place = lax.axis_index("cfg"), lax.axis_index("seq")

    if seq_count == 4:
        attended = attention_by_head(queries[0], keys[0], values[0], slot_clip)
    else:
        attended = attention_by_rows(queries[0], keys[0], values[0], slot_clip)

    w_half = lax.dynamic_slice_in_dim(w_out, side * (width // 2), width // 2, 0)
    w_got = [exchanged(w_half, "blk", mask) for mask in (1, 2, 3)]
    w_parts = [w_out] + w_got + [exchanged(piece, "cfg", 1) for piece in w_got]

    clip_wide = jnp.broadcast_to(slot_clip[:, None], (slots, 128))
    mod = modulation.reshape(CLIPS * 4, D)
    clip_half = lax.dynamic_slice_in_dim(slot_clip, side * half, half, 0)
    strength = jnp.zeros((half,), F32)
    for index in range(CLIPS):
        strength = jnp.where(clip_half == index, guide_scale[index], strength)
    strength = jnp.broadcast_to(strength[:, None], (half, 128))
    owner_half = lax.dynamic_slice_in_dim(owner[:, 0], side * half, half, 0)
    order = jnp.arange(half, dtype=jnp.int32)
    before = (owner_half[None, :] == owner_half[:, None]) & (order[None, :] < order[:, None])
    rank = jnp.sum(before.astype(jnp.int32), axis=1)
    if seq_count == 4:
        lane = lax.rem(owner_half - place + seq_count, seq_count)
    else:
        lane = owner_half
    target = jnp.where(clip_half < CLIPS, lane * capacity + rank, -1)
    placing = (
        jnp.arange(seq_count * capacity, dtype=jnp.int32)[:, None] == target[None, :]
    ).astype(BF16)

    parts = []
    for turn in range(2):
        piece = attended[turn]
        gathered = [piece] + [exchanged(piece, "blk", mask) for mask in (1, 2, 3)]
        parts.append(feed(turn, gathered, w_parts, w_up, w_down, residual[0], mod, clip_wide))
    other = exchanged(parts[0], "cfg", 1)
    own, *sent = pl.pallas_call(
        guide_kernel,
        out_shape=[shape_of((half, width), F32)] + [shape_of((half, width))] * 3,
        in_specs=[VMEM] * 3,
        out_specs=[VMEM] * 4,
        compiler_params=params(16),
        name="guide",
    )(parts[1], other, strength)
    got = [exchanged(piece, "blk", mask) for mask, piece in zip((1, 2, 3), sent)]
    by_step = seq_count == 4
    placed = pl.pallas_call(
        place_kernel,
        out_shape=[shape_of((capacity, width))] * 4
        if by_step
        else [shape_of((seq_count * capacity, width))],
        in_specs=[VMEM] * 5,
        out_specs=[VMEM] * (4 if by_step else 1),
        compiler_params=params(16),
        name="place",
    )(own, *got, placing)
    if not by_step:
        arrived = lax.all_to_all(
            placed[0].reshape(seq_count, capacity, width), "seq", split_axis=0, concat_axis=0,
            tiled=True,
        )
        return arrived.reshape(1, seq_count * capacity, width)
    home = [
        lax.ppermute(placed[step], "seq", [(i, (i + step) % 4) for i in range(4)])
        for step in (1, 2, 3)
    ]
    arranged = pl.pallas_call(
        arrange_kernel,
        out_shape=shape_of((4 * capacity, width)),
        in_specs=[VMEM] * 4,
        out_specs=VMEM,
        compiler_params=params(16),
        name="arrange",
    )(placed[0], *home)
    return arranged[None]


def solution(mesh):
    placed = (
        P("cfg", "seq", "blk"),
        P("cfg", "seq", "blk"),
        P("cfg", "seq", "blk"),
        P("cfg", "seq", None),
        P("blk", None),
        P(None, "blk"),
        P("blk", None),
        P(),
        P(),
        P("seq"),
        P("seq", None),
    )
    return jax.shard_map(
        shards, mesh=mesh, in_specs=placed, out_specs=P("cfg", "seq", "blk"), check_vma=False
    )
```

time: 248 us -> 125 us (0.50)
  waiting for transfers between devices: 120 us -> 44.2 us
  starting transfers between devices: 0.19 us -> 41.2 us
  matrix products: 35.1 us -> 0 us
  blocking collectives: 27.9 us -> 0 us
  Pallas kernels: 0 us -> 22 us
  other arithmetic: 21.2 us -> 2.32 us
  local copies, waits for them, and re-layouts: 29.2 us -> 14.3 us
  between operations: 13.3 us -> 0.3 us
    psum x1 -> x0, waiting for transfers between devices: 47.2 us -> none  [shards(): lax.psum(partial_out.astype(jnp.bfloat16), 'blk').astype(jnp.float32)]
    all_gather x2 -> x0, waiting for transfers between devices: 47 us -> none  [the longest x1 31.2 us: shards(): lax.all_gather(keys[0], 'seq', axis=0, tiled=True)]
    ppermute x1 -> x25, waiting for transfers between devices: 1.53 us -> 44.2 us  [the longest x16 29.5 us: exchanged(): return lax.ppermute(value, axis, pairs)]
    ppermute x1 -> x25, starting transfers between devices: 0.07 us -> 41.2 us  [the longest x6 19.6 us: hop(): return lax.ppermute(value, ('cfg', 'seq'), pairs)]
    dot_general x10 -> x0, matrix products: 35.1 us -> none  [the longest x1 10.1 us: shards(): terms = jnp.dot(hidden, w_down, preferred_element_type=jnp.float32)]
    unnamed x5 -> x0, waiting for transfers between devices: 24.5 us -> none
    pallas_call x0 -> x8, Pallas kernels: none -> 22 us  [the longest x2 14.4 us: feed(): pl.pallas_call(functools.partial(feed_kernel, turn), out_shape=shape_of((...]
    dynamic_slice x13 -> x2, local copies, waits for them, and re-layouts: 16.6 us -> 1.27 us  [the longest x1 1.19 us: shards(): w_half = lax.dynamic_slice_in_dim(w_out, side * (width // 2), width // 2, 0)]
  transfers between devices with their start and end apart: 5 -> 25, of which waited for: 5 -> 14; matrix products, arithmetic and copies ran while one was open for 7% -> 4% of each run, Pallas kernels for 0% -> 10%
where the time goes in v1:
time: 125 us; the launch traced here: 124 us
  waiting for transfers between devices  44.2 us (35%)
  starting transfers between devices  41.2 us (33%)
  Pallas kernels  22 us (18%)
  local copies, waits for them, and re-layouts  14.3 us (11%)
  other arithmetic  2.32 us (2%)
    ppermute x16, waiting for transfers between devices, exchanged(): return lax.ppermute(value, axis, pairs)  29.5 us
    ppermute x6, starting transfers between devices, hop(): return lax.ppermute(value, ('cfg', 'seq'), pairs)  19.6 us
    ppermute x16, starting transfers between devices, exchanged(): return lax.ppermute(value, axis, pairs)  16.5 us
    pallas_call x2, Pallas kernels, feed(): pl.pallas_call(functools.partial(feed_kernel, turn), out_shape=shape_of((...  14.4 us
    ppermute x6, waiting for transfers between devices, hop(): return lax.ppermute(value, ('cfg', 'seq'), pairs)  11.2 us
    unnamed x36, local copies, waits for them, and re-layouts  10.6 us
    ppermute x3, starting transfers between devices, shards(): lax.ppermute(placed[step], 'seq', [(i, (i + step) % 4) for i in range(4)])  5.07 us
    pallas_call x1, Pallas kernels, attention_by_head(): pl.pallas_call(attend_kernel, out_shape=[shape_of((slots, 128))] * 4, in_...  4.01 us
  transfers between devices with their start and end apart: 25, of which 14 were waited for; matrix products, arithmetic and copies ran while one was open for 4% of the time, Pallas kernels for 10%

profile of v1, /device:TPU:0, one launch (start us, length us, event | category | flops | bytes accessed | tf_op | source)
XLA Modules:
  0.0 124.2 jit_solution(9484467817279919974)
XLA Ops:
  0.0 1.2 constant_dynamic-slice_fusion.1
  1.2 3.0 %collective-permute-start.9 = (bf16[192,1536]{1,0:T(8,128)(2,1)S(1)}, bf16[192,1536]{1,0:T(8,128)(2,1)S(1)}, u32[]{:S(2)}, u32[]{:S(2)}) collective-permute-start(bf16[192,1536]{1,0:T(8,128)(2,1)S(1)} %constant_dynamic-slice_fusion.1), channel_id=1, source_target_pairs={{0,1},{1,0},{2,3},{3,2},{4,5},{5,4},{6,7},{7,6},{8,9},{9,8},{10,11... | collective-permute-start | bytes 1769480 | tf_op jit(solution)/shard_map/ppermute | solution.py:316
  4.2 1.5 %collective-permute-start.10 = (bf16[192,1536]{1,0:T(8,128)(2,1)S(1)}, bf16[192,1536]{1,0:T(8,128)(2,1)S(1)}, u32[]{:S(2)}, u32[]{:S(2)}) collective-permute-start(bf16[192,1536]{1,0:T(8,128)(2,1)S(1)} %constant_dynamic-slice_fusion.1), channel_id=1, source_target_pairs={{0,2},{1,3},{2,0},{3,1},{4,6},{5,7},{6,4},{7,5},{8,10},{9,11},{10,... | collective-permute-start | bytes 1769480 | tf_op jit(solution)/shard_map/ppermute | solution.py:316
  6.1 4.1 %collective-permute-start = (bf16[1168,128]{1,0:T(8,128)(2,1)S(1)}, bf16[1168,128]{1,0:T(8,128)(2,1)S(1)}, u32[]{:S(2)}, u32[]{:S(2)}) collective-permute-start(bf16[1168,128]{1,0:T(8,128)(2,1)S(1)} %get-tuple-element.24), channel_id=1, source_target_pairs={{0,4},{4,8},{12,0},{16,20},{20,24},{24,28},{1,5},{5,9},{13,1},{17,... | collective-permute-start | bytes 897032 | tf_op jit(solution)/shard_map/ppermute | solution.py:46
  10.2 2.3 %collective-permute-start.1 = (bf16[1168,128]{1,0:T(8,128)(2,1)S(1)}, bf16[1168,128]{1,0:T(8,128)(2,1)S(1)}, u32[]{:S(2)}, u32[]{:S(2)}) collective-permute-start(bf16[1168,128]{1,0:T(8,128)(2,1)S(1)} %get-tuple-element.25), channel_id=1, source_target_pairs={{0,8},{8,0},{12,4},{16,24},{20,28},{28,20},{1,9},{9,1},{13,5},{17,... | collective-permute-start | bytes 897032 | tf_op jit(solution)/shard_map/ppermute | solution.py:46
  12.5 5.6 %collective-permute-done.refs_1_ = bf16[1168,128]{1,0:T(8,128)(2,1)S(1)} collective-permute-done((bf16[1168,128]{1,0:T(8,128)(2,1)S(1)}, bf16[1168,128]{1,0:T(8,128)(2,1)S(1)}, u32[]{:S(2)}, u32[]{:S(2)}) %collective-permute-start) | collective-permute-done | bytes 299040 | tf_op jit(solution)/shard_map/ppermute | solution.py:46
  18.1 1.3 %collective-permute-start.2 = (bf16[1168,128]{1,0:T(8,128)(2,1)S(1)}, bf16[1168,128]{1,0:T(8,128)(2,1)S(1)}, u32[]{:S(2)}, u32[]{:S(2)}) collective-permute-start(bf16[1168,128]{1,0:T(8,128)(2,1)S(1)} %get-tuple-element.26), channel_id=1, source_target_pairs={{4,0},{8,4},{12,8},{16,28},{24,20},{28,24},{5,1},{9,5},{13,9},{17,... | collective-permute-start | bytes 897032 | tf_op jit(solution)/shard_map/ppermute | solution.py:46
  19.5 12.2 %collective-permute-done.10.refs_6_ = bf16[192,1536]{1,0:T(8,128)(2,1)S(1)} collective-permute-done((bf16[192,1536]{1,0:T(8,128)(2,1)S(1)}, bf16[192,1536]{1,0:T(8,128)(2,1)S(1)}, u32[]{:S(2)}, u32[]{:S(2)}) %collective-permute-start.10) | collective-permute-done | bytes 589856 | tf_op jit(solution)/shard_map/ppermute | solution.py:316
  32.2 3.3 %collective-permute-done.2.refs_3_ = bf16[1168,128]{1,0:T(8,128)(2,1)S(1)} collective-permute-done((bf16[1168,128]{1,0:T(8,128)(2,1)S(1)}, bf16[1168,128]{1,0:T(8,128)(2,1)S(1)}, u32[]{:S(2)}, u32[]{:S(2)}) %collective-permute-start.2) | collective-permute-done | bytes 299040 | tf_op jit(solution)/shard_map/ppermute | solution.py:46
  35.5 4.0 %attend.1 = (bf16[384,128]{1,0:T(8,128)(2,1)S(1)}, bf16[384,128]{1,0:T(8,128)(2,1)S(1)}, bf16[384,128]{1,0:T(8,128)(2,1)S(1)}, bf16[384,128]{1,0:T(8,128)(2,1)S(1)}) custom-call(bf16[1168,128]{1,0:T(8,128)(2,1)S(1)} %get-tuple-element.23.refs_0_, bf16[1168,128]{1,0:T(8,128)(2,1)S(1)} %collective-permute-done.refs_1_, ...), custom_call_target="tpu_custom_call" | custom-call | tf_op jit(solution)/shard_map/attend/pallas_call | solution.py:125
  39.5 4.8 %collective-permute-start.3 = (bf16[384,128]{1,0:T(8,128)(2,1)S(1)}, bf16[384,128]{1,0:T(8,128)(2,1)S(1)}, u32[]{:S(2)}, u32[]{:S(2)}) collective-permute-start(bf16[384,128]{1,0:T(8,128)(2,1)S(1)} %get-tuple-element.28), channel_id=1, source_target_pairs={{4,0},{8,4},{0,12},{20,16},{24,20},{28,24},{5,1},{9,5},{1,13},{21,... | collective-permute-start | bytes 294920 | tf_op jit(solution)/shard_map/ppermute | solution.py:46
  44.4 2.9 %collective-permute-start.4 = (bf16[384,128]{1,0:T(8,128)(2,1)S(1)}, bf16[384,128]{1,0:T(8,128)(2,1)S(1)}, u32[]{:S(2)}, u32[]{:S(2)}) collective-permute-start(bf16[384,128]{1,0:T(8,128)(2,1)S(1)} %get-tuple-element.29), channel_id=1, source_target_pairs={{8,0},{0,8},{4,12},{24,16},{28,20},{20,28},{9,1},{1,9},{5,13},{25,... | collective-permute-start | bytes 294920 | tf_op jit(solution)/shard_map/ppermute | solution.py:46
  47.3 4.2 %collective-permute-start.5 = (bf16[384,128]{1,0:T(8,128)(2,1)S(1)}, bf16[384,128]{1,0:T(8,128)(2,1)S(1)}, u32[]{:S(2)}, u32[]{:S(2)}) collective-permute-start(bf16[384,128]{1,0:T(8,128)(2,1)S(1)} %get-tuple-element.30), channel_id=1, source_target_pairs={{0,4},{4,8},{8,12},{28,16},{20,24},{24,28},{1,5},{5,9},{9,13},{29,... | collective-permute-start | bytes 294920 | tf_op jit(solution)/shard_map/ppermute | solution.py:46
  51.8 1.9 %collective-permute-done.5.back3 = bf16[384,128]{1,0:T(8,128)(2,1)S(1)} collective-permute-done((bf16[384,128]{1,0:T(8,128)(2,1)S(1)}, bf16[384,128]{1,0:T(8,128)(2,1)S(1)}, u32[]{:S(2)}, u32[]{:S(2)}) %collective-permute-start.5) | collective-permute-done | bytes 98336 | tf_op jit(solution)/shard_map/ppermute | solution.py:46
  53.7 1.0 regroup.1
  55.3 1.5 %collective-permute-start.15 = (bf16[192,384]{1,0:T(8,128)(2,1)}, bf16[192,384]{1,0:T(8,128)(2,1)S(1)}, u32[]{:S(2)}, u32[]{:S(2)}) collective-permute-start(bf16[192,384]{1,0:T(8,128)(2,1)} %get-tuple-element.32.refs_0_), channel_id=1, source_target_pairs={{0,1},{1,0},{2,3},{3,2},{4,5},{5,4},{6,7},{7,6},{8,9},{9,8},{10,11... | collective-permute-start | bytes 442376 | tf_op jit(solution)/shard_map/ppermute | solution.py:316
  56.8 1.5 %collective-permute-start.16 = (bf16[192,384]{1,0:T(8,128)(2,1)}, bf16[192,384]{1,0:T(8,128)(2,1)}, u32[]{:S(2)}, u32[]{:S(2)}) collective-permute-start(bf16[192,384]{1,0:T(8,128)(2,1)} %get-tuple-element.32.refs_0_), channel_id=1, source_target_pairs={{0,2},{1,3},{2,0},{3,1},{4,6},{5,7},{6,4},{7,5},{8,10},{9,11},{10,... | collective-permute-start | bytes 442376 | tf_op jit(solution)/shard_map/ppermute | solution.py:316
  58.3 3.9 %collective-permute-done.15.refs_1_ = bf16[192,384]{1,0:T(8,128)(2,1)S(1)} collective-permute-done((bf16[192,384]{1,0:T(8,128)(2,1)}, bf16[192,384]{1,0:T(8,128)(2,1)S(1)}, u32[]{:S(2)}, u32[]{:S(2)}) %collective-permute-start.15) | collective-permute-done | bytes 147488 | tf_op jit(solution)/shard_map/ppermute | solution.py:316
  62.2 0.7 copy-done.14
  62.8 1.3 %collective-permute-start.17 = (bf16[192,384]{1,0:T(8,128)(2,1)}, bf16[192,384]{1,0:T(8,128)(2,1)}, u32[]{:S(2)}, u32[]{:S(2)}) collective-permute-start(bf16[192,384]{1,0:T(8,128)(2,1)} %get-tuple-element.32.refs_0_), channel_id=1, source_target_pairs={{0,3},{1,2},{2,1},{3,0},{4,7},{5,6},{6,5},{7,4},{8,11},{9,10},{10,... | collective-permute-start | bytes 442376 | tf_op jit(solution)/shard_map/ppermute | solution.py:316
  64.1 1.5 %reshape.15.refs_14_ = f32[12,1536]{1,0:T(8,128)} reshape(f32[3,4,1536]{2,1,0:T(4,128)} %param.18) | data formatting | bytes 147456 | tf_op jit(solution)/shard_map/reshape | solution.py:338
  65.7 3.5 %collective-permute-done.17.refs_3_ = bf16[192,384]{1,0:T(8,128)(2,1)} collective-permute-done((bf16[192,384]{1,0:T(8,128)(2,1)}, bf16[192,384]{1,0:T(8,128)(2,1)}, u32[]{:S(2)}, u32[]{:S(2)}) %collective-permute-start.17) | collective-permute-done | bytes 147488 | tf_op jit(solution)/shard_map/ppermute | solution.py:316
  69.4 2.4 %copy-done.1 = bf16[1536,1536]{1,0:T(8,128)(2,1)S(1)} copy-done((bf16[1536,1536]{1,0:T(8,128)(2,1)S(1)}, bf16[1536,1536]{1,0:T(8,128)(2,1)}, u32[]{:S(2)}) %copy-start.1) | copy-done | bytes 4718616
  71.8 0.9 copy-done.7
  72.7 0.9 copy-done.15
  73.6 7.6 %feed.3 = bf16[192,1536]{1,0:T(8,128)(2,1)} custom-call(bf16[192,384]{1,0:T(8,128)(2,1)} %get-tuple-element.32.refs_0_, bf16[192,384]{1,0:T(8,128)(2,1)S(1)} %copy-done.15, bf16[192,384]{1,0:T(8,128)(2,1)} %collective-permute-done.16.refs_2_, bf16[192,384]{1,0:T(8,128)(2,1)} %collective-permute-done.17.refs_3_, bf16[384,1536]{1,0:T(8,128)(2,1)S(1)} %copy-done.3, ...), custom_call_target="tpu_custom_call" | custom-call | tf_op jit(solution)/shard_map/feed/pallas_call | solution.py:260
  82.1 1.3 %collective-permute-start.7 = (bf16[192,384]{1,0:T(8,128)(2,1)}, bf16[192,384]{1,0:T(8,128)(2,1)S(1)}, u32[]{:S(2)}, u32[]{:S(2)}) collective-permute-start(bf16[192,384]{1,0:T(8,128)(2,1)} %copy-done.12), channel_id=1, source_target_pairs={{0,2},{1,3},{2,0},{3,1},{4,6},{5,7},{6,4},{7,5},{8,10},{9,11},{10,... | collective-permute-start | bytes 442376 | tf_op jit(solution)/shard_map/ppermute | solution.py:316
  83.4 1.7 %collective-permute-start.8 = (bf16[192,384]{1,0:T(8,128)(2,1)}, bf16[192,384]{1,0:T(8,128)(2,1)S(1)}, u32[]{:S(2)}, u32[]{:S(2)}) collective-permute-start(bf16[192,384]{1,0:T(8,128)(2,1)} %copy-done.12), channel_id=1, source_target_pairs={{0,3},{1,2},{2,1},{3,0},{4,7},{5,6},{6,5},{7,4},{8,11},{9,10},{10,... | collective-permute-start | bytes 442376 | tf_op jit(solution)/shard_map/ppermute | solution.py:316
  85.1 0.6 fusion.5
  85.7 2.0 %compare_select_fusion.5 = f32[192]{0:T(256)S(1)} fusion(s32[384]{0:T(512)S(1)} %copy-done.16, s32[]{:T(128)S(6)} %select_n.19, f32[]{:T(128)} %bitcast.7, f32[]{:T(128)} %bitcast.6, f32[]{:T(128)} %bitcast.5), kind=kLoop, calls=%fused_computation.10 | loop fusion | flops 1152 | bytes 1552 | tf_op jit(solution)/shard_map/jit(_where)/select_n | solution.py:342
  87.7 0.7 collective-permute-done.6.refs_1_
  88.5 3.0 %collective-permute-done.7.refs_2_ = bf16[192,384]{1,0:T(8,128)(2,1)S(1)} collective-permute-done((bf16[192,384]{1,0:T(8,128)(2,1)}, bf16[192,384]{1,0:T(8,128)(2,1)S(1)}, u32[]{:S(2)}, u32[]{:S(2)}) %collective-permute-start.7) | collective-permute-done | bytes 147488 | tf_op jit(solution)/shard_map/ppermute | solution.py:316
  91.5 2.3 %copy-done.2 = bf16[1536,1536]{1,0:T(8,128)(2,1)S(1)} copy-done((bf16[1536,1536]{1,0:T(8,128)(2,1)S(1)}, bf16[1536,1536]{1,0:T(8,128)(2,1)}, u32[]{:S(2)}) %copy-start.2) | copy-done | bytes 4718616
  93.8 0.9 copy-done.6
  94.7 0.9 copy-done.8
  95.6 0.9 copy-done.13
  96.5 6.8 %feed.2.mine_ref = f32[192,1536]{1,0:T(8,128)S(1)} custom-call(bf16[192,384]{1,0:T(8,128)(2,1)S(1)} %copy-done.13, bf16[192,384]{1,0:T(8,128)(2,1)S(1)} %collective-permute-done.6.refs_1_, bf16[192,384]{1,0:T(8,128)(2,1)S(1)} %collective-permute-done.7.refs_2_, bf16[192,384]{1,0:T(8,128)(2,1)S(1)} %collective-permute-done.8.refs_3_, ...), custom_call_target="tpu_custom_call" | custom-call | tf_op jit(solution)/shard_map/feed/pallas_call | solution.py:260
  103.4 1.3 %guide.1 = (f32[192,384]{1,0:T(8,128)S(1)}, bf16[192,384]{1,0:T(8,128)(2,1)S(1)}, bf16[192,384]{1,0:T(8,128)(2,1)S(1)}, bf16[192,384]{1,0:T(8,128)(2,1)S(1)}) custom-call(f32[192,1536]{1,0:T(8,128)S(1)} %feed.2.mine_ref, bf16[192,1536]{1,0:T(8,128)(2,1)} %collective-permute-done.18.other_ref, f32[192,128]{1,0:T(8,128)S(1)} %broadcast_in_dim.43.strength_ref), custom_call_target="tpu_custom_call" | custom-call | tf_op jit(solution)/shard_map/guide/pallas_call | solution.py:363
  104.8 1.6 %collective-permute-start.19 = (bf16[192,384]{1,0:T(8,128)(2,1)S(1)}, bf16[192,384]{1,0:T(8,128)(2,1)S(1)}, u32[]{:S(2)}, u32[]{:S(2)}) collective-permute-start(bf16[192,384]{1,0:T(8,128)(2,1)S(1)} %get-tuple-element.34), channel_id=1, source_target_pairs={{0,1},{1,0},{2,3},{3,2},{4,5},{5,4},{6,7},{7,6},{8,9},{9,8},{10,11... | collective-permute-start | bytes 442376 | tf_op jit(solution)/shard_map/ppermute | solution.py:316
  106.9 1.5 %collective-permute-start.21 = (bf16[192,384]{1,0:T(8,128)(2,1)S(1)}, bf16[192,384]{1,0:T(8,128)(2,1)S(1)}, u32[]{:S(2)}, u32[]{:S(2)}) collective-permute-start(bf16[192,384]{1,0:T(8,128)(2,1)S(1)} %get-tuple-element.36), channel_id=1, source_target_pairs={{0,3},{1,2},{2,1},{3,0},{4,7},{5,6},{6,5},{7,4},{8,11},{9,10},{10,... | collective-permute-start | bytes 442376 | tf_op jit(solution)/shard_map/ppermute | solution.py:316
  108.4 2.6 %collective-permute-done.19.got1 = bf16[192,384]{1,0:T(8,128)(2,1)S(1)} collective-permute-done((bf16[192,384]{1,0:T(8,128)(2,1)S(1)}, bf16[192,384]{1,0:T(8,128)(2,1)S(1)}, u32[]{:S(2)}, u32[]{:S(2)}) %collective-permute-start.19) | collective-permute-done | bytes 147488 | tf_op jit(solution)/shard_map/ppermute | solution.py:316
  111.0 3.5 %collective-permute-done.20.got2 = bf16[192,384]{1,0:T(8,128)(2,1)S(1)} collective-permute-done((bf16[192,384]{1,0:T(8,128)(2,1)S(1)}, bf16[192,384]{1,0:T(8,128)(2,1)S(1)}, u32[]{:S(2)}, u32[]{:S(2)}) %collective-permute-start.20) | collective-permute-done | bytes 147488 | tf_op jit(solution)/shard_map/ppermute | solution.py:316
  114.8 1.7 %collective-permute-start.22 = (bf16[96,384]{1,0:T(8,128)(2,1)S(1)}, bf16[96,384]{1,0:T(8,128)(2,1)S(1)}, u32[]{:S(2)}, u32[]{:S(2)}) collective-permute-start(bf16[96,384]{1,0:T(8,128)(2,1)S(1)} %get-tuple-element.38), channel_id=1, source_target_pairs={{0,4},{4,8},{8,12},{12,0},{1,5},{5,9},{9,13},{13,1},{2,6},{6,10},{... | collective-permute-start | bytes 221192 | tf_op jit(solution)/shard_map/ppermute | solution.py:390
  116.6 1.8 %collective-permute-start.23 = (bf16[96,384]{1,0:T(8,128)(2,1)S(1)}, bf16[96,384]{1,0:T(8,128)(2,1)S(1)}, u32[]{:S(2)}, u32[]{:S(2)}) collective-permute-start(bf16[96,384]{1,0:T(8,128)(2,1)S(1)} %get-tuple-element.39), channel_id=1, source_target_pairs={{0,8},{4,12},{8,0},{12,4},{1,9},{5,13},{9,1},{13,5},{2,10},{6,14},... | collective-permute-start | bytes 221192 | tf_op jit(solution)/shard_map/ppermute | solution.py:390
  118.4 1.5 %collective-permute-start.24 = (bf16[96,384]{1,0:T(8,128)(2,1)S(1)}, bf16[96,384]{1,0:T(8,128)(2,1)S(1)}, u32[]{:S(2)}, u32[]{:S(2)}) collective-permute-start(bf16[96,384]{1,0:T(8,128)(2,1)S(1)} %get-tuple-element.40), channel_id=1, source_target_pairs={{0,12},{4,0},{8,4},{12,8},{1,13},{5,1},{9,5},{13,9},{2,14},{6,2},{... | collective-permute-start | bytes 221192 | tf_op jit(solution)/shard_map/ppermute | solution.py:390
  119.9 1.2 collective-permute-done.22.got1
  121.1 2.1 %collective-permute-done.23.got2 = bf16[96,384]{1,0:T(8,128)(2,1)S(1)} collective-permute-done((bf16[96,384]{1,0:T(8,128)(2,1)S(1)}, bf16[96,384]{1,0:T(8,128)(2,1)S(1)}, u32[]{:S(2)}, u32[]{:S(2)}) %collective-permute-start.23) | collective-permute-done | bytes 73760 | tf_op jit(solution)/shard_map/ppermute | solution.py:390
  123.4 0.8 arrange.1
  (58 shorter events, 4.1 us)
Async XLA Ops:
  0.0 81.2 %copy-start = (s32[384,1]{0,1:T(1,128)S(1)}, s32[384,1]{0,1:T(1,128)}, u32[]{:S(2)}) copy-start(s32[384,1]{0,1:T(1,128)} %param.21) | copy-start | bytes 4612
  0.0 5.8 %copy-start.16 = (s32[384]{0:T(512)S(1)}, s32[384]{0:T(512)}, u32[]{:S(2)}) copy-start(s32[384]{0:T(512)} %param.20) | copy-start | bytes 4612
  0.0 5.8 %copy-start.9 = (bf16[1,384,384]{2,1,0:T(8,128)(2,1)S(1)}, bf16[1,384,384]{2,1,0:T(8,128)(2,1)}, u32[]{:S(2)}) copy-start(bf16[1,384,384]{2,1,0:T(8,128)(2,1)} %param.11) | copy-start | bytes 884740
  0.0 5.8 %copy-start.10 = (bf16[1,384,384]{2,1,0:T(8,128)(2,1)S(1)}, bf16[1,384,384]{2,1,0:T(8,128)(2,1)}, u32[]{:S(2)}) copy-start(bf16[1,384,384]{2,1,0:T(8,128)(2,1)} %param.12) | copy-start | bytes 884740
  0.0 5.8 %copy-start.11 = (bf16[1,384,384]{2,1,0:T(8,128)(2,1)S(1)}, bf16[1,384,384]{2,1,0:T(8,128)(2,1)}, u32[]{:S(2)}) copy-start(bf16[1,384,384]{2,1,0:T(8,128)(2,1)} %param.13) | copy-start | bytes 884740
  1.2 18.2 %collective-permute-start.9 = (bf16[192,1536]{1,0:T(8,128)(2,1)S(1)}, bf16[192,1536]{1,0:T(8,128)(2,1)S(1)}, u32[]{:S(2)}, u32[]{:S(2)}) collective-permute-start(bf16[192,1536]{1,0:T(8,128)(2,1)S(1)} %constant_dynamic-slice_fusion.1), channel_id=1, source_target_pairs={{0,1},{1,0},{2,3},{3,2},{4,5},{5,4},{6,7},{7,6},{8,9},{9,8},{10,11... | collective-permute-start | bytes 1769480 | tf_op jit(solution)/shard_map/ppermute | solution.py:316
  4.2 27.4 %collective-permute-start.10 = (bf16[192,1536]{1,0:T(8,128)(2,1)S(1)}, bf16[192,1536]{1,0:T(8,128)(2,1)S(1)}, u32[]{:S(2)}, u32[]{:S(2)}) collective-permute-start(bf16[192,1536]{1,0:T(8,128)(2,1)S(1)} %constant_dynamic-slice_fusion.1), channel_id=1, source_target_pairs={{0,2},{1,3},{2,0},{3,1},{4,6},{5,7},{6,4},{7,5},{8,10},{9,11},{10,... | collective-permute-start | bytes 1769480 | tf_op jit(solution)/shard_map/ppermute | solution.py:316
  5.8 25.9 %collective-permute-start.11 = (bf16[192,1536]{1,0:T(8,128)(2,1)S(1)}, bf16[192,1536]{1,0:T(8,128)(2,1)}, u32[]{:S(2)}, u32[]{:S(2)}) collective-permute-start(bf16[192,1536]{1,0:T(8,128)(2,1)S(1)} %constant_dynamic-slice_fusion.1), channel_id=1, source_target_pairs={{0,3},{1,2},{2,1},{3,0},{4,7},{5,6},{6,5},{7,4},{8,11},{9,10},{10,... | collective-permute-start | bytes 1769480 | tf_op jit(solution)/shard_map/ppermute | solution.py:316
  5.8 63.5 %copy-start.4 = (bf16[1,384,1536]{2,1,0:T(8,128)(2,1)S(1)}, bf16[1,384,1536]{2,1,0:T(8,128)(2,1)}, u32[]{:S(2)}) copy-start(bf16[1,384,1536]{2,1,0:T(8,128)(2,1)} %param.14) | copy-start | bytes 3538948
  6.1 63.3 %copy-start.3 = (bf16[384,1536]{1,0:T(8,128)(2,1)S(1)}, bf16[384,1536]{1,0:T(8,128)(2,1)}, u32[]{:S(2)}) copy-start(bf16[384,1536]{1,0:T(8,128)(2,1)} %refs_4_.3) | copy-start | bytes 3538948
  6.1 12.0 %collective-permute-start = (bf16[1168,128]{1,0:T(8,128)(2,1)S(1)}, bf16[1168,128]{1,0:T(8,128)(2,1)S(1)}, u32[]{:S(2)}, u32[]{:S(2)}) collective-permute-start(bf16[1168,128]{1,0:T(8,128)(2,1)S(1)} %get-tuple-element.24), channel_id=1, source_target_pairs={{0,4},{4,8},{12,0},{16,20},{20,24},{24,28},{1,5},{5,9},{13,1},{17,... | collective-permute-start | bytes 897032 | tf_op jit(solution)/shard_map/ppermute | solution.py:46
  10.2 22.0 %collective-permute-start.1 = (bf16[1168,128]{1,0:T(8,128)(2,1)S(1)}, bf16[1168,128]{1,0:T(8,128)(2,1)S(1)}, u32[]{:S(2)}, u32[]{:S(2)}) collective-permute-start(bf16[1168,128]{1,0:T(8,128)(2,1)S(1)} %get-tuple-element.25), channel_id=1, source_target_pairs={{0,8},{8,0},{12,4},{16,24},{20,28},{28,20},{1,9},{9,1},{13,5},{17,... | collective-permute-start | bytes 897032 | tf_op jit(solution)/shard_map/ppermute | solution.py:46
  18.1 17.4 %collective-permute-start.2 = (bf16[1168,128]{1,0:T(8,128)(2,1)S(1)}, bf16[1168,128]{1,0:T(8,128)(2,1)S(1)}, u32[]{:S(2)}, u32[]{:S(2)}) collective-permute-start(bf16[1168,128]{1,0:T(8,128)(2,1)S(1)} %get-tuple-element.26), channel_id=1, source_target_pairs={{4,0},{8,4},{12,8},{16,28},{24,20},{28,24},{5,1},{9,5},{13,9},{17,... | collective-permute-start | bytes 897032 | tf_op jit(solution)/shard_map/ppermute | solution.py:46
  19.4 49.8 %collective-permute-start.12 = (bf16[192,1536]{1,0:T(8,128)(2,1)S(1)}, bf16[192,1536]{1,0:T(8,128)(2,1)}, u32[]{:S(2)}, u32[]{:S(2)}) collective-permute-start(bf16[192,1536]{1,0:T(8,128)(2,1)S(1)} %collective-permute-done.9.refs_5_), channel_id=1, source_target_pairs={{0,16},{16,0},{1,17},{17,1},{2,18},{18,2},{3,19},{19,3},{4,20},{20... | collective-permute-start | bytes 1769480 | tf_op jit(solution)/shard_map/ppermute | solution.py:316
  31.7 37.5 %collective-permute-start.13 = (bf16[192,1536]{1,0:T(8,128)(2,1)S(1)}, bf16[192,1536]{1,0:T(8,128)(2,1)}, u32[]{:S(2)}, u32[]{:S(2)}) collective-permute-start(bf16[192,1536]{1,0:T(8,128)(2,1)S(1)} %collective-permute-done.10.refs_6_), channel_id=1, source_target_pairs={{0,16},{16,0},{1,17},{17,1},{2,18},{18,2},{3,19},{19,3},{4,20},{20... | collective-permute-start | bytes 1769480 | tf_op jit(solution)/shard_map/ppermute | solution.py:316
  31.7 37.5 %collective-permute-start.14 = (bf16[192,1536]{1,0:T(8,128)(2,1)}, bf16[192,1536]{1,0:T(8,128)(2,1)}, u32[]{:S(2)}, u32[]{:S(2)}) collective-permute-start(bf16[192,1536]{1,0:T(8,128)(2,1)} %collective-permute-done.11.refs_7_), channel_id=1, source_target_pairs={{0,16},{16,0},{1,17},{17,1},{2,18},{18,2},{3,19},{19,3},{4,20},{20... | collective-permute-start | bytes 1769480 | tf_op jit(solution)/shard_map/ppermute | solution.py:316
  39.5 7.8 %collective-permute-start.3 = (bf16[384,128]{1,0:T(8,128)(2,1)S(1)}, bf16[384,128]{1,0:T(8,128)(2,1)S(1)}, u32[]{:S(2)}, u32[]{:S(2)}) collective-permute-start(bf16[384,128]{1,0:T(8,128)(2,1)S(1)} %get-tuple-element.28), channel_id=1, source_target_pairs={{4,0},{8,4},{0,12},{20,16},{24,20},{28,24},{5,1},{9,5},{1,13},{21,... | collective-permute-start | bytes 294920 | tf_op jit(solution)/shard_map/ppermute | solution.py:46
  44.4 7.4 %collective-permute-start.4 = (bf16[384,128]{1,0:T(8,128)(2,1)S(1)}, bf16[384,128]{1,0:T(8,128)(2,1)S(1)}, u32[]{:S(2)}, u32[]{:S(2)}) collective-permute-start(bf16[384,128]{1,0:T(8,128)(2,1)S(1)} %get-tuple-element.29), channel_id=1, source_target_pairs={{8,0},{0,8},{4,12},{24,16},{28,20},{20,28},{9,1},{1,9},{5,13},{25,... | collective-permute-start | bytes 294920 | tf_op jit(solution)/shard_map/ppermute | solution.py:46
  47.3 6.4 %collective-permute-start.5 = (bf16[384,128]{1,0:T(8,128)(2,1)S(1)}, bf16[384,128]{1,0:T(8,128)(2,1)S(1)}, u32[]{:S(2)}, u32[]{:S(2)}) collective-permute-start(bf16[384,128]{1,0:T(8,128)(2,1)S(1)} %get-tuple-element.30), channel_id=1, source_target_pairs={{0,4},{4,8},{8,12},{28,16},{20,24},{24,28},{1,5},{5,9},{9,13},{29,... | collective-permute-start | bytes 294920 | tf_op jit(solution)/shard_map/ppermute | solution.py:46
  54.6 0.6 copy-start.12
  55.3 6.9 %collective-permute-start.15 = (bf16[192,384]{1,0:T(8,128)(2,1)}, bf16[192,384]{1,0:T(8,128)(2,1)S(1)}, u32[]{:S(2)}, u32[]{:S(2)}) collective-permute-start(bf16[192,384]{1,0:T(8,128)(2,1)} %get-tuple-element.32.refs_0_), channel_id=1, source_target_pairs={{0,1},{1,0},{2,3},{3,2},{4,5},{5,4},{6,7},{7,6},{8,9},{9,8},{10,11... | collective-permute-start | bytes 442376 | tf_op jit(solution)/shard_map/ppermute | solution.py:316
  56.8 8.9 %collective-permute-start.16 = (bf16[192,384]{1,0:T(8,128)(2,1)}, bf16[192,384]{1,0:T(8,128)(2,1)}, u32[]{:S(2)}, u32[]{:S(2)}) collective-permute-start(bf16[192,384]{1,0:T(8,128)(2,1)} %get-tuple-element.32.refs_0_), channel_id=1, source_target_pairs={{0,2},{1,3},{2,0},{3,1},{4,6},{5,7},{6,4},{7,5},{8,10},{9,11},{10,... | collective-permute-start | bytes 442376 | tf_op jit(solution)/shard_map/ppermute | solution.py:316
  62.2 0.7 copy-start.14
  62.8 6.4 %collective-permute-start.17 = (bf16[192,384]{1,0:T(8,128)(2,1)}, bf16[192,384]{1,0:T(8,128)(2,1)}, u32[]{:S(2)}, u32[]{:S(2)}) collective-permute-start(bf16[192,384]{1,0:T(8,128)(2,1)} %get-tuple-element.32.refs_0_), channel_id=1, source_target_pairs={{0,3},{1,2},{2,1},{3,0},{4,7},{5,6},{6,5},{7,4},{8,11},{9,10},{10,... | collective-permute-start | bytes 442376 | tf_op jit(solution)/shard_map/ppermute | solution.py:316
  69.3 11.8 %copy-start.5 = (s32[384,128]{1,0:T(8,128)}, s32[384,128]{1,0:T(8,128)S(1)}, u32[]{:S(2)}) copy-start(s32[384,128]{1,0:T(8,128)S(1)} %broadcast_in_dim.38.refs_15_) | copy-start | bytes 589828
  69.4 2.4 %copy-start.1 = (bf16[1536,1536]{1,0:T(8,128)(2,1)S(1)}, bf16[1536,1536]{1,0:T(8,128)(2,1)}, u32[]{:S(2)}) copy-start(bf16[1536,1536]{1,0:T(8,128)(2,1)} %refs_11_.3) | copy-start | bytes 14155780
  71.8 0.9 copy-start.7
  72.7 0.9 copy-start.15
  73.6 11.5 %copy-start.17 = (f32[3]{0:T(128)S(1)}, f32[3]{0:T(128)}, u32[]{:S(2)}) copy-start(f32[3]{0:T(128)} %param.19) | copy-start | bytes 40
  81.2 22.2 %collective-permute-start.18 = (bf16[192,1536]{1,0:T(8,128)(2,1)}, bf16[192,1536]{1,0:T(8,128)(2,1)}, u32[]{:S(2)}, u32[]{:S(2)}) collective-permute-start(bf16[192,1536]{1,0:T(8,128)(2,1)} %feed.3), channel_id=1, source_target_pairs={{0,16},{16,0},{1,17},{17,1},{2,18},{18,2},{3,19},{19,3},{4,20},{20... | collective-permute-start | bytes 1769480 | tf_op jit(solution)/shard_map/ppermute | solution.py:316
  81.6 6.9 %collective-permute-start.6 = (bf16[192,384]{1,0:T(8,128)(2,1)}, bf16[192,384]{1,0:T(8,128)(2,1)S(1)}, u32[]{:S(2)}, u32[]{:S(2)}) collective-permute-start(bf16[192,384]{1,0:T(8,128)(2,1)} %copy-done.12), channel_id=1, source_target_pairs={{0,1},{1,0},{2,3},{3,2},{4,5},{5,4},{6,7},{7,6},{8,9},{9,8},{10,11... | collective-permute-start | bytes 442376 | tf_op jit(solution)/shard_map/ppermute | solution.py:316
  82.1 9.3 %collective-permute-start.7 = (bf16[192,384]{1,0:T(8,128)(2,1)}, bf16[192,384]{1,0:T(8,128)(2,1)S(1)}, u32[]{:S(2)}, u32[]{:S(2)}) collective-permute-start(bf16[192,384]{1,0:T(8,128)(2,1)} %copy-done.12), channel_id=1, source_target_pairs={{0,2},{1,3},{2,0},{3,1},{4,6},{5,7},{6,4},{7,5},{8,10},{9,11},{10,... | collective-permute-start | bytes 442376 | tf_op jit(solution)/shard_map/ppermute | solution.py:316
  83.4 8.0 %collective-permute-start.8 = (bf16[192,384]{1,0:T(8,128)(2,1)}, bf16[192,384]{1,0:T(8,128)(2,1)S(1)}, u32[]{:S(2)}, u32[]{:S(2)}) collective-permute-start(bf16[192,384]{1,0:T(8,128)(2,1)} %copy-done.12), channel_id=1, source_target_pairs={{0,3},{1,2},{2,1},{3,0},{4,7},{5,6},{6,5},{7,4},{8,11},{9,10},{10,... | collective-permute-start | bytes 442376 | tf_op jit(solution)/shard_map/ppermute | solution.py:316
  91.5 2.3 %copy-start.2 = (bf16[1536,1536]{1,0:T(8,128)(2,1)S(1)}, bf16[1536,1536]{1,0:T(8,128)(2,1)}, u32[]{:S(2)}) copy-start(bf16[1536,1536]{1,0:T(8,128)(2,1)} %refs_11_.3) | copy-start | bytes 14155780
  93.8 0.9 copy-start.6
  94.7 0.9 copy-start.8
  95.6 0.9 copy-start.13
  104.8 6.2 %collective-permute-start.19 = (bf16[192,384]{1,0:T(8,128)(2,1)S(1)}, bf16[192,384]{1,0:T(8,128)(2,1)S(1)}, u32[]{:S(2)}, u32[]{:S(2)}) collective-permute-start(bf16[192,384]{1,0:T(8,128)(2,1)S(1)} %get-tuple-element.34), channel_id=1, source_target_pairs={{0,1},{1,0},{2,3},{3,2},{4,5},{5,4},{6,7},{7,6},{8,9},{9,8},{10,11... | collective-permute-start | bytes 442376 | tf_op jit(solution)/shard_map/ppermute | solution.py:316
  106.3 8.2 %collective-permute-start.20 = (bf16[192,384]{1,0:T(8,128)(2,1)S(1)}, bf16[192,384]{1,0:T(8,128)(2,1)S(1)}, u32[]{:S(2)}, u32[]{:S(2)}) collective-permute-start(bf16[192,384]{1,0:T(8,128)(2,1)S(1)} %get-tuple-element.35), channel_id=1, source_target_pairs={{0,2},{1,3},{2,0},{3,1},{4,6},{5,7},{6,4},{7,5},{8,10},{9,11},{10,... | collective-permute-start | bytes 442376 | tf_op jit(solution)/shard_map/ppermute | solution.py:316
  106.9 7.6 %collective-permute-start.21 = (bf16[192,384]{1,0:T(8,128)(2,1)S(1)}, bf16[192,384]{1,0:T(8,128)(2,1)S(1)}, u32[]{:S(2)}, u32[]{:S(2)}) collective-permute-start(bf16[192,384]{1,0:T(8,128)(2,1)S(1)} %get-tuple-element.36), channel_id=1, source_target_pairs={{0,3},{1,2},{2,1},{3,0},{4,7},{5,6},{6,5},{7,4},{8,11},{9,10},{10,... | collective-permute-start | bytes 442376 | tf_op jit(solution)/shard_map/ppermute | solution.py:316
  114.8 6.3 %collective-permute-start.22 = (bf16[96,384]{1,0:T(8,128)(2,1)S(1)}, bf16[96,384]{1,0:T(8,128)(2,1)S(1)}, u32[]{:S(2)}, u32[]{:S(2)}) collective-permute-start(bf16[96,384]{1,0:T(8,128)(2,1)S(1)} %get-tuple-element.38), channel_id=1, source_target_pairs={{0,4},{4,8},{8,12},{12,0},{1,5},{5,9},{9,13},{13,1},{2,6},{6,10},{... | collective-permute-start | bytes 221192 | tf_op jit(solution)/shard_map/ppermute | solution.py:390
  116.6 6.7 %collective-permute-start.23 = (bf16[96,384]{1,0:T(8,128)(2,1)S(1)}, bf16[96,384]{1,0:T(8,128)(2,1)S(1)}, u32[]{:S(2)}, u32[]{:S(2)}) collective-permute-start(bf16[96,384]{1,0:T(8,128)(2,1)S(1)} %get-tuple-element.39), channel_id=1, source_target_pairs={{0,8},{4,12},{8,0},{12,4},{1,9},{5,13},{9,1},{13,5},{2,10},{6,14},... | collective-permute-start | bytes 221192 | tf_op jit(solution)/shard_map/ppermute | solution.py:390
  118.4 5.0 %collective-permute-start.24 = (bf16[96,384]{1,0:T(8,128)(2,1)S(1)}, bf16[96,384]{1,0:T(8,128)(2,1)S(1)}, u32[]{:S(2)}, u32[]{:S(2)}) collective-permute-start(bf16[96,384]{1,0:T(8,128)(2,1)S(1)} %get-tuple-element.40), channel_id=1, source_target_pairs={{0,12},{4,0},{8,4},{12,8},{1,13},{5,1},{9,5},{13,9},{2,14},{6,2},{... | collective-permute-start | bytes 221192 | tf_op jit(solution)/shard_map/ppermute | solution.py:390

commit v2 on v1

--- a/solution.py
+++ b/solution.py
@@ -27,6 +27,10 @@
     return pltpu.CompilerParams(vmem_limit_bytes=mib * 2**20)
 
 
+def cost(flops, moved):
+    return pl.CostEstimate(flops=flops, bytes_accessed=moved, transcendentals=0)
+
+
 def head_at(side, place):
     return jnp.where(side == 0, place, 3 - place)
 
@@ -46,19 +50,29 @@
     return lax.ppermute(value, ("cfg", "seq"), pairs)
 
 
-def pack_kernel(q_ref, k_ref, v_ref, clip_ref, *outs):
+def pack_kernel(q_ref, k_ref, v_ref, clip_ref, *refs):
+    outs, sems = refs[:4], refs[4]
     side, place = lax.axis_index("cfg"), lax.axis_index("seq")
     slots = q_ref.shape[0]
+    copies = []
     for step, out in enumerate(outs):
         head = jnp.clip(head_at(side, lax.rem(place + step, 4)), 0, 2)
         columns = pl.ds(pl.multiple_of(head * HEAD_DIM, HEAD_DIM), HEAD_DIM)
         for part, source in enumerate((q_ref, k_ref, v_ref)):
-            out[part * slots : (part + 1) * slots, :] = source[:, columns]
-        out[3 * slots :, :] = clip_ref[...]
+            target = out.at[part * slots : (part + 1) * slots, :]
+            copy = pltpu.make_async_copy(source.at[:, columns], target, sems.at[len(copies)])
+            copy.start()
+            copies.append(copy)
+    rows = clip_ref[...].astype(F32).astype(BF16)
+    for out in outs:
+        out[3 * slots :, :] = jnp.zeros((16, 128), BF16)
+        out[3 * slots : 3 * slots + rows.shape[0], :] = rows
+    for copy in copies:
+        copy.wait()
 
 
 def attend_kernel(*refs):
-    blocks, outs, (q_aug, k_aug, v_aug, clips) = refs[:4], refs[4:8], refs[8:]
+    blocks, outs, (q_aug, k_aug, v_aug, clips) = refs[:4], refs[9:13], refs[13:]
     slots = outs[0].shape[0]
     lane = lax.broadcasted_iota(jnp.int32, (128, 128), 1)
     row = lax.broadcasted_iota(jnp.int32, (128, 128), 0)
@@ -94,7 +108,7 @@
         out[...] = jnp.where(clips[here, :] < CLIPS, result, 0.0).astype(BF16)
 
 
-def regroup_kernel(own, back1, back2, back3, first, second):
+def regroup_kernel(own, back1, back2, back3, after, first, second):
     side, place = lax.axis_index("cfg"), lax.axis_index("seq")
     half = first.shape[0]
     for head in range(3):
@@ -110,38 +124,152 @@
                     out[:, columns] = source[rows, :]
 
 
-def attention_by_head(query, key, value, slot_clip):
+def kept(value):
+    return pltpu.with_memory_space_constraint(value, pltpu.VMEM)
+
+
+def afar(value):
+    return pltpu.with_memory_space_constraint(value, pltpu.HBM)
+
+
+def load_kernel(up, down, after, up_out, down_out, sems):
+    copies = [
+        pltpu.make_async_copy(source, target, sems.at[index])
+        for index, (source, target) in enumerate(((up, up_out), (down, down_out)))
+    ]
+    for copy in copies:
+        copy.start()
+    for copy in copies:
+        copy.wait()
+
+
+def load(up, down, after):
+    return pl.pallas_call(
+        load_kernel,
+        out_shape=[pltpu.VMEM(up.shape, BF16), pltpu.VMEM(down.shape, BF16)],
+        in_specs=[ANY] * 3,
+        out_specs=[VMEM] * 2,
+        scratch_shapes=[pltpu.SemaphoreType.DMA((2,))],
+        compiler_params=params(16),
+        name="load",
+    )(afar(up), afar(down), after)
+
+
+def across(value, masks):
+    pairs = [
+        (side * 4 + blk, side * 4 + (blk ^ masks[side])) for side in range(2) for blk in range(4)
+    ]
+    return lax.ppermute(value, ("cfg", "blk"), pairs)
+
+
+def cut_kernel(got, out, sem):
+    part = out.shape[0]
+    offset = pl.multiple_of((1 - lax.axis_index("cfg")) * part, part)
+    copy = pltpu.make_async_copy(got.at[pl.ds(offset, part), :], out, sem)
+    copy.start()
+    copy.wait()
+
+
+def join_kernel(own, near, near_swap, far, far_swap, after, out, sems):
+    side = lax.axis_index("cfg")
+    width, part = own.shape[0], far.shape[0]
+    plan = (
+        (own, 0, width),
+        (near, (1 + side) * width, width),
+        (near_swap, (2 - side) * width, width),
+        (far, 3 * width + (1 - side) * part, part),
+        (far_swap, 3 * width + side * part, part),
+    )
+    copies = []
+    for index, (source, offset, rows) in enumerate(plan):
+        target = out.at[pl.ds(pl.multiple_of(offset, part), rows), :]
+        copy = pltpu.make_async_copy(source, target, sems.at[index])
+        copy.start()
+        copies.append(copy)
+    for copy in copies:
+        copy.wait()
+
+
+def gate_kernel(value, after, out):
+    pass
+
+
+def gate(value, after):
+    return pl.pallas_call(
+        gate_kernel,
+        out_shape=shape_of(value.shape, value.dtype),
+        in_specs=[ANY] * 2,
+        out_specs=ANY,
+        input_output_aliases={0: 0},
+        compiler_params=params(1),
+        name="gate",
+    )(value, after)
+
+
+def fetch_near(w_out):
+    near = across(w_out, (1, 2))
+    half = pl.pallas_call(
+        cut_kernel,
+        out_shape=shape_of((w_out.shape[0] // 2, D)),
+        in_specs=[ANY],
+        out_specs=ANY,
+        scratch_shapes=[pltpu.SemaphoreType.DMA],
+        compiler_params=params(16),
+        name="cut",
+    )(near)
+    return near, half
+
+
+def fetch_rest(w_out, near, half, after):
+    far = across(half, (2, 1))
+    far = gate(far, after)
+    pieces = (afar(w_out), near, exchanged(near, "cfg", 1), far, exchanged(far, "cfg", 1))
+    return pl.pallas_call(
+        join_kernel,
+        out_shape=pltpu.VMEM((D, D), BF16),
+        in_specs=[ANY] * 6,
+        out_specs=VMEM,
+        scratch_shapes=[pltpu.SemaphoreType.DMA((5,))],
+        compiler_params=params(16),
+        name="join",
+    )(*pieces, after)
+
+
+def attention_by_head(query, key, value, slot_clip, early, weights, rest):
     slots = query.shape[0]
-    clip_rows = jnp.pad(slot_clip.reshape(slots // 128, 128), ((0, 16 - slots // 128), (0, 0)))
     packed = pl.pallas_call(
         pack_kernel,
         out_shape=[shape_of((3 * slots + 16, 128))] * 4,
-        in_specs=[VMEM] * 4,
+        in_specs=[ANY] * 3 + [VMEM],
         out_specs=[VMEM] * 4,
+        scratch_shapes=[pltpu.SemaphoreType.DMA((12,))],
         compiler_params=params(16),
         name="pack",
-    )(query, key, value, clip_rows.astype(BF16))
+    )(afar(query), afar(key), afar(value), slot_clip.reshape(slots // 128, 128))
     blocks = [packed[0]] + [hop(packed[step], step) for step in (1, 2, 3)]
+    early = (*early, *(kept(weight) for weight in load(*weights, packed[0])))
     results = pl.pallas_call(
         attend_kernel,
         out_shape=[shape_of((slots, 128))] * 4,
-        in_specs=[VMEM] * 4,
+        in_specs=[VMEM] * 4 + [ANY] * (len(early) - 2) + [VMEM] * 2,
         out_specs=[VMEM] * 4,
         scratch_shapes=[pltpu.VMEM((4 * slots, 256), BF16)] * 3
         + [pltpu.VMEM((4 * slots, 128), jnp.int32)],
-        compiler_params=params(32),
+        compiler_params=params(28),
+        cost_estimate=cost(2**32, 2**21),
         name="attend",
-    )(*blocks)
+    )(*blocks, *early)
     backs = [hop(results[step], step, back=True) for step in (1, 2, 3)]
     half = slots // 2
-    return pl.pallas_call(
+    whole = rest(results[0])
+    return whole, early[-2:], pl.pallas_call(
         regroup_kernel,
         out_shape=[shape_of((half, 3 * HEAD_DIM))] * 2,
-        in_specs=[VMEM] * 4,
+        in_specs=[VMEM] * 4 + [ANY],
         out_specs=[VMEM] * 2,
         compiler_params=params(16),
         name="regroup",
-    )(results[0], *backs)
+    )(results[0], *backs, whole)
 
 
 def attention_by_rows(query, key, value, slot_clip):
@@ -188,29 +316,16 @@
 
 
 def feed_kernel(turn, *refs):
-    (att, (w_own, *w_got), (up_hbm, down_hbm, res_hbm, mod, clip_ref)) = (
-        refs[:4],
-        refs[4:11],
-        refs[11:16],
-    )
-    out = refs[16]
-    rows_in, w_out, up, down, res, mixed, total, normed, hidden, sems = refs[17:]
+    (att, (w_out, up, down, res_hbm, mod, clip_ref), out) = refs[:4], refs[4:10], refs[10]
+    rows_in, res, mixed, total, normed, hidden, sems = refs[11:]
     side, blk = lax.axis_index("cfg"), lax.axis_index("blk")
     half = out.shape[0]
     which = 1 - side if turn == 0 else side
     rows = pl.ds(pl.multiple_of(which * half, half), half)
     width = att[0].shape[1]
-    part = width // 2
-    first = []
-    for step in range(4):
-        first.append((att[step], rows_in.at[:, step * width : (step + 1) * width]))
-    first.append((w_own, w_out.at[0:width, :]))
-    for step in range(1, 4):
-        for piece, where in ((w_got[step - 1], side), (w_got[step + 2], 1 - side)):
-            offset = pl.multiple_of(step * width + where * part, part)
-            first.append((piece, w_out.at[pl.ds(offset, part), :]))
-    first.append((res_hbm.at[rows, :], res))
-    plan = first + [(up_hbm, up), (down_hbm, down)]
+    plan = [
+        (att[step], rows_in.at[:, step * width : (step + 1) * width]) for step in range(4)
+    ] + [(res_hbm.at[rows, :], res)]
     copies = [
         pltpu.make_async_copy(source, target, sems.at[index])
         for index, (source, target) in enumerate(plan)
@@ -223,11 +338,11 @@
     def chosen(kind, columns):
         picked = jnp.zeros((half, tile), F32)
         for index in range(CLIPS):
-            line = mod[index * 4 + kind : index * 4 + kind + 1, columns]
+            line = mod[index, kind : kind + 1, columns]
             picked = jnp.where(clip == index, line, picked)
         return picked
 
-    for copy in copies[:-2]:
+    for copy in copies:
         copy.wait()
     for start in range(0, D, tile):
         columns = slice(start, start + tile)
@@ -240,12 +355,10 @@
         columns = slice(start, start + tile)
         value = centre[:, columns] * spread * (1.0 + chosen(2, columns)) + chosen(1, columns)
         normed[:, columns] = value.astype(BF16)
-    copies[-2].wait()
     for start in range(0, D, tile):
         columns = slice(start, start + tile)
         raised = jnp.dot(normed[...], up[:, columns], preferred_element_type=F32)
         hidden[:, columns] = jax.nn.gelu(raised, approximate=True).astype(BF16)
-    copies[-1].wait()
     for start in range(0, D, tile):
         columns = slice(start, start + tile)
         lowered = jnp.dot(hidden[...], down[:, columns], preferred_element_type=F32)
@@ -255,34 +368,35 @@
     out[...] = total[...].astype(out.dtype)
 
 
-def feed(turn, att, w_parts, w_up, w_down, residual, mod, clip_wide):
+def feed(turn, att, w_out, w_up, w_down, residual, mod, clip_wide):
     half, width = att[0].shape
     return pl.pallas_call(
         functools.partial(feed_kernel, turn),
         out_shape=shape_of((half, D), BF16 if turn == 0 else F32),
-        in_specs=[ANY] * 14 + [VMEM] * 2,
+        in_specs=[ANY] * 4 + [VMEM] * 3 + [ANY] + [VMEM] * 2,
         out_specs=VMEM,
         scratch_shapes=[
             pltpu.VMEM((half, D), BF16),
-            pltpu.VMEM((D, D), BF16),
-            pltpu.VMEM((D, D), BF16),
-            pltpu.VMEM((D, D), BF16),
             pltpu.VMEM((half, D), BF16),
             pltpu.VMEM((half, D), F32),
             pltpu.VMEM((half, D), F32),
             pltpu.VMEM((half, D), BF16),
             pltpu.VMEM((half, D), BF16),
-            pltpu.SemaphoreType.DMA((14,)),
+            pltpu.SemaphoreType.DMA((5,)),
         ],
-        compiler_params=params(40),
+        compiler_params=params(24),
+        cost_estimate=cost(2**36, 2**24),
         name="feed",
-    )(*att, *w_parts, w_up, w_down, residual, mod, clip_wide)
-
-
-def guide_kernel(mine_ref, other_ref, strength_ref, own, *sent):
+    )(*att, kept(w_out), kept(w_up), kept(w_down), afar(residual), mod, clip_wide)
+
+
+def guide_kernel(mine_ref, other_ref, clip_ref, scale_ref, own, *sent):
     side, blk = lax.axis_index("cfg"), lax.axis_index("blk")
-    width = own.shape[1]
-    strength = strength_ref[:, :1]
+    half, width = own.shape
+    clip = clip_ref[pl.ds(pl.multiple_of(side * half, half), half), :][:, :1]
+    strength = jnp.zeros((half, 1), F32)
+    for index in range(CLIPS):
+        strength = jnp.where(clip == index, scale_ref[index], strength)
     lean = jnp.where(side == 0, strength, 1.0 - strength)
     for step, out in enumerate((own, *sent)):
         target = jnp.bitwise_xor(blk, step)
@@ -325,22 +439,8 @@
     capacity = max(2, slots // seq_count)
     side, place = lax.axis_index("cfg"), lax.axis_index("seq")
 
-    if seq_count == 4:
-        attended = attention_by_head(queries[0], keys[0], values[0], slot_clip)
-    else:
-        attended = attention_by_rows(queries[0], keys[0], values[0], slot_clip)
-
-    w_half = lax.dynamic_slice_in_dim(w_out, side * (width // 2), width // 2, 0)
-    w_got = [exchanged(w_half, "blk", mask) for mask in (1, 2, 3)]
-    w_parts = [w_out] + w_got + [exchanged(piece, "cfg", 1) for piece in w_got]
-
     clip_wide = jnp.broadcast_to(slot_clip[:, None], (slots, 128))
-    mod = modulation.reshape(CLIPS * 4, D)
     clip_half = lax.dynamic_slice_in_dim(slot_clip, side * half, half, 0)
-    strength = jnp.zeros((half,), F32)
-    for index in range(CLIPS):
-        strength = jnp.where(clip_half == index, guide_scale[index], strength)
-    strength = jnp.broadcast_to(strength[:, None], (half, 128))
     owner_half = lax.dynamic_slice_in_dim(owner[:, 0], side * half, half, 0)
     order = jnp.arange(half, dtype=jnp.int32)
     before = (owner_half[None, :] == owner_half[:, None]) & (order[None, :] < order[:, None])
@@ -354,20 +454,36 @@
         jnp.arange(seq_count * capacity, dtype=jnp.int32)[:, None] == target[None, :]
     ).astype(BF16)
 
+    near, w_half = fetch_near(w_out)
+    if seq_count == 4:
+        whole, (up, down), attended = attention_by_head(
+            queries[0],
+            keys[0],
+            values[0],
+            slot_clip,
+            (clip_wide, placing, w_half),
+            (w_up, w_down),
+            functools.partial(fetch_rest, w_out, near, w_half),
+        )
+    else:
+        attended = attention_by_rows(queries[0], keys[0], values[0], slot_clip)
+        up, down = load(w_up, w_down, attended[0])
+        whole = fetch_rest(w_out, near, w_half, attended[0])
+
     parts = []
     for turn in range(2):
         piece = attended[turn]
         gathered = [piece] + [exchanged(piece, "blk", mask) for mask in (1, 2, 3)]
-        parts.append(feed(turn, gathered, w_parts, w_up, w_down, residual[0], mod, clip_wide))
+        parts.append(feed(turn, gathered, whole, up, down, residual[0], modulation, clip_wide))
     other = exchanged(parts[0], "cfg", 1)
     own, *sent = pl.pallas_call(
         guide_kernel,
         out_shape=[shape_of((half, width), F32)] + [shape_of((half, width))] * 3,
-        in_specs=[VMEM] * 3,
+        in_specs=[VMEM] * 3 + [pl.BlockSpec(memory_space=pltpu.SMEM)],
         out_specs=[VMEM] * 4,
         compiler_params=params(16),
         name="guide",
-    )(parts[1], other, strength)
+    )(parts[1], other, clip_wide, guide_scale)
     got = [exchanged(piece, "blk", mask) for mask, piece in zip((1, 2, 3), sent)]
     by_step = seq_count == 4
     placed = pl.pallas_call(

time: 125 us -> 90.6 us (0.72)
  waiting for transfers between devices: 44.2 us -> 25.7 us
  local copies, waits for them, and re-layouts: 14.3 us -> 0.88 us
  starting transfers between devices: 41.2 us -> 39.1 us
  other arithmetic: 2.32 us -> 1 us
    ppermute x16 -> x12, waiting for transfers between devices: 29.5 us -> 12.4 us  [exchanged(): return lax.ppermute(value, axis, pairs)]
    unnamed x36 -> x10, local copies, waits for them, and re-layouts: 10.6 us -> 0.7 us
    ppermute x16 -> x12, starting transfers between devices: 16.5 us -> 11.1 us  [exchanged(): return lax.ppermute(value, axis, pairs)]
    pallas_call x0 -> x4, Pallas kernels: none -> 5.26 us  [the longest x1 3.8 us: load(): pl.pallas_call(load_kernel, out_shape=[pltpu.VMEM(up.shape, BF16), pltpu....]
    ppermute x0 -> x2, starting transfers between devices: none -> 5.06 us  [across(): return lax.ppermute(value, ('cfg', 'blk'), pairs)]
    pallas_call x2, Pallas kernels: 14.4 us -> 10.3 us  [feed(): pl.pallas_call(functools.partial(feed_kernel, turn), out_shape=shape_of((...]
    ppermute x6, starting transfers between devices: 19.6 us -> 17.5 us  [hop(): return lax.ppermute(value, ('cfg', 'seq'), pairs)]
    select_n x1 -> x0, other arithmetic: 2 us -> none  [shards(): strength = jnp.where(clip_half == index, guide_scale[index], strength)]
  transfers between devices with their start and end apart: 25 -> 23, of which waited for: 14 -> 10; matrix products, arithmetic and copies ran while one was open for 4% -> 1% of each run, Pallas kernels for 10% -> 23%
where the time goes in v2:
time: 90.6 us; the launch traced here: 90.1 us
  starting transfers between devices  39.1 us (43%)
  waiting for transfers between devices  25.7 us (28%)
  Pallas kernels  23.2 us (26%)
  other arithmetic  1 us (1%)
    ppermute x6, starting transfers between devices, hop(): return lax.ppermute(value, ('cfg', 'seq'), pairs)  17.5 us
    ppermute x12, waiting for transfers between devices, exchanged(): return lax.ppermute(value, axis, pairs)  12.4 us
    ppermute x12, starting transfers between devices, exchanged(): return lax.ppermute(value, axis, pairs)  11.1 us
    pallas_call x2, Pallas kernels, feed(): pl.pallas_call(functools.partial(feed_kernel, turn), out_shape=shape_of((...  10.3 us
    ppermute x6, waiting for transfers between devices, hop(): return lax.ppermute(value, ('cfg', 'seq'), pairs)  9.59 us
    ppermute x3, starting transfers between devices, shards(): lax.ppermute(placed[step], 'seq', [(i, (i + step) % 4) for i in range(4)])  5.44 us
    ppermute x2, starting transfers between devices, across(): return lax.ppermute(value, ('cfg', 'blk'), pairs)  5.06 us
    pallas_call x1, Pallas kernels, attention_by_head(): pl.pallas_call(attend_kernel, out_shape=[shape_of((slots, 128))] * 4, in_...  4.01 us
  transfers between devices with their start and end apart: 23, of which 10 were waited for; matrix products, arithmetic and copies ran while one was open for 1% of the time, Pallas kernels for 23%

profile of v2, /device:TPU:0, one launch (start us, length us, event | category | flops | bytes accessed | tf_op | source)
XLA Modules:
  0.0 90.1 jit_solution(10444668509319261828)
XLA Ops:
  0.0 2.9 %collective-permute-start.3 = (bf16[384,1536]{1,0:T(8,128)(2,1)}, bf16[384,1536]{1,0:T(8,128)(2,1)S(1)}, u32[]{:S(2)}, u32[]{:S(2)}) collective-permute-start(bf16[384,1536]{1,0:T(8,128)(2,1)} %own.1), channel_id=1, source_target_pairs={{0,1},{1,0},{2,3},{3,2},{16,18},{17,19},{18,16},{19,17},{4,5},{5,4... | collective-permute-start | bytes 3538952 | tf_op jit(solution)/shard_map/ppermute | solution.py:162
  2.9 0.7 copy-done.1
  3.6 1.4 %pack.1 = (bf16[1168,128]{1,0:T(8,128)(2,1)S(1)}, bf16[1168,128]{1,0:T(8,128)(2,1)S(1)}, bf16[1168,128]{1,0:T(8,128)(2,1)S(1)}, bf16[1168,128]{1,0:T(8,128)(2,1)S(1)}) custom-call(bf16[384,384]{1,0:T(8,128)(2,1)} %bitcast.8, bf16[384,384]{1,0:T(8,128)(2,1)} %bitcast.9, bf16[384,384]{1,0:T(8,128)(2,1)} %bitcast.10, s32[3,128]{1,0:T(4,128)S(1)} %bitcast.7), custom_call_target="tpu_custom_call" | custom-call | tf_op jit(solution)/shard_map/pack/pallas_call | solution.py:240
  5.1 3.5 %collective-permute-start = (bf16[1168,128]{1,0:T(8,128)(2,1)S(1)}, bf16[1168,128]{1,0:T(8,128)(2,1)S(1)}, u32[]{:S(2)}, u32[]{:S(2)}) collective-permute-start(bf16[1168,128]{1,0:T(8,128)(2,1)S(1)} %get-tuple-element.26), channel_id=1, source_target_pairs={{0,4},{4,8},{12,0},{16,20},{20,24},{24,28},{1,5},{5,9},{13,1},{17,... | collective-permute-start | bytes 897032 | tf_op jit(solution)/shard_map/ppermute | solution.py:50
  8.6 2.3 %collective-permute-start.1 = (bf16[1168,128]{1,0:T(8,128)(2,1)S(1)}, bf16[1168,128]{1,0:T(8,128)(2,1)S(1)}, u32[]{:S(2)}, u32[]{:S(2)}) collective-permute-start(bf16[1168,128]{1,0:T(8,128)(2,1)S(1)} %get-tuple-element.27), channel_id=1, source_target_pairs={{0,8},{8,0},{12,4},{16,24},{20,28},{28,20},{1,9},{9,1},{13,5},{17,... | collective-permute-start | bytes 897032 | tf_op jit(solution)/shard_map/ppermute | solution.py:50
  10.9 1.3 %collective-permute-start.2 = (bf16[1168,128]{1,0:T(8,128)(2,1)S(1)}, bf16[1168,128]{1,0:T(8,128)(2,1)S(1)}, u32[]{:S(2)}, u32[]{:S(2)}) collective-permute-start(bf16[1168,128]{1,0:T(8,128)(2,1)S(1)} %get-tuple-element.28), channel_id=1, source_target_pairs={{4,0},{8,4},{12,8},{16,28},{24,20},{28,24},{5,1},{9,5},{13,9},{17,... | collective-permute-start | bytes 897032 | tf_op jit(solution)/shard_map/ppermute | solution.py:50
  12.2 0.1 constant_dynamic-slice_fusion
  12.3 0.2 convert_reduce_fusion
  12.5 0.8 compare_select_fusion.2
  13.2 3.8 %load.1 = (bf16[1536,1536]{1,0:T(8,128)(2,1)S(1)}, bf16[1536,1536]{1,0:T(8,128)(2,1)S(1)}) custom-call(bf16[1536,1536]{1,0:T(8,128)(2,1)} %up.1, bf16[1536,1536]{1,0:T(8,128)(2,1)} %down.1, bf16[1168,128]{1,0:T(8,128)(2,1)S(1)} %get-tuple-element.25.after.refs_0_), custom_call_target="tpu_custom_call" | custom-call | tf_op jit(solution)/shard_map/load/pallas_call | solution.py:147
  17.0 0.3 collective-permute-done.3.got.near
  17.3 0.1 cut.1.refs_6_
  17.5 2.1 %collective-permute-start.8 = (bf16[192,1536]{1,0:T(8,128)(2,1)S(1)}, bf16[192,1536]{1,0:T(8,128)(2,1)S(1)}, u32[]{:S(2)}, u32[]{:S(2)}) collective-permute-start(bf16[192,1536]{1,0:T(8,128)(2,1)S(1)} %cut.1.refs_6_), channel_id=1, source_target_pairs={{0,2},{1,3},{2,0},{3,1},{16,17},{17,16},{18,19},{19,18},{4,6},{5,7... | collective-permute-start | bytes 1769480 | tf_op jit(solution)/shard_map/ppermute | solution.py:162
  19.6 1.8 %collective-permute-start.7 = (bf16[384,1536]{1,0:T(8,128)(2,1)S(1)}, bf16[384,1536]{1,0:T(8,128)(2,1)S(1)}, u32[]{:S(2)}, u32[]{:S(2)}) collective-permute-start(bf16[384,1536]{1,0:T(8,128)(2,1)S(1)} %collective-permute-done.3.got.near), channel_id=1, source_target_pairs={{0,16},{16,0},{1,17},{17,1},{2,18},{18,2},{3,19},{19,3},{4,20},{20... | collective-permute-start | bytes 3538952 | tf_op jit(solution)/shard_map/ppermute | solution.py:430
  21.5 6.8 %collective-permute-done.1.refs_2_ = bf16[1168,128]{1,0:T(8,128)(2,1)S(1)} collective-permute-done((bf16[1168,128]{1,0:T(8,128)(2,1)S(1)}, bf16[1168,128]{1,0:T(8,128)(2,1)S(1)}, u32[]{:S(2)}, u32[]{:S(2)}) %collective-permute-start.1) | collective-permute-done | bytes 299040 | tf_op jit(solution)/shard_map/ppermute | solution.py:50
  28.3 0.1 broadcast_in_dim.7.refs_4_.refs_9_.clip_ref
  28.4 4.0 %attend.1 = (bf16[384,128]{1,0:T(8,128)(2,1)S(1)}, bf16[384,128]{1,0:T(8,128)(2,1)S(1)}, bf16[384,128]{1,0:T(8,128)(2,1)S(1)}, bf16[384,128]{1,0:T(8,128)(2,1)S(1)}) custom-call(bf16[1168,128]{1,0:T(8,128)(2,1)S(1)} %get-tuple-element.25.after.refs_0_, bf16[1168,128]{1,0:T(8,128)(2,1)S(1)} %collective-permute-done.refs_1_, ...), custom_call_target="tpu_custom_call" | custom-call | flops 4294967296 | bytes 2097152 | tf_op jit(solution)/shard_map/attend/pallas_call | solution.py:251
  32.4 0.1 collective-permute-start.9
  32.5 5.3 %collective-permute-start.4 = (bf16[384,128]{1,0:T(8,128)(2,1)S(1)}, bf16[384,128]{1,0:T(8,128)(2,1)S(1)}, u32[]{:S(2)}, u32[]{:S(2)}) collective-permute-start(bf16[384,128]{1,0:T(8,128)(2,1)S(1)} %get-tuple-element.32), channel_id=1, source_target_pairs={{4,0},{8,4},{0,12},{20,16},{24,20},{28,24},{5,1},{9,5},{1,13},{21,... | collective-permute-start | bytes 294920 | tf_op jit(solution)/shard_map/ppermute | solution.py:50
  37.8 3.8 %collective-permute-start.5 = (bf16[384,128]{1,0:T(8,128)(2,1)S(1)}, bf16[384,128]{1,0:T(8,128)(2,1)S(1)}, u32[]{:S(2)}, u32[]{:S(2)}) collective-permute-start(bf16[384,128]{1,0:T(8,128)(2,1)S(1)} %get-tuple-element.33), channel_id=1, source_target_pairs={{8,0},{0,8},{4,12},{24,16},{28,20},{20,28},{9,1},{1,9},{5,13},{25,... | collective-permute-start | bytes 294920 | tf_op jit(solution)/shard_map/ppermute | solution.py:50
  41.6 1.3 %collective-permute-start.6 = (bf16[384,128]{1,0:T(8,128)(2,1)S(1)}, bf16[384,128]{1,0:T(8,128)(2,1)S(1)}, u32[]{:S(2)}, u32[]{:S(2)}) collective-permute-start(bf16[384,128]{1,0:T(8,128)(2,1)S(1)} %get-tuple-element.34), channel_id=1, source_target_pairs={{0,4},{4,8},{8,12},{28,16},{20,24},{24,28},{1,5},{5,9},{9,13},{29,... | collective-permute-start | bytes 294920 | tf_op jit(solution)/shard_map/ppermute | solution.py:50
  43.0 1.3 %join.1.after.refs_4_ = bf16[1536,1536]{1,0:T(8,128)(2,1)S(1)} custom-call(bf16[384,1536]{1,0:T(8,128)(2,1)} %own.1, bf16[384,1536]{1,0:T(8,128)(2,1)S(1)} %collective-permute-done.3.got.near, bf16[384,1536]{1,0:T(8,128)(2,1)S(1)} %collective-permute-done.7.near_swap, bf16[192,1536]{1,0:T(8,128)(2,1)S(1)} %gate.1.far, ...), custom_call_target="tpu_custom_call" | custom-call | tf_op jit(solution)/shard_map/join/pallas_call | solution.py:227
  44.3 2.8 %collective-permute-done.5.back2 = bf16[384,128]{1,0:T(8,128)(2,1)S(1)} collective-permute-done((bf16[384,128]{1,0:T(8,128)(2,1)S(1)}, bf16[384,128]{1,0:T(8,128)(2,1)S(1)}, u32[]{:S(2)}, u32[]{:S(2)}) %collective-permute-start.5) | collective-permute-done | bytes 98336 | tf_op jit(solution)/shard_map/ppermute | solution.py:50
  47.1 0.3 regroup.1
  47.4 1.6 %collective-permute-start.15 = (bf16[192,384]{1,0:T(8,128)(2,1)S(1)}, bf16[192,384]{1,0:T(8,128)(2,1)S(1)}, u32[]{:S(2)}, u32[]{:S(2)}) collective-permute-start(bf16[192,384]{1,0:T(8,128)(2,1)S(1)} %get-tuple-element.36.refs_0_), channel_id=1, source_target_pairs={{0,3},{1,2},{2,1},{3,0},{4,7},{5,6},{6,5},{7,4},{8,11},{9,10},{10,... | collective-permute-start | bytes 442376 | tf_op jit(solution)/shard_map/ppermute | solution.py:430
  48.9 0.5 collective-permute-start.14
  49.5 1.5 %collective-permute-start.13 = (bf16[192,384]{1,0:T(8,128)(2,1)S(1)}, bf16[192,384]{1,0:T(8,128)(2,1)S(1)}, u32[]{:S(2)}, u32[]{:S(2)}) collective-permute-start(bf16[192,384]{1,0:T(8,128)(2,1)S(1)} %get-tuple-element.36.refs_0_), channel_id=1, source_target_pairs={{0,1},{1,0},{2,3},{3,2},{4,5},{5,4},{6,7},{7,6},{8,9},{9,8},{10,11... | collective-permute-start | bytes 442376 | tf_op jit(solution)/shard_map/ppermute | solution.py:430
  50.9 1.5 %collective-permute-start.12 = (bf16[192,384]{1,0:T(8,128)(2,1)S(1)}, bf16[192,384]{1,0:T(8,128)(2,1)S(1)}, u32[]{:S(2)}, u32[]{:S(2)}) collective-permute-start(bf16[192,384]{1,0:T(8,128)(2,1)S(1)} %get-tuple-element.35.refs_0_), channel_id=1, source_target_pairs={{0,3},{1,2},{2,1},{3,0},{4,7},{5,6},{6,5},{7,4},{8,11},{9,10},{10,... | collective-permute-start | bytes 442376 | tf_op jit(solution)/shard_map/ppermute | solution.py:430
  52.4 0.5 collective-permute-start.11
  52.9 2.2 %collective-permute-done.15.refs_3_ = bf16[192,384]{1,0:T(8,128)(2,1)S(1)} collective-permute-done((bf16[192,384]{1,0:T(8,128)(2,1)S(1)}, bf16[192,384]{1,0:T(8,128)(2,1)S(1)}, u32[]{:S(2)}, u32[]{:S(2)}) %collective-permute-start.15) | collective-permute-done | bytes 147488 | tf_op jit(solution)/shard_map/ppermute | solution.py:430
  55.1 3.7 %collective-permute-done.14.refs_2_ = bf16[192,384]{1,0:T(8,128)(2,1)S(1)} collective-permute-done((bf16[192,384]{1,0:T(8,128)(2,1)S(1)}, bf16[192,384]{1,0:T(8,128)(2,1)S(1)}, u32[]{:S(2)}, u32[]{:S(2)}) %collective-permute-start.14) | collective-permute-done | bytes 147488 | tf_op jit(solution)/shard_map/ppermute | solution.py:430
  58.8 5.1 %feed.3 = bf16[192,1536]{1,0:T(8,128)(2,1)S(1)} custom-call(bf16[192,384]{1,0:T(8,128)(2,1)S(1)} %get-tuple-element.36.refs_0_, bf16[192,384]{1,0:T(8,128)(2,1)S(1)} %collective-permute-done.13.refs_1_, bf16[192,384]{1,0:T(8,128)(2,1)S(1)} %collective-permute-done.14.refs_2_, bf16[192,384]{1,0:T(8,128)(2,1)S(1)} %collective-permute-done.15.refs_3_, ...), custom_call_target="tpu_custom_call" | custom-call | flops 68719476736 | bytes 16777216 | tf_op jit(solution)/shard_map/feed/pallas_call | solution.py:373
  64.0 0.1 collective-permute-start.16
  64.1 5.2 %feed.2.mine_ref = f32[192,1536]{1,0:T(8,128)S(1)} custom-call(bf16[192,384]{1,0:T(8,128)(2,1)S(1)} %get-tuple-element.35.refs_0_, bf16[192,384]{1,0:T(8,128)(2,1)S(1)} %collective-permute-done.10.refs_1_, bf16[192,384]{1,0:T(8,128)(2,1)S(1)} %collective-permute-done.11.refs_2_, bf16[192,384]{1,0:T(8,128)(2,1)S(1)} %collective-permute-done.12.refs_3_, ...), custom_call_target="tpu_custom_call" | custom-call | flops 68719476736 | bytes 16777216 | tf_op jit(solution)/shard_map/feed/pallas_call | solution.py:373
  69.3 0.8 guide.1
  70.1 0.9 %collective-permute-start.17 = (bf16[192,384]{1,0:T(8,128)(2,1)S(1)}, bf16[192,384]{1,0:T(8,128)(2,1)S(1)}, u32[]{:S(2)}, u32[]{:S(2)}) collective-permute-start(bf16[192,384]{1,0:T(8,128)(2,1)S(1)} %get-tuple-element.38), channel_id=1, source_target_pairs={{0,1},{1,0},{2,3},{3,2},{4,5},{5,4},{6,7},{7,6},{8,9},{9,8},{10,11... | collective-permute-start | bytes 442376 | tf_op jit(solution)/shard_map/ppermute | solution.py:430
  71.0 1.1 %collective-permute-start.18 = (bf16[192,384]{1,0:T(8,128)(2,1)S(1)}, bf16[192,384]{1,0:T(8,128)(2,1)S(1)}, u32[]{:S(2)}, u32[]{:S(2)}) collective-permute-start(bf16[192,384]{1,0:T(8,128)(2,1)S(1)} %get-tuple-element.39), channel_id=1, source_target_pairs={{0,2},{1,3},{2,0},{3,1},{4,6},{5,7},{6,4},{7,5},{8,10},{9,11},{10,... | collective-permute-start | bytes 442376 | tf_op jit(solution)/shard_map/ppermute | solution.py:430
  72.2 1.5 %collective-permute-start.19 = (bf16[192,384]{1,0:T(8,128)(2,1)S(1)}, bf16[192,384]{1,0:T(8,128)(2,1)S(1)}, u32[]{:S(2)}, u32[]{:S(2)}) collective-permute-start(bf16[192,384]{1,0:T(8,128)(2,1)S(1)} %get-tuple-element.40), channel_id=1, source_target_pairs={{0,3},{1,2},{2,1},{3,0},{4,7},{5,6},{6,5},{7,4},{8,11},{9,10},{10,... | collective-permute-start | bytes 442376 | tf_op jit(solution)/shard_map/ppermute | solution.py:430
  73.6 3.2 %collective-permute-done.17.got1 = bf16[192,384]{1,0:T(8,128)(2,1)S(1)} collective-permute-done((bf16[192,384]{1,0:T(8,128)(2,1)S(1)}, bf16[192,384]{1,0:T(8,128)(2,1)S(1)}, u32[]{:S(2)}, u32[]{:S(2)}) %collective-permute-start.17) | collective-permute-done | bytes 147488 | tf_op jit(solution)/shard_map/ppermute | solution.py:430
  76.8 0.6 collective-permute-done.18.got2
  77.4 2.8 %collective-permute-done.19.got3 = bf16[192,384]{1,0:T(8,128)(2,1)S(1)} collective-permute-done((bf16[192,384]{1,0:T(8,128)(2,1)S(1)}, bf16[192,384]{1,0:T(8,128)(2,1)S(1)}, u32[]{:S(2)}, u32[]{:S(2)}) %collective-permute-start.19) | collective-permute-done | bytes 147488 | tf_op jit(solution)/shard_map/ppermute | solution.py:430
  80.2 0.3 place.1
  80.5 0.7 collective-permute-start.20
  81.2 1.9 %collective-permute-start.21 = (bf16[96,384]{1,0:T(8,128)(2,1)S(1)}, bf16[96,384]{1,0:T(8,128)(2,1)S(1)}, u32[]{:S(2)}, u32[]{:S(2)}) collective-permute-start(bf16[96,384]{1,0:T(8,128)(2,1)S(1)} %get-tuple-element.43), channel_id=1, source_target_pairs={{0,8},{4,12},{8,0},{12,4},{1,9},{5,13},{9,1},{13,5},{2,10},{6,14},... | collective-permute-start | bytes 221192 | tf_op jit(solution)/shard_map/ppermute | solution.py:506
  83.1 2.8 %collective-permute-start.22 = (bf16[96,384]{1,0:T(8,128)(2,1)S(1)}, bf16[96,384]{1,0:T(8,128)(2,1)S(1)}, u32[]{:S(2)}, u32[]{:S(2)}) collective-permute-start(bf16[96,384]{1,0:T(8,128)(2,1)S(1)} %get-tuple-element.44), channel_id=1, source_target_pairs={{0,12},{4,0},{8,4},{12,8},{1,13},{5,1},{9,5},{13,9},{2,14},{6,2},{... | collective-permute-start | bytes 221192 | tf_op jit(solution)/shard_map/ppermute | solution.py:506
  85.9 1.5 %collective-permute-done.20.got1 = bf16[96,384]{1,0:T(8,128)(2,1)S(1)} collective-permute-done((bf16[96,384]{1,0:T(8,128)(2,1)S(1)}, bf16[96,384]{1,0:T(8,128)(2,1)S(1)}, u32[]{:S(2)}, u32[]{:S(2)}) %collective-permute-start.20) | collective-permute-done | bytes 73760 | tf_op jit(solution)/shard_map/ppermute | solution.py:506
  87.5 1.9 %collective-permute-done.21.got2 = bf16[96,384]{1,0:T(8,128)(2,1)S(1)} collective-permute-done((bf16[96,384]{1,0:T(8,128)(2,1)S(1)}, bf16[96,384]{1,0:T(8,128)(2,1)S(1)}, u32[]{:S(2)}, u32[]{:S(2)}) %collective-permute-start.21) | collective-permute-done | bytes 73760 | tf_op jit(solution)/shard_map/ppermute | solution.py:506
  89.4 0.8 arrange.1
  (25 shorter events, 0.1 us)
Async XLA Ops:
  0.0 12.2 %copy-start = (s32[384,1]{0,1:T(1,128)S(1)}, s32[384,1]{0,1:T(1,128)}, u32[]{:S(2)}) copy-start(s32[384,1]{0,1:T(1,128)} %param.21) | copy-start | bytes 4612
  0.0 17.3 %collective-permute-start.3 = (bf16[384,1536]{1,0:T(8,128)(2,1)}, bf16[384,1536]{1,0:T(8,128)(2,1)S(1)}, u32[]{:S(2)}, u32[]{:S(2)}) collective-permute-start(bf16[384,1536]{1,0:T(8,128)(2,1)} %own.1), channel_id=1, source_target_pairs={{0,1},{1,0},{2,3},{3,2},{16,18},{17,19},{18,16},{19,17},{4,5},{5,4... | collective-permute-start | bytes 3538952 | tf_op jit(solution)/shard_map/ppermute | solution.py:162
  2.9 0.7 copy-start.1
  5.1 16.4 %collective-permute-start = (bf16[1168,128]{1,0:T(8,128)(2,1)S(1)}, bf16[1168,128]{1,0:T(8,128)(2,1)S(1)}, u32[]{:S(2)}, u32[]{:S(2)}) collective-permute-start(bf16[1168,128]{1,0:T(8,128)(2,1)S(1)} %get-tuple-element.26), channel_id=1, source_target_pairs={{0,4},{4,8},{12,0},{16,20},{20,24},{24,28},{1,5},{5,9},{13,1},{17,... | collective-permute-start | bytes 897032 | tf_op jit(solution)/shard_map/ppermute | solution.py:50
  8.6 19.7 %collective-permute-start.1 = (bf16[1168,128]{1,0:T(8,128)(2,1)S(1)}, bf16[1168,128]{1,0:T(8,128)(2,1)S(1)}, u32[]{:S(2)}, u32[]{:S(2)}) collective-permute-start(bf16[1168,128]{1,0:T(8,128)(2,1)S(1)} %get-tuple-element.27), channel_id=1, source_target_pairs={{0,8},{8,0},{12,4},{16,24},{20,28},{28,20},{1,9},{9,1},{13,5},{17,... | collective-permute-start | bytes 897032 | tf_op jit(solution)/shard_map/ppermute | solution.py:50
  10.9 17.4 %collective-permute-start.2 = (bf16[1168,128]{1,0:T(8,128)(2,1)S(1)}, bf16[1168,128]{1,0:T(8,128)(2,1)S(1)}, u32[]{:S(2)}, u32[]{:S(2)}) collective-permute-start(bf16[1168,128]{1,0:T(8,128)(2,1)S(1)} %get-tuple-element.28), channel_id=1, source_target_pairs={{4,0},{8,4},{12,8},{16,28},{24,20},{28,24},{5,1},{9,5},{13,9},{17,... | collective-permute-start | bytes 897032 | tf_op jit(solution)/shard_map/ppermute | solution.py:50
  13.2 15.1 %copy-start.2 = (s32[384]{0:T(512)S(1)}, s32[384]{0:T(512)}, u32[]{:S(2)}) copy-start(s32[384]{0:T(512)} %param.20) | copy-start | bytes 4612
  17.5 14.9 %collective-permute-start.8 = (bf16[192,1536]{1,0:T(8,128)(2,1)S(1)}, bf16[192,1536]{1,0:T(8,128)(2,1)S(1)}, u32[]{:S(2)}, u32[]{:S(2)}) collective-permute-start(bf16[192,1536]{1,0:T(8,128)(2,1)S(1)} %cut.1.refs_6_), channel_id=1, source_target_pairs={{0,2},{1,3},{2,0},{3,1},{16,17},{17,16},{18,19},{19,18},{4,6},{5,7... | collective-permute-start | bytes 1769480 | tf_op jit(solution)/shard_map/ppermute | solution.py:162
  19.6 23.4 %collective-permute-start.7 = (bf16[384,1536]{1,0:T(8,128)(2,1)S(1)}, bf16[384,1536]{1,0:T(8,128)(2,1)S(1)}, u32[]{:S(2)}, u32[]{:S(2)}) collective-permute-start(bf16[384,1536]{1,0:T(8,128)(2,1)S(1)} %collective-permute-done.3.got.near), channel_id=1, source_target_pairs={{0,16},{16,0},{1,17},{17,1},{2,18},{18,2},{3,19},{19,3},{4,20},{20... | collective-permute-start | bytes 3538952 | tf_op jit(solution)/shard_map/ppermute | solution.py:430
  32.4 10.5 %collective-permute-start.9 = (bf16[192,1536]{1,0:T(8,128)(2,1)S(1)}, bf16[192,1536]{1,0:T(8,128)(2,1)S(1)}, u32[]{:S(2)}, u32[]{:S(2)}) collective-permute-start(bf16[192,1536]{1,0:T(8,128)(2,1)S(1)} %gate.1.far), channel_id=1, source_target_pairs={{0,16},{16,0},{1,17},{17,1},{2,18},{18,2},{3,19},{19,3},{4,20},{20... | collective-permute-start | bytes 1769480 | tf_op jit(solution)/shard_map/ppermute | solution.py:430
  32.5 11.8 %collective-permute-start.4 = (bf16[384,128]{1,0:T(8,128)(2,1)S(1)}, bf16[384,128]{1,0:T(8,128)(2,1)S(1)}, u32[]{:S(2)}, u32[]{:S(2)}) collective-permute-start(bf16[384,128]{1,0:T(8,128)(2,1)S(1)} %get-tuple-element.32), channel_id=1, source_target_pairs={{4,0},{8,4},{0,12},{20,16},{24,20},{28,24},{5,1},{9,5},{1,13},{21,... | collective-permute-start | bytes 294920 | tf_op jit(solution)/shard_map/ppermute | solution.py:50
  37.8 9.3 %collective-permute-start.5 = (bf16[384,128]{1,0:T(8,128)(2,1)S(1)}, bf16[384,128]{1,0:T(8,128)(2,1)S(1)}, u32[]{:S(2)}, u32[]{:S(2)}) collective-permute-start(bf16[384,128]{1,0:T(8,128)(2,1)S(1)} %get-tuple-element.33), channel_id=1, source_target_pairs={{8,0},{0,8},{4,12},{24,16},{28,20},{20,28},{9,1},{1,9},{5,13},{25,... | collective-permute-start | bytes 294920 | tf_op jit(solution)/shard_map/ppermute | solution.py:50
  41.6 5.4 %collective-permute-start.6 = (bf16[384,128]{1,0:T(8,128)(2,1)S(1)}, bf16[384,128]{1,0:T(8,128)(2,1)S(1)}, u32[]{:S(2)}, u32[]{:S(2)}) collective-permute-start(bf16[384,128]{1,0:T(8,128)(2,1)S(1)} %get-tuple-element.34), channel_id=1, source_target_pairs={{0,4},{4,8},{8,12},{28,16},{20,24},{24,28},{1,5},{5,9},{9,13},{29,... | collective-permute-start | bytes 294920 | tf_op jit(solution)/shard_map/ppermute | solution.py:50
  44.3 14.5 %copy-start.4 = (f32[3,4,1536]{2,1,0:T(4,128)S(1)}, f32[3,4,1536]{2,1,0:T(4,128)}, u32[]{:S(2)}) copy-start(f32[3,4,1536]{2,1,0:T(4,128)} %refs_8_.3) | copy-start | bytes 221188
  47.4 7.8 %collective-permute-start.15 = (bf16[192,384]{1,0:T(8,128)(2,1)S(1)}, bf16[192,384]{1,0:T(8,128)(2,1)S(1)}, u32[]{:S(2)}, u32[]{:S(2)}) collective-permute-start(bf16[192,384]{1,0:T(8,128)(2,1)S(1)} %get-tuple-element.36.refs_0_), channel_id=1, source_target_pairs={{0,3},{1,2},{2,1},{3,0},{4,7},{5,6},{6,5},{7,4},{8,11},{9,10},{10,... | collective-permute-start | bytes 442376 | tf_op jit(solution)/shard_map/ppermute | solution.py:430
  48.9 9.9 %collective-permute-start.14 = (bf16[192,384]{1,0:T(8,128)(2,1)S(1)}, bf16[192,384]{1,0:T(8,128)(2,1)S(1)}, u32[]{:S(2)}, u32[]{:S(2)}) collective-permute-start(bf16[192,384]{1,0:T(8,128)(2,1)S(1)} %get-tuple-element.36.refs_0_), channel_id=1, source_target_pairs={{0,2},{1,3},{2,0},{3,1},{4,6},{5,7},{6,4},{7,5},{8,10},{9,11},{10,... | collective-permute-start | bytes 442376 | tf_op jit(solution)/shard_map/ppermute | solution.py:430
  49.5 9.4 %collective-permute-start.13 = (bf16[192,384]{1,0:T(8,128)(2,1)S(1)}, bf16[192,384]{1,0:T(8,128)(2,1)S(1)}, u32[]{:S(2)}, u32[]{:S(2)}) collective-permute-start(bf16[192,384]{1,0:T(8,128)(2,1)S(1)} %get-tuple-element.36.refs_0_), channel_id=1, source_target_pairs={{0,1},{1,0},{2,3},{3,2},{4,5},{5,4},{6,7},{7,6},{8,9},{9,8},{10,11... | collective-permute-start | bytes 442376 | tf_op jit(solution)/shard_map/ppermute | solution.py:430
  50.9 13.1 %collective-permute-start.12 = (bf16[192,384]{1,0:T(8,128)(2,1)S(1)}, bf16[192,384]{1,0:T(8,128)(2,1)S(1)}, u32[]{:S(2)}, u32[]{:S(2)}) collective-permute-start(bf16[192,384]{1,0:T(8,128)(2,1)S(1)} %get-tuple-element.35.refs_0_), channel_id=1, source_target_pairs={{0,3},{1,2},{2,1},{3,0},{4,7},{5,6},{6,5},{7,4},{8,11},{9,10},{10,... | collective-permute-start | bytes 442376 | tf_op jit(solution)/shard_map/ppermute | solution.py:430
  52.4 11.6 %collective-permute-start.11 = (bf16[192,384]{1,0:T(8,128)(2,1)S(1)}, bf16[192,384]{1,0:T(8,128)(2,1)S(1)}, u32[]{:S(2)}, u32[]{:S(2)}) collective-permute-start(bf16[192,384]{1,0:T(8,128)(2,1)S(1)} %get-tuple-element.35.refs_0_), channel_id=1, source_target_pairs={{0,2},{1,3},{2,0},{3,1},{4,6},{5,7},{6,4},{7,5},{8,10},{9,11},{10,... | collective-permute-start | bytes 442376 | tf_op jit(solution)/shard_map/ppermute | solution.py:430
  55.1 8.9 %collective-permute-start.10 = (bf16[192,384]{1,0:T(8,128)(2,1)S(1)}, bf16[192,384]{1,0:T(8,128)(2,1)S(1)}, u32[]{:S(2)}, u32[]{:S(2)}) collective-permute-start(bf16[192,384]{1,0:T(8,128)(2,1)S(1)} %get-tuple-element.35.refs_0_), channel_id=1, source_target_pairs={{0,1},{1,0},{2,3},{3,2},{4,5},{5,4},{6,7},{7,6},{8,9},{9,8},{10,11... | collective-permute-start | bytes 442376 | tf_op jit(solution)/shard_map/ppermute | solution.py:430
  63.9 5.3 %copy-start.3 = (f32[3]{0:T(128)S(1)}, f32[3]{0:T(128)}, u32[]{:S(2)}) copy-start(f32[3]{0:T(128)} %scale_ref.1) | copy-start | bytes 40
  64.0 5.3 %collective-permute-start.16 = (bf16[192,1536]{1,0:T(8,128)(2,1)S(1)}, bf16[192,1536]{1,0:T(8,128)(2,1)S(1)}, u32[]{:S(2)}, u32[]{:S(2)}) collective-permute-start(bf16[192,1536]{1,0:T(8,128)(2,1)S(1)} %feed.3), channel_id=1, source_target_pairs={{0,16},{16,0},{1,17},{17,1},{2,18},{18,2},{3,19},{19,3},{4,20},{20... | collective-permute-start | bytes 1769480 | tf_op jit(solution)/shard_map/ppermute | solution.py:430
  70.1 6.7 %collective-permute-start.17 = (bf16[192,384]{1,0:T(8,128)(2,1)S(1)}, bf16[192,384]{1,0:T(8,128)(2,1)S(1)}, u32[]{:S(2)}, u32[]{:S(2)}) collective-permute-start(bf16[192,384]{1,0:T(8,128)(2,1)S(1)} %get-tuple-element.38), channel_id=1, source_target_pairs={{0,1},{1,0},{2,3},{3,2},{4,5},{5,4},{6,7},{7,6},{8,9},{9,8},{10,11... | collective-permute-start | bytes 442376 | tf_op jit(solution)/shard_map/ppermute | solution.py:430
  71.0 6.3 %collective-permute-start.18 = (bf16[192,384]{1,0:T(8,128)(2,1)S(1)}, bf16[192,384]{1,0:T(8,128)(2,1)S(1)}, u32[]{:S(2)}, u32[]{:S(2)}) collective-permute-start(bf16[192,384]{1,0:T(8,128)(2,1)S(1)} %get-tuple-element.39), channel_id=1, source_target_pairs={{0,2},{1,3},{2,0},{3,1},{4,6},{5,7},{6,4},{7,5},{8,10},{9,11},{10,... | collective-permute-start | bytes 442376 | tf_op jit(solution)/shard_map/ppermute | solution.py:430
  72.2 8.0 %collective-permute-start.19 = (bf16[192,384]{1,0:T(8,128)(2,1)S(1)}, bf16[192,384]{1,0:T(8,128)(2,1)S(1)}, u32[]{:S(2)}, u32[]{:S(2)}) collective-permute-start(bf16[192,384]{1,0:T(8,128)(2,1)S(1)} %get-tuple-element.40), channel_id=1, source_target_pairs={{0,3},{1,2},{2,1},{3,0},{4,7},{5,6},{6,5},{7,4},{8,11},{9,10},{10,... | collective-permute-start | bytes 442376 | tf_op jit(solution)/shard_map/ppermute | solution.py:430
  80.5 7.0 %collective-permute-start.20 = (bf16[96,384]{1,0:T(8,128)(2,1)S(1)}, bf16[96,384]{1,0:T(8,128)(2,1)S(1)}, u32[]{:S(2)}, u32[]{:S(2)}) collective-permute-start(bf16[96,384]{1,0:T(8,128)(2,1)S(1)} %get-tuple-element.42), channel_id=1, source_target_pairs={{0,4},{4,8},{8,12},{12,0},{1,5},{5,9},{9,13},{13,1},{2,6},{6,10},{... | collective-permute-start | bytes 221192 | tf_op jit(solution)/shard_map/ppermute | solution.py:506
  81.2 8.2 %collective-permute-start.21 = (bf16[96,384]{1,0:T(8,128)(2,1)S(1)}, bf16[96,384]{1,0:T(8,128)(2,1)S(1)}, u32[]{:S(2)}, u32[]{:S(2)}) collective-permute-start(bf16[96,384]{1,0:T(8,128)(2,1)S(1)} %get-tuple-element.43), channel_id=1, source_target_pairs={{0,8},{4,12},{8,0},{12,4},{1,9},{5,13},{9,1},{13,5},{2,10},{6,14},... | collective-permute-start | bytes 221192 | tf_op jit(solution)/shard_map/ppermute | solution.py:506
  83.1 6.3 %collective-permute-start.22 = (bf16[96,384]{1,0:T(8,128)(2,1)S(1)}, bf16[96,384]{1,0:T(8,128)(2,1)S(1)}, u32[]{:S(2)}, u32[]{:S(2)}) collective-permute-start(bf16[96,384]{1,0:T(8,128)(2,1)S(1)} %get-tuple-element.44), channel_id=1, source_target_pairs={{0,12},{4,0},{8,4},{12,8},{1,13},{5,1},{9,5},{13,9},{2,14},{6,2},{... | collective-permute-start | bytes 221192 | tf_op jit(solution)/shard_map/ppermute | solution.py:506

commit v3 on v2

--- a/solution.py
+++ b/solution.py
@@ -108,7 +108,7 @@
         out[...] = jnp.where(clips[here, :] < CLIPS, result, 0.0).astype(BF16)
 
 
-def regroup_kernel(own, back1, back2, back3, after, first, second):
+def regroup_kernel(own, back1, back2, back3, first, second):
     side, place = lax.axis_index("cfg"), lax.axis_index("seq")
     half = first.shape[0]
     for head in range(3):
@@ -235,7 +235,7 @@
     )(*pieces, after)
 
 
-def attention_by_head(query, key, value, slot_clip, early, weights, rest):
+def attention_by_head(query, key, value, slot_clip, early, weights):
     slots = query.shape[0]
     packed = pl.pallas_call(
         pack_kernel,
@@ -261,15 +261,14 @@
     )(*blocks, *early)
     backs = [hop(results[step], step, back=True) for step in (1, 2, 3)]
     half = slots // 2
-    whole = rest(results[0])
-    return whole, early[-2:], pl.pallas_call(
+    return early[-2:], pl.pallas_call(
         regroup_kernel,
         out_shape=[shape_of((half, 3 * HEAD_DIM))] * 2,
-        in_specs=[VMEM] * 4 + [ANY],
+        in_specs=[VMEM] * 4,
         out_specs=[VMEM] * 2,
         compiler_params=params(16),
         name="regroup",
-    )(results[0], *backs, whole)
+    )(results[0], *backs)
 
 
 def attention_by_rows(query, key, value, slot_clip):
@@ -317,21 +316,15 @@
 
 def feed_kernel(turn, *refs):
     (att, (w_out, up, down, res_hbm, mod, clip_ref), out) = refs[:4], refs[4:10], refs[10]
-    rows_in, res, mixed, total, normed, hidden, sems = refs[11:]
+    res, mixed, total, normed, hidden, sem = refs[11:]
     side, blk = lax.axis_index("cfg"), lax.axis_index("blk")
     half = out.shape[0]
     which = 1 - side if turn == 0 else side
     rows = pl.ds(pl.multiple_of(which * half, half), half)
     width = att[0].shape[1]
-    plan = [
-        (att[step], rows_in.at[:, step * width : (step + 1) * width]) for step in range(4)
-    ] + [(res_hbm.at[rows, :], res)]
-    copies = [
-        pltpu.make_async_copy(source, target, sems.at[index])
-        for index, (source, target) in enumerate(plan)
-    ]
-    for copy in copies:
-        copy.start()
+    copy = pltpu.make_async_copy(res_hbm.at[rows, :], res, sem)
+    copy.start()
+    rows_in = jnp.concatenate([piece[...] for piece in att], axis=1)
     clip = clip_ref[rows, :][:, :1]
     tile = 512
 
@@ -342,13 +335,13 @@
             picked = jnp.where(clip == index, line, picked)
         return picked
 
-    for copy in copies:
-        copy.wait()
     for start in range(0, D, tile):
         columns = slice(start, start + tile)
-        projected = jnp.dot(rows_in[...], w_out[:, columns], preferred_element_type=F32)
-        mixed[:, columns] = res[:, columns].astype(F32) + chosen(0, columns) * projected
-    held = mixed[...]
+        projected = jnp.dot(rows_in, w_out[:, columns], preferred_element_type=F32)
+        mixed[:, columns] = chosen(0, columns) * projected
+    copy.wait()
+    held = mixed[...] + res[...].astype(F32)
+    mixed[...] = held
     centre = held - jnp.mean(held, axis=1, keepdims=True)
     spread = lax.rsqrt(jnp.mean(centre * centre, axis=1, keepdims=True) + 1e-06)
     for start in range(0, D, tile):
@@ -373,16 +366,15 @@
     return pl.pallas_call(
         functools.partial(feed_kernel, turn),
         out_shape=shape_of((half, D), BF16 if turn == 0 else F32),
-        in_specs=[ANY] * 4 + [VMEM] * 3 + [ANY] + [VMEM] * 2,
+        in_specs=[VMEM] * 7 + [ANY] + [VMEM] * 2,
         out_specs=VMEM,
         scratch_shapes=[
-            pltpu.VMEM((half, D), BF16),
             pltpu.VMEM((half, D), BF16),
             pltpu.VMEM((half, D), F32),
             pltpu.VMEM((half, D), F32),
             pltpu.VMEM((half, D), BF16),
             pltpu.VMEM((half, D), BF16),
-            pltpu.SemaphoreType.DMA((5,)),
+            pltpu.SemaphoreType.DMA,
         ],
         compiler_params=params(24),
         cost_estimate=cost(2**36, 2**24),
@@ -456,20 +448,19 @@
 
     near, w_half = fetch_near(w_out)
     if seq_count == 4:
-        whole, (up, down), attended = attention_by_head(
+        (up, down), attended = attention_by_head(
             queries[0],
             keys[0],
             values[0],
             slot_clip,
             (clip_wide, placing, w_half),
             (w_up, w_down),
-            functools.partial(fetch_rest, w_out, near, w_half),
         )
     else:
         attended = attention_by_rows(queries[0], keys[0], values[0], slot_clip)
         up, down = load(w_up, w_down, attended[0])
-        whole = fetch_rest(w_out, near, w_half, attended[0])
-
+
+    whole = fetch_rest(w_out, near, w_half, attended[0])
     parts = []
     for turn in range(2):
         piece = attended[turn]

time: 90.6 us -> 87.2 us (0.962)
  waiting for transfers between devices: 25.7 us -> 23.2 us
  Pallas kernels: 23.2 us -> 22 us
    ppermute x2, waiting for transfers between devices: 0.3 us -> 4.11 us  [across(): return lax.ppermute(value, ('cfg', 'blk'), pairs)]
    ppermute x12, waiting for transfers between devices: 12.4 us -> 9.51 us  [exchanged(): return lax.ppermute(value, axis, pairs)]
    ppermute x6, waiting for transfers between devices: 9.59 us -> 7 us  [hop(): return lax.ppermute(value, ('cfg', 'seq'), pairs)]
    pallas_call x2, Pallas kernels: 10.3 us -> 9.12 us  [feed(): pl.pallas_call(functools.partial(feed_kernel, turn), out_shape=shape_of((...]
  transfers between devices with their start and end apart: 23 -> 23, of which waited for: 10 -> 11; matrix products, arithmetic and copies ran while one was open for 1% -> 1% of each run, Pallas kernels for 23% -> 23%
where the time goes in v3:
time: 87.2 us; the launch traced here: 86.7 us
  starting transfers between devices  39.4 us (45%)
  waiting for transfers between devices  23.2 us (27%)
  Pallas kernels  22 us (25%)
  other arithmetic  1 us (1%)
  local copies, waits for them, and re-layouts  0.88 us (1%)
    ppermute x6, starting transfers between devices, hop(): return lax.ppermute(value, ('cfg', 'seq'), pairs)  17.5 us
    ppermute x12, starting transfers between devices, exchanged(): return lax.ppermute(value, axis, pairs)  10.8 us
    ppermute x12, waiting for transfers between devices, exchanged(): return lax.ppermute(value, axis, pairs)  9.51 us
    pallas_call x2, Pallas kernels, feed(): pl.pallas_call(functools.partial(feed_kernel, turn), out_shape=shape_of((...  9.12 us
    ppermute x6, waiting for transfers between devices, hop(): return lax.ppermute(value, ('cfg', 'seq'), pairs)  7 us
    ppermute x3, starting transfers between devices, shards(): lax.ppermute(placed[step], 'seq', [(i, (i + step) % 4) for i in range(4)])  6.01 us
    ppermute x2, starting transfers between devices, across(): return lax.ppermute(value, ('cfg', 'blk'), pairs)  5.06 us
    ppermute x2, waiting for transfers between devices, across(): return lax.ppermute(value, ('cfg', 'blk'), pairs)  4.11 us
  transfers between devices with their start and end apart: 23, of which 11 were waited for; matrix products, arithmetic and copies ran while one was open for 1% of the time, Pallas kernels for 23%

profile of v3, /device:TPU:0, one launch (start us, length us, event | category | flops | bytes accessed | tf_op | source)
XLA Modules:
  0.0 86.7 jit_solution(598550940468801867)
XLA Ops:
  0.0 2.9 %collective-permute-start.3 = (bf16[384,1536]{1,0:T(8,128)(2,1)}, bf16[384,1536]{1,0:T(8,128)(2,1)S(1)}, u32[]{:S(2)}, u32[]{:S(2)}) collective-permute-start(bf16[384,1536]{1,0:T(8,128)(2,1)} %own.1), channel_id=1, source_target_pairs={{0,1},{1,0},{2,3},{3,2},{16,18},{17,19},{18,16},{19,17},{4,5},{5,4... | collective-permute-start | bytes 3538952 | tf_op jit(solution)/shard_map/ppermute | solution.py:162
  2.9 0.7 copy-done.1
  3.6 1.4 %pack.1 = (bf16[1168,128]{1,0:T(8,128)(2,1)S(1)}, bf16[1168,128]{1,0:T(8,128)(2,1)S(1)}, bf16[1168,128]{1,0:T(8,128)(2,1)S(1)}, bf16[1168,128]{1,0:T(8,128)(2,1)S(1)}) custom-call(bf16[384,384]{1,0:T(8,128)(2,1)} %bitcast.8, bf16[384,384]{1,0:T(8,128)(2,1)} %bitcast.9, bf16[384,384]{1,0:T(8,128)(2,1)} %bitcast.10, s32[3,128]{1,0:T(4,128)S(1)} %bitcast.7), custom_call_target="tpu_custom_call" | custom-call | tf_op jit(solution)/shard_map/pack/pallas_call | solution.py:240
  5.1 3.5 %collective-permute-start = (bf16[1168,128]{1,0:T(8,128)(2,1)S(1)}, bf16[1168,128]{1,0:T(8,128)(2,1)S(1)}, u32[]{:S(2)}, u32[]{:S(2)}) collective-permute-start(bf16[1168,128]{1,0:T(8,128)(2,1)S(1)} %get-tuple-element.26), channel_id=1, source_target_pairs={{0,4},{4,8},{12,0},{16,20},{20,24},{24,28},{1,5},{5,9},{13,1},{17,... | collective-permute-start | bytes 897032 | tf_op jit(solution)/shard_map/ppermute | solution.py:50
  8.6 2.3 %collective-permute-start.1 = (bf16[1168,128]{1,0:T(8,128)(2,1)S(1)}, bf16[1168,128]{1,0:T(8,128)(2,1)S(1)}, u32[]{:S(2)}, u32[]{:S(2)}) collective-permute-start(bf16[1168,128]{1,0:T(8,128)(2,1)S(1)} %get-tuple-element.27), channel_id=1, source_target_pairs={{0,8},{8,0},{12,4},{16,24},{20,28},{28,20},{1,9},{9,1},{13,5},{17,... | collective-permute-start | bytes 897032 | tf_op jit(solution)/shard_map/ppermute | solution.py:50
  10.9 1.3 %collective-permute-start.2 = (bf16[1168,128]{1,0:T(8,128)(2,1)S(1)}, bf16[1168,128]{1,0:T(8,128)(2,1)S(1)}, u32[]{:S(2)}, u32[]{:S(2)}) collective-permute-start(bf16[1168,128]{1,0:T(8,128)(2,1)S(1)} %get-tuple-element.28), channel_id=1, source_target_pairs={{4,0},{8,4},{12,8},{16,28},{24,20},{28,24},{5,1},{9,5},{13,9},{17,... | collective-permute-start | bytes 897032 | tf_op jit(solution)/shard_map/ppermute | solution.py:50
  12.2 0.1 constant_dynamic-slice_fusion
  12.3 0.2 convert_reduce_fusion
  12.5 0.8 compare_select_fusion.2
  13.2 4.1 %collective-permute-done.3.got.near = bf16[384,1536]{1,0:T(8,128)(2,1)S(1)} collective-permute-done((bf16[384,1536]{1,0:T(8,128)(2,1)}, bf16[384,1536]{1,0:T(8,128)(2,1)S(1)}, u32[]{:S(2)}, u32[]{:S(2)}) %collective-permute-start.3) | collective-permute-done | bytes 1179680 | tf_op jit(solution)/shard_map/ppermute | solution.py:162
  17.3 0.1 cut.1.refs_6_
  17.5 2.1 %collective-permute-start.11 = (bf16[192,1536]{1,0:T(8,128)(2,1)S(1)}, bf16[192,1536]{1,0:T(8,128)(2,1)S(1)}, u32[]{:S(2)}, u32[]{:S(2)}) collective-permute-start(bf16[192,1536]{1,0:T(8,128)(2,1)S(1)} %cut.1.refs_6_), channel_id=1, source_target_pairs={{0,2},{1,3},{2,0},{3,1},{16,17},{17,16},{18,19},{19,18},{4,6},{5,7... | collective-permute-start | bytes 1769480 | tf_op jit(solution)/shard_map/ppermute | solution.py:162
  19.6 3.8 %load.1 = (bf16[1536,1536]{1,0:T(8,128)(2,1)S(1)}, bf16[1536,1536]{1,0:T(8,128)(2,1)S(1)}) custom-call(bf16[1536,1536]{1,0:T(8,128)(2,1)} %up.1, bf16[1536,1536]{1,0:T(8,128)(2,1)} %down.1, bf16[1168,128]{1,0:T(8,128)(2,1)S(1)} %get-tuple-element.25.after.refs_0_), custom_call_target="tpu_custom_call" | custom-call | tf_op jit(solution)/shard_map/load/pallas_call | solution.py:147
  23.5 4.8 %collective-permute-done.1.refs_2_ = bf16[1168,128]{1,0:T(8,128)(2,1)S(1)} collective-permute-done((bf16[1168,128]{1,0:T(8,128)(2,1)S(1)}, bf16[1168,128]{1,0:T(8,128)(2,1)S(1)}, u32[]{:S(2)}, u32[]{:S(2)}) %collective-permute-start.1) | collective-permute-done | bytes 299040 | tf_op jit(solution)/shard_map/ppermute | solution.py:50
  28.3 0.1 broadcast_in_dim.7.refs_4_.refs_9_.clip_ref
  28.4 4.0 %attend.1 = (bf16[384,128]{1,0:T(8,128)(2,1)S(1)}, bf16[384,128]{1,0:T(8,128)(2,1)S(1)}, bf16[384,128]{1,0:T(8,128)(2,1)S(1)}, bf16[384,128]{1,0:T(8,128)(2,1)S(1)}) custom-call(bf16[1168,128]{1,0:T(8,128)(2,1)S(1)} %get-tuple-element.25.after.refs_0_, bf16[1168,128]{1,0:T(8,128)(2,1)S(1)} %collective-permute-done.refs_1_, ...), custom_call_target="tpu_custom_call" | custom-call | flops 4294967296 | bytes 2097152 | tf_op jit(solution)/shard_map/attend/pallas_call | solution.py:251
  32.4 1.9 %collective-permute-start.4 = (bf16[384,128]{1,0:T(8,128)(2,1)S(1)}, bf16[384,128]{1,0:T(8,128)(2,1)S(1)}, u32[]{:S(2)}, u32[]{:S(2)}) collective-permute-start(bf16[384,128]{1,0:T(8,128)(2,1)S(1)} %get-tuple-element.32), channel_id=1, source_target_pairs={{4,0},{8,4},{0,12},{20,16},{24,20},{28,24},{5,1},{9,5},{1,13},{21,... | collective-permute-start | bytes 294920 | tf_op jit(solution)/shard_map/ppermute | solution.py:50
  34.3 7.2 %collective-permute-start.5 = (bf16[384,128]{1,0:T(8,128)(2,1)S(1)}, bf16[384,128]{1,0:T(8,128)(2,1)S(1)}, u32[]{:S(2)}, u32[]{:S(2)}) collective-permute-start(bf16[384,128]{1,0:T(8,128)(2,1)S(1)} %get-tuple-element.33), channel_id=1, source_target_pairs={{8,0},{0,8},{4,12},{24,16},{28,20},{20,28},{9,1},{1,9},{5,13},{25,... | collective-permute-start | bytes 294920 | tf_op jit(solution)/shard_map/ppermute | solution.py:50
  41.5 1.3 %collective-permute-start.6 = (bf16[384,128]{1,0:T(8,128)(2,1)S(1)}, bf16[384,128]{1,0:T(8,128)(2,1)S(1)}, u32[]{:S(2)}, u32[]{:S(2)}) collective-permute-start(bf16[384,128]{1,0:T(8,128)(2,1)S(1)} %get-tuple-element.34), channel_id=1, source_target_pairs={{0,4},{4,8},{8,12},{28,16},{20,24},{24,28},{1,5},{5,9},{9,13},{29,... | collective-permute-start | bytes 294920 | tf_op jit(solution)/shard_map/ppermute | solution.py:50
  42.9 1.4 %collective-permute-done.5.back2 = bf16[384,128]{1,0:T(8,128)(2,1)S(1)} collective-permute-done((bf16[384,128]{1,0:T(8,128)(2,1)S(1)}, bf16[384,128]{1,0:T(8,128)(2,1)S(1)}, u32[]{:S(2)}, u32[]{:S(2)}) %collective-permute-start.5) | collective-permute-done | bytes 98336 | tf_op jit(solution)/shard_map/ppermute | solution.py:50
  44.3 0.7 collective-permute-done.6.back3
  45.0 0.3 regroup.1
  45.4 0.1 collective-permute-start.12
  45.4 0.4 collective-permute-start.13
  45.8 1.7 %collective-permute-start.14 = (bf16[192,384]{1,0:T(8,128)(2,1)S(1)}, bf16[192,384]{1,0:T(8,128)(2,1)S(1)}, u32[]{:S(2)}, u32[]{:S(2)}) collective-permute-start(bf16[192,384]{1,0:T(8,128)(2,1)S(1)} %get-tuple-element.36.after.refs_0_), channel_id=1, source_target_pairs={{0,2},{1,3},{2,0},{3,1},{4,6},{5,7},{6,4},{7,5},{8,10},{9,11},{10,... | collective-permute-start | bytes 442376 | tf_op jit(solution)/shard_map/ppermute | solution.py:422
  47.6 1.4 %collective-permute-start.15 = (bf16[192,384]{1,0:T(8,128)(2,1)S(1)}, bf16[192,384]{1,0:T(8,128)(2,1)S(1)}, u32[]{:S(2)}, u32[]{:S(2)}) collective-permute-start(bf16[192,384]{1,0:T(8,128)(2,1)S(1)} %get-tuple-element.36.after.refs_0_), channel_id=1, source_target_pairs={{0,3},{1,2},{2,1},{3,0},{4,7},{5,6},{6,5},{7,4},{8,11},{9,10},{10,... | collective-permute-start | bytes 442376 | tf_op jit(solution)/shard_map/ppermute | solution.py:422
  49.0 0.3 collective-permute-start.7
  49.3 1.7 %collective-permute-start.8 = (bf16[192,384]{1,0:T(8,128)(2,1)S(1)}, bf16[192,384]{1,0:T(8,128)(2,1)S(1)}, u32[]{:S(2)}, u32[]{:S(2)}) collective-permute-start(bf16[192,384]{1,0:T(8,128)(2,1)S(1)} %get-tuple-element.35.refs_0_), channel_id=1, source_target_pairs={{0,2},{1,3},{2,0},{3,1},{4,6},{5,7},{6,4},{7,5},{8,10},{9,11},{10,... | collective-permute-start | bytes 442376 | tf_op jit(solution)/shard_map/ppermute | solution.py:422
  51.1 1.3 %join.1.refs_4_ = bf16[1536,1536]{1,0:T(8,128)(2,1)S(1)} custom-call(bf16[384,1536]{1,0:T(8,128)(2,1)} %own.1, bf16[384,1536]{1,0:T(8,128)(2,1)S(1)} %collective-permute-done.3.got.near, bf16[384,1536]{1,0:T(8,128)(2,1)S(1)} %collective-permute-done.10.near_swap, bf16[192,1536]{1,0:T(8,128)(2,1)S(1)} %gate.1.far, ...), custom_call_target="tpu_custom_call" | custom-call | tf_op jit(solution)/shard_map/join/pallas_call | solution.py:227
  52.4 1.5 %collective-permute-start.9 = (bf16[192,384]{1,0:T(8,128)(2,1)S(1)}, bf16[192,384]{1,0:T(8,128)(2,1)S(1)}, u32[]{:S(2)}, u32[]{:S(2)}) collective-permute-start(bf16[192,384]{1,0:T(8,128)(2,1)S(1)} %get-tuple-element.35.refs_0_), channel_id=1, source_target_pairs={{0,3},{1,2},{2,1},{3,0},{4,7},{5,6},{6,5},{7,4},{8,11},{9,10},{10,... | collective-permute-start | bytes 442376 | tf_op jit(solution)/shard_map/ppermute | solution.py:422
  53.9 0.7 collective-permute-done.14.refs_2_
  54.6 1.7 %collective-permute-done.15.refs_3_ = bf16[192,384]{1,0:T(8,128)(2,1)S(1)} collective-permute-done((bf16[192,384]{1,0:T(8,128)(2,1)S(1)}, bf16[192,384]{1,0:T(8,128)(2,1)S(1)}, u32[]{:S(2)}, u32[]{:S(2)}) %collective-permute-start.15) | collective-permute-done | bytes 147488 | tf_op jit(solution)/shard_map/ppermute | solution.py:422
  56.3 4.2 %feed.3 = bf16[192,1536]{1,0:T(8,128)(2,1)S(1)} custom-call(bf16[192,384]{1,0:T(8,128)(2,1)S(1)} %get-tuple-element.36.after.refs_0_, bf16[192,384]{1,0:T(8,128)(2,1)S(1)} %collective-permute-done.13.refs_1_, bf16[192,384]{1,0:T(8,128)(2,1)S(1)} %collective-permute-done.14.refs_2_, bf16[192,384]{1,0:T(8,128)(2,1)S(1)} %collective-permute-done.15.refs_3_, ...), custom_call_target="tpu_custom_call" | custom-call | flops 68719476736 | bytes 16777216 | tf_op jit(solution)/shard_map/feed/pallas_call | solution.py:366
  60.7 1.5 %collective-permute-done.9.refs_3_ = bf16[192,384]{1,0:T(8,128)(2,1)S(1)} collective-permute-done((bf16[192,384]{1,0:T(8,128)(2,1)S(1)}, bf16[192,384]{1,0:T(8,128)(2,1)S(1)}, u32[]{:S(2)}, u32[]{:S(2)}) %collective-permute-start.9) | collective-permute-done | bytes 147488 | tf_op jit(solution)/shard_map/ppermute | solution.py:422
  62.2 4.9 %feed.2.mine_ref = f32[192,1536]{1,0:T(8,128)S(1)} custom-call(bf16[192,384]{1,0:T(8,128)(2,1)S(1)} %get-tuple-element.35.refs_0_, bf16[192,384]{1,0:T(8,128)(2,1)S(1)} %collective-permute-done.7.refs_1_, bf16[192,384]{1,0:T(8,128)(2,1)S(1)} %collective-permute-done.8.refs_2_, bf16[192,384]{1,0:T(8,128)(2,1)S(1)} %collective-permute-done.9.refs_3_, ...), custom_call_target="tpu_custom_call" | custom-call | flops 68719476736 | bytes 16777216 | tf_op jit(solution)/shard_map/feed/pallas_call | solution.py:366
  67.1 0.8 guide.1
  67.9 0.8 collective-permute-start.17
  68.7 1.5 %collective-permute-start.18 = (bf16[192,384]{1,0:T(8,128)(2,1)S(1)}, bf16[192,384]{1,0:T(8,128)(2,1)S(1)}, u32[]{:S(2)}, u32[]{:S(2)}) collective-permute-start(bf16[192,384]{1,0:T(8,128)(2,1)S(1)} %get-tuple-element.39), channel_id=1, source_target_pairs={{0,2},{1,3},{2,0},{3,1},{4,6},{5,7},{6,4},{7,5},{8,10},{9,11},{10,... | collective-permute-start | bytes 442376 | tf_op jit(solution)/shard_map/ppermute | solution.py:422
  70.3 1.2 %collective-permute-start.19 = (bf16[192,384]{1,0:T(8,128)(2,1)S(1)}, bf16[192,384]{1,0:T(8,128)(2,1)S(1)}, u32[]{:S(2)}, u32[]{:S(2)}) collective-permute-start(bf16[192,384]{1,0:T(8,128)(2,1)S(1)} %get-tuple-element.40), channel_id=1, source_target_pairs={{0,3},{1,2},{2,1},{3,0},{4,7},{5,6},{6,5},{7,4},{8,11},{9,10},{10,... | collective-permute-start | bytes 442376 | tf_op jit(solution)/shard_map/ppermute | solution.py:422
  71.5 3.3 %collective-permute-done.17.got1 = bf16[192,384]{1,0:T(8,128)(2,1)S(1)} collective-permute-done((bf16[192,384]{1,0:T(8,128)(2,1)S(1)}, bf16[192,384]{1,0:T(8,128)(2,1)S(1)}, u32[]{:S(2)}, u32[]{:S(2)}) %collective-permute-start.17) | collective-permute-done | bytes 147488 | tf_op jit(solution)/shard_map/ppermute | solution.py:422
  74.7 2.3 %collective-permute-done.18.got2 = bf16[192,384]{1,0:T(8,128)(2,1)S(1)} collective-permute-done((bf16[192,384]{1,0:T(8,128)(2,1)S(1)}, bf16[192,384]{1,0:T(8,128)(2,1)S(1)}, u32[]{:S(2)}, u32[]{:S(2)}) %collective-permute-start.18) | collective-permute-done | bytes 147488 | tf_op jit(solution)/shard_map/ppermute | solution.py:422
  77.0 0.3 place.1
  77.4 2.4 %collective-permute-start.20 = (bf16[96,384]{1,0:T(8,128)(2,1)S(1)}, bf16[96,384]{1,0:T(8,128)(2,1)S(1)}, u32[]{:S(2)}, u32[]{:S(2)}) collective-permute-start(bf16[96,384]{1,0:T(8,128)(2,1)S(1)} %get-tuple-element.42), channel_id=1, source_target_pairs={{0,4},{4,8},{8,12},{12,0},{1,5},{5,9},{9,13},{13,1},{2,6},{6,10},{... | collective-permute-start | bytes 221192 | tf_op jit(solution)/shard_map/ppermute | solution.py:497
  79.8 0.7 collective-permute-start.21
  80.5 2.8 %collective-permute-start.22 = (bf16[96,384]{1,0:T(8,128)(2,1)S(1)}, bf16[96,384]{1,0:T(8,128)(2,1)S(1)}, u32[]{:S(2)}, u32[]{:S(2)}) collective-permute-start(bf16[96,384]{1,0:T(8,128)(2,1)S(1)} %get-tuple-element.44), channel_id=1, source_target_pairs={{0,12},{4,0},{8,4},{12,8},{1,13},{5,1},{9,5},{13,9},{2,14},{6,2},{... | collective-permute-start | bytes 221192 | tf_op jit(solution)/shard_map/ppermute | solution.py:497
  83.4 1.0 %collective-permute-done.20.got1 = bf16[96,384]{1,0:T(8,128)(2,1)S(1)} collective-permute-done((bf16[96,384]{1,0:T(8,128)(2,1)S(1)}, bf16[96,384]{1,0:T(8,128)(2,1)S(1)}, u32[]{:S(2)}, u32[]{:S(2)}) %collective-permute-start.20) | collective-permute-done | bytes 73760 | tf_op jit(solution)/shard_map/ppermute | solution.py:497
  84.3 1.6 %collective-permute-done.21.got2 = bf16[96,384]{1,0:T(8,128)(2,1)S(1)} collective-permute-done((bf16[96,384]{1,0:T(8,128)(2,1)S(1)}, bf16[96,384]{1,0:T(8,128)(2,1)S(1)}, u32[]{:S(2)}, u32[]{:S(2)}) %collective-permute-start.21) | collective-permute-done | bytes 73760 | tf_op jit(solution)/shard_map/ppermute | solution.py:497
  86.0 0.8 arrange.1
  (25 shorter events, 0.2 us)
Async XLA Ops:
  0.0 12.2 %copy-start = (s32[384,1]{0,1:T(1,128)S(1)}, s32[384,1]{0,1:T(1,128)}, u32[]{:S(2)}) copy-start(s32[384,1]{0,1:T(1,128)} %param.21) | copy-start | bytes 4612
  0.0 17.3 %collective-permute-start.3 = (bf16[384,1536]{1,0:T(8,128)(2,1)}, bf16[384,1536]{1,0:T(8,128)(2,1)S(1)}, u32[]{:S(2)}, u32[]{:S(2)}) collective-permute-start(bf16[384,1536]{1,0:T(8,128)(2,1)} %own.1), channel_id=1, source_target_pairs={{0,1},{1,0},{2,3},{3,2},{16,18},{17,19},{18,16},{19,17},{4,5},{5,4... | collective-permute-start | bytes 3538952 | tf_op jit(solution)/shard_map/ppermute | solution.py:162
  2.9 0.7 copy-start.1
  5.1 18.4 %collective-permute-start = (bf16[1168,128]{1,0:T(8,128)(2,1)S(1)}, bf16[1168,128]{1,0:T(8,128)(2,1)S(1)}, u32[]{:S(2)}, u32[]{:S(2)}) collective-permute-start(bf16[1168,128]{1,0:T(8,128)(2,1)S(1)} %get-tuple-element.26), channel_id=1, source_target_pairs={{0,4},{4,8},{12,0},{16,20},{20,24},{24,28},{1,5},{5,9},{13,1},{17,... | collective-permute-start | bytes 897032 | tf_op jit(solution)/shard_map/ppermute | solution.py:50
  8.6 19.7 %collective-permute-start.1 = (bf16[1168,128]{1,0:T(8,128)(2,1)S(1)}, bf16[1168,128]{1,0:T(8,128)(2,1)S(1)}, u32[]{:S(2)}, u32[]{:S(2)}) collective-permute-start(bf16[1168,128]{1,0:T(8,128)(2,1)S(1)} %get-tuple-element.27), channel_id=1, source_target_pairs={{0,8},{8,0},{12,4},{16,24},{20,28},{28,20},{1,9},{9,1},{13,5},{17,... | collective-permute-start | bytes 897032 | tf_op jit(solution)/shard_map/ppermute | solution.py:50
  10.9 17.4 %collective-permute-start.2 = (bf16[1168,128]{1,0:T(8,128)(2,1)S(1)}, bf16[1168,128]{1,0:T(8,128)(2,1)S(1)}, u32[]{:S(2)}, u32[]{:S(2)}) collective-permute-start(bf16[1168,128]{1,0:T(8,128)(2,1)S(1)} %get-tuple-element.28), channel_id=1, source_target_pairs={{4,0},{8,4},{12,8},{16,28},{24,20},{28,24},{5,1},{9,5},{13,9},{17,... | collective-permute-start | bytes 897032 | tf_op jit(solution)/shard_map/ppermute | solution.py:50
  17.5 27.9 %collective-permute-start.11 = (bf16[192,1536]{1,0:T(8,128)(2,1)S(1)}, bf16[192,1536]{1,0:T(8,128)(2,1)S(1)}, u32[]{:S(2)}, u32[]{:S(2)}) collective-permute-start(bf16[192,1536]{1,0:T(8,128)(2,1)S(1)} %cut.1.refs_6_), channel_id=1, source_target_pairs={{0,2},{1,3},{2,0},{3,1},{16,17},{17,16},{18,19},{19,18},{4,6},{5,7... | collective-permute-start | bytes 1769480 | tf_op jit(solution)/shard_map/ppermute | solution.py:162
  19.6 29.7 %collective-permute-start.10 = (bf16[384,1536]{1,0:T(8,128)(2,1)S(1)}, bf16[384,1536]{1,0:T(8,128)(2,1)S(1)}, u32[]{:S(2)}, u32[]{:S(2)}) collective-permute-start(bf16[384,1536]{1,0:T(8,128)(2,1)S(1)} %collective-permute-done.3.got.near), channel_id=1, source_target_pairs={{0,16},{16,0},{1,17},{17,1},{2,18},{18,2},{3,19},{19,3},{4,20},{20... | collective-permute-start | bytes 3538952 | tf_op jit(solution)/shard_map/ppermute | solution.py:422
  19.6 8.6 %copy-start.2 = (s32[384]{0:T(512)S(1)}, s32[384]{0:T(512)}, u32[]{:S(2)}) copy-start(s32[384]{0:T(512)} %param.20) | copy-start | bytes 4612
  32.4 10.4 %collective-permute-start.4 = (bf16[384,128]{1,0:T(8,128)(2,1)S(1)}, bf16[384,128]{1,0:T(8,128)(2,1)S(1)}, u32[]{:S(2)}, u32[]{:S(2)}) collective-permute-start(bf16[384,128]{1,0:T(8,128)(2,1)S(1)} %get-tuple-element.32), channel_id=1, source_target_pairs={{4,0},{8,4},{0,12},{20,16},{24,20},{28,24},{5,1},{9,5},{1,13},{21,... | collective-permute-start | bytes 294920 | tf_op jit(solution)/shard_map/ppermute | solution.py:50
  34.3 10.0 %collective-permute-start.5 = (bf16[384,128]{1,0:T(8,128)(2,1)S(1)}, bf16[384,128]{1,0:T(8,128)(2,1)S(1)}, u32[]{:S(2)}, u32[]{:S(2)}) collective-permute-start(bf16[384,128]{1,0:T(8,128)(2,1)S(1)} %get-tuple-element.33), channel_id=1, source_target_pairs={{8,0},{0,8},{4,12},{24,16},{28,20},{20,28},{9,1},{1,9},{5,13},{25,... | collective-permute-start | bytes 294920 | tf_op jit(solution)/shard_map/ppermute | solution.py:50
  41.5 3.5 %collective-permute-start.6 = (bf16[384,128]{1,0:T(8,128)(2,1)S(1)}, bf16[384,128]{1,0:T(8,128)(2,1)S(1)}, u32[]{:S(2)}, u32[]{:S(2)}) collective-permute-start(bf16[384,128]{1,0:T(8,128)(2,1)S(1)} %get-tuple-element.34), channel_id=1, source_target_pairs={{0,4},{4,8},{8,12},{28,16},{20,24},{24,28},{1,5},{5,9},{9,13},{29,... | collective-permute-start | bytes 294920 | tf_op jit(solution)/shard_map/ppermute | solution.py:50
  45.4 3.6 %collective-permute-start.12 = (bf16[192,1536]{1,0:T(8,128)(2,1)S(1)}, bf16[192,1536]{1,0:T(8,128)(2,1)S(1)}, u32[]{:S(2)}, u32[]{:S(2)}) collective-permute-start(bf16[192,1536]{1,0:T(8,128)(2,1)S(1)} %gate.1.far), channel_id=1, source_target_pairs={{0,16},{16,0},{1,17},{17,1},{2,18},{18,2},{3,19},{19,3},{4,20},{20... | collective-permute-start | bytes 1769480 | tf_op jit(solution)/shard_map/ppermute | solution.py:422
  45.4 7.0 %collective-permute-start.13 = (bf16[192,384]{1,0:T(8,128)(2,1)S(1)}, bf16[192,384]{1,0:T(8,128)(2,1)S(1)}, u32[]{:S(2)}, u32[]{:S(2)}) collective-permute-start(bf16[192,384]{1,0:T(8,128)(2,1)S(1)} %get-tuple-element.36.after.refs_0_), channel_id=1, source_target_pairs={{0,1},{1,0},{2,3},{3,2},{4,5},{5,4},{6,7},{7,6},{8,9},{9,8},{10,11... | collective-permute-start | bytes 442376 | tf_op jit(solution)/shard_map/ppermute | solution.py:422
  45.8 8.7 %collective-permute-start.14 = (bf16[192,384]{1,0:T(8,128)(2,1)S(1)}, bf16[192,384]{1,0:T(8,128)(2,1)S(1)}, u32[]{:S(2)}, u32[]{:S(2)}) collective-permute-start(bf16[192,384]{1,0:T(8,128)(2,1)S(1)} %get-tuple-element.36.after.refs_0_), channel_id=1, source_target_pairs={{0,2},{1,3},{2,0},{3,1},{4,6},{5,7},{6,4},{7,5},{8,10},{9,11},{10,... | collective-permute-start | bytes 442376 | tf_op jit(solution)/shard_map/ppermute | solution.py:422
  47.6 8.8 %collective-permute-start.15 = (bf16[192,384]{1,0:T(8,128)(2,1)S(1)}, bf16[192,384]{1,0:T(8,128)(2,1)S(1)}, u32[]{:S(2)}, u32[]{:S(2)}) collective-permute-start(bf16[192,384]{1,0:T(8,128)(2,1)S(1)} %get-tuple-element.36.after.refs_0_), channel_id=1, source_target_pairs={{0,3},{1,2},{2,1},{3,0},{4,7},{5,6},{6,5},{7,4},{8,11},{9,10},{10,... | collective-permute-start | bytes 442376 | tf_op jit(solution)/shard_map/ppermute | solution.py:422
  49.0 7.3 %copy-start.4 = (f32[3,4,1536]{2,1,0:T(4,128)S(1)}, f32[3,4,1536]{2,1,0:T(4,128)}, u32[]{:S(2)}) copy-start(f32[3,4,1536]{2,1,0:T(4,128)} %refs_8_.3) | copy-start | bytes 221188
  49.0 11.7 %collective-permute-start.7 = (bf16[192,384]{1,0:T(8,128)(2,1)S(1)}, bf16[192,384]{1,0:T(8,128)(2,1)S(1)}, u32[]{:S(2)}, u32[]{:S(2)}) collective-permute-start(bf16[192,384]{1,0:T(8,128)(2,1)S(1)} %get-tuple-element.35.refs_0_), channel_id=1, source_target_pairs={{0,1},{1,0},{2,3},{3,2},{4,5},{5,4},{6,7},{7,6},{8,9},{9,8},{10,11... | collective-permute-start | bytes 442376 | tf_op jit(solution)/shard_map/ppermute | solution.py:422
  49.3 11.3 %collective-permute-start.8 = (bf16[192,384]{1,0:T(8,128)(2,1)S(1)}, bf16[192,384]{1,0:T(8,128)(2,1)S(1)}, u32[]{:S(2)}, u32[]{:S(2)}) collective-permute-start(bf16[192,384]{1,0:T(8,128)(2,1)S(1)} %get-tuple-element.35.refs_0_), channel_id=1, source_target_pairs={{0,2},{1,3},{2,0},{3,1},{4,6},{5,7},{6,4},{7,5},{8,10},{9,11},{10,... | collective-permute-start | bytes 442376 | tf_op jit(solution)/shard_map/ppermute | solution.py:422
  52.4 9.8 %collective-permute-start.9 = (bf16[192,384]{1,0:T(8,128)(2,1)S(1)}, bf16[192,384]{1,0:T(8,128)(2,1)S(1)}, u32[]{:S(2)}, u32[]{:S(2)}) collective-permute-start(bf16[192,384]{1,0:T(8,128)(2,1)S(1)} %get-tuple-element.35.refs_0_), channel_id=1, source_target_pairs={{0,3},{1,2},{2,1},{3,0},{4,7},{5,6},{6,5},{7,4},{8,11},{9,10},{10,... | collective-permute-start | bytes 442376 | tf_op jit(solution)/shard_map/ppermute | solution.py:422
  60.6 6.5 %copy-start.3 = (f32[3]{0:T(128)S(1)}, f32[3]{0:T(128)}, u32[]{:S(2)}) copy-start(f32[3]{0:T(128)} %scale_ref.1) | copy-start | bytes 40
  60.6 6.5 %collective-permute-start.16 = (bf16[192,1536]{1,0:T(8,128)(2,1)S(1)}, bf16[192,1536]{1,0:T(8,128)(2,1)S(1)}, u32[]{:S(2)}, u32[]{:S(2)}) collective-permute-start(bf16[192,1536]{1,0:T(8,128)(2,1)S(1)} %feed.3), channel_id=1, source_target_pairs={{0,16},{16,0},{1,17},{17,1},{2,18},{18,2},{3,19},{19,3},{4,20},{20... | collective-permute-start | bytes 1769480 | tf_op jit(solution)/shard_map/ppermute | solution.py:422
  67.9 6.8 %collective-permute-start.17 = (bf16[192,384]{1,0:T(8,128)(2,1)S(1)}, bf16[192,384]{1,0:T(8,128)(2,1)S(1)}, u32[]{:S(2)}, u32[]{:S(2)}) collective-permute-start(bf16[192,384]{1,0:T(8,128)(2,1)S(1)} %get-tuple-element.38), channel_id=1, source_target_pairs={{0,1},{1,0},{2,3},{3,2},{4,5},{5,4},{6,7},{7,6},{8,9},{9,8},{10,11... | collective-permute-start | bytes 442376 | tf_op jit(solution)/shard_map/ppermute | solution.py:422
  68.7 8.3 %collective-permute-start.18 = (bf16[192,384]{1,0:T(8,128)(2,1)S(1)}, bf16[192,384]{1,0:T(8,128)(2,1)S(1)}, u32[]{:S(2)}, u32[]{:S(2)}) collective-permute-start(bf16[192,384]{1,0:T(8,128)(2,1)S(1)} %get-tuple-element.39), channel_id=1, source_target_pairs={{0,2},{1,3},{2,0},{3,1},{4,6},{5,7},{6,4},{7,5},{8,10},{9,11},{10,... | collective-permute-start | bytes 442376 | tf_op jit(solution)/shard_map/ppermute | solution.py:422
  70.3 6.8 %collective-permute-start.19 = (bf16[192,384]{1,0:T(8,128)(2,1)S(1)}, bf16[192,384]{1,0:T(8,128)(2,1)S(1)}, u32[]{:S(2)}, u32[]{:S(2)}) collective-permute-start(bf16[192,384]{1,0:T(8,128)(2,1)S(1)} %get-tuple-element.40), channel_id=1, source_target_pairs={{0,3},{1,2},{2,1},{3,0},{4,7},{5,6},{6,5},{7,4},{8,11},{9,10},{10,... | collective-permute-start | bytes 442376 | tf_op jit(solution)/shard_map/ppermute | solution.py:422
  77.4 7.0 %collective-permute-start.20 = (bf16[96,384]{1,0:T(8,128)(2,1)S(1)}, bf16[96,384]{1,0:T(8,128)(2,1)S(1)}, u32[]{:S(2)}, u32[]{:S(2)}) collective-permute-start(bf16[96,384]{1,0:T(8,128)(2,1)S(1)} %get-tuple-element.42), channel_id=1, source_target_pairs={{0,4},{4,8},{8,12},{12,0},{1,5},{5,9},{9,13},{13,1},{2,6},{6,10},{... | collective-permute-start | bytes 221192 | tf_op jit(solution)/shard_map/ppermute | solution.py:497
  79.8 6.2 %collective-permute-start.21 = (bf16[96,384]{1,0:T(8,128)(2,1)S(1)}, bf16[96,384]{1,0:T(8,128)(2,1)S(1)}, u32[]{:S(2)}, u32[]{:S(2)}) collective-permute-start(bf16[96,384]{1,0:T(8,128)(2,1)S(1)} %get-tuple-element.43), channel_id=1, source_target_pairs={{0,8},{4,12},{8,0},{12,4},{1,9},{5,13},{9,1},{13,5},{2,10},{6,14},... | collective-permute-start | bytes 221192 | tf_op jit(solution)/shard_map/ppermute | solution.py:497
  80.5 5.4 %collective-permute-start.22 = (bf16[96,384]{1,0:T(8,128)(2,1)S(1)}, bf16[96,384]{1,0:T(8,128)(2,1)S(1)}, u32[]{:S(2)}, u32[]{:S(2)}) collective-permute-start(bf16[96,384]{1,0:T(8,128)(2,1)S(1)} %get-tuple-element.44), channel_id=1, source_target_pairs={{0,12},{4,0},{8,4},{12,8},{1,13},{5,1},{9,5},{13,9},{2,14},{6,2},{... | collective-permute-start | bytes 221192 | tf_op jit(solution)/shard_map/ppermute | solution.py:497

commit v4 on v3

--- a/solution.py
+++ b/solution.py
@@ -31,6 +31,9 @@
     return pl.CostEstimate(flops=flops, bytes_accessed=moved, transcendentals=0)
 
 
+STEPS = (0, 2, 3, 1)
+
+
 def head_at(side, place):
     return jnp.where(side == 0, place, 3 - place)
 
@@ -43,7 +46,7 @@
     pairs = []
     for side in range(2):
         for place in range(4):
-            target = (place + step) % 4
+            target = place ^ step
             if works(side, target):
                 pair = (side * 4 + place, side * 4 + target)
                 pairs.append(pair[::-1] if back else pair)
@@ -51,19 +54,22 @@
 
 
 def pack_kernel(q_ref, k_ref, v_ref, clip_ref, *refs):
-    outs, sems = refs[:4], refs[4]
+    outs, clips, sems = refs[:4], refs[4], refs[5]
     side, place = lax.axis_index("cfg"), lax.axis_index("seq")
     slots = q_ref.shape[0]
+    clip_copy = pltpu.make_async_copy(clip_ref, clips, sems.at[12])
+    clip_copy.start()
     copies = []
-    for step, out in enumerate(outs):
-        head = jnp.clip(head_at(side, lax.rem(place + step, 4)), 0, 2)
+    for step, out in zip(STEPS, outs):
+        head = jnp.clip(head_at(side, jnp.bitwise_xor(place, step)), 0, 2)
         columns = pl.ds(pl.multiple_of(head * HEAD_DIM, HEAD_DIM), HEAD_DIM)
         for part, source in enumerate((q_ref, k_ref, v_ref)):
             target = out.at[part * slots : (part + 1) * slots, :]
             copy = pltpu.make_async_copy(source.at[:, columns], target, sems.at[len(copies)])
             copy.start()
             copies.append(copy)
-    rows = clip_ref[...].astype(F32).astype(BF16)
+    clip_copy.wait()
+    rows = clips[...].astype(F32).astype(BF16)
     for out in outs:
         out[3 * slots :, :] = jnp.zeros((16, 128), BF16)
         out[3 * slots : 3 * slots + rows.shape[0], :] = rows
@@ -113,9 +119,9 @@
     half = first.shape[0]
     for head in range(3):
         home = jnp.where(side == 0, head, 3 - head)
-        step = lax.rem(home - place + 4, 4)
+        step = jnp.bitwise_xor(home, place)
         columns = slice(head * HEAD_DIM, (head + 1) * HEAD_DIM)
-        for index, source in enumerate((own, back1, back2, back3)):
+        for index, source in zip(STEPS, (own, back1, back2, back3)):
 
             @pl.when(step == index)
             def _():
@@ -240,13 +246,16 @@
     packed = pl.pallas_call(
         pack_kernel,
         out_shape=[shape_of((3 * slots + 16, 128))] * 4,
-        in_specs=[ANY] * 3 + [VMEM],
+        in_specs=[ANY] * 4,
         out_specs=[VMEM] * 4,
-        scratch_shapes=[pltpu.SemaphoreType.DMA((12,))],
+        scratch_shapes=[
+            pltpu.VMEM((slots // 128, 128), jnp.int32),
+            pltpu.SemaphoreType.DMA((13,)),
+        ],
         compiler_params=params(16),
         name="pack",
-    )(afar(query), afar(key), afar(value), slot_clip.reshape(slots // 128, 128))
-    blocks = [packed[0]] + [hop(packed[step], step) for step in (1, 2, 3)]
+    )(afar(query), afar(key), afar(value), afar(slot_clip.reshape(slots // 128, 128)))
+    blocks = [packed[0]] + [hop(packed[index], STEPS[index]) for index in (1, 2, 3)]
     early = (*early, *(kept(weight) for weight in load(*weights, packed[0])))
     results = pl.pallas_call(
         attend_kernel,
@@ -259,7 +268,7 @@
         cost_estimate=cost(2**32, 2**21),
         name="attend",
     )(*blocks, *early)
-    backs = [hop(results[step], step, back=True) for step in (1, 2, 3)]
+    backs = [hop(results[index], STEPS[index], back=True) for index in (1, 2, 3)]
     half = slots // 2
     return early[-2:], pl.pallas_call(
         regroup_kernel,
@@ -314,11 +323,21 @@
     ]
 
 
+def chosen(mod, kind, clip, columns):
+    picked = jnp.zeros((clip.shape[0], mod[0, :1, columns].shape[1]), F32)
+    for index in range(CLIPS):
+        picked = jnp.where(clip == index, mod[index, kind : kind + 1, columns], picked)
+    return picked
+
+
 def feed_kernel(turn, *refs):
-    (att, (w_out, up, down, res_hbm, mod, clip_ref), out) = refs[:4], refs[4:10], refs[10]
-    res, mixed, total, normed, hidden, sem = refs[11:]
+    att, (w_out, up, down, res_hbm, mod, clip_ref), refs = refs[:4], refs[4:10], refs[10:]
+    if turn == 0:
+        out, mixed, hidden, res, normed, sem = refs
+    else:
+        hidden, mixed, res, normed, sem = refs
     side, blk = lax.axis_index("cfg"), lax.axis_index("blk")
-    half = out.shape[0]
+    half = hidden.shape[0]
     which = 1 - side if turn == 0 else side
     rows = pl.ds(pl.multiple_of(which * half, half), half)
     width = att[0].shape[1]
@@ -326,63 +345,51 @@
     copy.start()
     rows_in = jnp.concatenate([piece[...] for piece in att], axis=1)
     clip = clip_ref[rows, :][:, :1]
-    tile = 512
-
-    def chosen(kind, columns):
-        picked = jnp.zeros((half, tile), F32)
-        for index in range(CLIPS):
-            line = mod[index, kind : kind + 1, columns]
-            picked = jnp.where(clip == index, line, picked)
-        return picked
-
-    for start in range(0, D, tile):
-        columns = slice(start, start + tile)
+    tiles = [slice(start, start + 512) for start in range(0, D, 512)]
+    for columns in tiles:
         projected = jnp.dot(rows_in, w_out[:, columns], preferred_element_type=F32)
-        mixed[:, columns] = chosen(0, columns) * projected
+        mixed[:, columns] = chosen(mod, 0, clip, columns) * projected
     copy.wait()
     held = mixed[...] + res[...].astype(F32)
     mixed[...] = held
     centre = held - jnp.mean(held, axis=1, keepdims=True)
     spread = lax.rsqrt(jnp.mean(centre * centre, axis=1, keepdims=True) + 1e-06)
-    for start in range(0, D, tile):
-        columns = slice(start, start + tile)
-        value = centre[:, columns] * spread * (1.0 + chosen(2, columns)) + chosen(1, columns)
-        normed[:, columns] = value.astype(BF16)
-    for start in range(0, D, tile):
-        columns = slice(start, start + tile)
+    for columns in tiles:
+        stretch, shift = chosen(mod, 2, clip, columns), chosen(mod, 1, clip, columns)
+        normed[:, columns] = (centre[:, columns] * spread * (1.0 + stretch) + shift).astype(BF16)
+    for columns in tiles:
         raised = jnp.dot(normed[...], up[:, columns], preferred_element_type=F32)
         hidden[:, columns] = jax.nn.gelu(raised, approximate=True).astype(BF16)
-    for start in range(0, D, tile):
-        columns = slice(start, start + tile)
-        lowered = jnp.dot(hidden[...], down[:, columns], preferred_element_type=F32)
-        total[:, columns] = chosen(3, columns) * lowered
-    own = pl.ds(pl.multiple_of(blk * width, width), width)
-    total[:, own] = total[:, own] + mixed[:, own]
-    out[...] = total[...].astype(out.dtype)
+    if turn == 0:
+        for columns in tiles:
+            lowered = jnp.dot(hidden[...], down[:, columns], preferred_element_type=F32)
+            out[:, columns] = (chosen(mod, 3, clip, columns) * lowered).astype(BF16)
+        own = pl.ds(pl.multiple_of(blk * width, width), width)
+        lowered = jnp.dot(hidden[...], down[:, own], preferred_element_type=F32)
+        out[:, own] = (chosen(mod, 3, clip, own) * lowered + mixed[:, own]).astype(BF16)
 
 
 def feed(turn, att, w_out, w_up, w_down, residual, mod, clip_wide):
     half, width = att[0].shape
+    inner = [pltpu.VMEM((half, D), BF16), pltpu.VMEM((half, D), BF16), pltpu.SemaphoreType.DMA]
+    if turn == 0:
+        out_shape = shape_of((half, D))
+        inner = [pltpu.VMEM((half, D), F32), pltpu.VMEM((half, D), BF16)] + inner
+    else:
+        out_shape = [shape_of((half, D)), shape_of((half, D), F32)]
     return pl.pallas_call(
         functools.partial(feed_kernel, turn),
-        out_shape=shape_of((half, D), BF16 if turn == 0 else F32),
+        out_shape=out_shape,
         in_specs=[VMEM] * 7 + [ANY] + [VMEM] * 2,
-        out_specs=VMEM,
-        scratch_shapes=[
-            pltpu.VMEM((half, D), BF16),
-            pltpu.VMEM((half, D), F32),
-            pltpu.VMEM((half, D), F32),
-            pltpu.VMEM((half, D), BF16),
-            pltpu.VMEM((half, D), BF16),
-            pltpu.SemaphoreType.DMA,
-        ],
+        out_specs=VMEM if turn == 0 else [VMEM] * 2,
+        scratch_shapes=inner,
         compiler_params=params(24),
         cost_estimate=cost(2**36, 2**24),
         name="feed",
     )(*att, kept(w_out), kept(w_up), kept(w_down), afar(residual), mod, clip_wide)
 
 
-def guide_kernel(mine_ref, other_ref, clip_ref, scale_ref, own, *sent):
+def guide_kernel(hidden, mixed, down, other_ref, clip_ref, mod, scale_ref, own, *sent):
     side, blk = lax.axis_index("cfg"), lax.axis_index("blk")
     half, width = own.shape
     clip = clip_ref[pl.ds(pl.multiple_of(side * half, half), half), :][:, :1]
@@ -393,9 +400,12 @@
     for step, out in enumerate((own, *sent)):
         target = jnp.bitwise_xor(blk, step)
         columns = pl.ds(pl.multiple_of(target * width, width), width)
+        lowered = jnp.dot(hidden[...], down[:, columns], preferred_element_type=F32)
+        mine = chosen(mod, 3, clip, columns) * lowered
+        if step == 0:
+            mine = mine + mixed[:, columns]
         other = other_ref[:, columns].astype(F32)
-        guided = other + lean * (mine_ref[:, columns] - other)
-        out[...] = guided.astype(out.dtype)
+        out[...] = (other + lean * (mine - other)).astype(out.dtype)
 
 
 def place_kernel(own, got1, got2, got3, placing, *outs):
@@ -409,11 +419,12 @@
             out[...] = placed[index * count : (index + 1) * count, :]
 
 
-def arrange_kernel(own, got1, got2, got3, out):
+def arrange_kernel(*refs):
+    out = refs[4]
     place = lax.axis_index("seq")
-    count = own.shape[0]
-    for step, source in enumerate((own, got1, got2, got3)):
-        origin = lax.rem(place + 4 - step, 4)
+    count = refs[0].shape[0]
+    for step, source in zip(STEPS, refs):
+        origin = jnp.bitwise_xor(place, step)
         out[pl.ds(pl.multiple_of(origin * count, count), count), :] = source[...]
 
 
@@ -438,7 +449,7 @@
     before = (owner_half[None, :] == owner_half[:, None]) & (order[None, :] < order[:, None])
     rank = jnp.sum(before.astype(jnp.int32), axis=1)
     if seq_count == 4:
-        lane = lax.rem(owner_half - place + seq_count, seq_count)
+        lane = jnp.bitwise_xor(owner_half, place)
     else:
         lane = owner_half
     target = jnp.where(clip_half < CLIPS, lane * capacity + rank, -1)
@@ -470,11 +481,11 @@
     own, *sent = pl.pallas_call(
         guide_kernel,
         out_shape=[shape_of((half, width), F32)] + [shape_of((half, width))] * 3,
-        in_specs=[VMEM] * 3 + [pl.BlockSpec(memory_space=pltpu.SMEM)],
+        in_specs=[VMEM] * 6 + [pl.BlockSpec(memory_space=pltpu.SMEM)],
         out_specs=[VMEM] * 4,
         compiler_params=params(16),
         name="guide",
-    )(parts[1], other, clip_wide, guide_scale)
+    )(*parts[1], kept(down), other, clip_wide, modulation, guide_scale)
     got = [exchanged(piece, "blk", mask) for mask, piece in zip((1, 2, 3), sent)]
     by_step = seq_count == 4
     placed = pl.pallas_call(
@@ -494,8 +505,7 @@
         )
         return arrived.reshape(1, seq_count * capacity, width)
     home = [
-        lax.ppermute(placed[step], "seq", [(i, (i + step) % 4) for i in range(4)])
-        for step in (1, 2, 3)
+        exchanged(placed[step], "seq", step) for step in STEPS[1:]
     ]
     arranged = pl.pallas_call(
         arrange_kernel,

time: 87.2 us -> 84.3 us (0.967)
  starting transfers between devices: 39.4 us -> 37.8 us
    ppermute x3 -> x0, starting transfers between devices: 6.01 us -> none  [shards(): lax.ppermute(placed[step], 'seq', [(i, (i + step) % 4) for i in range(4)])]
    ppermute x12 -> x15, waiting for transfers between devices: 9.51 us -> 14.1 us  [exchanged(): return lax.ppermute(value, axis, pairs)]
    ppermute x12 -> x15, starting transfers between devices: 10.8 us -> 14.4 us  [exchanged(): return lax.ppermute(value, axis, pairs)]
    ppermute x3 -> x0, waiting for transfers between devices: 2.57 us -> none  [shards(): lax.ppermute(placed[step], 'seq', [(i, (i + step) % 4) for i in range(4)])]
    pallas_call x2, Pallas kernels: 9.12 us -> 7.38 us  [feed(): pl.pallas_call(functools.partial(feed_kernel, turn), out_shape=out_shape,...]
    ppermute x2, waiting for transfers between devices: 4.11 us -> 2.65 us  [across(): return lax.ppermute(value, ('cfg', 'blk'), pairs)]
    pallas_call x1, Pallas kernels: 0.83 us -> 2.13 us  [shards(): pl.pallas_call(guide_kernel, out_shape=[shape_of((half, width), F32)] + [...]
    ppermute x6, starting transfers between devices: 17.5 us -> 18.4 us  [hop(): return lax.ppermute(value, ('cfg', 'seq'), pairs)]
  transfers between devices with their start and end apart: 23 -> 23, of which waited for: 11 -> 9; matrix products, arithmetic and copies ran while one was open for 1% -> 1% of each run, Pallas kernels for 23% -> 22%
where the time goes in v4:
time: 84.3 us; the launch traced here: 83.9 us
  starting transfers between devices  37.8 us (45%)
  waiting for transfers between devices  23 us (27%)
  Pallas kernels  21.6 us (26%)
  other arithmetic  1 us (1%)
    ppermute x6, starting transfers between devices, hop(): return lax.ppermute(value, ('cfg', 'seq'), pairs)  18.4 us
    ppermute x15, starting transfers between devices, exchanged(): return lax.ppermute(value, axis, pairs)  14.4 us
    ppermute x15, waiting for transfers between devices, exchanged(): return lax.ppermute(value, axis, pairs)  14.1 us
    pallas_call x2, Pallas kernels, feed(): pl.pallas_call(functools.partial(feed_kernel, turn), out_shape=out_shape,...  7.38 us
    ppermute x6, waiting for transfers between devices, hop(): return lax.ppermute(value, ('cfg', 'seq'), pairs)  6.28 us
    ppermute x2, starting transfers between devices, across(): return lax.ppermute(value, ('cfg', 'blk'), pairs)  5.06 us
    pallas_call x1, Pallas kernels, attention_by_head(): pl.pallas_call(attend_kernel, out_shape=[shape_of((slots, 128))] * 4, in_...  4.01 us
    pallas_call x1, Pallas kernels, load(): pl.pallas_call(load_kernel, out_shape=[pltpu.VMEM(up.shape, BF16), pltpu....  3.8 us
  transfers between devices with their start and end apart: 23, of which 9 were waited for; matrix products, arithmetic and copies ran while one was open for 1% of the time, Pallas kernels for 22%

profile of v4, /device:TPU:0, one launch (start us, length us, event | category | flops | bytes accessed | tf_op | source)
XLA Modules:
  0.0 83.9 jit_solution(7868341195388716974)
XLA Ops:
  0.0 2.9 %collective-permute-start.3 = (bf16[384,1536]{1,0:T(8,128)(2,1)}, bf16[384,1536]{1,0:T(8,128)(2,1)S(1)}, u32[]{:S(2)}, u32[]{:S(2)}) collective-permute-start(bf16[384,1536]{1,0:T(8,128)(2,1)} %own.1), channel_id=1, source_target_pairs={{0,1},{1,0},{2,3},{3,2},{16,18},{17,19},{18,16},{19,17},{4,5},{5,4... | collective-permute-start | bytes 3538952 | tf_op jit(solution)/shard_map/ppermute | solution.py:168
  2.9 1.5 %pack.1 = (bf16[1168,128]{1,0:T(8,128)(2,1)S(1)}, bf16[1168,128]{1,0:T(8,128)(2,1)S(1)}, bf16[1168,128]{1,0:T(8,128)(2,1)S(1)}, bf16[1168,128]{1,0:T(8,128)(2,1)S(1)}) custom-call(bf16[384,384]{1,0:T(8,128)(2,1)} %bitcast.7, bf16[384,384]{1,0:T(8,128)(2,1)} %bitcast.8, bf16[384,384]{1,0:T(8,128)(2,1)} %bitcast.9, s32[3,128]{1,0:T(4,128)} %bitcast.12), custom_call_target="tpu_custom_call" | custom-call | tf_op jit(solution)/shard_map/pack/pallas_call | solution.py:246
  4.4 4.5 %collective-permute-start = (bf16[1168,128]{1,0:T(8,128)(2,1)S(1)}, bf16[1168,128]{1,0:T(8,128)(2,1)S(1)}, u32[]{:S(2)}, u32[]{:S(2)}) collective-permute-start(bf16[1168,128]{1,0:T(8,128)(2,1)S(1)} %get-tuple-element.28), channel_id=1, source_target_pairs={{0,8},{8,0},{12,4},{16,24},{20,28},{28,20},{1,9},{9,1},{13,5},{17,... | collective-permute-start | bytes 897032 | tf_op jit(solution)/shard_map/ppermute | solution.py:53
  8.9 1.3 %collective-permute-start.1 = (bf16[1168,128]{1,0:T(8,128)(2,1)S(1)}, bf16[1168,128]{1,0:T(8,128)(2,1)S(1)}, u32[]{:S(2)}, u32[]{:S(2)}) collective-permute-start(bf16[1168,128]{1,0:T(8,128)(2,1)S(1)} %get-tuple-element.29), channel_id=1, source_target_pairs={{4,8},{8,4},{12,0},{16,28},{20,24},{24,20},{5,9},{9,5},{13,1},{17,... | collective-permute-start | bytes 897032 | tf_op jit(solution)/shard_map/ppermute | solution.py:53
  10.2 3.4 %collective-permute-start.2 = (bf16[1168,128]{1,0:T(8,128)(2,1)S(1)}, bf16[1168,128]{1,0:T(8,128)(2,1)S(1)}, u32[]{:S(2)}, u32[]{:S(2)}) collective-permute-start(bf16[1168,128]{1,0:T(8,128)(2,1)S(1)} %get-tuple-element.30), channel_id=1, source_target_pairs={{0,4},{4,0},{12,8},{16,20},{24,28},{28,24},{1,5},{5,1},{13,9},{17,... | collective-permute-start | bytes 897032 | tf_op jit(solution)/shard_map/ppermute | solution.py:53
  13.7 0.1 constant_dynamic-slice_fusion
  13.7 0.2 convert_reduce_fusion
  13.9 0.8 compare_select_fusion
  14.7 2.6 %collective-permute-done.3.got.near = bf16[384,1536]{1,0:T(8,128)(2,1)S(1)} collective-permute-done((bf16[384,1536]{1,0:T(8,128)(2,1)}, bf16[384,1536]{1,0:T(8,128)(2,1)S(1)}, u32[]{:S(2)}, u32[]{:S(2)}) %collective-permute-start.3) | collective-permute-done | bytes 1179680 | tf_op jit(solution)/shard_map/ppermute | solution.py:168
  17.3 0.1 cut.1.refs_6_
  17.5 2.1 %collective-permute-start.11 = (bf16[192,1536]{1,0:T(8,128)(2,1)S(1)}, bf16[192,1536]{1,0:T(8,128)(2,1)S(1)}, u32[]{:S(2)}, u32[]{:S(2)}) collective-permute-start(bf16[192,1536]{1,0:T(8,128)(2,1)S(1)} %cut.1.refs_6_), channel_id=1, source_target_pairs={{0,2},{1,3},{2,0},{3,1},{16,17},{17,16},{18,19},{19,18},{4,6},{5,7... | collective-permute-start | bytes 1769480 | tf_op jit(solution)/shard_map/ppermute | solution.py:168
  19.6 0.0 copy-start.3
  19.6 3.8 %load.1 = (bf16[1536,1536]{1,0:T(8,128)(2,1)S(1)}, bf16[1536,1536]{1,0:T(8,128)(2,1)S(1)}) custom-call(bf16[1536,1536]{1,0:T(8,128)(2,1)} %up.1, bf16[1536,1536]{1,0:T(8,128)(2,1)} %down.1, bf16[1168,128]{1,0:T(8,128)(2,1)S(1)} %get-tuple-element.27.after.refs_0_), custom_call_target="tpu_custom_call" | custom-call | tf_op jit(solution)/shard_map/load/pallas_call | solution.py:153
  23.5 2.8 %collective-permute-done.refs_1_ = bf16[1168,128]{1,0:T(8,128)(2,1)S(1)} collective-permute-done((bf16[1168,128]{1,0:T(8,128)(2,1)S(1)}, bf16[1168,128]{1,0:T(8,128)(2,1)S(1)}, u32[]{:S(2)}, u32[]{:S(2)}) %collective-permute-start) | collective-permute-done | bytes 299040 | tf_op jit(solution)/shard_map/ppermute | solution.py:53
  26.3 0.1 broadcast_in_dim.7.refs_4_.refs_9_.clip_ref
  26.4 4.0 %attend.1 = (bf16[384,128]{1,0:T(8,128)(2,1)S(1)}, bf16[384,128]{1,0:T(8,128)(2,1)S(1)}, bf16[384,128]{1,0:T(8,128)(2,1)S(1)}, bf16[384,128]{1,0:T(8,128)(2,1)S(1)}) custom-call(bf16[1168,128]{1,0:T(8,128)(2,1)S(1)} %get-tuple-element.27.after.refs_0_, bf16[1168,128]{1,0:T(8,128)(2,1)S(1)} %collective-permute-done.refs_1_, ...), custom_call_target="tpu_custom_call" | custom-call | flops 4294967296 | bytes 2097152 | tf_op jit(solution)/shard_map/attend/pallas_call | solution.py:260
  30.4 4.8 %collective-permute-start.4 = (bf16[384,128]{1,0:T(8,128)(2,1)S(1)}, bf16[384,128]{1,0:T(8,128)(2,1)S(1)}, u32[]{:S(2)}, u32[]{:S(2)}) collective-permute-start(bf16[384,128]{1,0:T(8,128)(2,1)S(1)} %get-tuple-element.34), channel_id=1, source_target_pairs={{8,0},{0,8},{4,12},{24,16},{28,20},{20,28},{9,1},{1,9},{5,13},{25,... | collective-permute-start | bytes 294920 | tf_op jit(solution)/shard_map/ppermute | solution.py:53
  35.2 1.3 %collective-permute-start.5 = (bf16[384,128]{1,0:T(8,128)(2,1)S(1)}, bf16[384,128]{1,0:T(8,128)(2,1)S(1)}, u32[]{:S(2)}, u32[]{:S(2)}) collective-permute-start(bf16[384,128]{1,0:T(8,128)(2,1)S(1)} %get-tuple-element.35), channel_id=1, source_target_pairs={{8,4},{4,8},{0,12},{28,16},{24,20},{20,24},{9,5},{5,9},{1,13},{29,... | collective-permute-start | bytes 294920 | tf_op jit(solution)/shard_map/ppermute | solution.py:53
  36.5 3.2 %collective-permute-start.6 = (bf16[384,128]{1,0:T(8,128)(2,1)S(1)}, bf16[384,128]{1,0:T(8,128)(2,1)S(1)}, u32[]{:S(2)}, u32[]{:S(2)}) collective-permute-start(bf16[384,128]{1,0:T(8,128)(2,1)S(1)} %get-tuple-element.36), channel_id=1, source_target_pairs={{4,0},{0,4},{8,12},{20,16},{28,24},{24,28},{5,1},{1,5},{9,13},{21,... | collective-permute-start | bytes 294920 | tf_op jit(solution)/shard_map/ppermute | solution.py:53
  39.7 3.4 %collective-permute-done.6.back3 = bf16[384,128]{1,0:T(8,128)(2,1)S(1)} collective-permute-done((bf16[384,128]{1,0:T(8,128)(2,1)S(1)}, bf16[384,128]{1,0:T(8,128)(2,1)S(1)}, u32[]{:S(2)}, u32[]{:S(2)}) %collective-permute-start.6) | collective-permute-done | bytes 98336 | tf_op jit(solution)/shard_map/ppermute | solution.py:53
  43.1 0.3 regroup.1
  43.4 0.1 collective-permute-start.12
  43.5 1.3 %collective-permute-start.13 = (bf16[192,384]{1,0:T(8,128)(2,1)S(1)}, bf16[192,384]{1,0:T(8,128)(2,1)S(1)}, u32[]{:S(2)}, u32[]{:S(2)}) collective-permute-start(bf16[192,384]{1,0:T(8,128)(2,1)S(1)} %get-tuple-element.38.after.refs_0_), channel_id=1, source_target_pairs={{0,1},{1,0},{2,3},{3,2},{4,5},{5,4},{6,7},{7,6},{8,9},{9,8},{10,11... | collective-permute-start | bytes 442376 | tf_op jit(solution)/shard_map/ppermute | solution.py:433
  44.8 0.9 %collective-permute-start.14 = (bf16[192,384]{1,0:T(8,128)(2,1)S(1)}, bf16[192,384]{1,0:T(8,128)(2,1)S(1)}, u32[]{:S(2)}, u32[]{:S(2)}) collective-permute-start(bf16[192,384]{1,0:T(8,128)(2,1)S(1)} %get-tuple-element.38.after.refs_0_), channel_id=1, source_target_pairs={{0,2},{1,3},{2,0},{3,1},{4,6},{5,7},{6,4},{7,5},{8,10},{9,11},{10,... | collective-permute-start | bytes 442376 | tf_op jit(solution)/shard_map/ppermute | solution.py:433
  45.7 1.3 %collective-permute-start.15 = (bf16[192,384]{1,0:T(8,128)(2,1)S(1)}, bf16[192,384]{1,0:T(8,128)(2,1)S(1)}, u32[]{:S(2)}, u32[]{:S(2)}) collective-permute-start(bf16[192,384]{1,0:T(8,128)(2,1)S(1)} %get-tuple-element.38.after.refs_0_), channel_id=1, source_target_pairs={{0,3},{1,2},{2,1},{3,0},{4,7},{5,6},{6,5},{7,4},{8,11},{9,10},{10,... | collective-permute-start | bytes 442376 | tf_op jit(solution)/shard_map/ppermute | solution.py:433
  47.1 1.2 %collective-permute-start.7 = (bf16[192,384]{1,0:T(8,128)(2,1)S(1)}, bf16[192,384]{1,0:T(8,128)(2,1)S(1)}, u32[]{:S(2)}, u32[]{:S(2)}) collective-permute-start(bf16[192,384]{1,0:T(8,128)(2,1)S(1)} %get-tuple-element.37.refs_0_), channel_id=1, source_target_pairs={{0,1},{1,0},{2,3},{3,2},{4,5},{5,4},{6,7},{7,6},{8,9},{9,8},{10,11... | collective-permute-start | bytes 442376 | tf_op jit(solution)/shard_map/ppermute | solution.py:433
  48.3 0.9 %collective-permute-start.8 = (bf16[192,384]{1,0:T(8,128)(2,1)S(1)}, bf16[192,384]{1,0:T(8,128)(2,1)S(1)}, u32[]{:S(2)}, u32[]{:S(2)}) collective-permute-start(bf16[192,384]{1,0:T(8,128)(2,1)S(1)} %get-tuple-element.37.refs_0_), channel_id=1, source_target_pairs={{0,2},{1,3},{2,0},{3,1},{4,6},{5,7},{6,4},{7,5},{8,10},{9,11},{10,... | collective-permute-start | bytes 442376 | tf_op jit(solution)/shard_map/ppermute | solution.py:433
  49.2 1.3 %join.1.refs_4_ = bf16[1536,1536]{1,0:T(8,128)(2,1)S(1)} custom-call(bf16[384,1536]{1,0:T(8,128)(2,1)} %own.1, bf16[384,1536]{1,0:T(8,128)(2,1)S(1)} %collective-permute-done.3.got.near, bf16[384,1536]{1,0:T(8,128)(2,1)S(1)} %collective-permute-done.10.near_swap, bf16[192,1536]{1,0:T(8,128)(2,1)S(1)} %gate.1.far, ...), custom_call_target="tpu_custom_call" | custom-call | tf_op jit(solution)/shard_map/join/pallas_call | solution.py:233
  50.6 1.4 %collective-permute-start.9 = (bf16[192,384]{1,0:T(8,128)(2,1)S(1)}, bf16[192,384]{1,0:T(8,128)(2,1)S(1)}, u32[]{:S(2)}, u32[]{:S(2)}) collective-permute-start(bf16[192,384]{1,0:T(8,128)(2,1)S(1)} %get-tuple-element.37.refs_0_), channel_id=1, source_target_pairs={{0,3},{1,2},{2,1},{3,0},{4,7},{5,6},{6,5},{7,4},{8,11},{9,10},{10,... | collective-permute-start | bytes 442376 | tf_op jit(solution)/shard_map/ppermute | solution.py:433
  52.0 2.7 %collective-permute-done.14.refs_2_ = bf16[192,384]{1,0:T(8,128)(2,1)S(1)} collective-permute-done((bf16[192,384]{1,0:T(8,128)(2,1)S(1)}, bf16[192,384]{1,0:T(8,128)(2,1)S(1)}, u32[]{:S(2)}, u32[]{:S(2)}) %collective-permute-start.14) | collective-permute-done | bytes 147488 | tf_op jit(solution)/shard_map/ppermute | solution.py:433
  54.7 4.3 %feed.3 = bf16[192,1536]{1,0:T(8,128)(2,1)S(1)} custom-call(bf16[192,384]{1,0:T(8,128)(2,1)S(1)} %get-tuple-element.38.after.refs_0_, bf16[192,384]{1,0:T(8,128)(2,1)S(1)} %collective-permute-done.13.refs_1_, bf16[192,384]{1,0:T(8,128)(2,1)S(1)} %collective-permute-done.14.refs_2_, bf16[192,384]{1,0:T(8,128)(2,1)S(1)} %collective-permute-done.15.refs_3_, ...), custom_call_target="tpu_custom_call" | custom-call | flops 68719476736 | bytes 16777216 | tf_op jit(solution)/shard_map/feed/pallas_call | solution.py:380
  59.0 0.0 copy-start.2
  59.0 0.1 collective-permute-start.16
  59.1 1.1 %collective-permute-done.8.refs_2_ = bf16[192,384]{1,0:T(8,128)(2,1)S(1)} collective-permute-done((bf16[192,384]{1,0:T(8,128)(2,1)S(1)}, bf16[192,384]{1,0:T(8,128)(2,1)S(1)}, u32[]{:S(2)}, u32[]{:S(2)}) %collective-permute-start.8) | collective-permute-done | bytes 147488 | tf_op jit(solution)/shard_map/ppermute | solution.py:433
  60.2 3.0 %feed.2 = (bf16[192,1536]{1,0:T(8,128)(2,1)S(1)}, f32[192,1536]{1,0:T(8,128)S(1)}) custom-call(bf16[192,384]{1,0:T(8,128)(2,1)S(1)} %get-tuple-element.37.refs_0_, bf16[192,384]{1,0:T(8,128)(2,1)S(1)} %collective-permute-done.7.refs_1_, bf16[192,384]{1,0:T(8,128)(2,1)S(1)} %collective-permute-done.8.refs_2_, ...), custom_call_target="tpu_custom_call" | custom-call | flops 68719476736 | bytes 16777216 | tf_op jit(solution)/shard_map/feed/pallas_call | solution.py:380
  63.3 2.1 %guide.1 = (f32[192,384]{1,0:T(8,128)S(1)}, bf16[192,384]{1,0:T(8,128)(2,1)S(1)}, bf16[192,384]{1,0:T(8,128)(2,1)S(1)}, bf16[192,384]{1,0:T(8,128)(2,1)S(1)}) custom-call(bf16[192,1536]{1,0:T(8,128)(2,1)S(1)} %get-tuple-element.39.hidden, f32[192,1536]{1,0:T(8,128)S(1)} %get-tuple-element.40.mixed, ...), custom_call_target="tpu_custom_call" | custom-call | tf_op jit(solution)/shard_map/guide/pallas_call | solution.py:481
  65.4 0.9 %collective-permute-start.17 = (bf16[192,384]{1,0:T(8,128)(2,1)S(1)}, bf16[192,384]{1,0:T(8,128)(2,1)S(1)}, u32[]{:S(2)}, u32[]{:S(2)}) collective-permute-start(bf16[192,384]{1,0:T(8,128)(2,1)S(1)} %get-tuple-element.42), channel_id=1, source_target_pairs={{0,1},{1,0},{2,3},{3,2},{4,5},{5,4},{6,7},{7,6},{8,9},{9,8},{10,11... | collective-permute-start | bytes 442376 | tf_op jit(solution)/shard_map/ppermute | solution.py:433
  66.3 1.0 %collective-permute-start.18 = (bf16[192,384]{1,0:T(8,128)(2,1)S(1)}, bf16[192,384]{1,0:T(8,128)(2,1)S(1)}, u32[]{:S(2)}, u32[]{:S(2)}) collective-permute-start(bf16[192,384]{1,0:T(8,128)(2,1)S(1)} %get-tuple-element.43), channel_id=1, source_target_pairs={{0,2},{1,3},{2,0},{3,1},{4,6},{5,7},{6,4},{7,5},{8,10},{9,11},{10,... | collective-permute-start | bytes 442376 | tf_op jit(solution)/shard_map/ppermute | solution.py:433
  67.3 1.7 %collective-permute-start.19 = (bf16[192,384]{1,0:T(8,128)(2,1)S(1)}, bf16[192,384]{1,0:T(8,128)(2,1)S(1)}, u32[]{:S(2)}, u32[]{:S(2)}) collective-permute-start(bf16[192,384]{1,0:T(8,128)(2,1)S(1)} %get-tuple-element.44), channel_id=1, source_target_pairs={{0,3},{1,2},{2,1},{3,0},{4,7},{5,6},{6,5},{7,4},{8,11},{9,10},{10,... | collective-permute-start | bytes 442376 | tf_op jit(solution)/shard_map/ppermute | solution.py:433
  69.0 3.0 %collective-permute-done.17.got1 = bf16[192,384]{1,0:T(8,128)(2,1)S(1)} collective-permute-done((bf16[192,384]{1,0:T(8,128)(2,1)S(1)}, bf16[192,384]{1,0:T(8,128)(2,1)S(1)}, u32[]{:S(2)}, u32[]{:S(2)}) %collective-permute-start.17) | collective-permute-done | bytes 147488 | tf_op jit(solution)/shard_map/ppermute | solution.py:433
  72.0 2.6 %collective-permute-done.18.got2 = bf16[192,384]{1,0:T(8,128)(2,1)S(1)} collective-permute-done((bf16[192,384]{1,0:T(8,128)(2,1)S(1)}, bf16[192,384]{1,0:T(8,128)(2,1)S(1)}, u32[]{:S(2)}, u32[]{:S(2)}) %collective-permute-start.18) | collective-permute-done | bytes 147488 | tf_op jit(solution)/shard_map/ppermute | solution.py:433
  74.6 0.3 place.1
  74.9 0.9 %collective-permute-start.20 = (bf16[96,384]{1,0:T(8,128)(2,1)S(1)}, bf16[96,384]{1,0:T(8,128)(2,1)S(1)}, u32[]{:S(2)}, u32[]{:S(2)}) collective-permute-start(bf16[96,384]{1,0:T(8,128)(2,1)S(1)} %get-tuple-element.46), channel_id=1, source_target_pairs={{0,8},{4,12},{8,0},{12,4},{1,9},{5,13},{9,1},{13,5},{2,10},{6,14},... | collective-permute-start | bytes 221192 | tf_op jit(solution)/shard_map/ppermute | solution.py:433
  75.8 2.4 %collective-permute-start.21 = (bf16[96,384]{1,0:T(8,128)(2,1)S(1)}, bf16[96,384]{1,0:T(8,128)(2,1)S(1)}, u32[]{:S(2)}, u32[]{:S(2)}) collective-permute-start(bf16[96,384]{1,0:T(8,128)(2,1)S(1)} %get-tuple-element.47), channel_id=1, source_target_pairs={{0,12},{4,8},{8,4},{12,0},{1,13},{5,9},{9,5},{13,1},{2,14},{6,10},... | collective-permute-start | bytes 221192 | tf_op jit(solution)/shard_map/ppermute | solution.py:433
  78.2 0.2 collective-permute-start.22
  78.5 4.0 %collective-permute-done.20.refs_1_ = bf16[96,384]{1,0:T(8,128)(2,1)S(1)} collective-permute-done((bf16[96,384]{1,0:T(8,128)(2,1)S(1)}, bf16[96,384]{1,0:T(8,128)(2,1)S(1)}, u32[]{:S(2)}, u32[]{:S(2)}) %collective-permute-start.20) | collective-permute-done | bytes 73760 | tf_op jit(solution)/shard_map/ppermute | solution.py:433
  82.5 0.6 collective-permute-done.22.refs_3_
  83.1 0.8 arrange.1
  (23 shorter events, 0.1 us)
Async XLA Ops:
  0.0 13.6 %copy-start = (s32[384,1]{0,1:T(1,128)S(1)}, s32[384,1]{0,1:T(1,128)}, u32[]{:S(2)}) copy-start(s32[384,1]{0,1:T(1,128)} %param.21) | copy-start | bytes 4612
  0.0 17.3 %collective-permute-start.3 = (bf16[384,1536]{1,0:T(8,128)(2,1)}, bf16[384,1536]{1,0:T(8,128)(2,1)S(1)}, u32[]{:S(2)}, u32[]{:S(2)}) collective-permute-start(bf16[384,1536]{1,0:T(8,128)(2,1)} %own.1), channel_id=1, source_target_pairs={{0,1},{1,0},{2,3},{3,2},{16,18},{17,19},{18,16},{19,17},{4,5},{5,4... | collective-permute-start | bytes 3538952 | tf_op jit(solution)/shard_map/ppermute | solution.py:168
  4.4 21.9 %collective-permute-start = (bf16[1168,128]{1,0:T(8,128)(2,1)S(1)}, bf16[1168,128]{1,0:T(8,128)(2,1)S(1)}, u32[]{:S(2)}, u32[]{:S(2)}) collective-permute-start(bf16[1168,128]{1,0:T(8,128)(2,1)S(1)} %get-tuple-element.28), channel_id=1, source_target_pairs={{0,8},{8,0},{12,4},{16,24},{20,28},{28,20},{1,9},{9,1},{13,5},{17,... | collective-permute-start | bytes 897032 | tf_op jit(solution)/shard_map/ppermute | solution.py:53
  8.9 17.4 %collective-permute-start.1 = (bf16[1168,128]{1,0:T(8,128)(2,1)S(1)}, bf16[1168,128]{1,0:T(8,128)(2,1)S(1)}, u32[]{:S(2)}, u32[]{:S(2)}) collective-permute-start(bf16[1168,128]{1,0:T(8,128)(2,1)S(1)} %get-tuple-element.29), channel_id=1, source_target_pairs={{4,8},{8,4},{12,0},{16,28},{20,24},{24,20},{5,9},{9,5},{13,1},{17,... | collective-permute-start | bytes 897032 | tf_op jit(solution)/shard_map/ppermute | solution.py:53
  10.2 16.1 %collective-permute-start.2 = (bf16[1168,128]{1,0:T(8,128)(2,1)S(1)}, bf16[1168,128]{1,0:T(8,128)(2,1)S(1)}, u32[]{:S(2)}, u32[]{:S(2)}) collective-permute-start(bf16[1168,128]{1,0:T(8,128)(2,1)S(1)} %get-tuple-element.30), channel_id=1, source_target_pairs={{0,4},{4,0},{12,8},{16,20},{24,28},{28,24},{1,5},{5,1},{13,9},{17,... | collective-permute-start | bytes 897032 | tf_op jit(solution)/shard_map/ppermute | solution.py:53
  17.5 26.0 %collective-permute-start.11 = (bf16[192,1536]{1,0:T(8,128)(2,1)S(1)}, bf16[192,1536]{1,0:T(8,128)(2,1)S(1)}, u32[]{:S(2)}, u32[]{:S(2)}) collective-permute-start(bf16[192,1536]{1,0:T(8,128)(2,1)S(1)} %cut.1.refs_6_), channel_id=1, source_target_pairs={{0,2},{1,3},{2,0},{3,1},{16,17},{17,16},{18,19},{19,18},{4,6},{5,7... | collective-permute-start | bytes 1769480 | tf_op jit(solution)/shard_map/ppermute | solution.py:168
  19.6 28.7 %collective-permute-start.10 = (bf16[384,1536]{1,0:T(8,128)(2,1)S(1)}, bf16[384,1536]{1,0:T(8,128)(2,1)S(1)}, u32[]{:S(2)}, u32[]{:S(2)}) collective-permute-start(bf16[384,1536]{1,0:T(8,128)(2,1)S(1)} %collective-permute-done.3.got.near), channel_id=1, source_target_pairs={{0,16},{16,0},{1,17},{17,1},{2,18},{18,2},{3,19},{19,3},{4,20},{20... | collective-permute-start | bytes 3538952 | tf_op jit(solution)/shard_map/ppermute | solution.py:433
  19.6 6.7 %copy-start.3 = (s32[384]{0:T(512)S(1)}, s32[384]{0:T(512)}, u32[]{:S(2)}) copy-start(s32[384]{0:T(512)} %param.20) | copy-start | bytes 4612
  30.4 9.2 %collective-permute-start.4 = (bf16[384,128]{1,0:T(8,128)(2,1)S(1)}, bf16[384,128]{1,0:T(8,128)(2,1)S(1)}, u32[]{:S(2)}, u32[]{:S(2)}) collective-permute-start(bf16[384,128]{1,0:T(8,128)(2,1)S(1)} %get-tuple-element.34), channel_id=1, source_target_pairs={{8,0},{0,8},{4,12},{24,16},{28,20},{20,28},{9,1},{1,9},{5,13},{25,... | collective-permute-start | bytes 294920 | tf_op jit(solution)/shard_map/ppermute | solution.py:53
  35.2 4.5 %collective-permute-start.5 = (bf16[384,128]{1,0:T(8,128)(2,1)S(1)}, bf16[384,128]{1,0:T(8,128)(2,1)S(1)}, u32[]{:S(2)}, u32[]{:S(2)}) collective-permute-start(bf16[384,128]{1,0:T(8,128)(2,1)S(1)} %get-tuple-element.35), channel_id=1, source_target_pairs={{8,4},{4,8},{0,12},{28,16},{24,20},{20,24},{9,5},{5,9},{1,13},{29,... | collective-permute-start | bytes 294920 | tf_op jit(solution)/shard_map/ppermute | solution.py:53
  36.5 6.6 %collective-permute-start.6 = (bf16[384,128]{1,0:T(8,128)(2,1)S(1)}, bf16[384,128]{1,0:T(8,128)(2,1)S(1)}, u32[]{:S(2)}, u32[]{:S(2)}) collective-permute-start(bf16[384,128]{1,0:T(8,128)(2,1)S(1)} %get-tuple-element.36), channel_id=1, source_target_pairs={{4,0},{0,4},{8,12},{20,16},{28,24},{24,28},{5,1},{1,5},{9,13},{21,... | collective-permute-start | bytes 294920 | tf_op jit(solution)/shard_map/ppermute | solution.py:53
  43.4 3.6 %collective-permute-start.12 = (bf16[192,1536]{1,0:T(8,128)(2,1)S(1)}, bf16[192,1536]{1,0:T(8,128)(2,1)S(1)}, u32[]{:S(2)}, u32[]{:S(2)}) collective-permute-start(bf16[192,1536]{1,0:T(8,128)(2,1)S(1)} %gate.1.far), channel_id=1, source_target_pairs={{0,16},{16,0},{1,17},{17,1},{2,18},{18,2},{3,19},{19,3},{4,20},{20... | collective-permute-start | bytes 1769480 | tf_op jit(solution)/shard_map/ppermute | solution.py:433
  43.5 7.0 %collective-permute-start.13 = (bf16[192,384]{1,0:T(8,128)(2,1)S(1)}, bf16[192,384]{1,0:T(8,128)(2,1)S(1)}, u32[]{:S(2)}, u32[]{:S(2)}) collective-permute-start(bf16[192,384]{1,0:T(8,128)(2,1)S(1)} %get-tuple-element.38.after.refs_0_), channel_id=1, source_target_pairs={{0,1},{1,0},{2,3},{3,2},{4,5},{5,4},{6,7},{7,6},{8,9},{9,8},{10,11... | collective-permute-start | bytes 442376 | tf_op jit(solution)/shard_map/ppermute | solution.py:433
  44.8 9.9 %collective-permute-start.14 = (bf16[192,384]{1,0:T(8,128)(2,1)S(1)}, bf16[192,384]{1,0:T(8,128)(2,1)S(1)}, u32[]{:S(2)}, u32[]{:S(2)}) collective-permute-start(bf16[192,384]{1,0:T(8,128)(2,1)S(1)} %get-tuple-element.38.after.refs_0_), channel_id=1, source_target_pairs={{0,2},{1,3},{2,0},{3,1},{4,6},{5,7},{6,4},{7,5},{8,10},{9,11},{10,... | collective-permute-start | bytes 442376 | tf_op jit(solution)/shard_map/ppermute | solution.py:433
  45.7 8.9 %collective-permute-start.15 = (bf16[192,384]{1,0:T(8,128)(2,1)S(1)}, bf16[192,384]{1,0:T(8,128)(2,1)S(1)}, u32[]{:S(2)}, u32[]{:S(2)}) collective-permute-start(bf16[192,384]{1,0:T(8,128)(2,1)S(1)} %get-tuple-element.38.after.refs_0_), channel_id=1, source_target_pairs={{0,3},{1,2},{2,1},{3,0},{4,7},{5,6},{6,5},{7,4},{8,11},{9,10},{10,... | collective-permute-start | bytes 442376 | tf_op jit(solution)/shard_map/ppermute | solution.py:433
  47.1 7.6 %copy-start.1 = (f32[3,4,1536]{2,1,0:T(4,128)S(1)}, f32[3,4,1536]{2,1,0:T(4,128)}, u32[]{:S(2)}) copy-start(f32[3,4,1536]{2,1,0:T(4,128)} %mod.1) | copy-start | bytes 221188
  47.1 12.0 %collective-permute-start.7 = (bf16[192,384]{1,0:T(8,128)(2,1)S(1)}, bf16[192,384]{1,0:T(8,128)(2,1)S(1)}, u32[]{:S(2)}, u32[]{:S(2)}) collective-permute-start(bf16[192,384]{1,0:T(8,128)(2,1)S(1)} %get-tuple-element.37.refs_0_), channel_id=1, source_target_pairs={{0,1},{1,0},{2,3},{3,2},{4,5},{5,4},{6,7},{7,6},{8,9},{9,8},{10,11... | collective-permute-start | bytes 442376 | tf_op jit(solution)/shard_map/ppermute | solution.py:433
  48.3 11.9 %collective-permute-start.8 = (bf16[192,384]{1,0:T(8,128)(2,1)S(1)}, bf16[192,384]{1,0:T(8,128)(2,1)S(1)}, u32[]{:S(2)}, u32[]{:S(2)}) collective-permute-start(bf16[192,384]{1,0:T(8,128)(2,1)S(1)} %get-tuple-element.37.refs_0_), channel_id=1, source_target_pairs={{0,2},{1,3},{2,0},{3,1},{4,6},{5,7},{6,4},{7,5},{8,10},{9,11},{10,... | collective-permute-start | bytes 442376 | tf_op jit(solution)/shard_map/ppermute | solution.py:433
  50.6 9.7 %collective-permute-start.9 = (bf16[192,384]{1,0:T(8,128)(2,1)S(1)}, bf16[192,384]{1,0:T(8,128)(2,1)S(1)}, u32[]{:S(2)}, u32[]{:S(2)}) collective-permute-start(bf16[192,384]{1,0:T(8,128)(2,1)S(1)} %get-tuple-element.37.refs_0_), channel_id=1, source_target_pairs={{0,3},{1,2},{2,1},{3,0},{4,7},{5,6},{6,5},{7,4},{8,11},{9,10},{10,... | collective-permute-start | bytes 442376 | tf_op jit(solution)/shard_map/ppermute | solution.py:433
  59.0 4.3 %copy-start.2 = (f32[3]{0:T(128)S(1)}, f32[3]{0:T(128)}, u32[]{:S(2)}) copy-start(f32[3]{0:T(128)} %scale_ref.1) | copy-start | bytes 40
  59.0 4.2 %collective-permute-start.16 = (bf16[192,1536]{1,0:T(8,128)(2,1)S(1)}, bf16[192,1536]{1,0:T(8,128)(2,1)S(1)}, u32[]{:S(2)}, u32[]{:S(2)}) collective-permute-start(bf16[192,1536]{1,0:T(8,128)(2,1)S(1)} %feed.3), channel_id=1, source_target_pairs={{0,16},{16,0},{1,17},{17,1},{2,18},{18,2},{3,19},{19,3},{4,20},{20... | collective-permute-start | bytes 1769480 | tf_op jit(solution)/shard_map/ppermute | solution.py:433
  65.4 6.5 %collective-permute-start.17 = (bf16[192,384]{1,0:T(8,128)(2,1)S(1)}, bf16[192,384]{1,0:T(8,128)(2,1)S(1)}, u32[]{:S(2)}, u32[]{:S(2)}) collective-permute-start(bf16[192,384]{1,0:T(8,128)(2,1)S(1)} %get-tuple-element.42), channel_id=1, source_target_pairs={{0,1},{1,0},{2,3},{3,2},{4,5},{5,4},{6,7},{7,6},{8,9},{9,8},{10,11... | collective-permute-start | bytes 442376 | tf_op jit(solution)/shard_map/ppermute | solution.py:433
  66.3 8.3 %collective-permute-start.18 = (bf16[192,384]{1,0:T(8,128)(2,1)S(1)}, bf16[192,384]{1,0:T(8,128)(2,1)S(1)}, u32[]{:S(2)}, u32[]{:S(2)}) collective-permute-start(bf16[192,384]{1,0:T(8,128)(2,1)S(1)} %get-tuple-element.43), channel_id=1, source_target_pairs={{0,2},{1,3},{2,0},{3,1},{4,6},{5,7},{6,4},{7,5},{8,10},{9,11},{10,... | collective-permute-start | bytes 442376 | tf_op jit(solution)/shard_map/ppermute | solution.py:433
  67.3 7.3 %collective-permute-start.19 = (bf16[192,384]{1,0:T(8,128)(2,1)S(1)}, bf16[192,384]{1,0:T(8,128)(2,1)S(1)}, u32[]{:S(2)}, u32[]{:S(2)}) collective-permute-start(bf16[192,384]{1,0:T(8,128)(2,1)S(1)} %get-tuple-element.44), channel_id=1, source_target_pairs={{0,3},{1,2},{2,1},{3,0},{4,7},{5,6},{6,5},{7,4},{8,11},{9,10},{10,... | collective-permute-start | bytes 442376 | tf_op jit(solution)/shard_map/ppermute | solution.py:433
  74.9 7.6 %collective-permute-start.20 = (bf16[96,384]{1,0:T(8,128)(2,1)S(1)}, bf16[96,384]{1,0:T(8,128)(2,1)S(1)}, u32[]{:S(2)}, u32[]{:S(2)}) collective-permute-start(bf16[96,384]{1,0:T(8,128)(2,1)S(1)} %get-tuple-element.46), channel_id=1, source_target_pairs={{0,8},{4,12},{8,0},{12,4},{1,9},{5,13},{9,1},{13,5},{2,10},{6,14},... | collective-permute-start | bytes 221192 | tf_op jit(solution)/shard_map/ppermute | solution.py:433
  75.8 6.7 %collective-permute-start.21 = (bf16[96,384]{1,0:T(8,128)(2,1)S(1)}, bf16[96,384]{1,0:T(8,128)(2,1)S(1)}, u32[]{:S(2)}, u32[]{:S(2)}) collective-permute-start(bf16[96,384]{1,0:T(8,128)(2,1)S(1)} %get-tuple-element.47), channel_id=1, source_target_pairs={{0,12},{4,8},{8,4},{12,0},{1,13},{5,9},{9,5},{13,1},{2,14},{6,10},... | collective-permute-start | bytes 221192 | tf_op jit(solution)/shard_map/ppermute | solution.py:433
  78.2 4.9 %collective-permute-start.22 = (bf16[96,384]{1,0:T(8,128)(2,1)S(1)}, bf16[96,384]{1,0:T(8,128)(2,1)S(1)}, u32[]{:S(2)}, u32[]{:S(2)}) collective-permute-start(bf16[96,384]{1,0:T(8,128)(2,1)S(1)} %get-tuple-element.48), channel_id=1, source_target_pairs={{0,4},{4,0},{8,12},{12,8},{1,5},{5,1},{9,13},{13,9},{2,6},{6,2},{1... | collective-permute-start | bytes 221192 | tf_op jit(solution)/shard_map/ppermute | solution.py:433

commit v5 on v4

--- a/solution.py
+++ b/solution.py
@@ -78,7 +78,7 @@
 
 
 def attend_kernel(*refs):
-    blocks, outs, (q_aug, k_aug, v_aug, clips) = refs[:4], refs[9:13], refs[13:]
+    blocks, outs, (q_aug, k_aug, v_aug, clips) = refs[:4], refs[-8:-4], refs[-4:]
     slots = outs[0].shape[0]
     lane = lax.broadcasted_iota(jnp.int32, (128, 128), 1)
     row = lax.broadcasted_iota(jnp.int32, (128, 128), 0)
@@ -102,16 +102,28 @@
             q_aug[part, 128:] = jnp.where(kept | (lane > CLIPS), 0.0, -FAR).astype(BF16)
             v_aug[part, 128:] = (lane == 0).astype(BF16)
     scale = math.log2(math.e) / math.sqrt(HEAD_DIM)
-    for index, out in enumerate(outs):
-        here = slice(index * slots, (index + 1) * slots)
-        scores = lax.dot_general(
-            q_aug[here, :], k_aug[...], (((1,), (1,)), ((), ())), preferred_element_type=F32
+    rows = 384
+
+    def score(first):
+        return lax.dot_general(
+            q_aug[first : first + rows, :],
+            k_aug[...],
+            (((1,), (1,)), ((), ())),
+            preferred_element_type=F32,
         )
+
+    firsts = range(0, 4 * slots, rows)
+    ahead = score(0)
+    for first in firsts:
+        scores = ahead
+        if first + rows < 4 * slots:
+            ahead = score(first + rows)
         peak = jnp.max(scores, axis=1, keepdims=True)
         probs = jnp.exp2((scores - peak) * scale).astype(BF16)
         summed = jnp.dot(probs, v_aug[...], preferred_element_type=F32)
         result = summed[:, :128] / summed[:, 128:129]
-        out[...] = jnp.where(clips[here, :] < CLIPS, result, 0.0).astype(BF16)
+        result = jnp.where(clips[first : first + rows, :] < CLIPS, result, 0.0).astype(BF16)
+        outs[first // slots][first % slots : first % slots + rows, :] = result
 
 
 def regroup_kernel(own, back1, back2, back3, first, second):
@@ -138,10 +150,10 @@
     return pltpu.with_memory_space_constraint(value, pltpu.HBM)
 
 
-def load_kernel(up, down, after, up_out, down_out, sems):
+def load_kernel(*refs):
+    outs, sems = refs[4:7], refs[7]
     copies = [
-        pltpu.make_async_copy(source, target, sems.at[index])
-        for index, (source, target) in enumerate(((up, up_out), (down, down_out)))
+        pltpu.make_async_copy(refs[index], out, sems.at[index]) for index, out in enumerate(outs)
     ]
     for copy in copies:
         copy.start()
@@ -149,16 +161,16 @@
         copy.wait()
 
 
-def load(up, down, after):
+def load(arrays, after):
     return pl.pallas_call(
         load_kernel,
-        out_shape=[pltpu.VMEM(up.shape, BF16), pltpu.VMEM(down.shape, BF16)],
-        in_specs=[ANY] * 3,
-        out_specs=[VMEM] * 2,
-        scratch_shapes=[pltpu.SemaphoreType.DMA((2,))],
+        out_shape=[pltpu.VMEM(array.shape, BF16) for array in arrays],
+        in_specs=[ANY] * 4,
+        out_specs=[VMEM] * 3,
+        scratch_shapes=[pltpu.SemaphoreType.DMA((3,))],
         compiler_params=params(16),
         name="load",
-    )(afar(up), afar(down), after)
+    )(*(afar(array) for array in arrays), after)
 
 
 def across(value, masks):
@@ -256,11 +268,11 @@
         name="pack",
     )(afar(query), afar(key), afar(value), afar(slot_clip.reshape(slots // 128, 128)))
     blocks = [packed[0]] + [hop(packed[index], STEPS[index]) for index in (1, 2, 3)]
-    early = (*early, *(kept(weight) for weight in load(*weights, packed[0])))
+    early = (*early, *(kept(weight) for weight in load(weights, packed[0])))
     results = pl.pallas_call(
         attend_kernel,
         out_shape=[shape_of((slots, 128))] * 4,
-        in_specs=[VMEM] * 4 + [ANY] * (len(early) - 2) + [VMEM] * 2,
+        in_specs=[VMEM] * 4 + [ANY] * (len(early) - 3) + [VMEM] * 3,
         out_specs=[VMEM] * 4,
         scratch_shapes=[pltpu.VMEM((4 * slots, 256), BF16)] * 3
         + [pltpu.VMEM((4 * slots, 128), jnp.int32)],
@@ -270,7 +282,7 @@
     )(*blocks, *early)
     backs = [hop(results[index], STEPS[index], back=True) for index in (1, 2, 3)]
     half = slots // 2
-    return early[-2:], pl.pallas_call(
+    return early[-3:], pl.pallas_call(
         regroup_kernel,
         out_shape=[shape_of((half, 3 * HEAD_DIM))] * 2,
         in_specs=[VMEM] * 4,
@@ -324,34 +336,44 @@
 
 
 def chosen(mod, kind, clip, columns):
-    picked = jnp.zeros((clip.shape[0], mod[0, :1, columns].shape[1]), F32)
+    picked = jnp.zeros((clip.shape[0], columns.stop - columns.start), F32)
     for index in range(CLIPS):
         picked = jnp.where(clip == index, mod[index, kind : kind + 1, columns], picked)
     return picked
 
 
+def lowered_tiles(hidden, mixed, down, mod, clip):
+    blk = lax.axis_index("blk")
+    width = D // lax.axis_size("blk")
+    for start in range(0, D, 2 * width):
+        columns = slice(start, start + 2 * width)
+        lowered = jnp.dot(hidden[...], down[:, columns], preferred_element_type=F32)
+        lowered = chosen(mod, 3, clip, columns) * lowered
+        for index in range(2):
+            part = slice(start + index * width, start + (index + 1) * width)
+            stream = jnp.where(blk == part.start // width, mixed[:, part], 0.0)
+            yield part, lowered[:, index * width : (index + 1) * width] + stream
+
+
 def feed_kernel(turn, *refs):
-    att, (w_out, up, down, res_hbm, mod, clip_ref), refs = refs[:4], refs[4:10], refs[10:]
+    att, (w_out, up, down, res, mod, clip_ref), refs = refs[:4], refs[4:10], refs[10:]
     if turn == 0:
-        out, mixed, hidden, res, normed, sem = refs
+        out, mixed, hidden, normed = refs
     else:
-        hidden, mixed, res, normed, sem = refs
-    side, blk = lax.axis_index("cfg"), lax.axis_index("blk")
+        hidden, mixed, normed = refs
+    side = lax.axis_index("cfg")
     half = hidden.shape[0]
     which = 1 - side if turn == 0 else side
     rows = pl.ds(pl.multiple_of(which * half, half), half)
-    width = att[0].shape[1]
-    copy = pltpu.make_async_copy(res_hbm.at[rows, :], res, sem)
-    copy.start()
     rows_in = jnp.concatenate([piece[...] for piece in att], axis=1)
     clip = clip_ref[rows, :][:, :1]
     tiles = [slice(start, start + 512) for start in range(0, D, 512)]
     for columns in tiles:
         projected = jnp.dot(rows_in, w_out[:, columns], preferred_element_type=F32)
-        mixed[:, columns] = chosen(mod, 0, clip, columns) * projected
-    copy.wait()
-    held = mixed[...] + res[...].astype(F32)
-    mixed[...] = held
+        mixed[:, columns] = (
+            res[rows, columns].astype(F32) + chosen(mod, 0, clip, columns) * projected
+        )
+    held = mixed[...]
     centre = held - jnp.mean(held, axis=1, keepdims=True)
     spread = lax.rsqrt(jnp.mean(centre * centre, axis=1, keepdims=True) + 1e-06)
     for columns in tiles:
@@ -361,17 +383,13 @@
         raised = jnp.dot(normed[...], up[:, columns], preferred_element_type=F32)
         hidden[:, columns] = jax.nn.gelu(raised, approximate=True).astype(BF16)
     if turn == 0:
-        for columns in tiles:
-            lowered = jnp.dot(hidden[...], down[:, columns], preferred_element_type=F32)
-            out[:, columns] = (chosen(mod, 3, clip, columns) * lowered).astype(BF16)
-        own = pl.ds(pl.multiple_of(blk * width, width), width)
-        lowered = jnp.dot(hidden[...], down[:, own], preferred_element_type=F32)
-        out[:, own] = (chosen(mod, 3, clip, own) * lowered + mixed[:, own]).astype(BF16)
+        for columns, terms in lowered_tiles(hidden, mixed, down, mod, clip):
+            out[:, columns] = terms.astype(BF16)
 
 
 def feed(turn, att, w_out, w_up, w_down, residual, mod, clip_wide):
     half, width = att[0].shape
-    inner = [pltpu.VMEM((half, D), BF16), pltpu.VMEM((half, D), BF16), pltpu.SemaphoreType.DMA]
+    inner = [pltpu.VMEM((half, D), BF16)]
     if turn == 0:
         out_shape = shape_of((half, D))
         inner = [pltpu.VMEM((half, D), F32), pltpu.VMEM((half, D), BF16)] + inner
@@ -380,32 +398,31 @@
     return pl.pallas_call(
         functools.partial(feed_kernel, turn),
         out_shape=out_shape,
-        in_specs=[VMEM] * 7 + [ANY] + [VMEM] * 2,
+        in_specs=[VMEM] * 10,
         out_specs=VMEM if turn == 0 else [VMEM] * 2,
         scratch_shapes=inner,
         compiler_params=params(24),
         cost_estimate=cost(2**36, 2**24),
         name="feed",
-    )(*att, kept(w_out), kept(w_up), kept(w_down), afar(residual), mod, clip_wide)
-
-
-def guide_kernel(hidden, mixed, down, other_ref, clip_ref, mod, scale_ref, own, *sent):
+    )(*att, kept(w_out), kept(w_up), kept(w_down), kept(residual), mod, clip_wide)
+
+
+def guide_kernel(hidden, mixed, down, other_ref, clip_ref, mod, scale_ref, *refs):
+    outs, held = refs[:4], refs[4]
     side, blk = lax.axis_index("cfg"), lax.axis_index("blk")
-    half, width = own.shape
+    half, width = outs[0].shape
     clip = clip_ref[pl.ds(pl.multiple_of(side * half, half), half), :][:, :1]
     strength = jnp.zeros((half, 1), F32)
     for index in range(CLIPS):
         strength = jnp.where(clip == index, scale_ref[index], strength)
     lean = jnp.where(side == 0, strength, 1.0 - strength)
-    for step, out in enumerate((own, *sent)):
+    for columns, mine in lowered_tiles(hidden, mixed, down, mod, clip):
+        other = other_ref[:, columns].astype(F32)
+        held[:, columns] = other + lean * (mine - other)
+    for step, out in enumerate(outs):
         target = jnp.bitwise_xor(blk, step)
         columns = pl.ds(pl.multiple_of(target * width, width), width)
-        lowered = jnp.dot(hidden[...], down[:, columns], preferred_element_type=F32)
-        mine = chosen(mod, 3, clip, columns) * lowered
-        if step == 0:
-            mine = mine + mixed[:, columns]
-        other = other_ref[:, columns].astype(F32)
-        out[...] = (other + lean * (mine - other)).astype(out.dtype)
+        out[...] = held[:, columns].astype(out.dtype)
 
 
 def place_kernel(own, got1, got2, got3, placing, *outs):
@@ -459,30 +476,31 @@
 
     near, w_half = fetch_near(w_out)
     if seq_count == 4:
-        (up, down), attended = attention_by_head(
+        (up, down, stream), attended = attention_by_head(
             queries[0],
             keys[0],
             values[0],
             slot_clip,
             (clip_wide, placing, w_half),
-            (w_up, w_down),
+            (w_up, w_down, residual[0]),
         )
     else:
         attended = attention_by_rows(queries[0], keys[0], values[0], slot_clip)
-        up, down = load(w_up, w_down, attended[0])
+        up, down, stream = load((w_up, w_down, residual[0]), attended[0])
 
     whole = fetch_rest(w_out, near, w_half, attended[0])
     parts = []
     for turn in range(2):
         piece = attended[turn]
         gathered = [piece] + [exchanged(piece, "blk", mask) for mask in (1, 2, 3)]
-        parts.append(feed(turn, gathered, whole, up, down, residual[0], modulation, clip_wide))
+        parts.append(feed(turn, gathered, whole, up, down, stream, modulation, clip_wide))
     other = exchanged(parts[0], "cfg", 1)
     own, *sent = pl.pallas_call(
         guide_kernel,
         out_shape=[shape_of((half, width), F32)] + [shape_of((half, width))] * 3,
         in_specs=[VMEM] * 6 + [pl.BlockSpec(memory_space=pltpu.SMEM)],
         out_specs=[VMEM] * 4,
+        scratch_shapes=[pltpu.VMEM((half, D), F32)],
         compiler_params=params(16),
         name="guide",
     )(*parts[1], kept(down), other, clip_wide, modulation, guide_scale)

time: 84.3 us -> 83.4 us (0.989)
  Pallas kernels: 21.6 us -> 20.4 us
  transfers between devices with their start and end apart: 23 -> 23, of which waited for: 9 -> 9; matrix products, arithmetic and copies ran while one was open for 1% -> 1% of each run, Pallas kernels for 22% -> 21%
where the time goes in v5:
time: 83.4 us; the launch traced here: 83 us
  starting transfers between devices  37.8 us (45%)
  waiting for transfers between devices  23.3 us (28%)
  Pallas kernels  20.4 us (24%)
  other arithmetic  1 us (1%)
    ppermute x6, starting transfers between devices, hop(): return lax.ppermute(value, ('cfg', 'seq'), pairs)  18.4 us
    ppermute x15, waiting for transfers between devices, exchanged(): return lax.ppermute(value, axis, pairs)  14.7 us
    ppermute x15, starting transfers between devices, exchanged(): return lax.ppermute(value, axis, pairs)  14.4 us
    pallas_call x2, Pallas kernels, feed(): pl.pallas_call(functools.partial(feed_kernel, turn), out_shape=out_shape,...  6.56 us
    ppermute x6, waiting for transfers between devices, hop(): return lax.ppermute(value, ('cfg', 'seq'), pairs)  6.01 us
    ppermute x2, starting transfers between devices, across(): return lax.ppermute(value, ('cfg', 'blk'), pairs)  5.06 us
    pallas_call x1, Pallas kernels, load(): pl.pallas_call(load_kernel, out_shape=[pltpu.VMEM(array.shape, BF16) for...  4.07 us
    pallas_call x1, Pallas kernels, attention_by_head(): pl.pallas_call(attend_kernel, out_shape=[shape_of((slots, 128))] * 4, in_...  3.66 us
  transfers between devices with their start and end apart: 23, of which 9 were waited for; matrix products, arithmetic and copies ran while one was open for 1% of the time, Pallas kernels for 21%

profile of v5, /device:TPU:0, one launch (start us, length us, event | category | flops | bytes accessed | tf_op | source)
XLA Modules:
  0.0 83.0 jit_solution(13570222657938221562)
XLA Ops:
  0.0 2.9 %collective-permute-start.3 = (bf16[384,1536]{1,0:T(8,128)(2,1)}, bf16[384,1536]{1,0:T(8,128)(2,1)S(1)}, u32[]{:S(2)}, u32[]{:S(2)}) collective-permute-start(bf16[384,1536]{1,0:T(8,128)(2,1)} %own.1), channel_id=1, source_target_pairs={{0,1},{1,0},{2,3},{3,2},{16,18},{17,19},{18,16},{19,17},{4,5},{5,4... | collective-permute-start | bytes 3538952 | tf_op jit(solution)/shard_map/ppermute | solution.py:180
  2.9 1.5 %pack.1 = (bf16[1168,128]{1,0:T(8,128)(2,1)S(1)}, bf16[1168,128]{1,0:T(8,128)(2,1)S(1)}, bf16[1168,128]{1,0:T(8,128)(2,1)S(1)}, bf16[1168,128]{1,0:T(8,128)(2,1)S(1)}) custom-call(bf16[384,384]{1,0:T(8,128)(2,1)} %bitcast.8, bf16[384,384]{1,0:T(8,128)(2,1)} %bitcast.9, bf16[384,384]{1,0:T(8,128)(2,1)} %bitcast.10, s32[3,128]{1,0:T(4,128)} %bitcast.13), custom_call_target="tpu_custom_call" | custom-call | tf_op jit(solution)/shard_map/pack/pallas_call | solution.py:258
  4.4 4.5 %collective-permute-start = (bf16[1168,128]{1,0:T(8,128)(2,1)S(1)}, bf16[1168,128]{1,0:T(8,128)(2,1)S(1)}, u32[]{:S(2)}, u32[]{:S(2)}) collective-permute-start(bf16[1168,128]{1,0:T(8,128)(2,1)S(1)} %get-tuple-element.29), channel_id=1, source_target_pairs={{0,8},{8,0},{12,4},{16,24},{20,28},{28,20},{1,9},{9,1},{13,5},{17,... | collective-permute-start | bytes 897032 | tf_op jit(solution)/shard_map/ppermute | solution.py:53
  8.9 1.3 %collective-permute-start.1 = (bf16[1168,128]{1,0:T(8,128)(2,1)S(1)}, bf16[1168,128]{1,0:T(8,128)(2,1)S(1)}, u32[]{:S(2)}, u32[]{:S(2)}) collective-permute-start(bf16[1168,128]{1,0:T(8,128)(2,1)S(1)} %get-tuple-element.30), channel_id=1, source_target_pairs={{4,8},{8,4},{12,0},{16,28},{20,24},{24,20},{5,9},{9,5},{13,1},{17,... | collective-permute-start | bytes 897032 | tf_op jit(solution)/shard_map/ppermute | solution.py:53
  10.2 3.4 %collective-permute-start.2 = (bf16[1168,128]{1,0:T(8,128)(2,1)S(1)}, bf16[1168,128]{1,0:T(8,128)(2,1)S(1)}, u32[]{:S(2)}, u32[]{:S(2)}) collective-permute-start(bf16[1168,128]{1,0:T(8,128)(2,1)S(1)} %get-tuple-element.31), channel_id=1, source_target_pairs={{0,4},{4,0},{12,8},{16,20},{24,28},{28,24},{1,5},{5,1},{13,9},{17,... | collective-permute-start | bytes 897032 | tf_op jit(solution)/shard_map/ppermute | solution.py:53
  13.7 0.1 constant_dynamic-slice_fusion
  13.7 0.2 convert_reduce_fusion
  13.9 0.8 compare_select_fusion
  14.7 2.6 %collective-permute-done.3.got.near = bf16[384,1536]{1,0:T(8,128)(2,1)S(1)} collective-permute-done((bf16[384,1536]{1,0:T(8,128)(2,1)}, bf16[384,1536]{1,0:T(8,128)(2,1)S(1)}, u32[]{:S(2)}, u32[]{:S(2)}) %collective-permute-start.3) | collective-permute-done | bytes 1179680 | tf_op jit(solution)/shard_map/ppermute | solution.py:180
  17.3 0.1 cut.1.refs_6_
  17.5 2.1 %collective-permute-start.11 = (bf16[192,1536]{1,0:T(8,128)(2,1)S(1)}, bf16[192,1536]{1,0:T(8,128)(2,1)S(1)}, u32[]{:S(2)}, u32[]{:S(2)}) collective-permute-start(bf16[192,1536]{1,0:T(8,128)(2,1)S(1)} %cut.1.refs_6_), channel_id=1, source_target_pairs={{0,2},{1,3},{2,0},{3,1},{16,17},{17,16},{18,19},{19,18},{4,6},{5,7... | collective-permute-start | bytes 1769480 | tf_op jit(solution)/shard_map/ppermute | solution.py:180
  19.6 0.0 copy-start.3
  19.6 4.1 %load.1 = (bf16[1536,1536]{1,0:T(8,128)(2,1)S(1)}, bf16[1536,1536]{1,0:T(8,128)(2,1)S(1)}, bf16[384,1536]{1,0:T(8,128)(2,1)S(1)}) custom-call(bf16[1536,1536]{1,0:T(8,128)(2,1)} %refs_0_.1, bf16[1536,1536]{1,0:T(8,128)(2,1)} %refs_1_.1, bf16[384,1536]{1,0:T(8,128)(2,1)} %bitcast.7, bf16[1168,128]{1,0:T(8,128)(2,1)S(1)} %get-tuple-element.28.refs_3_.refs_0_), custom_call_target="tpu_custom_call" | custom-call | tf_op jit(solution)/shard_map/load/pallas_call | solution.py:165
  23.7 2.6 %collective-permute-done.refs_1_ = bf16[1168,128]{1,0:T(8,128)(2,1)S(1)} collective-permute-done((bf16[1168,128]{1,0:T(8,128)(2,1)S(1)}, bf16[1168,128]{1,0:T(8,128)(2,1)S(1)}, u32[]{:S(2)}, u32[]{:S(2)}) %collective-permute-start) | collective-permute-done | bytes 299040 | tf_op jit(solution)/shard_map/ppermute | solution.py:53
  26.3 0.1 broadcast_in_dim.7.refs_4_.refs_9_.clip_ref
  26.4 3.7 %attend.1 = (bf16[384,128]{1,0:T(8,128)(2,1)S(1)}, bf16[384,128]{1,0:T(8,128)(2,1)S(1)}, bf16[384,128]{1,0:T(8,128)(2,1)S(1)}, bf16[384,128]{1,0:T(8,128)(2,1)S(1)}) custom-call(bf16[1168,128]{1,0:T(8,128)(2,1)S(1)} %get-tuple-element.28.refs_3_.refs_0_, bf16[1168,128]{1,0:T(8,128)(2,1)S(1)} %collective-permute-done.refs_1_, ...), custom_call_target="tpu_custom_call" | custom-call | flops 4294967296 | bytes 2097152 | tf_op jit(solution)/shard_map/attend/pallas_call | solution.py:272
  30.1 4.8 %collective-permute-start.4 = (bf16[384,128]{1,0:T(8,128)(2,1)S(1)}, bf16[384,128]{1,0:T(8,128)(2,1)S(1)}, u32[]{:S(2)}, u32[]{:S(2)}) collective-permute-start(bf16[384,128]{1,0:T(8,128)(2,1)S(1)} %get-tuple-element.36), channel_id=1, source_target_pairs={{8,0},{0,8},{4,12},{24,16},{28,20},{20,28},{9,1},{1,9},{5,13},{25,... | collective-permute-start | bytes 294920 | tf_op jit(solution)/shard_map/ppermute | solution.py:53
  34.9 1.3 %collective-permute-start.5 = (bf16[384,128]{1,0:T(8,128)(2,1)S(1)}, bf16[384,128]{1,0:T(8,128)(2,1)S(1)}, u32[]{:S(2)}, u32[]{:S(2)}) collective-permute-start(bf16[384,128]{1,0:T(8,128)(2,1)S(1)} %get-tuple-element.37), channel_id=1, source_target_pairs={{8,4},{4,8},{0,12},{28,16},{24,20},{20,24},{9,5},{5,9},{1,13},{29,... | collective-permute-start | bytes 294920 | tf_op jit(solution)/shard_map/ppermute | solution.py:53
  36.2 3.2 %collective-permute-start.6 = (bf16[384,128]{1,0:T(8,128)(2,1)S(1)}, bf16[384,128]{1,0:T(8,128)(2,1)S(1)}, u32[]{:S(2)}, u32[]{:S(2)}) collective-permute-start(bf16[384,128]{1,0:T(8,128)(2,1)S(1)} %get-tuple-element.38), channel_id=1, source_target_pairs={{4,0},{0,4},{8,12},{20,16},{28,24},{24,28},{5,1},{1,5},{9,13},{21,... | collective-permute-start | bytes 294920 | tf_op jit(solution)/shard_map/ppermute | solution.py:53
  39.4 3.4 %collective-permute-done.6.back3 = bf16[384,128]{1,0:T(8,128)(2,1)S(1)} collective-permute-done((bf16[384,128]{1,0:T(8,128)(2,1)S(1)}, bf16[384,128]{1,0:T(8,128)(2,1)S(1)}, u32[]{:S(2)}, u32[]{:S(2)}) %collective-permute-start.6) | collective-permute-done | bytes 98336 | tf_op jit(solution)/shard_map/ppermute | solution.py:53
  42.8 0.3 regroup.1
  43.1 0.1 collective-permute-start.12
  43.2 1.3 %collective-permute-start.13 = (bf16[192,384]{1,0:T(8,128)(2,1)S(1)}, bf16[192,384]{1,0:T(8,128)(2,1)S(1)}, u32[]{:S(2)}, u32[]{:S(2)}) collective-permute-start(bf16[192,384]{1,0:T(8,128)(2,1)S(1)} %get-tuple-element.40.after.refs_0_), channel_id=1, source_target_pairs={{0,1},{1,0},{2,3},{3,2},{4,5},{5,4},{6,7},{7,6},{8,9},{9,8},{10,11... | collective-permute-start | bytes 442376 | tf_op jit(solution)/shard_map/ppermute | solution.py:450
  44.5 0.9 %collective-permute-start.14 = (bf16[192,384]{1,0:T(8,128)(2,1)S(1)}, bf16[192,384]{1,0:T(8,128)(2,1)S(1)}, u32[]{:S(2)}, u32[]{:S(2)}) collective-permute-start(bf16[192,384]{1,0:T(8,128)(2,1)S(1)} %get-tuple-element.40.after.refs_0_), channel_id=1, source_target_pairs={{0,2},{1,3},{2,0},{3,1},{4,6},{5,7},{6,4},{7,5},{8,10},{9,11},{10,... | collective-permute-start | bytes 442376 | tf_op jit(solution)/shard_map/ppermute | solution.py:450
  45.4 1.3 %collective-permute-start.15 = (bf16[192,384]{1,0:T(8,128)(2,1)S(1)}, bf16[192,384]{1,0:T(8,128)(2,1)S(1)}, u32[]{:S(2)}, u32[]{:S(2)}) collective-permute-start(bf16[192,384]{1,0:T(8,128)(2,1)S(1)} %get-tuple-element.40.after.refs_0_), channel_id=1, source_target_pairs={{0,3},{1,2},{2,1},{3,0},{4,7},{5,6},{6,5},{7,4},{8,11},{9,10},{10,... | collective-permute-start | bytes 442376 | tf_op jit(solution)/shard_map/ppermute | solution.py:450
  46.7 1.2 %collective-permute-start.7 = (bf16[192,384]{1,0:T(8,128)(2,1)S(1)}, bf16[192,384]{1,0:T(8,128)(2,1)S(1)}, u32[]{:S(2)}, u32[]{:S(2)}) collective-permute-start(bf16[192,384]{1,0:T(8,128)(2,1)S(1)} %get-tuple-element.39.refs_0_), channel_id=1, source_target_pairs={{0,1},{1,0},{2,3},{3,2},{4,5},{5,4},{6,7},{7,6},{8,9},{9,8},{10,11... | collective-permute-start | bytes 442376 | tf_op jit(solution)/shard_map/ppermute | solution.py:450
  48.0 0.9 %collective-permute-start.8 = (bf16[192,384]{1,0:T(8,128)(2,1)S(1)}, bf16[192,384]{1,0:T(8,128)(2,1)S(1)}, u32[]{:S(2)}, u32[]{:S(2)}) collective-permute-start(bf16[192,384]{1,0:T(8,128)(2,1)S(1)} %get-tuple-element.39.refs_0_), channel_id=1, source_target_pairs={{0,2},{1,3},{2,0},{3,1},{4,6},{5,7},{6,4},{7,5},{8,10},{9,11},{10,... | collective-permute-start | bytes 442376 | tf_op jit(solution)/shard_map/ppermute | solution.py:450
  48.9 1.3 %join.1.refs_4_ = bf16[1536,1536]{1,0:T(8,128)(2,1)S(1)} custom-call(bf16[384,1536]{1,0:T(8,128)(2,1)} %own.1, bf16[384,1536]{1,0:T(8,128)(2,1)S(1)} %collective-permute-done.3.got.near, bf16[384,1536]{1,0:T(8,128)(2,1)S(1)} %collective-permute-done.10.near_swap, bf16[192,1536]{1,0:T(8,128)(2,1)S(1)} %gate.1.far, ...), custom_call_target="tpu_custom_call" | custom-call | tf_op jit(solution)/shard_map/join/pallas_call | solution.py:245
  50.2 1.4 %collective-permute-start.9 = (bf16[192,384]{1,0:T(8,128)(2,1)S(1)}, bf16[192,384]{1,0:T(8,128)(2,1)S(1)}, u32[]{:S(2)}, u32[]{:S(2)}) collective-permute-start(bf16[192,384]{1,0:T(8,128)(2,1)S(1)} %get-tuple-element.39.refs_0_), channel_id=1, source_target_pairs={{0,3},{1,2},{2,1},{3,0},{4,7},{5,6},{6,5},{7,4},{8,11},{9,10},{10,... | collective-permute-start | bytes 442376 | tf_op jit(solution)/shard_map/ppermute | solution.py:450
  51.6 2.7 %collective-permute-done.14.refs_2_ = bf16[192,384]{1,0:T(8,128)(2,1)S(1)} collective-permute-done((bf16[192,384]{1,0:T(8,128)(2,1)S(1)}, bf16[192,384]{1,0:T(8,128)(2,1)S(1)}, u32[]{:S(2)}, u32[]{:S(2)}) %collective-permute-start.14) | collective-permute-done | bytes 147488 | tf_op jit(solution)/shard_map/ppermute | solution.py:450
  54.3 3.7 %feed.3 = bf16[192,1536]{1,0:T(8,128)(2,1)S(1)} custom-call(bf16[192,384]{1,0:T(8,128)(2,1)S(1)} %get-tuple-element.40.after.refs_0_, bf16[192,384]{1,0:T(8,128)(2,1)S(1)} %collective-permute-done.13.refs_1_, bf16[192,384]{1,0:T(8,128)(2,1)S(1)} %collective-permute-done.14.refs_2_, bf16[192,384]{1,0:T(8,128)(2,1)S(1)} %collective-permute-done.15.refs_3_, ...), custom_call_target="tpu_custom_call" | custom-call | flops 68719476736 | bytes 16777216 | tf_op jit(solution)/shard_map/feed/pallas_call | solution.py:398
  58.1 0.0 copy-start.2
  58.1 0.1 collective-permute-start.16
  58.2 1.7 %collective-permute-done.8.refs_2_ = bf16[192,384]{1,0:T(8,128)(2,1)S(1)} collective-permute-done((bf16[192,384]{1,0:T(8,128)(2,1)S(1)}, bf16[192,384]{1,0:T(8,128)(2,1)S(1)}, u32[]{:S(2)}, u32[]{:S(2)}) %collective-permute-start.8) | collective-permute-done | bytes 147488 | tf_op jit(solution)/shard_map/ppermute | solution.py:450
  59.9 2.8 %feed.2 = (bf16[192,1536]{1,0:T(8,128)(2,1)S(1)}, f32[192,1536]{1,0:T(8,128)S(1)}) custom-call(bf16[192,384]{1,0:T(8,128)(2,1)S(1)} %get-tuple-element.39.refs_0_, bf16[192,384]{1,0:T(8,128)(2,1)S(1)} %collective-permute-done.7.refs_1_, bf16[192,384]{1,0:T(8,128)(2,1)S(1)} %collective-permute-done.8.refs_2_, ...), custom_call_target="tpu_custom_call" | custom-call | flops 68719476736 | bytes 16777216 | tf_op jit(solution)/shard_map/feed/pallas_call | solution.py:398
  62.7 1.9 %guide.1 = (f32[192,384]{1,0:T(8,128)S(1)}, bf16[192,384]{1,0:T(8,128)(2,1)S(1)}, bf16[192,384]{1,0:T(8,128)(2,1)S(1)}, bf16[192,384]{1,0:T(8,128)(2,1)S(1)}) custom-call(bf16[192,1536]{1,0:T(8,128)(2,1)S(1)} %get-tuple-element.41.hidden, f32[192,1536]{1,0:T(8,128)S(1)} %get-tuple-element.42.mixed, ...), custom_call_target="tpu_custom_call" | custom-call | tf_op jit(solution)/shard_map/guide/pallas_call | solution.py:498
  64.6 0.9 %collective-permute-start.17 = (bf16[192,384]{1,0:T(8,128)(2,1)S(1)}, bf16[192,384]{1,0:T(8,128)(2,1)S(1)}, u32[]{:S(2)}, u32[]{:S(2)}) collective-permute-start(bf16[192,384]{1,0:T(8,128)(2,1)S(1)} %get-tuple-element.44), channel_id=1, source_target_pairs={{0,1},{1,0},{2,3},{3,2},{4,5},{5,4},{6,7},{7,6},{8,9},{9,8},{10,11... | collective-permute-start | bytes 442376 | tf_op jit(solution)/shard_map/ppermute | solution.py:450
  65.5 1.0 %collective-permute-start.18 = (bf16[192,384]{1,0:T(8,128)(2,1)S(1)}, bf16[192,384]{1,0:T(8,128)(2,1)S(1)}, u32[]{:S(2)}, u32[]{:S(2)}) collective-permute-start(bf16[192,384]{1,0:T(8,128)(2,1)S(1)} %get-tuple-element.45), channel_id=1, source_target_pairs={{0,2},{1,3},{2,0},{3,1},{4,6},{5,7},{6,4},{7,5},{8,10},{9,11},{10,... | collective-permute-start | bytes 442376 | tf_op jit(solution)/shard_map/ppermute | solution.py:450
  66.5 1.7 %collective-permute-start.19 = (bf16[192,384]{1,0:T(8,128)(2,1)S(1)}, bf16[192,384]{1,0:T(8,128)(2,1)S(1)}, u32[]{:S(2)}, u32[]{:S(2)}) collective-permute-start(bf16[192,384]{1,0:T(8,128)(2,1)S(1)} %get-tuple-element.46), channel_id=1, source_target_pairs={{0,3},{1,2},{2,1},{3,0},{4,7},{5,6},{6,5},{7,4},{8,11},{9,10},{10,... | collective-permute-start | bytes 442376 | tf_op jit(solution)/shard_map/ppermute | solution.py:450
  68.2 2.9 %collective-permute-done.17.got1 = bf16[192,384]{1,0:T(8,128)(2,1)S(1)} collective-permute-done((bf16[192,384]{1,0:T(8,128)(2,1)S(1)}, bf16[192,384]{1,0:T(8,128)(2,1)S(1)}, u32[]{:S(2)}, u32[]{:S(2)}) %collective-permute-start.17) | collective-permute-done | bytes 147488 | tf_op jit(solution)/shard_map/ppermute | solution.py:450
  71.1 2.7 %collective-permute-done.18.got2 = bf16[192,384]{1,0:T(8,128)(2,1)S(1)} collective-permute-done((bf16[192,384]{1,0:T(8,128)(2,1)S(1)}, bf16[192,384]{1,0:T(8,128)(2,1)S(1)}, u32[]{:S(2)}, u32[]{:S(2)}) %collective-permute-start.18) | collective-permute-done | bytes 147488 | tf_op jit(solution)/shard_map/ppermute | solution.py:450
  73.8 0.3 place.1
  74.1 0.9 %collective-permute-start.20 = (bf16[96,384]{1,0:T(8,128)(2,1)S(1)}, bf16[96,384]{1,0:T(8,128)(2,1)S(1)}, u32[]{:S(2)}, u32[]{:S(2)}) collective-permute-start(bf16[96,384]{1,0:T(8,128)(2,1)S(1)} %get-tuple-element.48), channel_id=1, source_target_pairs={{0,8},{4,12},{8,0},{12,4},{1,9},{5,13},{9,1},{13,5},{2,10},{6,14},... | collective-permute-start | bytes 221192 | tf_op jit(solution)/shard_map/ppermute | solution.py:450
  75.0 2.4 %collective-permute-start.21 = (bf16[96,384]{1,0:T(8,128)(2,1)S(1)}, bf16[96,384]{1,0:T(8,128)(2,1)S(1)}, u32[]{:S(2)}, u32[]{:S(2)}) collective-permute-start(bf16[96,384]{1,0:T(8,128)(2,1)S(1)} %get-tuple-element.49), channel_id=1, source_target_pairs={{0,12},{4,8},{8,4},{12,0},{1,13},{5,9},{9,5},{13,1},{2,14},{6,10},... | collective-permute-start | bytes 221192 | tf_op jit(solution)/shard_map/ppermute | solution.py:450
  77.4 0.2 collective-permute-start.22
  77.6 4.1 %collective-permute-done.20.refs_1_ = bf16[96,384]{1,0:T(8,128)(2,1)S(1)} collective-permute-done((bf16[96,384]{1,0:T(8,128)(2,1)S(1)}, bf16[96,384]{1,0:T(8,128)(2,1)S(1)}, u32[]{:S(2)}, u32[]{:S(2)}) %collective-permute-start.20) | collective-permute-done | bytes 73760 | tf_op jit(solution)/shard_map/ppermute | solution.py:450
  81.7 0.6 collective-permute-done.22.refs_3_
  82.3 0.8 arrange.1
  (23 shorter events, 0.1 us)
Async XLA Ops:
  0.0 13.6 %copy-start = (s32[384,1]{0,1:T(1,128)S(1)}, s32[384,1]{0,1:T(1,128)}, u32[]{:S(2)}) copy-start(s32[384,1]{0,1:T(1,128)} %param.21) | copy-start | bytes 4612
  0.0 17.3 %collective-permute-start.3 = (bf16[384,1536]{1,0:T(8,128)(2,1)}, bf16[384,1536]{1,0:T(8,128)(2,1)S(1)}, u32[]{:S(2)}, u32[]{:S(2)}) collective-permute-start(bf16[384,1536]{1,0:T(8,128)(2,1)} %own.1), channel_id=1, source_target_pairs={{0,1},{1,0},{2,3},{3,2},{16,18},{17,19},{18,16},{19,17},{4,5},{5,4... | collective-permute-start | bytes 3538952 | tf_op jit(solution)/shard_map/ppermute | solution.py:180
  4.4 21.9 %collective-permute-start = (bf16[1168,128]{1,0:T(8,128)(2,1)S(1)}, bf16[1168,128]{1,0:T(8,128)(2,1)S(1)}, u32[]{:S(2)}, u32[]{:S(2)}) collective-permute-start(bf16[1168,128]{1,0:T(8,128)(2,1)S(1)} %get-tuple-element.29), channel_id=1, source_target_pairs={{0,8},{8,0},{12,4},{16,24},{20,28},{28,20},{1,9},{9,1},{13,5},{17,... | collective-permute-start | bytes 897032 | tf_op jit(solution)/shard_map/ppermute | solution.py:53
  8.9 17.4 %collective-permute-start.1 = (bf16[1168,128]{1,0:T(8,128)(2,1)S(1)}, bf16[1168,128]{1,0:T(8,128)(2,1)S(1)}, u32[]{:S(2)}, u32[]{:S(2)}) collective-permute-start(bf16[1168,128]{1,0:T(8,128)(2,1)S(1)} %get-tuple-element.30), channel_id=1, source_target_pairs={{4,8},{8,4},{12,0},{16,28},{20,24},{24,20},{5,9},{9,5},{13,1},{17,... | collective-permute-start | bytes 897032 | tf_op jit(solution)/shard_map/ppermute | solution.py:53
  10.2 16.1 %collective-permute-start.2 = (bf16[1168,128]{1,0:T(8,128)(2,1)S(1)}, bf16[1168,128]{1,0:T(8,128)(2,1)S(1)}, u32[]{:S(2)}, u32[]{:S(2)}) collective-permute-start(bf16[1168,128]{1,0:T(8,128)(2,1)S(1)} %get-tuple-element.31), channel_id=1, source_target_pairs={{0,4},{4,0},{12,8},{16,20},{24,28},{28,24},{1,5},{5,1},{13,9},{17,... | collective-permute-start | bytes 897032 | tf_op jit(solution)/shard_map/ppermute | solution.py:53
  17.5 25.6 %collective-permute-start.11 = (bf16[192,1536]{1,0:T(8,128)(2,1)S(1)}, bf16[192,1536]{1,0:T(8,128)(2,1)S(1)}, u32[]{:S(2)}, u32[]{:S(2)}) collective-permute-start(bf16[192,1536]{1,0:T(8,128)(2,1)S(1)} %cut.1.refs_6_), channel_id=1, source_target_pairs={{0,2},{1,3},{2,0},{3,1},{16,17},{17,16},{18,19},{19,18},{4,6},{5,7... | collective-permute-start | bytes 1769480 | tf_op jit(solution)/shard_map/ppermute | solution.py:180
  19.6 28.4 %collective-permute-start.10 = (bf16[384,1536]{1,0:T(8,128)(2,1)S(1)}, bf16[384,1536]{1,0:T(8,128)(2,1)S(1)}, u32[]{:S(2)}, u32[]{:S(2)}) collective-permute-start(bf16[384,1536]{1,0:T(8,128)(2,1)S(1)} %collective-permute-done.3.got.near), channel_id=1, source_target_pairs={{0,16},{16,0},{1,17},{17,1},{2,18},{18,2},{3,19},{19,3},{4,20},{20... | collective-permute-start | bytes 3538952 | tf_op jit(solution)/shard_map/ppermute | solution.py:450
  19.6 6.7 %copy-start.3 = (s32[384]{0:T(512)S(1)}, s32[384]{0:T(512)}, u32[]{:S(2)}) copy-start(s32[384]{0:T(512)} %param.20) | copy-start | bytes 4612
  30.1 9.2 %collective-permute-start.4 = (bf16[384,128]{1,0:T(8,128)(2,1)S(1)}, bf16[384,128]{1,0:T(8,128)(2,1)S(1)}, u32[]{:S(2)}, u32[]{:S(2)}) collective-permute-start(bf16[384,128]{1,0:T(8,128)(2,1)S(1)} %get-tuple-element.36), channel_id=1, source_target_pairs={{8,0},{0,8},{4,12},{24,16},{28,20},{20,28},{9,1},{1,9},{5,13},{25,... | collective-permute-start | bytes 294920 | tf_op jit(solution)/shard_map/ppermute | solution.py:53
  34.9 4.5 %collective-permute-start.5 = (bf16[384,128]{1,0:T(8,128)(2,1)S(1)}, bf16[384,128]{1,0:T(8,128)(2,1)S(1)}, u32[]{:S(2)}, u32[]{:S(2)}) collective-permute-start(bf16[384,128]{1,0:T(8,128)(2,1)S(1)} %get-tuple-element.37), channel_id=1, source_target_pairs={{8,4},{4,8},{0,12},{28,16},{24,20},{20,24},{9,5},{5,9},{1,13},{29,... | collective-permute-start | bytes 294920 | tf_op jit(solution)/shard_map/ppermute | solution.py:53
  36.2 6.6 %collective-permute-start.6 = (bf16[384,128]{1,0:T(8,128)(2,1)S(1)}, bf16[384,128]{1,0:T(8,128)(2,1)S(1)}, u32[]{:S(2)}, u32[]{:S(2)}) collective-permute-start(bf16[384,128]{1,0:T(8,128)(2,1)S(1)} %get-tuple-element.38), channel_id=1, source_target_pairs={{4,0},{0,4},{8,12},{20,16},{28,24},{24,28},{5,1},{1,5},{9,13},{21,... | collective-permute-start | bytes 294920 | tf_op jit(solution)/shard_map/ppermute | solution.py:53
  43.1 3.6 %collective-permute-start.12 = (bf16[192,1536]{1,0:T(8,128)(2,1)S(1)}, bf16[192,1536]{1,0:T(8,128)(2,1)S(1)}, u32[]{:S(2)}, u32[]{:S(2)}) collective-permute-start(bf16[192,1536]{1,0:T(8,128)(2,1)S(1)} %gate.1.far), channel_id=1, source_target_pairs={{0,16},{16,0},{1,17},{17,1},{2,18},{18,2},{3,19},{19,3},{4,20},{20... | collective-permute-start | bytes 1769480 | tf_op jit(solution)/shard_map/ppermute | solution.py:450
  43.2 7.0 %collective-permute-start.13 = (bf16[192,384]{1,0:T(8,128)(2,1)S(1)}, bf16[192,384]{1,0:T(8,128)(2,1)S(1)}, u32[]{:S(2)}, u32[]{:S(2)}) collective-permute-start(bf16[192,384]{1,0:T(8,128)(2,1)S(1)} %get-tuple-element.40.after.refs_0_), channel_id=1, source_target_pairs={{0,1},{1,0},{2,3},{3,2},{4,5},{5,4},{6,7},{7,6},{8,9},{9,8},{10,11... | collective-permute-start | bytes 442376 | tf_op jit(solution)/shard_map/ppermute | solution.py:450
  44.5 9.9 %collective-permute-start.14 = (bf16[192,384]{1,0:T(8,128)(2,1)S(1)}, bf16[192,384]{1,0:T(8,128)(2,1)S(1)}, u32[]{:S(2)}, u32[]{:S(2)}) collective-permute-start(bf16[192,384]{1,0:T(8,128)(2,1)S(1)} %get-tuple-element.40.after.refs_0_), channel_id=1, source_target_pairs={{0,2},{1,3},{2,0},{3,1},{4,6},{5,7},{6,4},{7,5},{8,10},{9,11},{10,... | collective-permute-start | bytes 442376 | tf_op jit(solution)/shard_map/ppermute | solution.py:450
  45.4 9.0 %collective-permute-start.15 = (bf16[192,384]{1,0:T(8,128)(2,1)S(1)}, bf16[192,384]{1,0:T(8,128)(2,1)S(1)}, u32[]{:S(2)}, u32[]{:S(2)}) collective-permute-start(bf16[192,384]{1,0:T(8,128)(2,1)S(1)} %get-tuple-element.40.after.refs_0_), channel_id=1, source_target_pairs={{0,3},{1,2},{2,1},{3,0},{4,7},{5,6},{6,5},{7,4},{8,11},{9,10},{10,... | collective-permute-start | bytes 442376 | tf_op jit(solution)/shard_map/ppermute | solution.py:450
  46.7 7.6 %copy-start.1 = (f32[3,4,1536]{2,1,0:T(4,128)S(1)}, f32[3,4,1536]{2,1,0:T(4,128)}, u32[]{:S(2)}) copy-start(f32[3,4,1536]{2,1,0:T(4,128)} %mod.1) | copy-start | bytes 221188
  46.7 11.4 %collective-permute-start.7 = (bf16[192,384]{1,0:T(8,128)(2,1)S(1)}, bf16[192,384]{1,0:T(8,128)(2,1)S(1)}, u32[]{:S(2)}, u32[]{:S(2)}) collective-permute-start(bf16[192,384]{1,0:T(8,128)(2,1)S(1)} %get-tuple-element.39.refs_0_), channel_id=1, source_target_pairs={{0,1},{1,0},{2,3},{3,2},{4,5},{5,4},{6,7},{7,6},{8,9},{9,8},{10,11... | collective-permute-start | bytes 442376 | tf_op jit(solution)/shard_map/ppermute | solution.py:450
  48.0 11.9 %collective-permute-start.8 = (bf16[192,384]{1,0:T(8,128)(2,1)S(1)}, bf16[192,384]{1,0:T(8,128)(2,1)S(1)}, u32[]{:S(2)}, u32[]{:S(2)}) collective-permute-start(bf16[192,384]{1,0:T(8,128)(2,1)S(1)} %get-tuple-element.39.refs_0_), channel_id=1, source_target_pairs={{0,2},{1,3},{2,0},{3,1},{4,6},{5,7},{6,4},{7,5},{8,10},{9,11},{10,... | collective-permute-start | bytes 442376 | tf_op jit(solution)/shard_map/ppermute | solution.py:450
  50.2 9.7 %collective-permute-start.9 = (bf16[192,384]{1,0:T(8,128)(2,1)S(1)}, bf16[192,384]{1,0:T(8,128)(2,1)S(1)}, u32[]{:S(2)}, u32[]{:S(2)}) collective-permute-start(bf16[192,384]{1,0:T(8,128)(2,1)S(1)} %get-tuple-element.39.refs_0_), channel_id=1, source_target_pairs={{0,3},{1,2},{2,1},{3,0},{4,7},{5,6},{6,5},{7,4},{8,11},{9,10},{10,... | collective-permute-start | bytes 442376 | tf_op jit(solution)/shard_map/ppermute | solution.py:450
  58.1 4.6 %copy-start.2 = (f32[3]{0:T(128)S(1)}, f32[3]{0:T(128)}, u32[]{:S(2)}) copy-start(f32[3]{0:T(128)} %scale_ref.1) | copy-start | bytes 40
  58.1 4.6 %collective-permute-start.16 = (bf16[192,1536]{1,0:T(8,128)(2,1)S(1)}, bf16[192,1536]{1,0:T(8,128)(2,1)S(1)}, u32[]{:S(2)}, u32[]{:S(2)}) collective-permute-start(bf16[192,1536]{1,0:T(8,128)(2,1)S(1)} %feed.3), channel_id=1, source_target_pairs={{0,16},{16,0},{1,17},{17,1},{2,18},{18,2},{3,19},{19,3},{4,20},{20... | collective-permute-start | bytes 1769480 | tf_op jit(solution)/shard_map/ppermute | solution.py:450
  64.6 6.5 %collective-permute-start.17 = (bf16[192,384]{1,0:T(8,128)(2,1)S(1)}, bf16[192,384]{1,0:T(8,128)(2,1)S(1)}, u32[]{:S(2)}, u32[]{:S(2)}) collective-permute-start(bf16[192,384]{1,0:T(8,128)(2,1)S(1)} %get-tuple-element.44), channel_id=1, source_target_pairs={{0,1},{1,0},{2,3},{3,2},{4,5},{5,4},{6,7},{7,6},{8,9},{9,8},{10,11... | collective-permute-start | bytes 442376 | tf_op jit(solution)/shard_map/ppermute | solution.py:450
  65.5 8.3 %collective-permute-start.18 = (bf16[192,384]{1,0:T(8,128)(2,1)S(1)}, bf16[192,384]{1,0:T(8,128)(2,1)S(1)}, u32[]{:S(2)}, u32[]{:S(2)}) collective-permute-start(bf16[192,384]{1,0:T(8,128)(2,1)S(1)} %get-tuple-element.45), channel_id=1, source_target_pairs={{0,2},{1,3},{2,0},{3,1},{4,6},{5,7},{6,4},{7,5},{8,10},{9,11},{10,... | collective-permute-start | bytes 442376 | tf_op jit(solution)/shard_map/ppermute | solution.py:450
  66.5 7.3 %collective-permute-start.19 = (bf16[192,384]{1,0:T(8,128)(2,1)S(1)}, bf16[192,384]{1,0:T(8,128)(2,1)S(1)}, u32[]{:S(2)}, u32[]{:S(2)}) collective-permute-start(bf16[192,384]{1,0:T(8,128)(2,1)S(1)} %get-tuple-element.46), channel_id=1, source_target_pairs={{0,3},{1,2},{2,1},{3,0},{4,7},{5,6},{6,5},{7,4},{8,11},{9,10},{10,... | collective-permute-start | bytes 442376 | tf_op jit(solution)/shard_map/ppermute | solution.py:450
  74.1 7.6 %collective-permute-start.20 = (bf16[96,384]{1,0:T(8,128)(2,1)S(1)}, bf16[96,384]{1,0:T(8,128)(2,1)S(1)}, u32[]{:S(2)}, u32[]{:S(2)}) collective-permute-start(bf16[96,384]{1,0:T(8,128)(2,1)S(1)} %get-tuple-element.48), channel_id=1, source_target_pairs={{0,8},{4,12},{8,0},{12,4},{1,9},{5,13},{9,1},{13,5},{2,10},{6,14},... | collective-permute-start | bytes 221192 | tf_op jit(solution)/shard_map/ppermute | solution.py:450
  75.0 6.7 %collective-permute-start.21 = (bf16[96,384]{1,0:T(8,128)(2,1)S(1)}, bf16[96,384]{1,0:T(8,128)(2,1)S(1)}, u32[]{:S(2)}, u32[]{:S(2)}) collective-permute-start(bf16[96,384]{1,0:T(8,128)(2,1)S(1)} %get-tuple-element.49), channel_id=1, source_target_pairs={{0,12},{4,8},{8,4},{12,0},{1,13},{5,9},{9,5},{13,1},{2,14},{6,10},... | collective-permute-start | bytes 221192 | tf_op jit(solution)/shard_map/ppermute | solution.py:450
  77.4 4.9 %collective-permute-start.22 = (bf16[96,384]{1,0:T(8,128)(2,1)S(1)}, bf16[96,384]{1,0:T(8,128)(2,1)S(1)}, u32[]{:S(2)}, u32[]{:S(2)}) collective-permute-start(bf16[96,384]{1,0:T(8,128)(2,1)S(1)} %get-tuple-element.50), channel_id=1, source_target_pairs={{0,4},{4,0},{8,12},{12,8},{1,5},{5,1},{9,13},{13,9},{2,6},{6,2},{1... | collective-permute-start | bytes 221192 | tf_op jit(solution)/shard_map/ppermute | solution.py:450

commit v6 on v5

--- a/solution.py
+++ b/solution.py
@@ -78,52 +78,60 @@
 
 
 def attend_kernel(*refs):
-    blocks, outs, (q_aug, k_aug, v_aug, clips) = refs[:4], refs[-8:-4], refs[-4:]
+    blocks, outs, (q_aug, k_aug, v_aug, wide, found) = refs[:4], refs[-9:-5], refs[-5:]
     slots = outs[0].shape[0]
-    lane = lax.broadcasted_iota(jnp.int32, (128, 128), 1)
-    row = lax.broadcasted_iota(jnp.int32, (128, 128), 0)
-    eye = (lane == row).astype(BF16)
+    count = slots // CLIPS
+    group = 4 * count
+    lane = lax.broadcasted_iota(jnp.int32, (count, 128), 1)
+    row = lax.broadcasted_iota(jnp.int32, (count, 128), 0)
+    q_tail = jnp.where(lane == 0, -FAR, 0.0).astype(BF16)
+    v_tail = (lane == 0).astype(BF16)
+    fills, bases = [], []
     for index, block in enumerate(blocks):
-        base = index * slots
-        here = slice(base, base + slots)
-        q_aug[here, :128] = block[:slots, :]
-        k_aug[here, :128] = block[slots : 2 * slots, :]
-        v_aug[here, :128] = block[2 * slots : 3 * slots, :]
-        turned = lax.dot_general(
-            eye, block[3 * slots :, :], (((1,), (1,)), ((), ())), preferred_element_type=F32
+        numbers = block[3 * slots :, :].astype(F32)
+        line = lax.broadcasted_iota(jnp.int32, numbers.shape, 0)
+        spot = lax.broadcasted_iota(jnp.int32, numbers.shape, 1)
+        live = (line < slots // 128) & (numbers < CLIPS - 0.5)
+        filled = jnp.sum(live.astype(F32)).astype(jnp.int32)
+        first = jnp.sum(jnp.where((line == 0) & (spot == 0), numbers, 0.0)).astype(jnp.int32)
+        fills.append(filled)
+        wide[index, :, :] = block[: 3 * slots, :].astype(F32)
+        for turn in range(CLIPS):
+            clip = lax.rem(first + turn, CLIPS)
+            base = pl.multiple_of((clip * 4 + index) * count, count)
+            bases.append(base)
+            here = pl.ds(base, count)
+            for part, target in enumerate((q_aug, k_aug, v_aug)):
+                rows = pl.ds(part * slots + turn, count, stride=CLIPS)
+                target[here, :128] = wide[index, rows, :].astype(BF16)
+            padding = (lane == 0) & (CLIPS * row + turn >= filled)
+            q_aug[here, 128:] = q_tail
+            k_aug[here, 128:] = padding.astype(BF16)
+            v_aug[here, 128:] = v_tail
+    scale = math.log2(math.e) / math.sqrt(HEAD_DIM)
+
+    def score(clip):
+        here = slice(clip * group, (clip + 1) * group)
+        return lax.dot_general(
+            q_aug[here, :], k_aug[here, :], (((1,), (1,)), ((), ())), preferred_element_type=F32
         )
-        for group in range(slots // 128):
-            part = slice(base + group * 128, base + (group + 1) * 128)
-            clip = jnp.broadcast_to(turned[:, group : group + 1], (128, 128)).astype(jnp.int32)
-            clips[part, :] = clip
-            same = lane == clip
-            kept = same & (clip < CLIPS)
-            k_aug[part, 128:] = same.astype(BF16)
-            q_aug[part, 128:] = jnp.where(kept | (lane > CLIPS), 0.0, -FAR).astype(BF16)
-            v_aug[part, 128:] = (lane == 0).astype(BF16)
-    scale = math.log2(math.e) / math.sqrt(HEAD_DIM)
-    rows = 384
-
-    def score(first):
-        return lax.dot_general(
-            q_aug[first : first + rows, :],
-            k_aug[...],
-            (((1,), (1,)), ((), ())),
-            preferred_element_type=F32,
-        )
-
-    firsts = range(0, 4 * slots, rows)
+
     ahead = score(0)
-    for first in firsts:
+    for clip in range(CLIPS):
         scores = ahead
-        if first + rows < 4 * slots:
-            ahead = score(first + rows)
+        if clip + 1 < CLIPS:
+            ahead = score(clip + 1)
+        here = slice(clip * group, (clip + 1) * group)
         peak = jnp.max(scores, axis=1, keepdims=True)
         probs = jnp.exp2((scores - peak) * scale).astype(BF16)
-        summed = jnp.dot(probs, v_aug[...], preferred_element_type=F32)
-        result = summed[:, :128] / summed[:, 128:129]
-        result = jnp.where(clips[first : first + rows, :] < CLIPS, result, 0.0).astype(BF16)
-        outs[first // slots][first % slots : first % slots + rows, :] = result
+        summed = jnp.dot(probs, v_aug[here, :], preferred_element_type=F32)
+        found[here, :] = summed[:, :128] / summed[:, 128:129]
+    line = lax.broadcasted_iota(jnp.int32, (slots, 128), 0)
+    for index, out in enumerate(outs):
+        for turn in range(CLIPS):
+            base = bases[index * CLIPS + turn]
+            wide[index, pl.ds(turn, count, stride=CLIPS), :] = found[pl.ds(base, count), :]
+        out[...] = jnp.where(line < fills[index], wide[index, :slots, :], 0.0).astype(BF16)
 
 
 def regroup_kernel(own, back1, back2, back3, first, second):
@@ -169,6 +177,7 @@
         out_specs=[VMEM] * 3,
         scratch_shapes=[pltpu.SemaphoreType.DMA((3,))],
         compiler_params=params(16),
+        cost_estimate=cost(2**34, 2**24),
         name="load",
     )(*(afar(array) for array in arrays), after)
 
@@ -275,7 +284,7 @@
         in_specs=[VMEM] * 4 + [ANY] * (len(early) - 3) + [VMEM] * 3,
         out_specs=[VMEM] * 4,
         scratch_shapes=[pltpu.VMEM((4 * slots, 256), BF16)] * 3
-        + [pltpu.VMEM((4 * slots, 128), jnp.int32)],
+        + [pltpu.VMEM((4, 3 * slots, 128), F32), pltpu.VMEM((4 * slots, 128), F32)],
         compiler_params=params(28),
         cost_estimate=cost(2**32, 2**21),
         name="attend",

time: 83.4 us -> 81.6 us (0.978)
  Pallas kernels: 20.4 us -> 18.6 us
  waiting for transfers between devices: 23.3 us -> 24.5 us
    ppermute x6, waiting for transfers between devices: 6.01 us -> 9.85 us  [hop(): return lax.ppermute(value, ('cfg', 'seq'), pairs)]
    ppermute x2, waiting for transfers between devices: 2.65 us -> 0.01 us  [across(): return lax.ppermute(value, ('cfg', 'blk'), pairs)]
    pallas_call x1, Pallas kernels: 3.66 us -> 2.09 us  [attention_by_head(): pl.pallas_call(attend_kernel, out_shape=[shape_of((slots, 128))] * 4, in_...]
  transfers between devices with their start and end apart: 23 -> 23, of which waited for: 9 -> 8; matrix products, arithmetic and copies ran while one was open for 1% -> 1% of each run, Pallas kernels for 21% -> 19%
where the time goes in v6:
time: 81.6 us; the launch traced here: 81.3 us
  starting transfers between devices  37.3 us (46%)
  waiting for transfers between devices  24.5 us (30%)
  Pallas kernels  18.6 us (23%)
    ppermute x6, starting transfers between devices, hop(): return lax.ppermute(value, ('cfg', 'seq'), pairs)  18.4 us
    ppermute x15, waiting for transfers between devices, exchanged(): return lax.ppermute(value, axis, pairs)  14.7 us
    ppermute x15, starting transfers between devices, exchanged(): return lax.ppermute(value, axis, pairs)  14.4 us
    ppermute x6, waiting for transfers between devices, hop(): return lax.ppermute(value, ('cfg', 'seq'), pairs)  9.85 us
    pallas_call x2, Pallas kernels, feed(): pl.pallas_call(functools.partial(feed_kernel, turn), out_shape=out_shape,...  6.56 us
    ppermute x2, starting transfers between devices, across(): return lax.ppermute(value, ('cfg', 'blk'), pairs)  4.52 us
    pallas_call x1, Pallas kernels, load(): pl.pallas_call(load_kernel, out_shape=[pltpu.VMEM(array.shape, BF16) for...  4.07 us
    pallas_call x1, Pallas kernels, attention_by_head(): pl.pallas_call(attend_kernel, out_shape=[shape_of((slots, 128))] * 4, in_...  2.09 us
  transfers between devices with their start and end apart: 23, of which 8 were waited for; matrix products, arithmetic and copies ran while one was open for 1% of the time, Pallas kernels for 19%

profile of v6, /device:TPU:0, one launch (start us, length us, event | category | flops | bytes accessed | tf_op | source)
XLA Modules:
  0.0 81.3 jit_solution(15179460426800558631)
XLA Ops:
  0.0 2.9 %collective-permute-start.3 = (bf16[384,1536]{1,0:T(8,128)(2,1)}, bf16[384,1536]{1,0:T(8,128)(2,1)S(1)}, u32[]{:S(2)}, u32[]{:S(2)}) collective-permute-start(bf16[384,1536]{1,0:T(8,128)(2,1)} %own.1), channel_id=1, source_target_pairs={{0,1},{1,0},{2,3},{3,2},{16,18},{17,19},{18,16},{19,17},{4,5},{5,4... | collective-permute-start | bytes 3538952 | tf_op jit(solution)/shard_map/ppermute | solution.py:189
  2.9 1.5 %pack.1 = (bf16[1168,128]{1,0:T(8,128)(2,1)S(1)}, bf16[1168,128]{1,0:T(8,128)(2,1)S(1)}, bf16[1168,128]{1,0:T(8,128)(2,1)S(1)}, bf16[1168,128]{1,0:T(8,128)(2,1)S(1)}) custom-call(bf16[384,384]{1,0:T(8,128)(2,1)} %bitcast.7, bf16[384,384]{1,0:T(8,128)(2,1)} %bitcast.8, bf16[384,384]{1,0:T(8,128)(2,1)} %bitcast.9, s32[3,128]{1,0:T(4,128)} %bitcast.12), custom_call_target="tpu_custom_call" | custom-call | tf_op jit(solution)/shard_map/pack/pallas_call | solution.py:267
  4.4 4.5 %collective-permute-start = (bf16[1168,128]{1,0:T(8,128)(2,1)S(1)}, bf16[1168,128]{1,0:T(8,128)(2,1)S(1)}, u32[]{:S(2)}, u32[]{:S(2)}) collective-permute-start(bf16[1168,128]{1,0:T(8,128)(2,1)S(1)} %get-tuple-element.29), channel_id=1, source_target_pairs={{0,8},{8,0},{12,4},{16,24},{20,28},{28,20},{1,9},{9,1},{13,5},{17,... | collective-permute-start | bytes 897032 | tf_op jit(solution)/shard_map/ppermute | solution.py:53
  8.9 1.3 %collective-permute-start.1 = (bf16[1168,128]{1,0:T(8,128)(2,1)S(1)}, bf16[1168,128]{1,0:T(8,128)(2,1)S(1)}, u32[]{:S(2)}, u32[]{:S(2)}) collective-permute-start(bf16[1168,128]{1,0:T(8,128)(2,1)S(1)} %get-tuple-element.30), channel_id=1, source_target_pairs={{4,8},{8,4},{12,0},{16,28},{20,24},{24,20},{5,9},{9,5},{13,1},{17,... | collective-permute-start | bytes 897032 | tf_op jit(solution)/shard_map/ppermute | solution.py:53
  10.2 3.4 %collective-permute-start.2 = (bf16[1168,128]{1,0:T(8,128)(2,1)S(1)}, bf16[1168,128]{1,0:T(8,128)(2,1)S(1)}, u32[]{:S(2)}, u32[]{:S(2)}) collective-permute-start(bf16[1168,128]{1,0:T(8,128)(2,1)S(1)} %get-tuple-element.31), channel_id=1, source_target_pairs={{0,4},{4,0},{12,8},{16,20},{24,28},{28,24},{1,5},{5,1},{13,9},{17,... | collective-permute-start | bytes 897032 | tf_op jit(solution)/shard_map/ppermute | solution.py:53
  13.7 0.1 constant_dynamic-slice_fusion
  13.7 0.2 convert_reduce_fusion
  13.9 0.0 copy-start.3
  13.9 4.1 %load.1 = (bf16[1536,1536]{1,0:T(8,128)(2,1)S(1)}, bf16[1536,1536]{1,0:T(8,128)(2,1)S(1)}, bf16[384,1536]{1,0:T(8,128)(2,1)S(1)}) custom-call(bf16[1536,1536]{1,0:T(8,128)(2,1)} %refs_0_.1, bf16[1536,1536]{1,0:T(8,128)(2,1)} %refs_1_.1, bf16[384,1536]{1,0:T(8,128)(2,1)} %bitcast.13, bf16[1168,128]{1,0:T(8,128)(2,1)S(1)} %get-tuple-element.28.refs_3_.refs_0_), custom_call_target="tpu_custom_call" | custom-call | flops 17179869184 | bytes 16777216 | tf_op jit(solution)/shard_map/load/pallas_call | solution.py:173
  18.0 0.1 compare_select_fusion
  18.1 0.1 cut.1.refs_6_
  18.2 1.6 %collective-permute-start.11 = (bf16[192,1536]{1,0:T(8,128)(2,1)S(1)}, bf16[192,1536]{1,0:T(8,128)(2,1)S(1)}, u32[]{:S(2)}, u32[]{:S(2)}) collective-permute-start(bf16[192,1536]{1,0:T(8,128)(2,1)S(1)} %cut.1.refs_6_), channel_id=1, source_target_pairs={{0,2},{1,3},{2,0},{3,1},{16,17},{17,16},{18,19},{19,18},{4,6},{5,7... | collective-permute-start | bytes 1769480 | tf_op jit(solution)/shard_map/ppermute | solution.py:189
  19.8 0.0 collective-permute-start.10
  19.9 6.4 %collective-permute-done.refs_1_ = bf16[1168,128]{1,0:T(8,128)(2,1)S(1)} collective-permute-done((bf16[1168,128]{1,0:T(8,128)(2,1)S(1)}, bf16[1168,128]{1,0:T(8,128)(2,1)S(1)}, u32[]{:S(2)}, u32[]{:S(2)}) %collective-permute-start) | collective-permute-done | bytes 299040 | tf_op jit(solution)/shard_map/ppermute | solution.py:53
  26.3 0.1 broadcast_in_dim.7.refs_4_.refs_9_.clip_ref
  26.4 2.1 %attend.1 = (bf16[384,128]{1,0:T(8,128)(2,1)S(1)}, bf16[384,128]{1,0:T(8,128)(2,1)S(1)}, bf16[384,128]{1,0:T(8,128)(2,1)S(1)}, bf16[384,128]{1,0:T(8,128)(2,1)S(1)}) custom-call(bf16[1168,128]{1,0:T(8,128)(2,1)S(1)} %get-tuple-element.28.refs_3_.refs_0_, bf16[1168,128]{1,0:T(8,128)(2,1)S(1)} %collective-permute-done.refs_1_, ...), custom_call_target="tpu_custom_call" | custom-call | flops 4294967296 | bytes 2097152 | tf_op jit(solution)/shard_map/attend/pallas_call | solution.py:281
  28.5 4.8 %collective-permute-start.4 = (bf16[384,128]{1,0:T(8,128)(2,1)S(1)}, bf16[384,128]{1,0:T(8,128)(2,1)S(1)}, u32[]{:S(2)}, u32[]{:S(2)}) collective-permute-start(bf16[384,128]{1,0:T(8,128)(2,1)S(1)} %get-tuple-element.36), channel_id=1, source_target_pairs={{8,0},{0,8},{4,12},{24,16},{28,20},{20,28},{9,1},{1,9},{5,13},{25,... | collective-permute-start | bytes 294920 | tf_op jit(solution)/shard_map/ppermute | solution.py:53
  33.3 1.3 %collective-permute-start.5 = (bf16[384,128]{1,0:T(8,128)(2,1)S(1)}, bf16[384,128]{1,0:T(8,128)(2,1)S(1)}, u32[]{:S(2)}, u32[]{:S(2)}) collective-permute-start(bf16[384,128]{1,0:T(8,128)(2,1)S(1)} %get-tuple-element.37), channel_id=1, source_target_pairs={{8,4},{4,8},{0,12},{28,16},{24,20},{20,24},{9,5},{5,9},{1,13},{29,... | collective-permute-start | bytes 294920 | tf_op jit(solution)/shard_map/ppermute | solution.py:53
  34.6 3.2 %collective-permute-start.6 = (bf16[384,128]{1,0:T(8,128)(2,1)S(1)}, bf16[384,128]{1,0:T(8,128)(2,1)S(1)}, u32[]{:S(2)}, u32[]{:S(2)}) collective-permute-start(bf16[384,128]{1,0:T(8,128)(2,1)S(1)} %get-tuple-element.38), channel_id=1, source_target_pairs={{4,0},{0,4},{8,12},{20,16},{28,24},{24,28},{5,1},{1,5},{9,13},{21,... | collective-permute-start | bytes 294920 | tf_op jit(solution)/shard_map/ppermute | solution.py:53
  37.8 3.4 %collective-permute-done.6.back3 = bf16[384,128]{1,0:T(8,128)(2,1)S(1)} collective-permute-done((bf16[384,128]{1,0:T(8,128)(2,1)S(1)}, bf16[384,128]{1,0:T(8,128)(2,1)S(1)}, u32[]{:S(2)}, u32[]{:S(2)}) %collective-permute-start.6) | collective-permute-done | bytes 98336 | tf_op jit(solution)/shard_map/ppermute | solution.py:53
  41.2 0.1 regroup.1
  41.3 0.1 collective-permute-start.12
  41.4 1.3 %collective-permute-start.13 = (bf16[192,384]{1,0:T(8,128)(2,1)S(1)}, bf16[192,384]{1,0:T(8,128)(2,1)S(1)}, u32[]{:S(2)}, u32[]{:S(2)}) collective-permute-start(bf16[192,384]{1,0:T(8,128)(2,1)S(1)} %get-tuple-element.40.after.refs_0_), channel_id=1, source_target_pairs={{0,1},{1,0},{2,3},{3,2},{4,5},{5,4},{6,7},{7,6},{8,9},{9,8},{10,11... | collective-permute-start | bytes 442376 | tf_op jit(solution)/shard_map/ppermute | solution.py:459
  42.7 0.9 %collective-permute-start.14 = (bf16[192,384]{1,0:T(8,128)(2,1)S(1)}, bf16[192,384]{1,0:T(8,128)(2,1)S(1)}, u32[]{:S(2)}, u32[]{:S(2)}) collective-permute-start(bf16[192,384]{1,0:T(8,128)(2,1)S(1)} %get-tuple-element.40.after.refs_0_), channel_id=1, source_target_pairs={{0,2},{1,3},{2,0},{3,1},{4,6},{5,7},{6,4},{7,5},{8,10},{9,11},{10,... | collective-permute-start | bytes 442376 | tf_op jit(solution)/shard_map/ppermute | solution.py:459
  43.6 1.3 %collective-permute-start.15 = (bf16[192,384]{1,0:T(8,128)(2,1)S(1)}, bf16[192,384]{1,0:T(8,128)(2,1)S(1)}, u32[]{:S(2)}, u32[]{:S(2)}) collective-permute-start(bf16[192,384]{1,0:T(8,128)(2,1)S(1)} %get-tuple-element.40.after.refs_0_), channel_id=1, source_target_pairs={{0,3},{1,2},{2,1},{3,0},{4,7},{5,6},{6,5},{7,4},{8,11},{9,10},{10,... | collective-permute-start | bytes 442376 | tf_op jit(solution)/shard_map/ppermute | solution.py:459
  45.0 1.2 %collective-permute-start.7 = (bf16[192,384]{1,0:T(8,128)(2,1)S(1)}, bf16[192,384]{1,0:T(8,128)(2,1)S(1)}, u32[]{:S(2)}, u32[]{:S(2)}) collective-permute-start(bf16[192,384]{1,0:T(8,128)(2,1)S(1)} %get-tuple-element.39.refs_0_), channel_id=1, source_target_pairs={{0,1},{1,0},{2,3},{3,2},{4,5},{5,4},{6,7},{7,6},{8,9},{9,8},{10,11... | collective-permute-start | bytes 442376 | tf_op jit(solution)/shard_map/ppermute | solution.py:459
  46.2 0.9 %collective-permute-start.8 = (bf16[192,384]{1,0:T(8,128)(2,1)S(1)}, bf16[192,384]{1,0:T(8,128)(2,1)S(1)}, u32[]{:S(2)}, u32[]{:S(2)}) collective-permute-start(bf16[192,384]{1,0:T(8,128)(2,1)S(1)} %get-tuple-element.39.refs_0_), channel_id=1, source_target_pairs={{0,2},{1,3},{2,0},{3,1},{4,6},{5,7},{6,4},{7,5},{8,10},{9,11},{10,... | collective-permute-start | bytes 442376 | tf_op jit(solution)/shard_map/ppermute | solution.py:459
  47.1 1.3 %join.1.refs_4_ = bf16[1536,1536]{1,0:T(8,128)(2,1)S(1)} custom-call(bf16[384,1536]{1,0:T(8,128)(2,1)} %own.1, bf16[384,1536]{1,0:T(8,128)(2,1)S(1)} %collective-permute-done.3.got.near, bf16[384,1536]{1,0:T(8,128)(2,1)S(1)} %collective-permute-done.10.near_swap, bf16[192,1536]{1,0:T(8,128)(2,1)S(1)} %gate.1.far, ...), custom_call_target="tpu_custom_call" | custom-call | tf_op jit(solution)/shard_map/join/pallas_call | solution.py:254
  48.5 1.4 %collective-permute-start.9 = (bf16[192,384]{1,0:T(8,128)(2,1)S(1)}, bf16[192,384]{1,0:T(8,128)(2,1)S(1)}, u32[]{:S(2)}, u32[]{:S(2)}) collective-permute-start(bf16[192,384]{1,0:T(8,128)(2,1)S(1)} %get-tuple-element.39.refs_0_), channel_id=1, source_target_pairs={{0,3},{1,2},{2,1},{3,0},{4,7},{5,6},{6,5},{7,4},{8,11},{9,10},{10,... | collective-permute-start | bytes 442376 | tf_op jit(solution)/shard_map/ppermute | solution.py:459
  49.9 2.7 %collective-permute-done.14.refs_2_ = bf16[192,384]{1,0:T(8,128)(2,1)S(1)} collective-permute-done((bf16[192,384]{1,0:T(8,128)(2,1)S(1)}, bf16[192,384]{1,0:T(8,128)(2,1)S(1)}, u32[]{:S(2)}, u32[]{:S(2)}) %collective-permute-start.14) | collective-permute-done | bytes 147488 | tf_op jit(solution)/shard_map/ppermute | solution.py:459
  52.6 3.7 %feed.3 = bf16[192,1536]{1,0:T(8,128)(2,1)S(1)} custom-call(bf16[192,384]{1,0:T(8,128)(2,1)S(1)} %get-tuple-element.40.after.refs_0_, bf16[192,384]{1,0:T(8,128)(2,1)S(1)} %collective-permute-done.13.refs_1_, bf16[192,384]{1,0:T(8,128)(2,1)S(1)} %collective-permute-done.14.refs_2_, bf16[192,384]{1,0:T(8,128)(2,1)S(1)} %collective-permute-done.15.refs_3_, ...), custom_call_target="tpu_custom_call" | custom-call | flops 68719476736 | bytes 16777216 | tf_op jit(solution)/shard_map/feed/pallas_call | solution.py:407
  56.3 0.0 copy-start.2
  56.3 0.1 collective-permute-start.16
  56.4 1.7 %collective-permute-done.8.refs_2_ = bf16[192,384]{1,0:T(8,128)(2,1)S(1)} collective-permute-done((bf16[192,384]{1,0:T(8,128)(2,1)S(1)}, bf16[192,384]{1,0:T(8,128)(2,1)S(1)}, u32[]{:S(2)}, u32[]{:S(2)}) %collective-permute-start.8) | collective-permute-done | bytes 147488 | tf_op jit(solution)/shard_map/ppermute | solution.py:459
  58.1 2.8 %feed.2 = (bf16[192,1536]{1,0:T(8,128)(2,1)S(1)}, f32[192,1536]{1,0:T(8,128)S(1)}) custom-call(bf16[192,384]{1,0:T(8,128)(2,1)S(1)} %get-tuple-element.39.refs_0_, bf16[192,384]{1,0:T(8,128)(2,1)S(1)} %collective-permute-done.7.refs_1_, bf16[192,384]{1,0:T(8,128)(2,1)S(1)} %collective-permute-done.8.refs_2_, ...), custom_call_target="tpu_custom_call" | custom-call | flops 68719476736 | bytes 16777216 | tf_op jit(solution)/shard_map/feed/pallas_call | solution.py:407
  61.0 1.9 %guide.1 = (f32[192,384]{1,0:T(8,128)S(1)}, bf16[192,384]{1,0:T(8,128)(2,1)S(1)}, bf16[192,384]{1,0:T(8,128)(2,1)S(1)}, bf16[192,384]{1,0:T(8,128)(2,1)S(1)}) custom-call(bf16[192,1536]{1,0:T(8,128)(2,1)S(1)} %get-tuple-element.41.hidden, f32[192,1536]{1,0:T(8,128)S(1)} %get-tuple-element.42.mixed, ...), custom_call_target="tpu_custom_call" | custom-call | tf_op jit(solution)/shard_map/guide/pallas_call | solution.py:507
  62.8 0.8 %collective-permute-start.17 = (bf16[192,384]{1,0:T(8,128)(2,1)S(1)}, bf16[192,384]{1,0:T(8,128)(2,1)S(1)}, u32[]{:S(2)}, u32[]{:S(2)}) collective-permute-start(bf16[192,384]{1,0:T(8,128)(2,1)S(1)} %get-tuple-element.44), channel_id=1, source_target_pairs={{0,1},{1,0},{2,3},{3,2},{4,5},{5,4},{6,7},{7,6},{8,9},{9,8},{10,11... | collective-permute-start | bytes 442376 | tf_op jit(solution)/shard_map/ppermute | solution.py:459
  63.7 1.0 %collective-permute-start.18 = (bf16[192,384]{1,0:T(8,128)(2,1)S(1)}, bf16[192,384]{1,0:T(8,128)(2,1)S(1)}, u32[]{:S(2)}, u32[]{:S(2)}) collective-permute-start(bf16[192,384]{1,0:T(8,128)(2,1)S(1)} %get-tuple-element.45), channel_id=1, source_target_pairs={{0,2},{1,3},{2,0},{3,1},{4,6},{5,7},{6,4},{7,5},{8,10},{9,11},{10,... | collective-permute-start | bytes 442376 | tf_op jit(solution)/shard_map/ppermute | solution.py:459
  64.7 1.7 %collective-permute-start.19 = (bf16[192,384]{1,0:T(8,128)(2,1)S(1)}, bf16[192,384]{1,0:T(8,128)(2,1)S(1)}, u32[]{:S(2)}, u32[]{:S(2)}) collective-permute-start(bf16[192,384]{1,0:T(8,128)(2,1)S(1)} %get-tuple-element.46), channel_id=1, source_target_pairs={{0,3},{1,2},{2,1},{3,0},{4,7},{5,6},{6,5},{7,4},{8,11},{9,10},{10,... | collective-permute-start | bytes 442376 | tf_op jit(solution)/shard_map/ppermute | solution.py:459
  66.4 2.9 %collective-permute-done.17.got1 = bf16[192,384]{1,0:T(8,128)(2,1)S(1)} collective-permute-done((bf16[192,384]{1,0:T(8,128)(2,1)S(1)}, bf16[192,384]{1,0:T(8,128)(2,1)S(1)}, u32[]{:S(2)}, u32[]{:S(2)}) %collective-permute-start.17) | collective-permute-done | bytes 147488 | tf_op jit(solution)/shard_map/ppermute | solution.py:459
  69.3 2.7 %collective-permute-done.18.got2 = bf16[192,384]{1,0:T(8,128)(2,1)S(1)} collective-permute-done((bf16[192,384]{1,0:T(8,128)(2,1)S(1)}, bf16[192,384]{1,0:T(8,128)(2,1)S(1)}, u32[]{:S(2)}, u32[]{:S(2)}) %collective-permute-start.18) | collective-permute-done | bytes 147488 | tf_op jit(solution)/shard_map/ppermute | solution.py:459
  72.0 0.3 place.1
  72.3 0.9 %collective-permute-start.20 = (bf16[96,384]{1,0:T(8,128)(2,1)S(1)}, bf16[96,384]{1,0:T(8,128)(2,1)S(1)}, u32[]{:S(2)}, u32[]{:S(2)}) collective-permute-start(bf16[96,384]{1,0:T(8,128)(2,1)S(1)} %get-tuple-element.48), channel_id=1, source_target_pairs={{0,8},{4,12},{8,0},{12,4},{1,9},{5,13},{9,1},{13,5},{2,10},{6,14},... | collective-permute-start | bytes 221192 | tf_op jit(solution)/shard_map/ppermute | solution.py:459
  73.2 2.4 %collective-permute-start.21 = (bf16[96,384]{1,0:T(8,128)(2,1)S(1)}, bf16[96,384]{1,0:T(8,128)(2,1)S(1)}, u32[]{:S(2)}, u32[]{:S(2)}) collective-permute-start(bf16[96,384]{1,0:T(8,128)(2,1)S(1)} %get-tuple-element.49), channel_id=1, source_target_pairs={{0,12},{4,8},{8,4},{12,0},{1,13},{5,9},{9,5},{13,1},{2,14},{6,10},... | collective-permute-start | bytes 221192 | tf_op jit(solution)/shard_map/ppermute | solution.py:459
  75.6 0.2 collective-permute-start.22
  75.9 4.0 %collective-permute-done.20.refs_1_ = bf16[96,384]{1,0:T(8,128)(2,1)S(1)} collective-permute-done((bf16[96,384]{1,0:T(8,128)(2,1)S(1)}, bf16[96,384]{1,0:T(8,128)(2,1)S(1)}, u32[]{:S(2)}, u32[]{:S(2)}) %collective-permute-start.20) | collective-permute-done | bytes 73760 | tf_op jit(solution)/shard_map/ppermute | solution.py:459
  79.9 0.6 collective-permute-done.22.refs_3_
  80.5 0.8 arrange.1
  (23 shorter events, 0.1 us)
Async XLA Ops:
  0.0 13.6 %copy-start = (s32[384,1]{0,1:T(1,128)S(1)}, s32[384,1]{0,1:T(1,128)}, u32[]{:S(2)}) copy-start(s32[384,1]{0,1:T(1,128)} %param.21) | copy-start | bytes 4612
  0.0 18.1 %collective-permute-start.3 = (bf16[384,1536]{1,0:T(8,128)(2,1)}, bf16[384,1536]{1,0:T(8,128)(2,1)S(1)}, u32[]{:S(2)}, u32[]{:S(2)}) collective-permute-start(bf16[384,1536]{1,0:T(8,128)(2,1)} %own.1), channel_id=1, source_target_pairs={{0,1},{1,0},{2,3},{3,2},{16,18},{17,19},{18,16},{19,17},{4,5},{5,4... | collective-permute-start | bytes 3538952 | tf_op jit(solution)/shard_map/ppermute | solution.py:189
  4.4 21.9 %collective-permute-start = (bf16[1168,128]{1,0:T(8,128)(2,1)S(1)}, bf16[1168,128]{1,0:T(8,128)(2,1)S(1)}, u32[]{:S(2)}, u32[]{:S(2)}) collective-permute-start(bf16[1168,128]{1,0:T(8,128)(2,1)S(1)} %get-tuple-element.29), channel_id=1, source_target_pairs={{0,8},{8,0},{12,4},{16,24},{20,28},{28,20},{1,9},{9,1},{13,5},{17,... | collective-permute-start | bytes 897032 | tf_op jit(solution)/shard_map/ppermute | solution.py:53
  8.9 17.4 %collective-permute-start.1 = (bf16[1168,128]{1,0:T(8,128)(2,1)S(1)}, bf16[1168,128]{1,0:T(8,128)(2,1)S(1)}, u32[]{:S(2)}, u32[]{:S(2)}) collective-permute-start(bf16[1168,128]{1,0:T(8,128)(2,1)S(1)} %get-tuple-element.30), channel_id=1, source_target_pairs={{4,8},{8,4},{12,0},{16,28},{20,24},{24,20},{5,9},{9,5},{13,1},{17,... | collective-permute-start | bytes 897032 | tf_op jit(solution)/shard_map/ppermute | solution.py:53
  10.2 16.1 %collective-permute-start.2 = (bf16[1168,128]{1,0:T(8,128)(2,1)S(1)}, bf16[1168,128]{1,0:T(8,128)(2,1)S(1)}, u32[]{:S(2)}, u32[]{:S(2)}) collective-permute-start(bf16[1168,128]{1,0:T(8,128)(2,1)S(1)} %get-tuple-element.31), channel_id=1, source_target_pairs={{0,4},{4,0},{12,8},{16,20},{24,28},{28,24},{1,5},{5,1},{13,9},{17,... | collective-permute-start | bytes 897032 | tf_op jit(solution)/shard_map/ppermute | solution.py:53
  13.9 4.1 %copy-start.3 = (s32[384]{0:T(512)S(1)}, s32[384]{0:T(512)}, u32[]{:S(2)}) copy-start(s32[384]{0:T(512)} %param.20) | copy-start | bytes 4612
  18.2 23.1 %collective-permute-start.11 = (bf16[192,1536]{1,0:T(8,128)(2,1)S(1)}, bf16[192,1536]{1,0:T(8,128)(2,1)S(1)}, u32[]{:S(2)}, u32[]{:S(2)}) collective-permute-start(bf16[192,1536]{1,0:T(8,128)(2,1)S(1)} %cut.1.refs_6_), channel_id=1, source_target_pairs={{0,2},{1,3},{2,0},{3,1},{16,17},{17,16},{18,19},{19,18},{4,6},{5,7... | collective-permute-start | bytes 1769480 | tf_op jit(solution)/shard_map/ppermute | solution.py:189
  19.8 26.4 %collective-permute-start.10 = (bf16[384,1536]{1,0:T(8,128)(2,1)S(1)}, bf16[384,1536]{1,0:T(8,128)(2,1)S(1)}, u32[]{:S(2)}, u32[]{:S(2)}) collective-permute-start(bf16[384,1536]{1,0:T(8,128)(2,1)S(1)} %collective-permute-done.3.got.near), channel_id=1, source_target_pairs={{0,16},{16,0},{1,17},{17,1},{2,18},{18,2},{3,19},{19,3},{4,20},{20... | collective-permute-start | bytes 3538952 | tf_op jit(solution)/shard_map/ppermute | solution.py:459
  28.5 9.2 %collective-permute-start.4 = (bf16[384,128]{1,0:T(8,128)(2,1)S(1)}, bf16[384,128]{1,0:T(8,128)(2,1)S(1)}, u32[]{:S(2)}, u32[]{:S(2)}) collective-permute-start(bf16[384,128]{1,0:T(8,128)(2,1)S(1)} %get-tuple-element.36), channel_id=1, source_target_pairs={{8,0},{0,8},{4,12},{24,16},{28,20},{20,28},{9,1},{1,9},{5,13},{25,... | collective-permute-start | bytes 294920 | tf_op jit(solution)/shard_map/ppermute | solution.py:53
  33.3 4.5 %collective-permute-start.5 = (bf16[384,128]{1,0:T(8,128)(2,1)S(1)}, bf16[384,128]{1,0:T(8,128)(2,1)S(1)}, u32[]{:S(2)}, u32[]{:S(2)}) collective-permute-start(bf16[384,128]{1,0:T(8,128)(2,1)S(1)} %get-tuple-element.37), channel_id=1, source_target_pairs={{8,4},{4,8},{0,12},{28,16},{24,20},{20,24},{9,5},{5,9},{1,13},{29,... | collective-permute-start | bytes 294920 | tf_op jit(solution)/shard_map/ppermute | solution.py:53
  34.6 6.6 %collective-permute-start.6 = (bf16[384,128]{1,0:T(8,128)(2,1)S(1)}, bf16[384,128]{1,0:T(8,128)(2,1)S(1)}, u32[]{:S(2)}, u32[]{:S(2)}) collective-permute-start(bf16[384,128]{1,0:T(8,128)(2,1)S(1)} %get-tuple-element.38), channel_id=1, source_target_pairs={{4,0},{0,4},{8,12},{20,16},{28,24},{24,28},{5,1},{1,5},{9,13},{21,... | collective-permute-start | bytes 294920 | tf_op jit(solution)/shard_map/ppermute | solution.py:53
  41.3 3.6 %collective-permute-start.12 = (bf16[192,1536]{1,0:T(8,128)(2,1)S(1)}, bf16[192,1536]{1,0:T(8,128)(2,1)S(1)}, u32[]{:S(2)}, u32[]{:S(2)}) collective-permute-start(bf16[192,1536]{1,0:T(8,128)(2,1)S(1)} %gate.1.far), channel_id=1, source_target_pairs={{0,16},{16,0},{1,17},{17,1},{2,18},{18,2},{3,19},{19,3},{4,20},{20... | collective-permute-start | bytes 1769480 | tf_op jit(solution)/shard_map/ppermute | solution.py:459
  41.4 7.0 %collective-permute-start.13 = (bf16[192,384]{1,0:T(8,128)(2,1)S(1)}, bf16[192,384]{1,0:T(8,128)(2,1)S(1)}, u32[]{:S(2)}, u32[]{:S(2)}) collective-permute-start(bf16[192,384]{1,0:T(8,128)(2,1)S(1)} %get-tuple-element.40.after.refs_0_), channel_id=1, source_target_pairs={{0,1},{1,0},{2,3},{3,2},{4,5},{5,4},{6,7},{7,6},{8,9},{9,8},{10,11... | collective-permute-start | bytes 442376 | tf_op jit(solution)/shard_map/ppermute | solution.py:459
  42.7 9.9 %collective-permute-start.14 = (bf16[192,384]{1,0:T(8,128)(2,1)S(1)}, bf16[192,384]{1,0:T(8,128)(2,1)S(1)}, u32[]{:S(2)}, u32[]{:S(2)}) collective-permute-start(bf16[192,384]{1,0:T(8,128)(2,1)S(1)} %get-tuple-element.40.after.refs_0_), channel_id=1, source_target_pairs={{0,2},{1,3},{2,0},{3,1},{4,6},{5,7},{6,4},{7,5},{8,10},{9,11},{10,... | collective-permute-start | bytes 442376 | tf_op jit(solution)/shard_map/ppermute | solution.py:459
  43.6 8.9 %collective-permute-start.15 = (bf16[192,384]{1,0:T(8,128)(2,1)S(1)}, bf16[192,384]{1,0:T(8,128)(2,1)S(1)}, u32[]{:S(2)}, u32[]{:S(2)}) collective-permute-start(bf16[192,384]{1,0:T(8,128)(2,1)S(1)} %get-tuple-element.40.after.refs_0_), channel_id=1, source_target_pairs={{0,3},{1,2},{2,1},{3,0},{4,7},{5,6},{6,5},{7,4},{8,11},{9,10},{10,... | collective-permute-start | bytes 442376 | tf_op jit(solution)/shard_map/ppermute | solution.py:459
  45.0 7.6 %copy-start.1 = (f32[3,4,1536]{2,1,0:T(4,128)S(1)}, f32[3,4,1536]{2,1,0:T(4,128)}, u32[]{:S(2)}) copy-start(f32[3,4,1536]{2,1,0:T(4,128)} %mod.1) | copy-start | bytes 221188
  45.0 11.4 %collective-permute-start.7 = (bf16[192,384]{1,0:T(8,128)(2,1)S(1)}, bf16[192,384]{1,0:T(8,128)(2,1)S(1)}, u32[]{:S(2)}, u32[]{:S(2)}) collective-permute-start(bf16[192,384]{1,0:T(8,128)(2,1)S(1)} %get-tuple-element.39.refs_0_), channel_id=1, source_target_pairs={{0,1},{1,0},{2,3},{3,2},{4,5},{5,4},{6,7},{7,6},{8,9},{9,8},{10,11... | collective-permute-start | bytes 442376 | tf_op jit(solution)/shard_map/ppermute | solution.py:459
  46.2 11.9 %collective-permute-start.8 = (bf16[192,384]{1,0:T(8,128)(2,1)S(1)}, bf16[192,384]{1,0:T(8,128)(2,1)S(1)}, u32[]{:S(2)}, u32[]{:S(2)}) collective-permute-start(bf16[192,384]{1,0:T(8,128)(2,1)S(1)} %get-tuple-element.39.refs_0_), channel_id=1, source_target_pairs={{0,2},{1,3},{2,0},{3,1},{4,6},{5,7},{6,4},{7,5},{8,10},{9,11},{10,... | collective-permute-start | bytes 442376 | tf_op jit(solution)/shard_map/ppermute | solution.py:459
  48.5 9.7 %collective-permute-start.9 = (bf16[192,384]{1,0:T(8,128)(2,1)S(1)}, bf16[192,384]{1,0:T(8,128)(2,1)S(1)}, u32[]{:S(2)}, u32[]{:S(2)}) collective-permute-start(bf16[192,384]{1,0:T(8,128)(2,1)S(1)} %get-tuple-element.39.refs_0_), channel_id=1, source_target_pairs={{0,3},{1,2},{2,1},{3,0},{4,7},{5,6},{6,5},{7,4},{8,11},{9,10},{10,... | collective-permute-start | bytes 442376 | tf_op jit(solution)/shard_map/ppermute | solution.py:459
  56.3 4.7 %copy-start.2 = (f32[3]{0:T(128)S(1)}, f32[3]{0:T(128)}, u32[]{:S(2)}) copy-start(f32[3]{0:T(128)} %scale_ref.1) | copy-start | bytes 40
  56.3 4.6 %collective-permute-start.16 = (bf16[192,1536]{1,0:T(8,128)(2,1)S(1)}, bf16[192,1536]{1,0:T(8,128)(2,1)S(1)}, u32[]{:S(2)}, u32[]{:S(2)}) collective-permute-start(bf16[192,1536]{1,0:T(8,128)(2,1)S(1)} %feed.3), channel_id=1, source_target_pairs={{0,16},{16,0},{1,17},{17,1},{2,18},{18,2},{3,19},{19,3},{4,20},{20... | collective-permute-start | bytes 1769480 | tf_op jit(solution)/shard_map/ppermute | solution.py:459
  62.8 6.5 %collective-permute-start.17 = (bf16[192,384]{1,0:T(8,128)(2,1)S(1)}, bf16[192,384]{1,0:T(8,128)(2,1)S(1)}, u32[]{:S(2)}, u32[]{:S(2)}) collective-permute-start(bf16[192,384]{1,0:T(8,128)(2,1)S(1)} %get-tuple-element.44), channel_id=1, source_target_pairs={{0,1},{1,0},{2,3},{3,2},{4,5},{5,4},{6,7},{7,6},{8,9},{9,8},{10,11... | collective-permute-start | bytes 442376 | tf_op jit(solution)/shard_map/ppermute | solution.py:459
  63.7 8.3 %collective-permute-start.18 = (bf16[192,384]{1,0:T(8,128)(2,1)S(1)}, bf16[192,384]{1,0:T(8,128)(2,1)S(1)}, u32[]{:S(2)}, u32[]{:S(2)}) collective-permute-start(bf16[192,384]{1,0:T(8,128)(2,1)S(1)} %get-tuple-element.45), channel_id=1, source_target_pairs={{0,2},{1,3},{2,0},{3,1},{4,6},{5,7},{6,4},{7,5},{8,10},{9,11},{10,... | collective-permute-start | bytes 442376 | tf_op jit(solution)/shard_map/ppermute | solution.py:459
  64.7 7.3 %collective-permute-start.19 = (bf16[192,384]{1,0:T(8,128)(2,1)S(1)}, bf16[192,384]{1,0:T(8,128)(2,1)S(1)}, u32[]{:S(2)}, u32[]{:S(2)}) collective-permute-start(bf16[192,384]{1,0:T(8,128)(2,1)S(1)} %get-tuple-element.46), channel_id=1, source_target_pairs={{0,3},{1,2},{2,1},{3,0},{4,7},{5,6},{6,5},{7,4},{8,11},{9,10},{10,... | collective-permute-start | bytes 442376 | tf_op jit(solution)/shard_map/ppermute | solution.py:459
  72.3 7.6 %collective-permute-start.20 = (bf16[96,384]{1,0:T(8,128)(2,1)S(1)}, bf16[96,384]{1,0:T(8,128)(2,1)S(1)}, u32[]{:S(2)}, u32[]{:S(2)}) collective-permute-start(bf16[96,384]{1,0:T(8,128)(2,1)S(1)} %get-tuple-element.48), channel_id=1, source_target_pairs={{0,8},{4,12},{8,0},{12,4},{1,9},{5,13},{9,1},{13,5},{2,10},{6,14},... | collective-permute-start | bytes 221192 | tf_op jit(solution)/shard_map/ppermute | solution.py:459
  73.2 6.7 %collective-permute-start.21 = (bf16[96,384]{1,0:T(8,128)(2,1)S(1)}, bf16[96,384]{1,0:T(8,128)(2,1)S(1)}, u32[]{:S(2)}, u32[]{:S(2)}) collective-permute-start(bf16[96,384]{1,0:T(8,128)(2,1)S(1)} %get-tuple-element.49), channel_id=1, source_target_pairs={{0,12},{4,8},{8,4},{12,0},{1,13},{5,9},{9,5},{13,1},{2,14},{6,10},... | collective-permute-start | bytes 221192 | tf_op jit(solution)/shard_map/ppermute | solution.py:459
  75.6 4.9 %collective-permute-start.22 = (bf16[96,384]{1,0:T(8,128)(2,1)S(1)}, bf16[96,384]{1,0:T(8,128)(2,1)S(1)}, u32[]{:S(2)}, u32[]{:S(2)}) collective-permute-start(bf16[96,384]{1,0:T(8,128)(2,1)S(1)} %get-tuple-element.50), channel_id=1, source_target_pairs={{0,4},{4,0},{8,12},{12,8},{1,5},{5,1},{9,13},{13,9},{2,6},{6,2},{1... | collective-permute-start | bytes 221192 | tf_op jit(solution)/shard_map/ppermute | solution.py:459

commit v7 on v6

--- a/solution.py
+++ b/solution.py
@@ -54,27 +54,26 @@
 
 
 def pack_kernel(q_ref, k_ref, v_ref, clip_ref, *refs):
-    outs, clips, sems = refs[:4], refs[4], refs[5]
+    outs, clips, held, sems = refs[:4], refs[4], refs[5], refs[6]
     side, place = lax.axis_index("cfg"), lax.axis_index("seq")
     slots = q_ref.shape[0]
-    clip_copy = pltpu.make_async_copy(clip_ref, clips, sems.at[12])
-    clip_copy.start()
-    copies = []
-    for step, out in zip(STEPS, outs):
-        head = jnp.clip(head_at(side, jnp.bitwise_xor(place, step)), 0, 2)
-        columns = pl.ds(pl.multiple_of(head * HEAD_DIM, HEAD_DIM), HEAD_DIM)
-        for part, source in enumerate((q_ref, k_ref, v_ref)):
-            target = out.at[part * slots : (part + 1) * slots, :]
-            copy = pltpu.make_async_copy(source.at[:, columns], target, sems.at[len(copies)])
-            copy.start()
-            copies.append(copy)
-    clip_copy.wait()
-    rows = clips[...].astype(F32).astype(BF16)
+    copies = [pltpu.make_async_copy(clip_ref, clips, sems.at[3])]
+    for part, source in enumerate((q_ref, k_ref, v_ref)):
+        copies.append(pltpu.make_async_copy(source, held.at[part], sems.at[part]))
+    for copy in copies:
+        copy.start()
+    copies[0].wait()
+    numbers = clips[...].astype(F32)
+    rest = jnp.zeros((16 - numbers.shape[0], 128), F32)
+    rows = jnp.concatenate([numbers, rest], axis=0).astype(BF16)
     for out in outs:
-        out[3 * slots :, :] = jnp.zeros((16, 128), BF16)
-        out[3 * slots : 3 * slots + rows.shape[0], :] = rows
-    for copy in copies:
-        copy.wait()
+        out[3 * slots :, :] = rows
+    for part in range(3):
+        copies[1 + part].wait()
+        for step, out in zip(STEPS, outs):
+            head = jnp.clip(head_at(side, jnp.bitwise_xor(place, step)), 0, 2)
+            columns = pl.ds(pl.multiple_of(head * HEAD_DIM, HEAD_DIM), HEAD_DIM)
+            out[part * slots : (part + 1) * slots, :] = held[part, :, columns]
 
 
 def attend_kernel(*refs):
@@ -271,7 +270,8 @@
         out_specs=[VMEM] * 4,
         scratch_shapes=[
             pltpu.VMEM((slots // 128, 128), jnp.int32),
-            pltpu.SemaphoreType.DMA((13,)),
+            pltpu.VMEM((3, slots, 3 * HEAD_DIM), BF16),
+            pltpu.SemaphoreType.DMA((4,)),
         ],
         compiler_params=params(16),
         name="pack",
@@ -364,21 +364,51 @@
             yield part, lowered[:, index * width : (index + 1) * width] + stream
 
 
-def feed_kernel(turn, *refs):
-    att, (w_out, up, down, res, mod, clip_ref), refs = refs[:4], refs[4:10], refs[10:]
+def project_kernel(*refs):
+    att, w_out, out = refs[:3], refs[3], refs[4]
+    rows_in = jnp.concatenate([piece[...] for piece in att], axis=1)
+    depth = rows_in.shape[1]
+    for start in range(0, D, 512):
+        columns = slice(start, start + 512)
+        out[:, columns] = jnp.dot(
+            rows_in, w_out[:depth, columns], preferred_element_type=F32
+        )
+
+
+def project(att, w_out):
+    return pl.pallas_call(
+        project_kernel,
+        out_shape=shape_of((att[0].shape[0], D), F32),
+        in_specs=[VMEM] * 4,
+        out_specs=VMEM,
+        compiler_params=params(16),
+        cost_estimate=cost(2**32, 2**22),
+        name="project",
+    )(*att, kept(w_out))
+
+
+def feed_kernel(turn, count, *refs):
+    att, (w_out, up, down, res, mod, clip_ref), refs = (
+        refs[:count],
+        refs[count : count + 6],
+        refs[count + 6 :],
+    )
     if turn == 0:
         out, mixed, hidden, normed = refs
     else:
-        hidden, mixed, normed = refs
+        partial, hidden, mixed, normed = refs
     side = lax.axis_index("cfg")
     half = hidden.shape[0]
     which = 1 - side if turn == 0 else side
     rows = pl.ds(pl.multiple_of(which * half, half), half)
     rows_in = jnp.concatenate([piece[...] for piece in att], axis=1)
+    depth = rows_in.shape[1]
     clip = clip_ref[rows, :][:, :1]
     tiles = [slice(start, start + 512) for start in range(0, D, 512)]
     for columns in tiles:
-        projected = jnp.dot(rows_in, w_out[:, columns], preferred_element_type=F32)
+        projected = jnp.dot(rows_in, w_out[D - depth :, columns], preferred_element_type=F32)
+        if turn == 1:
+            projected = projected + partial[:, columns]
         mixed[:, columns] = (
             res[rows, columns].astype(F32) + chosen(mod, 0, clip, columns) * projected
         )
@@ -397,23 +427,26 @@
 
 
 def feed(turn, att, w_out, w_up, w_down, residual, mod, clip_wide):
-    half, width = att[0].shape
+    half = att[0].shape[0]
     inner = [pltpu.VMEM((half, D), BF16)]
+    more = []
     if turn == 0:
         out_shape = shape_of((half, D))
         inner = [pltpu.VMEM((half, D), F32), pltpu.VMEM((half, D), BF16)] + inner
     else:
         out_shape = [shape_of((half, D)), shape_of((half, D), F32)]
+        more = [project(att[:3], w_out)]
+        att = att[3:]
     return pl.pallas_call(
-        functools.partial(feed_kernel, turn),
+        functools.partial(feed_kernel, turn, len(att)),
         out_shape=out_shape,
-        in_specs=[VMEM] * 10,
+        in_specs=[VMEM] * (len(att) + 6 + len(more)),
         out_specs=VMEM if turn == 0 else [VMEM] * 2,
         scratch_shapes=inner,
         compiler_params=params(24),
         cost_estimate=cost(2**36, 2**24),
         name="feed",
-    )(*att, kept(w_out), kept(w_up), kept(w_down), kept(residual), mod, clip_wide)
+    )(*att, kept(w_out), kept(w_up), kept(w_down), kept(residual), mod, clip_wide, *more)
 
 
 def guide_kernel(hidden, mixed, down, other_ref, clip_ref, mod, scale_ref, *refs):

time: 81.6 us -> 81.3 us (level)
    pallas_call x2 -> x3, Pallas kernels: 6.56 us -> 6.89 us  [the longest x2 5.95 us: feed(): pl.pallas_call(functools.partial(feed_kernel, turn, len(att)), out_shape=...]
  transfers between devices with their start and end apart: 23 -> 23, of which waited for: 8 -> 9; matrix products, arithmetic and copies ran while one was open for 1% -> 1% of each run, Pallas kernels for 19% -> 20%
where the time goes in v7:
time: 81.3 us; the launch traced here: 81 us
  starting transfers between devices  37.3 us (46%)
  waiting for transfers between devices  23.9 us (29%)
  Pallas kernels  19 us (23%)
    ppermute x6, starting transfers between devices, hop(): return lax.ppermute(value, ('cfg', 'seq'), pairs)  18.4 us
    ppermute x15, starting transfers between devices, exchanged(): return lax.ppermute(value, axis, pairs)  14.4 us
    ppermute x15, waiting for transfers between devices, exchanged(): return lax.ppermute(value, axis, pairs)  14 us
    ppermute x6, waiting for transfers between devices, hop(): return lax.ppermute(value, ('cfg', 'seq'), pairs)  9.84 us
    pallas_call x2, Pallas kernels, feed(): pl.pallas_call(functools.partial(feed_kernel, turn, len(att)), out_shape=...  5.95 us
    ppermute x2, starting transfers between devices, across(): return lax.ppermute(value, ('cfg', 'blk'), pairs)  4.52 us
    pallas_call x1, Pallas kernels, load(): pl.pallas_call(load_kernel, out_shape=[pltpu.VMEM(array.shape, BF16) for...  4.07 us
    pallas_call x1, Pallas kernels, attention_by_head(): pl.pallas_call(attend_kernel, out_shape=[shape_of((slots, 128))] * 4, in_...  2.09 us
  transfers between devices with their start and end apart: 23, of which 9 were waited for; matrix products, arithmetic and copies ran while one was open for 1% of the time, Pallas kernels for 20%

profile of v7, /device:TPU:0, one launch (start us, length us, event | category | flops | bytes accessed | tf_op | source)
XLA Modules:
  0.0 81.0 jit_solution(7190656644824693853)
XLA Ops:
  0.0 2.9 %collective-permute-start.3 = (bf16[384,1536]{1,0:T(8,128)(2,1)}, bf16[384,1536]{1,0:T(8,128)(2,1)S(1)}, u32[]{:S(2)}, u32[]{:S(2)}) collective-permute-start(bf16[384,1536]{1,0:T(8,128)(2,1)} %own.1), channel_id=1, source_target_pairs={{0,1},{1,0},{2,3},{3,2},{16,18},{17,19},{18,16},{19,17},{4,5},{5,4... | collective-permute-start | bytes 3538952 | tf_op jit(solution)/shard_map/ppermute | solution.py:188
  2.9 1.3 %pack.1 = (bf16[1168,128]{1,0:T(8,128)(2,1)S(1)}, bf16[1168,128]{1,0:T(8,128)(2,1)S(1)}, bf16[1168,128]{1,0:T(8,128)(2,1)S(1)}, bf16[1168,128]{1,0:T(8,128)(2,1)S(1)}) custom-call(bf16[384,384]{1,0:T(8,128)(2,1)} %bitcast.7, bf16[384,384]{1,0:T(8,128)(2,1)} %bitcast.8, bf16[384,384]{1,0:T(8,128)(2,1)} %bitcast.9, s32[3,128]{1,0:T(4,128)} %bitcast.12), custom_call_target="tpu_custom_call" | custom-call | tf_op jit(solution)/shard_map/pack/pallas_call | solution.py:266
  4.2 4.5 %collective-permute-start = (bf16[1168,128]{1,0:T(8,128)(2,1)S(1)}, bf16[1168,128]{1,0:T(8,128)(2,1)S(1)}, u32[]{:S(2)}, u32[]{:S(2)}) collective-permute-start(bf16[1168,128]{1,0:T(8,128)(2,1)S(1)} %get-tuple-element.29), channel_id=1, source_target_pairs={{0,8},{8,0},{12,4},{16,24},{20,28},{28,20},{1,9},{9,1},{13,5},{17,... | collective-permute-start | bytes 897032 | tf_op jit(solution)/shard_map/ppermute | solution.py:53
  8.7 1.3 %collective-permute-start.1 = (bf16[1168,128]{1,0:T(8,128)(2,1)S(1)}, bf16[1168,128]{1,0:T(8,128)(2,1)S(1)}, u32[]{:S(2)}, u32[]{:S(2)}) collective-permute-start(bf16[1168,128]{1,0:T(8,128)(2,1)S(1)} %get-tuple-element.30), channel_id=1, source_target_pairs={{4,8},{8,4},{12,0},{16,28},{20,24},{24,20},{5,9},{9,5},{13,1},{17,... | collective-permute-start | bytes 897032 | tf_op jit(solution)/shard_map/ppermute | solution.py:53
  10.0 3.4 %collective-permute-start.2 = (bf16[1168,128]{1,0:T(8,128)(2,1)S(1)}, bf16[1168,128]{1,0:T(8,128)(2,1)S(1)}, u32[]{:S(2)}, u32[]{:S(2)}) collective-permute-start(bf16[1168,128]{1,0:T(8,128)(2,1)S(1)} %get-tuple-element.31), channel_id=1, source_target_pairs={{0,4},{4,0},{12,8},{16,20},{24,28},{28,24},{1,5},{5,1},{13,9},{17,... | collective-permute-start | bytes 897032 | tf_op jit(solution)/shard_map/ppermute | solution.py:53
  13.5 0.1 constant_dynamic-slice_fusion
  13.5 0.2 convert_reduce_fusion
  13.7 4.1 %load.1 = (bf16[1536,1536]{1,0:T(8,128)(2,1)S(1)}, bf16[1536,1536]{1,0:T(8,128)(2,1)S(1)}, bf16[384,1536]{1,0:T(8,128)(2,1)S(1)}) custom-call(bf16[1536,1536]{1,0:T(8,128)(2,1)} %refs_0_.1, bf16[1536,1536]{1,0:T(8,128)(2,1)} %refs_1_.1, bf16[384,1536]{1,0:T(8,128)(2,1)} %bitcast.13, bf16[1168,128]{1,0:T(8,128)(2,1)S(1)} %get-tuple-element.28.refs_3_.refs_0_), custom_call_target="tpu_custom_call" | custom-call | flops 17179869184 | bytes 16777216 | tf_op jit(solution)/shard_map/load/pallas_call | solution.py:172
  17.8 0.1 compare_select_fusion
  17.9 0.1 cut.1.refs_6_
  18.0 1.6 %collective-permute-start.9 = (bf16[192,1536]{1,0:T(8,128)(2,1)S(1)}, bf16[192,1536]{1,0:T(8,128)(2,1)S(1)}, u32[]{:S(2)}, u32[]{:S(2)}) collective-permute-start(bf16[192,1536]{1,0:T(8,128)(2,1)S(1)} %cut.1.refs_6_), channel_id=1, source_target_pairs={{0,2},{1,3},{2,0},{3,1},{16,17},{17,16},{18,19},{19,18},{4,6},{5,7... | collective-permute-start | bytes 1769480 | tf_op jit(solution)/shard_map/ppermute | solution.py:188
  19.7 0.0 copy-start.1
  19.7 6.4 %collective-permute-done.refs_1_ = bf16[1168,128]{1,0:T(8,128)(2,1)S(1)} collective-permute-done((bf16[1168,128]{1,0:T(8,128)(2,1)S(1)}, bf16[1168,128]{1,0:T(8,128)(2,1)S(1)}, u32[]{:S(2)}, u32[]{:S(2)}) %collective-permute-start) | collective-permute-done | bytes 299040 | tf_op jit(solution)/shard_map/ppermute | solution.py:53
  26.1 0.1 broadcast_in_dim.7.refs_4_.refs_6_.refs_9_.clip_ref
  26.2 2.1 %attend.1 = (bf16[384,128]{1,0:T(8,128)(2,1)S(1)}, bf16[384,128]{1,0:T(8,128)(2,1)S(1)}, bf16[384,128]{1,0:T(8,128)(2,1)S(1)}, bf16[384,128]{1,0:T(8,128)(2,1)S(1)}) custom-call(bf16[1168,128]{1,0:T(8,128)(2,1)S(1)} %get-tuple-element.28.refs_3_.refs_0_, bf16[1168,128]{1,0:T(8,128)(2,1)S(1)} %collective-permute-done.refs_1_, ...), custom_call_target="tpu_custom_call" | custom-call | flops 4294967296 | bytes 2097152 | tf_op jit(solution)/shard_map/attend/pallas_call | solution.py:281
  28.3 4.8 %collective-permute-start.4 = (bf16[384,128]{1,0:T(8,128)(2,1)S(1)}, bf16[384,128]{1,0:T(8,128)(2,1)S(1)}, u32[]{:S(2)}, u32[]{:S(2)}) collective-permute-start(bf16[384,128]{1,0:T(8,128)(2,1)S(1)} %get-tuple-element.36), channel_id=1, source_target_pairs={{8,0},{0,8},{4,12},{24,16},{28,20},{20,28},{9,1},{1,9},{5,13},{25,... | collective-permute-start | bytes 294920 | tf_op jit(solution)/shard_map/ppermute | solution.py:53
  33.1 1.3 %collective-permute-start.5 = (bf16[384,128]{1,0:T(8,128)(2,1)S(1)}, bf16[384,128]{1,0:T(8,128)(2,1)S(1)}, u32[]{:S(2)}, u32[]{:S(2)}) collective-permute-start(bf16[384,128]{1,0:T(8,128)(2,1)S(1)} %get-tuple-element.37), channel_id=1, source_target_pairs={{8,4},{4,8},{0,12},{28,16},{24,20},{20,24},{9,5},{5,9},{1,13},{29,... | collective-permute-start | bytes 294920 | tf_op jit(solution)/shard_map/ppermute | solution.py:53
  34.4 3.2 %collective-permute-start.6 = (bf16[384,128]{1,0:T(8,128)(2,1)S(1)}, bf16[384,128]{1,0:T(8,128)(2,1)S(1)}, u32[]{:S(2)}, u32[]{:S(2)}) collective-permute-start(bf16[384,128]{1,0:T(8,128)(2,1)S(1)} %get-tuple-element.38), channel_id=1, source_target_pairs={{4,0},{0,4},{8,12},{20,16},{28,24},{24,28},{5,1},{1,5},{9,13},{21,... | collective-permute-start | bytes 294920 | tf_op jit(solution)/shard_map/ppermute | solution.py:53
  37.6 3.4 %collective-permute-done.6.back3 = bf16[384,128]{1,0:T(8,128)(2,1)S(1)} collective-permute-done((bf16[384,128]{1,0:T(8,128)(2,1)S(1)}, bf16[384,128]{1,0:T(8,128)(2,1)S(1)}, u32[]{:S(2)}, u32[]{:S(2)}) %collective-permute-start.6) | collective-permute-done | bytes 98336 | tf_op jit(solution)/shard_map/ppermute | solution.py:53
  41.0 0.3 regroup.1
  41.3 0.1 collective-permute-start.10
  41.4 1.3 %collective-permute-start.13 = (bf16[192,384]{1,0:T(8,128)(2,1)S(1)}, bf16[192,384]{1,0:T(8,128)(2,1)S(1)}, u32[]{:S(2)}, u32[]{:S(2)}) collective-permute-start(bf16[192,384]{1,0:T(8,128)(2,1)S(1)} %get-tuple-element.40.after.refs_0_), channel_id=1, source_target_pairs={{0,1},{1,0},{2,3},{3,2},{4,5},{5,4},{6,7},{7,6},{8,9},{9,8},{10,11... | collective-permute-start | bytes 442376 | tf_op jit(solution)/shard_map/ppermute | solution.py:492
  42.7 0.9 %collective-permute-start.14 = (bf16[192,384]{1,0:T(8,128)(2,1)S(1)}, bf16[192,384]{1,0:T(8,128)(2,1)S(1)}, u32[]{:S(2)}, u32[]{:S(2)}) collective-permute-start(bf16[192,384]{1,0:T(8,128)(2,1)S(1)} %get-tuple-element.40.after.refs_0_), channel_id=1, source_target_pairs={{0,2},{1,3},{2,0},{3,1},{4,6},{5,7},{6,4},{7,5},{8,10},{9,11},{10,... | collective-permute-start | bytes 442376 | tf_op jit(solution)/shard_map/ppermute | solution.py:492
  43.6 1.3 %collective-permute-start.15 = (bf16[192,384]{1,0:T(8,128)(2,1)S(1)}, bf16[192,384]{1,0:T(8,128)(2,1)S(1)}, u32[]{:S(2)}, u32[]{:S(2)}) collective-permute-start(bf16[192,384]{1,0:T(8,128)(2,1)S(1)} %get-tuple-element.40.after.refs_0_), channel_id=1, source_target_pairs={{0,3},{1,2},{2,1},{3,0},{4,7},{5,6},{6,5},{7,4},{8,11},{9,10},{10,... | collective-permute-start | bytes 442376 | tf_op jit(solution)/shard_map/ppermute | solution.py:492
  45.0 1.2 %collective-permute-start.11 = (bf16[192,384]{1,0:T(8,128)(2,1)S(1)}, bf16[192,384]{1,0:T(8,128)(2,1)S(1)}, u32[]{:S(2)}, u32[]{:S(2)}) collective-permute-start(bf16[192,384]{1,0:T(8,128)(2,1)S(1)} %get-tuple-element.39.refs_0_), channel_id=1, source_target_pairs={{0,1},{1,0},{2,3},{3,2},{4,5},{5,4},{6,7},{7,6},{8,9},{9,8},{10,11... | collective-permute-start | bytes 442376 | tf_op jit(solution)/shard_map/ppermute | solution.py:492
  46.2 0.9 %collective-permute-start.12 = (bf16[192,384]{1,0:T(8,128)(2,1)S(1)}, bf16[192,384]{1,0:T(8,128)(2,1)S(1)}, u32[]{:S(2)}, u32[]{:S(2)}) collective-permute-start(bf16[192,384]{1,0:T(8,128)(2,1)S(1)} %get-tuple-element.39.refs_0_), channel_id=1, source_target_pairs={{0,2},{1,3},{2,0},{3,1},{4,6},{5,7},{6,4},{7,5},{8,10},{9,11},{10,... | collective-permute-start | bytes 442376 | tf_op jit(solution)/shard_map/ppermute | solution.py:492
  47.1 1.3 %join.1.refs_3_.refs_1_.refs_4_ = bf16[1536,1536]{1,0:T(8,128)(2,1)S(1)} custom-call(bf16[384,1536]{1,0:T(8,128)(2,1)} %own.1, bf16[384,1536]{1,0:T(8,128)(2,1)S(1)} %collective-permute-done.3.got.near, bf16[384,1536]{1,0:T(8,128)(2,1)S(1)} %collective-permute-done.8.near_swap, bf16[192,1536]{1,0:T(8,128)(2,1)S(1)} %gate.1.far, ...), custom_call_target="tpu_custom_call" | custom-call | tf_op jit(solution)/shard_map/join/pallas_call | solution.py:253
  48.5 1.4 %collective-permute-start.7 = (bf16[192,384]{1,0:T(8,128)(2,1)S(1)}, bf16[192,384]{1,0:T(8,128)(2,1)S(1)}, u32[]{:S(2)}, u32[]{:S(2)}) collective-permute-start(bf16[192,384]{1,0:T(8,128)(2,1)S(1)} %get-tuple-element.39.refs_0_), channel_id=1, source_target_pairs={{0,3},{1,2},{2,1},{3,0},{4,7},{5,6},{6,5},{7,4},{8,11},{9,10},{10,... | collective-permute-start | bytes 442376 | tf_op jit(solution)/shard_map/ppermute | solution.py:492
  49.9 2.7 %collective-permute-done.14.refs_2_ = bf16[192,384]{1,0:T(8,128)(2,1)S(1)} collective-permute-done((bf16[192,384]{1,0:T(8,128)(2,1)S(1)}, bf16[192,384]{1,0:T(8,128)(2,1)S(1)}, u32[]{:S(2)}, u32[]{:S(2)}) %collective-permute-start.14) | collective-permute-done | bytes 147488 | tf_op jit(solution)/shard_map/ppermute | solution.py:492
  52.6 3.8 %feed.3 = bf16[192,1536]{1,0:T(8,128)(2,1)S(1)} custom-call(bf16[192,384]{1,0:T(8,128)(2,1)S(1)} %get-tuple-element.40.after.refs_0_, bf16[192,384]{1,0:T(8,128)(2,1)S(1)} %collective-permute-done.13.refs_1_, bf16[192,384]{1,0:T(8,128)(2,1)S(1)} %collective-permute-done.14.refs_2_, bf16[192,384]{1,0:T(8,128)(2,1)S(1)} %collective-permute-done.15.refs_3_, ...), custom_call_target="tpu_custom_call" | custom-call | flops 68719476736 | bytes 16777216 | tf_op jit(solution)/shard_map/feed/pallas_call | solution.py:440
  56.3 0.1 collective-permute-start.16
  56.4 1.7 %collective-permute-done.12.refs_2_ = bf16[192,384]{1,0:T(8,128)(2,1)S(1)} collective-permute-done((bf16[192,384]{1,0:T(8,128)(2,1)S(1)}, bf16[192,384]{1,0:T(8,128)(2,1)S(1)}, u32[]{:S(2)}, u32[]{:S(2)}) %collective-permute-start.12) | collective-permute-done | bytes 147488 | tf_op jit(solution)/shard_map/ppermute | solution.py:492
  58.1 0.9 %project.1.refs_7_ = f32[192,1536]{1,0:T(8,128)S(1)} custom-call(bf16[192,384]{1,0:T(8,128)(2,1)S(1)} %get-tuple-element.39.refs_0_, bf16[192,384]{1,0:T(8,128)(2,1)S(1)} %collective-permute-done.11.refs_1_, bf16[192,384]{1,0:T(8,128)(2,1)S(1)} %collective-permute-done.12.refs_2_, bf16[1536,1536]{1,0:T(8,128)(2,1)S(1)} %join.1.refs_3_.refs_1_.refs_4_), custom_call_target="tpu_custom_call" | custom-call | flops 4294967296 | bytes 4194304 | tf_op jit(solution)/shard_map/project/pallas_call | solution.py:379
  59.1 2.2 %feed.2 = (bf16[192,1536]{1,0:T(8,128)(2,1)S(1)}, f32[192,1536]{1,0:T(8,128)S(1)}) custom-call(bf16[192,384]{1,0:T(8,128)(2,1)S(1)} %collective-permute-done.7.refs_0_, bf16[1536,1536]{1,0:T(8,128)(2,1)S(1)} %join.1.refs_3_.refs_1_.refs_4_, bf16[1536,1536]{1,0:T(8,128)(2,1)S(1)} %get-tuple-element.32.refs_7_.refs_2_.refs_5_, ...), custom_call_target="tpu_custom_call" | custom-call | flops 68719476736 | bytes 16777216 | tf_op jit(solution)/shard_map/feed/pallas_call | solution.py:440
  61.3 1.9 %guide.1 = (f32[192,384]{1,0:T(8,128)S(1)}, bf16[192,384]{1,0:T(8,128)(2,1)S(1)}, bf16[192,384]{1,0:T(8,128)(2,1)S(1)}, bf16[192,384]{1,0:T(8,128)(2,1)S(1)}) custom-call(bf16[192,1536]{1,0:T(8,128)(2,1)S(1)} %get-tuple-element.41.hidden, f32[192,1536]{1,0:T(8,128)S(1)} %get-tuple-element.42.mixed, ...), custom_call_target="tpu_custom_call" | custom-call | tf_op jit(solution)/shard_map/guide/pallas_call | solution.py:540
  63.2 0.9 %collective-permute-start.17 = (bf16[192,384]{1,0:T(8,128)(2,1)S(1)}, bf16[192,384]{1,0:T(8,128)(2,1)S(1)}, u32[]{:S(2)}, u32[]{:S(2)}) collective-permute-start(bf16[192,384]{1,0:T(8,128)(2,1)S(1)} %get-tuple-element.44), channel_id=1, source_target_pairs={{0,1},{1,0},{2,3},{3,2},{4,5},{5,4},{6,7},{7,6},{8,9},{9,8},{10,11... | collective-permute-start | bytes 442376 | tf_op jit(solution)/shard_map/ppermute | solution.py:492
  64.1 0.2 collective-permute-start.18
  64.3 2.5 %collective-permute-start.19 = (bf16[192,384]{1,0:T(8,128)(2,1)S(1)}, bf16[192,384]{1,0:T(8,128)(2,1)S(1)}, u32[]{:S(2)}, u32[]{:S(2)}) collective-permute-start(bf16[192,384]{1,0:T(8,128)(2,1)S(1)} %get-tuple-element.46), channel_id=1, source_target_pairs={{0,3},{1,2},{2,1},{3,0},{4,7},{5,6},{6,5},{7,4},{8,11},{9,10},{10,... | collective-permute-start | bytes 442376 | tf_op jit(solution)/shard_map/ppermute | solution.py:492
  66.8 2.7 %collective-permute-done.17.got1 = bf16[192,384]{1,0:T(8,128)(2,1)S(1)} collective-permute-done((bf16[192,384]{1,0:T(8,128)(2,1)S(1)}, bf16[192,384]{1,0:T(8,128)(2,1)S(1)}, u32[]{:S(2)}, u32[]{:S(2)}) %collective-permute-start.17) | collective-permute-done | bytes 147488 | tf_op jit(solution)/shard_map/ppermute | solution.py:492
  69.4 2.3 %collective-permute-done.18.got2 = bf16[192,384]{1,0:T(8,128)(2,1)S(1)} collective-permute-done((bf16[192,384]{1,0:T(8,128)(2,1)S(1)}, bf16[192,384]{1,0:T(8,128)(2,1)S(1)}, u32[]{:S(2)}, u32[]{:S(2)}) %collective-permute-start.18) | collective-permute-done | bytes 147488 | tf_op jit(solution)/shard_map/ppermute | solution.py:492
  71.7 0.3 place.1
  72.0 1.2 %collective-permute-start.20 = (bf16[96,384]{1,0:T(8,128)(2,1)S(1)}, bf16[96,384]{1,0:T(8,128)(2,1)S(1)}, u32[]{:S(2)}, u32[]{:S(2)}) collective-permute-start(bf16[96,384]{1,0:T(8,128)(2,1)S(1)} %get-tuple-element.48), channel_id=1, source_target_pairs={{0,8},{4,12},{8,0},{12,4},{1,9},{5,13},{9,1},{13,5},{2,10},{6,14},... | collective-permute-start | bytes 221192 | tf_op jit(solution)/shard_map/ppermute | solution.py:492
  73.2 2.0 %collective-permute-start.21 = (bf16[96,384]{1,0:T(8,128)(2,1)S(1)}, bf16[96,384]{1,0:T(8,128)(2,1)S(1)}, u32[]{:S(2)}, u32[]{:S(2)}) collective-permute-start(bf16[96,384]{1,0:T(8,128)(2,1)S(1)} %get-tuple-element.49), channel_id=1, source_target_pairs={{0,12},{4,8},{8,4},{12,0},{1,13},{5,9},{9,5},{13,1},{2,14},{6,10},... | collective-permute-start | bytes 221192 | tf_op jit(solution)/shard_map/ppermute | solution.py:492
  75.2 0.4 collective-permute-start.22
  75.6 2.6 %collective-permute-done.20.refs_1_ = bf16[96,384]{1,0:T(8,128)(2,1)S(1)} collective-permute-done((bf16[96,384]{1,0:T(8,128)(2,1)S(1)}, bf16[96,384]{1,0:T(8,128)(2,1)S(1)}, u32[]{:S(2)}, u32[]{:S(2)}) %collective-permute-start.20) | collective-permute-done | bytes 73760 | tf_op jit(solution)/shard_map/ppermute | solution.py:492
  78.1 1.4 %collective-permute-done.21.refs_2_ = bf16[96,384]{1,0:T(8,128)(2,1)S(1)} collective-permute-done((bf16[96,384]{1,0:T(8,128)(2,1)S(1)}, bf16[96,384]{1,0:T(8,128)(2,1)S(1)}, u32[]{:S(2)}, u32[]{:S(2)}) %collective-permute-start.21) | collective-permute-done | bytes 73760 | tf_op jit(solution)/shard_map/ppermute | solution.py:492
  79.5 0.7 collective-permute-done.22.refs_3_
  80.2 0.8 arrange.1
  (28 shorter events, 0.1 us)
Async XLA Ops:
  0.0 13.5 %copy-start = (s32[384,1]{0,1:T(1,128)S(1)}, s32[384,1]{0,1:T(1,128)}, u32[]{:S(2)}) copy-start(s32[384,1]{0,1:T(1,128)} %param.21) | copy-start | bytes 4612
  0.0 17.9 %collective-permute-start.3 = (bf16[384,1536]{1,0:T(8,128)(2,1)}, bf16[384,1536]{1,0:T(8,128)(2,1)S(1)}, u32[]{:S(2)}, u32[]{:S(2)}) collective-permute-start(bf16[384,1536]{1,0:T(8,128)(2,1)} %own.1), channel_id=1, source_target_pairs={{0,1},{1,0},{2,3},{3,2},{16,18},{17,19},{18,16},{19,17},{4,5},{5,4... | collective-permute-start | bytes 3538952 | tf_op jit(solution)/shard_map/ppermute | solution.py:188
  4.2 21.9 %collective-permute-start = (bf16[1168,128]{1,0:T(8,128)(2,1)S(1)}, bf16[1168,128]{1,0:T(8,128)(2,1)S(1)}, u32[]{:S(2)}, u32[]{:S(2)}) collective-permute-start(bf16[1168,128]{1,0:T(8,128)(2,1)S(1)} %get-tuple-element.29), channel_id=1, source_target_pairs={{0,8},{8,0},{12,4},{16,24},{20,28},{28,20},{1,9},{9,1},{13,5},{17,... | collective-permute-start | bytes 897032 | tf_op jit(solution)/shard_map/ppermute | solution.py:53
  8.7 17.4 %collective-permute-start.1 = (bf16[1168,128]{1,0:T(8,128)(2,1)S(1)}, bf16[1168,128]{1,0:T(8,128)(2,1)S(1)}, u32[]{:S(2)}, u32[]{:S(2)}) collective-permute-start(bf16[1168,128]{1,0:T(8,128)(2,1)S(1)} %get-tuple-element.30), channel_id=1, source_target_pairs={{4,8},{8,4},{12,0},{16,28},{20,24},{24,20},{5,9},{9,5},{13,1},{17,... | collective-permute-start | bytes 897032 | tf_op jit(solution)/shard_map/ppermute | solution.py:53
  10.0 16.1 %collective-permute-start.2 = (bf16[1168,128]{1,0:T(8,128)(2,1)S(1)}, bf16[1168,128]{1,0:T(8,128)(2,1)S(1)}, u32[]{:S(2)}, u32[]{:S(2)}) collective-permute-start(bf16[1168,128]{1,0:T(8,128)(2,1)S(1)} %get-tuple-element.31), channel_id=1, source_target_pairs={{0,4},{4,0},{12,8},{16,20},{24,28},{28,24},{1,5},{5,1},{13,9},{17,... | collective-permute-start | bytes 897032 | tf_op jit(solution)/shard_map/ppermute | solution.py:53
  13.7 4.1 %copy-start.5 = (s32[384]{0:T(512)S(1)}, s32[384]{0:T(512)}, u32[]{:S(2)}) copy-start(s32[384]{0:T(512)} %param.20) | copy-start | bytes 4612
  18.0 23.3 %collective-permute-start.9 = (bf16[192,1536]{1,0:T(8,128)(2,1)S(1)}, bf16[192,1536]{1,0:T(8,128)(2,1)S(1)}, u32[]{:S(2)}, u32[]{:S(2)}) collective-permute-start(bf16[192,1536]{1,0:T(8,128)(2,1)S(1)} %cut.1.refs_6_), channel_id=1, source_target_pairs={{0,2},{1,3},{2,0},{3,1},{16,17},{17,16},{18,19},{19,18},{4,6},{5,7... | collective-permute-start | bytes 1769480 | tf_op jit(solution)/shard_map/ppermute | solution.py:188
  19.6 26.6 %collective-permute-start.8 = (bf16[384,1536]{1,0:T(8,128)(2,1)S(1)}, bf16[384,1536]{1,0:T(8,128)(2,1)S(1)}, u32[]{:S(2)}, u32[]{:S(2)}) collective-permute-start(bf16[384,1536]{1,0:T(8,128)(2,1)S(1)} %collective-permute-done.3.got.near), channel_id=1, source_target_pairs={{0,16},{16,0},{1,17},{17,1},{2,18},{18,2},{3,19},{19,3},{4,20},{20... | collective-permute-start | bytes 3538952 | tf_op jit(solution)/shard_map/ppermute | solution.py:492
  19.7 8.6 %copy-start.1 = (bf16[384,192]{1,0:T(8,128)(2,1)}, bf16[384,192]{1,0:T(8,128)(2,1)S(1)}, u32[]{:S(2)}) copy-start(bf16[384,192]{1,0:T(8,128)(2,1)S(1)} %fusion.refs_5_.placing) | copy-start | bytes 442372
  28.3 9.2 %collective-permute-start.4 = (bf16[384,128]{1,0:T(8,128)(2,1)S(1)}, bf16[384,128]{1,0:T(8,128)(2,1)S(1)}, u32[]{:S(2)}, u32[]{:S(2)}) collective-permute-start(bf16[384,128]{1,0:T(8,128)(2,1)S(1)} %get-tuple-element.36), channel_id=1, source_target_pairs={{8,0},{0,8},{4,12},{24,16},{28,20},{20,28},{9,1},{1,9},{5,13},{25,... | collective-permute-start | bytes 294920 | tf_op jit(solution)/shard_map/ppermute | solution.py:53
  33.1 4.5 %collective-permute-start.5 = (bf16[384,128]{1,0:T(8,128)(2,1)S(1)}, bf16[384,128]{1,0:T(8,128)(2,1)S(1)}, u32[]{:S(2)}, u32[]{:S(2)}) collective-permute-start(bf16[384,128]{1,0:T(8,128)(2,1)S(1)} %get-tuple-element.37), channel_id=1, source_target_pairs={{8,4},{4,8},{0,12},{28,16},{24,20},{20,24},{9,5},{5,9},{1,13},{29,... | collective-permute-start | bytes 294920 | tf_op jit(solution)/shard_map/ppermute | solution.py:53
  34.4 6.6 %collective-permute-start.6 = (bf16[384,128]{1,0:T(8,128)(2,1)S(1)}, bf16[384,128]{1,0:T(8,128)(2,1)S(1)}, u32[]{:S(2)}, u32[]{:S(2)}) collective-permute-start(bf16[384,128]{1,0:T(8,128)(2,1)S(1)} %get-tuple-element.38), channel_id=1, source_target_pairs={{4,0},{0,4},{8,12},{20,16},{28,24},{24,28},{5,1},{1,5},{9,13},{21,... | collective-permute-start | bytes 294920 | tf_op jit(solution)/shard_map/ppermute | solution.py:53
  41.3 3.6 %collective-permute-start.10 = (bf16[192,1536]{1,0:T(8,128)(2,1)S(1)}, bf16[192,1536]{1,0:T(8,128)(2,1)S(1)}, u32[]{:S(2)}, u32[]{:S(2)}) collective-permute-start(bf16[192,1536]{1,0:T(8,128)(2,1)S(1)} %gate.1.far), channel_id=1, source_target_pairs={{0,16},{16,0},{1,17},{17,1},{2,18},{18,2},{3,19},{19,3},{4,20},{20... | collective-permute-start | bytes 1769480 | tf_op jit(solution)/shard_map/ppermute | solution.py:492
  41.4 7.0 %collective-permute-start.13 = (bf16[192,384]{1,0:T(8,128)(2,1)S(1)}, bf16[192,384]{1,0:T(8,128)(2,1)S(1)}, u32[]{:S(2)}, u32[]{:S(2)}) collective-permute-start(bf16[192,384]{1,0:T(8,128)(2,1)S(1)} %get-tuple-element.40.after.refs_0_), channel_id=1, source_target_pairs={{0,1},{1,0},{2,3},{3,2},{4,5},{5,4},{6,7},{7,6},{8,9},{9,8},{10,11... | collective-permute-start | bytes 442376 | tf_op jit(solution)/shard_map/ppermute | solution.py:492
  42.7 9.9 %collective-permute-start.14 = (bf16[192,384]{1,0:T(8,128)(2,1)S(1)}, bf16[192,384]{1,0:T(8,128)(2,1)S(1)}, u32[]{:S(2)}, u32[]{:S(2)}) collective-permute-start(bf16[192,384]{1,0:T(8,128)(2,1)S(1)} %get-tuple-element.40.after.refs_0_), channel_id=1, source_target_pairs={{0,2},{1,3},{2,0},{3,1},{4,6},{5,7},{6,4},{7,5},{8,10},{9,11},{10,... | collective-permute-start | bytes 442376 | tf_op jit(solution)/shard_map/ppermute | solution.py:492
  43.6 8.9 %collective-permute-start.15 = (bf16[192,384]{1,0:T(8,128)(2,1)S(1)}, bf16[192,384]{1,0:T(8,128)(2,1)S(1)}, u32[]{:S(2)}, u32[]{:S(2)}) collective-permute-start(bf16[192,384]{1,0:T(8,128)(2,1)S(1)} %get-tuple-element.40.after.refs_0_), channel_id=1, source_target_pairs={{0,3},{1,2},{2,1},{3,0},{4,7},{5,6},{6,5},{7,4},{8,11},{9,10},{10,... | collective-permute-start | bytes 442376 | tf_op jit(solution)/shard_map/ppermute | solution.py:492
  45.0 7.6 %copy-start.3 = (f32[3,4,1536]{2,1,0:T(4,128)S(1)}, f32[3,4,1536]{2,1,0:T(4,128)}, u32[]{:S(2)}) copy-start(f32[3,4,1536]{2,1,0:T(4,128)} %mod.1) | copy-start | bytes 221188
  45.0 11.4 %collective-permute-start.11 = (bf16[192,384]{1,0:T(8,128)(2,1)S(1)}, bf16[192,384]{1,0:T(8,128)(2,1)S(1)}, u32[]{:S(2)}, u32[]{:S(2)}) collective-permute-start(bf16[192,384]{1,0:T(8,128)(2,1)S(1)} %get-tuple-element.39.refs_0_), channel_id=1, source_target_pairs={{0,1},{1,0},{2,3},{3,2},{4,5},{5,4},{6,7},{7,6},{8,9},{9,8},{10,11... | collective-permute-start | bytes 442376 | tf_op jit(solution)/shard_map/ppermute | solution.py:492
  46.2 11.9 %collective-permute-start.12 = (bf16[192,384]{1,0:T(8,128)(2,1)S(1)}, bf16[192,384]{1,0:T(8,128)(2,1)S(1)}, u32[]{:S(2)}, u32[]{:S(2)}) collective-permute-start(bf16[192,384]{1,0:T(8,128)(2,1)S(1)} %get-tuple-element.39.refs_0_), channel_id=1, source_target_pairs={{0,2},{1,3},{2,0},{3,1},{4,6},{5,7},{6,4},{7,5},{8,10},{9,11},{10,... | collective-permute-start | bytes 442376 | tf_op jit(solution)/shard_map/ppermute | solution.py:492
  48.5 10.6 %collective-permute-start.7 = (bf16[192,384]{1,0:T(8,128)(2,1)S(1)}, bf16[192,384]{1,0:T(8,128)(2,1)S(1)}, u32[]{:S(2)}, u32[]{:S(2)}) collective-permute-start(bf16[192,384]{1,0:T(8,128)(2,1)S(1)} %get-tuple-element.39.refs_0_), channel_id=1, source_target_pairs={{0,3},{1,2},{2,1},{3,0},{4,7},{5,6},{6,5},{7,4},{8,11},{9,10},{10,... | collective-permute-start | bytes 442376 | tf_op jit(solution)/shard_map/ppermute | solution.py:492
  56.3 5.0 %collective-permute-start.16 = (bf16[192,1536]{1,0:T(8,128)(2,1)S(1)}, bf16[192,1536]{1,0:T(8,128)(2,1)S(1)}, u32[]{:S(2)}, u32[]{:S(2)}) collective-permute-start(bf16[192,1536]{1,0:T(8,128)(2,1)S(1)} %feed.3), channel_id=1, source_target_pairs={{0,16},{16,0},{1,17},{17,1},{2,18},{18,2},{3,19},{19,3},{4,20},{20... | collective-permute-start | bytes 1769480 | tf_op jit(solution)/shard_map/ppermute | solution.py:492
  59.1 2.2 %copy-start.4 = (f32[3]{0:T(128)S(1)}, f32[3]{0:T(128)}, u32[]{:S(2)}) copy-start(f32[3]{0:T(128)} %scale_ref.1) | copy-start | bytes 40
  61.3 10.4 %copy-start.2 = (bf16[384,192]{1,0:T(8,128)(2,1)S(1)}, bf16[384,192]{1,0:T(8,128)(2,1)}, u32[]{:S(2)}) copy-start(bf16[384,192]{1,0:T(8,128)(2,1)} %copy-done.1) | copy-start | bytes 442372
  63.2 6.2 %collective-permute-start.17 = (bf16[192,384]{1,0:T(8,128)(2,1)S(1)}, bf16[192,384]{1,0:T(8,128)(2,1)S(1)}, u32[]{:S(2)}, u32[]{:S(2)}) collective-permute-start(bf16[192,384]{1,0:T(8,128)(2,1)S(1)} %get-tuple-element.44), channel_id=1, source_target_pairs={{0,1},{1,0},{2,3},{3,2},{4,5},{5,4},{6,7},{7,6},{8,9},{9,8},{10,11... | collective-permute-start | bytes 442376 | tf_op jit(solution)/shard_map/ppermute | solution.py:492
  64.1 7.6 %collective-permute-start.18 = (bf16[192,384]{1,0:T(8,128)(2,1)S(1)}, bf16[192,384]{1,0:T(8,128)(2,1)S(1)}, u32[]{:S(2)}, u32[]{:S(2)}) collective-permute-start(bf16[192,384]{1,0:T(8,128)(2,1)S(1)} %get-tuple-element.45), channel_id=1, source_target_pairs={{0,2},{1,3},{2,0},{3,1},{4,6},{5,7},{6,4},{7,5},{8,10},{9,11},{10,... | collective-permute-start | bytes 442376 | tf_op jit(solution)/shard_map/ppermute | solution.py:492
  64.3 7.4 %collective-permute-start.19 = (bf16[192,384]{1,0:T(8,128)(2,1)S(1)}, bf16[192,384]{1,0:T(8,128)(2,1)S(1)}, u32[]{:S(2)}, u32[]{:S(2)}) collective-permute-start(bf16[192,384]{1,0:T(8,128)(2,1)S(1)} %get-tuple-element.46), channel_id=1, source_target_pairs={{0,3},{1,2},{2,1},{3,0},{4,7},{5,6},{6,5},{7,4},{8,11},{9,10},{10,... | collective-permute-start | bytes 442376 | tf_op jit(solution)/shard_map/ppermute | solution.py:492
  72.0 6.1 %collective-permute-start.20 = (bf16[96,384]{1,0:T(8,128)(2,1)S(1)}, bf16[96,384]{1,0:T(8,128)(2,1)S(1)}, u32[]{:S(2)}, u32[]{:S(2)}) collective-permute-start(bf16[96,384]{1,0:T(8,128)(2,1)S(1)} %get-tuple-element.48), channel_id=1, source_target_pairs={{0,8},{4,12},{8,0},{12,4},{1,9},{5,13},{9,1},{13,5},{2,10},{6,14},... | collective-permute-start | bytes 221192 | tf_op jit(solution)/shard_map/ppermute | solution.py:492
  73.2 6.3 %collective-permute-start.21 = (bf16[96,384]{1,0:T(8,128)(2,1)S(1)}, bf16[96,384]{1,0:T(8,128)(2,1)S(1)}, u32[]{:S(2)}, u32[]{:S(2)}) collective-permute-start(bf16[96,384]{1,0:T(8,128)(2,1)S(1)} %get-tuple-element.49), channel_id=1, source_target_pairs={{0,12},{4,8},{8,4},{12,0},{1,13},{5,9},{9,5},{13,1},{2,14},{6,10},... | collective-permute-start | bytes 221192 | tf_op jit(solution)/shard_map/ppermute | solution.py:492
  75.2 5.1 %collective-permute-start.22 = (bf16[96,384]{1,0:T(8,128)(2,1)S(1)}, bf16[96,384]{1,0:T(8,128)(2,1)S(1)}, u32[]{:S(2)}, u32[]{:S(2)}) collective-permute-start(bf16[96,384]{1,0:T(8,128)(2,1)S(1)} %get-tuple-element.50), channel_id=1, source_target_pairs={{0,4},{4,0},{8,12},{12,8},{1,5},{5,1},{9,13},{13,9},{2,6},{6,2},{1... | collective-permute-start | bytes 221192 | tf_op jit(solution)/shard_map/ppermute | solution.py:492

commit v8 on v7

--- a/solution.py
+++ b/solution.py
@@ -94,7 +94,7 @@
         filled = jnp.sum(live.astype(F32)).astype(jnp.int32)
         first = jnp.sum(jnp.where((line == 0) & (spot == 0), numbers, 0.0)).astype(jnp.int32)
         fills.append(filled)
-        wide[index, :, :] = block[: 3 * slots, :].astype(F32)
+        wide[index, : 3 * slots, :] = block[: 3 * slots, :].astype(F32)
         for turn in range(CLIPS):
             clip = lax.rem(first + turn, CLIPS)
             base = pl.multiple_of((clip * 4 + index) * count, count)
@@ -284,7 +284,7 @@
         in_specs=[VMEM] * 4 + [ANY] * (len(early) - 3) + [VMEM] * 3,
         out_specs=[VMEM] * 4,
         scratch_shapes=[pltpu.VMEM((4 * slots, 256), BF16)] * 3
-        + [pltpu.VMEM((4, 3 * slots, 128), F32), pltpu.VMEM((4 * slots, 128), F32)],
+        + [pltpu.VMEM((4, 3 * slots + 8, 128), F32), pltpu.VMEM((4 * slots, 128), F32)],
         compiler_params=params(28),
         cost_estimate=cost(2**32, 2**21),
         name="attend",

time: 81.3 us -> 81.3 us (level)
  no operation moved by 1% of the time
where the time goes in v8:
time: 81.3 us; the launch traced here: 81 us
  starting transfers between devices  37.3 us (46%)
  waiting for transfers between devices  23.9 us (29%)
  Pallas kernels  19 us (23%)
    ppermute x6, starting transfers between devices, hop(): return lax.ppermute(value, ('cfg', 'seq'), pairs)  18.4 us
    ppermute x15, starting transfers between devices, exchanged(): return lax.ppermute(value, axis, pairs)  14.4 us
    ppermute x15, waiting for transfers between devices, exchanged(): return lax.ppermute(value, axis, pairs)  14 us
    ppermute x6, waiting for transfers between devices, hop(): return lax.ppermute(value, ('cfg', 'seq'), pairs)  9.84 us
    pallas_call x2, Pallas kernels, feed(): pl.pallas_call(functools.partial(feed_kernel, turn, len(att)), out_shape=...  5.95 us
    ppermute x2, starting transfers between devices, across(): return lax.ppermute(value, ('cfg', 'blk'), pairs)  4.52 us
    pallas_call x1, Pallas kernels, load(): pl.pallas_call(load_kernel, out_shape=[pltpu.VMEM(array.shape, BF16) for...  4.07 us
    pallas_call x1, Pallas kernels, attention_by_head(): pl.pallas_call(attend_kernel, out_shape=[shape_of((slots, 128))] * 4, in_...  2.09 us
  transfers between devices with their start and end apart: 23, of which 9 were waited for; matrix products, arithmetic and copies ran while one was open for 1% of the time, Pallas kernels for 20%

profile of v8, /device:TPU:0, one launch (start us, length us, event | category | flops | bytes accessed | tf_op | source)
XLA Modules:
  0.0 81.0 jit_solution(2160347040578447875)
XLA Ops:
  0.0 2.9 %collective-permute-start.3 = (bf16[384,1536]{1,0:T(8,128)(2,1)}, bf16[384,1536]{1,0:T(8,128)(2,1)S(1)}, u32[]{:S(2)}, u32[]{:S(2)}) collective-permute-start(bf16[384,1536]{1,0:T(8,128)(2,1)} %own.1), channel_id=1, source_target_pairs={{0,1},{1,0},{2,3},{3,2},{16,18},{17,19},{18,16},{19,17},{4,5},{5,4... | collective-permute-start | bytes 3538952 | tf_op jit(solution)/shard_map/ppermute | solution.py:188
  2.9 1.3 %pack.1 = (bf16[1168,128]{1,0:T(8,128)(2,1)S(1)}, bf16[1168,128]{1,0:T(8,128)(2,1)S(1)}, bf16[1168,128]{1,0:T(8,128)(2,1)S(1)}, bf16[1168,128]{1,0:T(8,128)(2,1)S(1)}) custom-call(bf16[384,384]{1,0:T(8,128)(2,1)} %bitcast.7, bf16[384,384]{1,0:T(8,128)(2,1)} %bitcast.8, bf16[384,384]{1,0:T(8,128)(2,1)} %bitcast.9, s32[3,128]{1,0:T(4,128)} %bitcast.12), custom_call_target="tpu_custom_call" | custom-call | tf_op jit(solution)/shard_map/pack/pallas_call | solution.py:266
  4.2 4.5 %collective-permute-start = (bf16[1168,128]{1,0:T(8,128)(2,1)S(1)}, bf16[1168,128]{1,0:T(8,128)(2,1)S(1)}, u32[]{:S(2)}, u32[]{:S(2)}) collective-permute-start(bf16[1168,128]{1,0:T(8,128)(2,1)S(1)} %get-tuple-element.29), channel_id=1, source_target_pairs={{0,8},{8,0},{12,4},{16,24},{20,28},{28,20},{1,9},{9,1},{13,5},{17,... | collective-permute-start | bytes 897032 | tf_op jit(solution)/shard_map/ppermute | solution.py:53
  8.7 1.3 %collective-permute-start.1 = (bf16[1168,128]{1,0:T(8,128)(2,1)S(1)}, bf16[1168,128]{1,0:T(8,128)(2,1)S(1)}, u32[]{:S(2)}, u32[]{:S(2)}) collective-permute-start(bf16[1168,128]{1,0:T(8,128)(2,1)S(1)} %get-tuple-element.30), channel_id=1, source_target_pairs={{4,8},{8,4},{12,0},{16,28},{20,24},{24,20},{5,9},{9,5},{13,1},{17,... | collective-permute-start | bytes 897032 | tf_op jit(solution)/shard_map/ppermute | solution.py:53
  10.0 3.4 %collective-permute-start.2 = (bf16[1168,128]{1,0:T(8,128)(2,1)S(1)}, bf16[1168,128]{1,0:T(8,128)(2,1)S(1)}, u32[]{:S(2)}, u32[]{:S(2)}) collective-permute-start(bf16[1168,128]{1,0:T(8,128)(2,1)S(1)} %get-tuple-element.31), channel_id=1, source_target_pairs={{0,4},{4,0},{12,8},{16,20},{24,28},{28,24},{1,5},{5,1},{13,9},{17,... | collective-permute-start | bytes 897032 | tf_op jit(solution)/shard_map/ppermute | solution.py:53
  13.5 0.1 constant_dynamic-slice_fusion
  13.5 0.2 convert_reduce_fusion
  13.7 0.0 copy-start.5
  13.7 4.1 %load.1 = (bf16[1536,1536]{1,0:T(8,128)(2,1)S(1)}, bf16[1536,1536]{1,0:T(8,128)(2,1)S(1)}, bf16[384,1536]{1,0:T(8,128)(2,1)S(1)}) custom-call(bf16[1536,1536]{1,0:T(8,128)(2,1)} %refs_0_.1, bf16[1536,1536]{1,0:T(8,128)(2,1)} %refs_1_.1, bf16[384,1536]{1,0:T(8,128)(2,1)} %bitcast.13, bf16[1168,128]{1,0:T(8,128)(2,1)S(1)} %get-tuple-element.28.refs_3_.refs_0_), custom_call_target="tpu_custom_call" | custom-call | flops 17179869184 | bytes 16777216 | tf_op jit(solution)/shard_map/load/pallas_call | solution.py:172
  17.8 0.1 compare_select_fusion
  17.9 0.1 cut.1.refs_6_
  18.0 1.6 %collective-permute-start.9 = (bf16[192,1536]{1,0:T(8,128)(2,1)S(1)}, bf16[192,1536]{1,0:T(8,128)(2,1)S(1)}, u32[]{:S(2)}, u32[]{:S(2)}) collective-permute-start(bf16[192,1536]{1,0:T(8,128)(2,1)S(1)} %cut.1.refs_6_), channel_id=1, source_target_pairs={{0,2},{1,3},{2,0},{3,1},{16,17},{17,16},{18,19},{19,18},{4,6},{5,7... | collective-permute-start | bytes 1769480 | tf_op jit(solution)/shard_map/ppermute | solution.py:188
  19.7 6.4 %collective-permute-done.refs_1_ = bf16[1168,128]{1,0:T(8,128)(2,1)S(1)} collective-permute-done((bf16[1168,128]{1,0:T(8,128)(2,1)S(1)}, bf16[1168,128]{1,0:T(8,128)(2,1)S(1)}, u32[]{:S(2)}, u32[]{:S(2)}) %collective-permute-start) | collective-permute-done | bytes 299040 | tf_op jit(solution)/shard_map/ppermute | solution.py:53
  26.1 0.1 broadcast_in_dim.7.refs_4_.refs_6_.refs_9_.clip_ref
  26.2 2.1 %attend.1 = (bf16[384,128]{1,0:T(8,128)(2,1)S(1)}, bf16[384,128]{1,0:T(8,128)(2,1)S(1)}, bf16[384,128]{1,0:T(8,128)(2,1)S(1)}, bf16[384,128]{1,0:T(8,128)(2,1)S(1)}) custom-call(bf16[1168,128]{1,0:T(8,128)(2,1)S(1)} %get-tuple-element.28.refs_3_.refs_0_, bf16[1168,128]{1,0:T(8,128)(2,1)S(1)} %collective-permute-done.refs_1_, ...), custom_call_target="tpu_custom_call" | custom-call | flops 4294967296 | bytes 2097152 | tf_op jit(solution)/shard_map/attend/pallas_call | solution.py:281
  28.3 4.7 %collective-permute-start.4 = (bf16[384,128]{1,0:T(8,128)(2,1)S(1)}, bf16[384,128]{1,0:T(8,128)(2,1)S(1)}, u32[]{:S(2)}, u32[]{:S(2)}) collective-permute-start(bf16[384,128]{1,0:T(8,128)(2,1)S(1)} %get-tuple-element.36), channel_id=1, source_target_pairs={{8,0},{0,8},{4,12},{24,16},{28,20},{20,28},{9,1},{1,9},{5,13},{25,... | collective-permute-start | bytes 294920 | tf_op jit(solution)/shard_map/ppermute | solution.py:53
  33.1 1.3 %collective-permute-start.5 = (bf16[384,128]{1,0:T(8,128)(2,1)S(1)}, bf16[384,128]{1,0:T(8,128)(2,1)S(1)}, u32[]{:S(2)}, u32[]{:S(2)}) collective-permute-start(bf16[384,128]{1,0:T(8,128)(2,1)S(1)} %get-tuple-element.37), channel_id=1, source_target_pairs={{8,4},{4,8},{0,12},{28,16},{24,20},{20,24},{9,5},{5,9},{1,13},{29,... | collective-permute-start | bytes 294920 | tf_op jit(solution)/shard_map/ppermute | solution.py:53
  34.4 3.2 %collective-permute-start.6 = (bf16[384,128]{1,0:T(8,128)(2,1)S(1)}, bf16[384,128]{1,0:T(8,128)(2,1)S(1)}, u32[]{:S(2)}, u32[]{:S(2)}) collective-permute-start(bf16[384,128]{1,0:T(8,128)(2,1)S(1)} %get-tuple-element.38), channel_id=1, source_target_pairs={{4,0},{0,4},{8,12},{20,16},{28,24},{24,28},{5,1},{1,5},{9,13},{21,... | collective-permute-start | bytes 294920 | tf_op jit(solution)/shard_map/ppermute | solution.py:53
  37.6 3.4 %collective-permute-done.6.back3 = bf16[384,128]{1,0:T(8,128)(2,1)S(1)} collective-permute-done((bf16[384,128]{1,0:T(8,128)(2,1)S(1)}, bf16[384,128]{1,0:T(8,128)(2,1)S(1)}, u32[]{:S(2)}, u32[]{:S(2)}) %collective-permute-start.6) | collective-permute-done | bytes 98336 | tf_op jit(solution)/shard_map/ppermute | solution.py:53
  41.0 0.3 regroup.1
  41.3 0.1 collective-permute-start.10
  41.4 1.3 %collective-permute-start.13 = (bf16[192,384]{1,0:T(8,128)(2,1)S(1)}, bf16[192,384]{1,0:T(8,128)(2,1)S(1)}, u32[]{:S(2)}, u32[]{:S(2)}) collective-permute-start(bf16[192,384]{1,0:T(8,128)(2,1)S(1)} %get-tuple-element.40.after.refs_0_), channel_id=1, source_target_pairs={{0,1},{1,0},{2,3},{3,2},{4,5},{5,4},{6,7},{7,6},{8,9},{9,8},{10,11... | collective-permute-start | bytes 442376 | tf_op jit(solution)/shard_map/ppermute | solution.py:492
  42.7 0.9 %collective-permute-start.14 = (bf16[192,384]{1,0:T(8,128)(2,1)S(1)}, bf16[192,384]{1,0:T(8,128)(2,1)S(1)}, u32[]{:S(2)}, u32[]{:S(2)}) collective-permute-start(bf16[192,384]{1,0:T(8,128)(2,1)S(1)} %get-tuple-element.40.after.refs_0_), channel_id=1, source_target_pairs={{0,2},{1,3},{2,0},{3,1},{4,6},{5,7},{6,4},{7,5},{8,10},{9,11},{10,... | collective-permute-start | bytes 442376 | tf_op jit(solution)/shard_map/ppermute | solution.py:492
  43.6 1.3 %collective-permute-start.15 = (bf16[192,384]{1,0:T(8,128)(2,1)S(1)}, bf16[192,384]{1,0:T(8,128)(2,1)S(1)}, u32[]{:S(2)}, u32[]{:S(2)}) collective-permute-start(bf16[192,384]{1,0:T(8,128)(2,1)S(1)} %get-tuple-element.40.after.refs_0_), channel_id=1, source_target_pairs={{0,3},{1,2},{2,1},{3,0},{4,7},{5,6},{6,5},{7,4},{8,11},{9,10},{10,... | collective-permute-start | bytes 442376 | tf_op jit(solution)/shard_map/ppermute | solution.py:492
  45.0 1.2 %collective-permute-start.11 = (bf16[192,384]{1,0:T(8,128)(2,1)S(1)}, bf16[192,384]{1,0:T(8,128)(2,1)S(1)}, u32[]{:S(2)}, u32[]{:S(2)}) collective-permute-start(bf16[192,384]{1,0:T(8,128)(2,1)S(1)} %get-tuple-element.39.refs_0_), channel_id=1, source_target_pairs={{0,1},{1,0},{2,3},{3,2},{4,5},{5,4},{6,7},{7,6},{8,9},{9,8},{10,11... | collective-permute-start | bytes 442376 | tf_op jit(solution)/shard_map/ppermute | solution.py:492
  46.2 0.9 %collective-permute-start.12 = (bf16[192,384]{1,0:T(8,128)(2,1)S(1)}, bf16[192,384]{1,0:T(8,128)(2,1)S(1)}, u32[]{:S(2)}, u32[]{:S(2)}) collective-permute-start(bf16[192,384]{1,0:T(8,128)(2,1)S(1)} %get-tuple-element.39.refs_0_), channel_id=1, source_target_pairs={{0,2},{1,3},{2,0},{3,1},{4,6},{5,7},{6,4},{7,5},{8,10},{9,11},{10,... | collective-permute-start | bytes 442376 | tf_op jit(solution)/shard_map/ppermute | solution.py:492
  47.1 1.3 %join.1.refs_3_.refs_1_.refs_4_ = bf16[1536,1536]{1,0:T(8,128)(2,1)S(1)} custom-call(bf16[384,1536]{1,0:T(8,128)(2,1)} %own.1, bf16[384,1536]{1,0:T(8,128)(2,1)S(1)} %collective-permute-done.3.got.near, bf16[384,1536]{1,0:T(8,128)(2,1)S(1)} %collective-permute-done.8.near_swap, bf16[192,1536]{1,0:T(8,128)(2,1)S(1)} %gate.1.far, ...), custom_call_target="tpu_custom_call" | custom-call | tf_op jit(solution)/shard_map/join/pallas_call | solution.py:253
  48.5 1.4 %collective-permute-start.7 = (bf16[192,384]{1,0:T(8,128)(2,1)S(1)}, bf16[192,384]{1,0:T(8,128)(2,1)S(1)}, u32[]{:S(2)}, u32[]{:S(2)}) collective-permute-start(bf16[192,384]{1,0:T(8,128)(2,1)S(1)} %get-tuple-element.39.refs_0_), channel_id=1, source_target_pairs={{0,3},{1,2},{2,1},{3,0},{4,7},{5,6},{6,5},{7,4},{8,11},{9,10},{10,... | collective-permute-start | bytes 442376 | tf_op jit(solution)/shard_map/ppermute | solution.py:492
  49.9 2.7 %collective-permute-done.14.refs_2_ = bf16[192,384]{1,0:T(8,128)(2,1)S(1)} collective-permute-done((bf16[192,384]{1,0:T(8,128)(2,1)S(1)}, bf16[192,384]{1,0:T(8,128)(2,1)S(1)}, u32[]{:S(2)}, u32[]{:S(2)}) %collective-permute-start.14) | collective-permute-done | bytes 147488 | tf_op jit(solution)/shard_map/ppermute | solution.py:492
  52.6 3.7 %feed.3 = bf16[192,1536]{1,0:T(8,128)(2,1)S(1)} custom-call(bf16[192,384]{1,0:T(8,128)(2,1)S(1)} %get-tuple-element.40.after.refs_0_, bf16[192,384]{1,0:T(8,128)(2,1)S(1)} %collective-permute-done.13.refs_1_, bf16[192,384]{1,0:T(8,128)(2,1)S(1)} %collective-permute-done.14.refs_2_, bf16[192,384]{1,0:T(8,128)(2,1)S(1)} %collective-permute-done.15.refs_3_, ...), custom_call_target="tpu_custom_call" | custom-call | flops 68719476736 | bytes 16777216 | tf_op jit(solution)/shard_map/feed/pallas_call | solution.py:440
  56.3 0.1 collective-permute-start.16
  56.4 1.7 %collective-permute-done.12.refs_2_ = bf16[192,384]{1,0:T(8,128)(2,1)S(1)} collective-permute-done((bf16[192,384]{1,0:T(8,128)(2,1)S(1)}, bf16[192,384]{1,0:T(8,128)(2,1)S(1)}, u32[]{:S(2)}, u32[]{:S(2)}) %collective-permute-start.12) | collective-permute-done | bytes 147488 | tf_op jit(solution)/shard_map/ppermute | solution.py:492
  58.1 0.9 %project.1.refs_7_ = f32[192,1536]{1,0:T(8,128)S(1)} custom-call(bf16[192,384]{1,0:T(8,128)(2,1)S(1)} %get-tuple-element.39.refs_0_, bf16[192,384]{1,0:T(8,128)(2,1)S(1)} %collective-permute-done.11.refs_1_, bf16[192,384]{1,0:T(8,128)(2,1)S(1)} %collective-permute-done.12.refs_2_, bf16[1536,1536]{1,0:T(8,128)(2,1)S(1)} %join.1.refs_3_.refs_1_.refs_4_), custom_call_target="tpu_custom_call" | custom-call | flops 4294967296 | bytes 4194304 | tf_op jit(solution)/shard_map/project/pallas_call | solution.py:379
  59.1 2.2 %feed.2 = (bf16[192,1536]{1,0:T(8,128)(2,1)S(1)}, f32[192,1536]{1,0:T(8,128)S(1)}) custom-call(bf16[192,384]{1,0:T(8,128)(2,1)S(1)} %collective-permute-done.7.refs_0_, bf16[1536,1536]{1,0:T(8,128)(2,1)S(1)} %join.1.refs_3_.refs_1_.refs_4_, bf16[1536,1536]{1,0:T(8,128)(2,1)S(1)} %get-tuple-element.32.refs_7_.refs_2_.refs_5_, ...), custom_call_target="tpu_custom_call" | custom-call | flops 68719476736 | bytes 16777216 | tf_op jit(solution)/shard_map/feed/pallas_call | solution.py:440
  61.3 1.9 %guide.1 = (f32[192,384]{1,0:T(8,128)S(1)}, bf16[192,384]{1,0:T(8,128)(2,1)S(1)}, bf16[192,384]{1,0:T(8,128)(2,1)S(1)}, bf16[192,384]{1,0:T(8,128)(2,1)S(1)}) custom-call(bf16[192,1536]{1,0:T(8,128)(2,1)S(1)} %get-tuple-element.41.hidden, f32[192,1536]{1,0:T(8,128)S(1)} %get-tuple-element.42.mixed, ...), custom_call_target="tpu_custom_call" | custom-call | tf_op jit(solution)/shard_map/guide/pallas_call | solution.py:540
  63.2 0.9 %collective-permute-start.17 = (bf16[192,384]{1,0:T(8,128)(2,1)S(1)}, bf16[192,384]{1,0:T(8,128)(2,1)S(1)}, u32[]{:S(2)}, u32[]{:S(2)}) collective-permute-start(bf16[192,384]{1,0:T(8,128)(2,1)S(1)} %get-tuple-element.44), channel_id=1, source_target_pairs={{0,1},{1,0},{2,3},{3,2},{4,5},{5,4},{6,7},{7,6},{8,9},{9,8},{10,11... | collective-permute-start | bytes 442376 | tf_op jit(solution)/shard_map/ppermute | solution.py:492
  64.1 0.2 collective-permute-start.18
  64.3 2.5 %collective-permute-start.19 = (bf16[192,384]{1,0:T(8,128)(2,1)S(1)}, bf16[192,384]{1,0:T(8,128)(2,1)S(1)}, u32[]{:S(2)}, u32[]{:S(2)}) collective-permute-start(bf16[192,384]{1,0:T(8,128)(2,1)S(1)} %get-tuple-element.46), channel_id=1, source_target_pairs={{0,3},{1,2},{2,1},{3,0},{4,7},{5,6},{6,5},{7,4},{8,11},{9,10},{10,... | collective-permute-start | bytes 442376 | tf_op jit(solution)/shard_map/ppermute | solution.py:492
  66.8 2.6 %collective-permute-done.17.got1 = bf16[192,384]{1,0:T(8,128)(2,1)S(1)} collective-permute-done((bf16[192,384]{1,0:T(8,128)(2,1)S(1)}, bf16[192,384]{1,0:T(8,128)(2,1)S(1)}, u32[]{:S(2)}, u32[]{:S(2)}) %collective-permute-start.17) | collective-permute-done | bytes 147488 | tf_op jit(solution)/shard_map/ppermute | solution.py:492
  69.4 2.3 %collective-permute-done.18.got2 = bf16[192,384]{1,0:T(8,128)(2,1)S(1)} collective-permute-done((bf16[192,384]{1,0:T(8,128)(2,1)S(1)}, bf16[192,384]{1,0:T(8,128)(2,1)S(1)}, u32[]{:S(2)}, u32[]{:S(2)}) %collective-permute-start.18) | collective-permute-done | bytes 147488 | tf_op jit(solution)/shard_map/ppermute | solution.py:492
  71.7 0.3 place.1
  72.0 1.2 %collective-permute-start.20 = (bf16[96,384]{1,0:T(8,128)(2,1)S(1)}, bf16[96,384]{1,0:T(8,128)(2,1)S(1)}, u32[]{:S(2)}, u32[]{:S(2)}) collective-permute-start(bf16[96,384]{1,0:T(8,128)(2,1)S(1)} %get-tuple-element.48), channel_id=1, source_target_pairs={{0,8},{4,12},{8,0},{12,4},{1,9},{5,13},{9,1},{13,5},{2,10},{6,14},... | collective-permute-start | bytes 221192 | tf_op jit(solution)/shard_map/ppermute | solution.py:492
  73.2 2.0 %collective-permute-start.21 = (bf16[96,384]{1,0:T(8,128)(2,1)S(1)}, bf16[96,384]{1,0:T(8,128)(2,1)S(1)}, u32[]{:S(2)}, u32[]{:S(2)}) collective-permute-start(bf16[96,384]{1,0:T(8,128)(2,1)S(1)} %get-tuple-element.49), channel_id=1, source_target_pairs={{0,12},{4,8},{8,4},{12,0},{1,13},{5,9},{9,5},{13,1},{2,14},{6,10},... | collective-permute-start | bytes 221192 | tf_op jit(solution)/shard_map/ppermute | solution.py:492
  75.2 0.4 collective-permute-start.22
  75.6 2.6 %collective-permute-done.20.refs_1_ = bf16[96,384]{1,0:T(8,128)(2,1)S(1)} collective-permute-done((bf16[96,384]{1,0:T(8,128)(2,1)S(1)}, bf16[96,384]{1,0:T(8,128)(2,1)S(1)}, u32[]{:S(2)}, u32[]{:S(2)}) %collective-permute-start.20) | collective-permute-done | bytes 73760 | tf_op jit(solution)/shard_map/ppermute | solution.py:492
  78.1 1.4 %collective-permute-done.21.refs_2_ = bf16[96,384]{1,0:T(8,128)(2,1)S(1)} collective-permute-done((bf16[96,384]{1,0:T(8,128)(2,1)S(1)}, bf16[96,384]{1,0:T(8,128)(2,1)S(1)}, u32[]{:S(2)}, u32[]{:S(2)}) %collective-permute-start.21) | collective-permute-done | bytes 73760 | tf_op jit(solution)/shard_map/ppermute | solution.py:492
  79.5 0.7 collective-permute-done.22.refs_3_
  80.2 0.8 arrange.1
  (28 shorter events, 0.1 us)
Async XLA Ops:
  0.0 13.5 %copy-start = (s32[384,1]{0,1:T(1,128)S(1)}, s32[384,1]{0,1:T(1,128)}, u32[]{:S(2)}) copy-start(s32[384,1]{0,1:T(1,128)} %param.21) | copy-start | bytes 4612
  0.0 17.9 %collective-permute-start.3 = (bf16[384,1536]{1,0:T(8,128)(2,1)}, bf16[384,1536]{1,0:T(8,128)(2,1)S(1)}, u32[]{:S(2)}, u32[]{:S(2)}) collective-permute-start(bf16[384,1536]{1,0:T(8,128)(2,1)} %own.1), channel_id=1, source_target_pairs={{0,1},{1,0},{2,3},{3,2},{16,18},{17,19},{18,16},{19,17},{4,5},{5,4... | collective-permute-start | bytes 3538952 | tf_op jit(solution)/shard_map/ppermute | solution.py:188
  4.2 21.9 %collective-permute-start = (bf16[1168,128]{1,0:T(8,128)(2,1)S(1)}, bf16[1168,128]{1,0:T(8,128)(2,1)S(1)}, u32[]{:S(2)}, u32[]{:S(2)}) collective-permute-start(bf16[1168,128]{1,0:T(8,128)(2,1)S(1)} %get-tuple-element.29), channel_id=1, source_target_pairs={{0,8},{8,0},{12,4},{16,24},{20,28},{28,20},{1,9},{9,1},{13,5},{17,... | collective-permute-start | bytes 897032 | tf_op jit(solution)/shard_map/ppermute | solution.py:53
  8.7 17.4 %collective-permute-start.1 = (bf16[1168,128]{1,0:T(8,128)(2,1)S(1)}, bf16[1168,128]{1,0:T(8,128)(2,1)S(1)}, u32[]{:S(2)}, u32[]{:S(2)}) collective-permute-start(bf16[1168,128]{1,0:T(8,128)(2,1)S(1)} %get-tuple-element.30), channel_id=1, source_target_pairs={{4,8},{8,4},{12,0},{16,28},{20,24},{24,20},{5,9},{9,5},{13,1},{17,... | collective-permute-start | bytes 897032 | tf_op jit(solution)/shard_map/ppermute | solution.py:53
  10.0 16.1 %collective-permute-start.2 = (bf16[1168,128]{1,0:T(8,128)(2,1)S(1)}, bf16[1168,128]{1,0:T(8,128)(2,1)S(1)}, u32[]{:S(2)}, u32[]{:S(2)}) collective-permute-start(bf16[1168,128]{1,0:T(8,128)(2,1)S(1)} %get-tuple-element.31), channel_id=1, source_target_pairs={{0,4},{4,0},{12,8},{16,20},{24,28},{28,24},{1,5},{5,1},{13,9},{17,... | collective-permute-start | bytes 897032 | tf_op jit(solution)/shard_map/ppermute | solution.py:53
  13.7 4.1 %copy-start.5 = (s32[384]{0:T(512)S(1)}, s32[384]{0:T(512)}, u32[]{:S(2)}) copy-start(s32[384]{0:T(512)} %param.20) | copy-start | bytes 4612
  18.0 23.3 %collective-permute-start.9 = (bf16[192,1536]{1,0:T(8,128)(2,1)S(1)}, bf16[192,1536]{1,0:T(8,128)(2,1)S(1)}, u32[]{:S(2)}, u32[]{:S(2)}) collective-permute-start(bf16[192,1536]{1,0:T(8,128)(2,1)S(1)} %cut.1.refs_6_), channel_id=1, source_target_pairs={{0,2},{1,3},{2,0},{3,1},{16,17},{17,16},{18,19},{19,18},{4,6},{5,7... | collective-permute-start | bytes 1769480 | tf_op jit(solution)/shard_map/ppermute | solution.py:188
  19.6 26.6 %collective-permute-start.8 = (bf16[384,1536]{1,0:T(8,128)(2,1)S(1)}, bf16[384,1536]{1,0:T(8,128)(2,1)S(1)}, u32[]{:S(2)}, u32[]{:S(2)}) collective-permute-start(bf16[384,1536]{1,0:T(8,128)(2,1)S(1)} %collective-permute-done.3.got.near), channel_id=1, source_target_pairs={{0,16},{16,0},{1,17},{17,1},{2,18},{18,2},{3,19},{19,3},{4,20},{20... | collective-permute-start | bytes 3538952 | tf_op jit(solution)/shard_map/ppermute | solution.py:492
  19.7 8.6 %copy-start.1 = (bf16[384,192]{1,0:T(8,128)(2,1)}, bf16[384,192]{1,0:T(8,128)(2,1)S(1)}, u32[]{:S(2)}) copy-start(bf16[384,192]{1,0:T(8,128)(2,1)S(1)} %fusion.refs_5_.placing) | copy-start | bytes 442372
  28.3 9.2 %collective-permute-start.4 = (bf16[384,128]{1,0:T(8,128)(2,1)S(1)}, bf16[384,128]{1,0:T(8,128)(2,1)S(1)}, u32[]{:S(2)}, u32[]{:S(2)}) collective-permute-start(bf16[384,128]{1,0:T(8,128)(2,1)S(1)} %get-tuple-element.36), channel_id=1, source_target_pairs={{8,0},{0,8},{4,12},{24,16},{28,20},{20,28},{9,1},{1,9},{5,13},{25,... | collective-permute-start | bytes 294920 | tf_op jit(solution)/shard_map/ppermute | solution.py:53
  33.1 4.5 %collective-permute-start.5 = (bf16[384,128]{1,0:T(8,128)(2,1)S(1)}, bf16[384,128]{1,0:T(8,128)(2,1)S(1)}, u32[]{:S(2)}, u32[]{:S(2)}) collective-permute-start(bf16[384,128]{1,0:T(8,128)(2,1)S(1)} %get-tuple-element.37), channel_id=1, source_target_pairs={{8,4},{4,8},{0,12},{28,16},{24,20},{20,24},{9,5},{5,9},{1,13},{29,... | collective-permute-start | bytes 294920 | tf_op jit(solution)/shard_map/ppermute | solution.py:53
  34.4 6.6 %collective-permute-start.6 = (bf16[384,128]{1,0:T(8,128)(2,1)S(1)}, bf16[384,128]{1,0:T(8,128)(2,1)S(1)}, u32[]{:S(2)}, u32[]{:S(2)}) collective-permute-start(bf16[384,128]{1,0:T(8,128)(2,1)S(1)} %get-tuple-element.38), channel_id=1, source_target_pairs={{4,0},{0,4},{8,12},{20,16},{28,24},{24,28},{5,1},{1,5},{9,13},{21,... | collective-permute-start | bytes 294920 | tf_op jit(solution)/shard_map/ppermute | solution.py:53
  41.3 3.6 %collective-permute-start.10 = (bf16[192,1536]{1,0:T(8,128)(2,1)S(1)}, bf16[192,1536]{1,0:T(8,128)(2,1)S(1)}, u32[]{:S(2)}, u32[]{:S(2)}) collective-permute-start(bf16[192,1536]{1,0:T(8,128)(2,1)S(1)} %gate.1.far), channel_id=1, source_target_pairs={{0,16},{16,0},{1,17},{17,1},{2,18},{18,2},{3,19},{19,3},{4,20},{20... | collective-permute-start | bytes 1769480 | tf_op jit(solution)/shard_map/ppermute | solution.py:492
  41.4 7.0 %collective-permute-start.13 = (bf16[192,384]{1,0:T(8,128)(2,1)S(1)}, bf16[192,384]{1,0:T(8,128)(2,1)S(1)}, u32[]{:S(2)}, u32[]{:S(2)}) collective-permute-start(bf16[192,384]{1,0:T(8,128)(2,1)S(1)} %get-tuple-element.40.after.refs_0_), channel_id=1, source_target_pairs={{0,1},{1,0},{2,3},{3,2},{4,5},{5,4},{6,7},{7,6},{8,9},{9,8},{10,11... | collective-permute-start | bytes 442376 | tf_op jit(solution)/shard_map/ppermute | solution.py:492
  42.7 9.9 %collective-permute-start.14 = (bf16[192,384]{1,0:T(8,128)(2,1)S(1)}, bf16[192,384]{1,0:T(8,128)(2,1)S(1)}, u32[]{:S(2)}, u32[]{:S(2)}) collective-permute-start(bf16[192,384]{1,0:T(8,128)(2,1)S(1)} %get-tuple-element.40.after.refs_0_), channel_id=1, source_target_pairs={{0,2},{1,3},{2,0},{3,1},{4,6},{5,7},{6,4},{7,5},{8,10},{9,11},{10,... | collective-permute-start | bytes 442376 | tf_op jit(solution)/shard_map/ppermute | solution.py:492
  43.6 9.0 %collective-permute-start.15 = (bf16[192,384]{1,0:T(8,128)(2,1)S(1)}, bf16[192,384]{1,0:T(8,128)(2,1)S(1)}, u32[]{:S(2)}, u32[]{:S(2)}) collective-permute-start(bf16[192,384]{1,0:T(8,128)(2,1)S(1)} %get-tuple-element.40.after.refs_0_), channel_id=1, source_target_pairs={{0,3},{1,2},{2,1},{3,0},{4,7},{5,6},{6,5},{7,4},{8,11},{9,10},{10,... | collective-permute-start | bytes 442376 | tf_op jit(solution)/shard_map/ppermute | solution.py:492
  45.0 7.6 %copy-start.3 = (f32[3,4,1536]{2,1,0:T(4,128)S(1)}, f32[3,4,1536]{2,1,0:T(4,128)}, u32[]{:S(2)}) copy-start(f32[3,4,1536]{2,1,0:T(4,128)} %mod.1) | copy-start | bytes 221188
  45.0 11.4 %collective-permute-start.11 = (bf16[192,384]{1,0:T(8,128)(2,1)S(1)}, bf16[192,384]{1,0:T(8,128)(2,1)S(1)}, u32[]{:S(2)}, u32[]{:S(2)}) collective-permute-start(bf16[192,384]{1,0:T(8,128)(2,1)S(1)} %get-tuple-element.39.refs_0_), channel_id=1, source_target_pairs={{0,1},{1,0},{2,3},{3,2},{4,5},{5,4},{6,7},{7,6},{8,9},{9,8},{10,11... | collective-permute-start | bytes 442376 | tf_op jit(solution)/shard_map/ppermute | solution.py:492
  46.2 11.9 %collective-permute-start.12 = (bf16[192,384]{1,0:T(8,128)(2,1)S(1)}, bf16[192,384]{1,0:T(8,128)(2,1)S(1)}, u32[]{:S(2)}, u32[]{:S(2)}) collective-permute-start(bf16[192,384]{1,0:T(8,128)(2,1)S(1)} %get-tuple-element.39.refs_0_), channel_id=1, source_target_pairs={{0,2},{1,3},{2,0},{3,1},{4,6},{5,7},{6,4},{7,5},{8,10},{9,11},{10,... | collective-permute-start | bytes 442376 | tf_op jit(solution)/shard_map/ppermute | solution.py:492
  48.5 10.6 %collective-permute-start.7 = (bf16[192,384]{1,0:T(8,128)(2,1)S(1)}, bf16[192,384]{1,0:T(8,128)(2,1)S(1)}, u32[]{:S(2)}, u32[]{:S(2)}) collective-permute-start(bf16[192,384]{1,0:T(8,128)(2,1)S(1)} %get-tuple-element.39.refs_0_), channel_id=1, source_target_pairs={{0,3},{1,2},{2,1},{3,0},{4,7},{5,6},{6,5},{7,4},{8,11},{9,10},{10,... | collective-permute-start | bytes 442376 | tf_op jit(solution)/shard_map/ppermute | solution.py:492
  56.3 5.0 %collective-permute-start.16 = (bf16[192,1536]{1,0:T(8,128)(2,1)S(1)}, bf16[192,1536]{1,0:T(8,128)(2,1)S(1)}, u32[]{:S(2)}, u32[]{:S(2)}) collective-permute-start(bf16[192,1536]{1,0:T(8,128)(2,1)S(1)} %feed.3), channel_id=1, source_target_pairs={{0,16},{16,0},{1,17},{17,1},{2,18},{18,2},{3,19},{19,3},{4,20},{20... | collective-permute-start | bytes 1769480 | tf_op jit(solution)/shard_map/ppermute | solution.py:492
  59.1 2.2 %copy-start.4 = (f32[3]{0:T(128)S(1)}, f32[3]{0:T(128)}, u32[]{:S(2)}) copy-start(f32[3]{0:T(128)} %scale_ref.1) | copy-start | bytes 40
  61.3 10.4 %copy-start.2 = (bf16[384,192]{1,0:T(8,128)(2,1)S(1)}, bf16[384,192]{1,0:T(8,128)(2,1)}, u32[]{:S(2)}) copy-start(bf16[384,192]{1,0:T(8,128)(2,1)} %copy-done.1) | copy-start | bytes 442372
  63.2 6.2 %collective-permute-start.17 = (bf16[192,384]{1,0:T(8,128)(2,1)S(1)}, bf16[192,384]{1,0:T(8,128)(2,1)S(1)}, u32[]{:S(2)}, u32[]{:S(2)}) collective-permute-start(bf16[192,384]{1,0:T(8,128)(2,1)S(1)} %get-tuple-element.44), channel_id=1, source_target_pairs={{0,1},{1,0},{2,3},{3,2},{4,5},{5,4},{6,7},{7,6},{8,9},{9,8},{10,11... | collective-permute-start | bytes 442376 | tf_op jit(solution)/shard_map/ppermute | solution.py:492
  64.1 7.6 %collective-permute-start.18 = (bf16[192,384]{1,0:T(8,128)(2,1)S(1)}, bf16[192,384]{1,0:T(8,128)(2,1)S(1)}, u32[]{:S(2)}, u32[]{:S(2)}) collective-permute-start(bf16[192,384]{1,0:T(8,128)(2,1)S(1)} %get-tuple-element.45), channel_id=1, source_target_pairs={{0,2},{1,3},{2,0},{3,1},{4,6},{5,7},{6,4},{7,5},{8,10},{9,11},{10,... | collective-permute-start | bytes 442376 | tf_op jit(solution)/shard_map/ppermute | solution.py:492
  64.3 7.5 %collective-permute-start.19 = (bf16[192,384]{1,0:T(8,128)(2,1)S(1)}, bf16[192,384]{1,0:T(8,128)(2,1)S(1)}, u32[]{:S(2)}, u32[]{:S(2)}) collective-permute-start(bf16[192,384]{1,0:T(8,128)(2,1)S(1)} %get-tuple-element.46), channel_id=1, source_target_pairs={{0,3},{1,2},{2,1},{3,0},{4,7},{5,6},{6,5},{7,4},{8,11},{9,10},{10,... | collective-permute-start | bytes 442376 | tf_op jit(solution)/shard_map/ppermute | solution.py:492
  72.0 6.1 %collective-permute-start.20 = (bf16[96,384]{1,0:T(8,128)(2,1)S(1)}, bf16[96,384]{1,0:T(8,128)(2,1)S(1)}, u32[]{:S(2)}, u32[]{:S(2)}) collective-permute-start(bf16[96,384]{1,0:T(8,128)(2,1)S(1)} %get-tuple-element.48), channel_id=1, source_target_pairs={{0,8},{4,12},{8,0},{12,4},{1,9},{5,13},{9,1},{13,5},{2,10},{6,14},... | collective-permute-start | bytes 221192 | tf_op jit(solution)/shard_map/ppermute | solution.py:492
  73.2 6.3 %collective-permute-start.21 = (bf16[96,384]{1,0:T(8,128)(2,1)S(1)}, bf16[96,384]{1,0:T(8,128)(2,1)S(1)}, u32[]{:S(2)}, u32[]{:S(2)}) collective-permute-start(bf16[96,384]{1,0:T(8,128)(2,1)S(1)} %get-tuple-element.49), channel_id=1, source_target_pairs={{0,12},{4,8},{8,4},{12,0},{1,13},{5,9},{9,5},{13,1},{2,14},{6,10},... | collective-permute-start | bytes 221192 | tf_op jit(solution)/shard_map/ppermute | solution.py:492
  75.2 5.1 %collective-permute-start.22 = (bf16[96,384]{1,0:T(8,128)(2,1)S(1)}, bf16[96,384]{1,0:T(8,128)(2,1)S(1)}, u32[]{:S(2)}, u32[]{:S(2)}) collective-permute-start(bf16[96,384]{1,0:T(8,128)(2,1)S(1)} %get-tuple-element.50), channel_id=1, source_target_pairs={{0,4},{4,0},{8,12},{12,8},{1,5},{5,1},{9,13},{13,9},{2,6},{6,2},{1... | collective-permute-start | bytes 221192 | tf_op jit(solution)/shard_map/ppermute | solution.py:492

commit v9 on v8

--- a/solution.py
+++ b/solution.py
@@ -456,7 +456,7 @@
     clip = clip_ref[pl.ds(pl.multiple_of(side * half, half), half), :][:, :1]
     strength = jnp.zeros((half, 1), F32)
     for index in range(CLIPS):
-        strength = jnp.where(clip == index, scale_ref[index], strength)
+        strength = jnp.where(clip == index, scale_ref[index : index + 1, :1], strength)
     lean = jnp.where(side == 0, strength, 1.0 - strength)
     for columns, mine in lowered_tiles(hidden, mixed, down, mod, clip):
         other = other_ref[:, columns].astype(F32)
@@ -502,6 +502,7 @@
     side, place = lax.axis_index("cfg"), lax.axis_index("seq")
 
     clip_wide = jnp.broadcast_to(slot_clip[:, None], (slots, 128))
+    scale_wide = jnp.broadcast_to(guide_scale[:, None], (CLIPS, 128))
     clip_half = lax.dynamic_slice_in_dim(slot_clip, side * half, half, 0)
     owner_half = lax.dynamic_slice_in_dim(owner[:, 0], side * half, half, 0)
     order = jnp.arange(half, dtype=jnp.int32)
@@ -523,7 +524,7 @@
             keys[0],
             values[0],
             slot_clip,
-            (clip_wide, placing, w_half),
+            (clip_wide, placing, w_half, scale_wide),
             (w_up, w_down, residual[0]),
         )
     else:
@@ -540,12 +541,12 @@
     own, *sent = pl.pallas_call(
         guide_kernel,
         out_shape=[shape_of((half, width), F32)] + [shape_of((half, width))] * 3,
-        in_specs=[VMEM] * 6 + [pl.BlockSpec(memory_space=pltpu.SMEM)],
+        in_specs=[VMEM] * 7,
         out_specs=[VMEM] * 4,
         scratch_shapes=[pltpu.VMEM((half, D), F32)],
         compiler_params=params(16),
         name="guide",
-    )(*parts[1], kept(down), other, clip_wide, modulation, guide_scale)
+    )(*parts[1], kept(down), other, clip_wide, modulation, scale_wide)
     got = [exchanged(piece, "blk", mask) for mask, piece in zip((1, 2, 3), sent)]
     by_step = seq_count == 4
     placed = pl.pallas_call(

time: 81.3 us -> 80.8 us (level)
  no operation moved by 1% of the time
where the time goes in v9:
time: 80.8 us; the launch traced here: 80.5 us
  starting transfers between devices  37.3 us (46%)
  waiting for transfers between devices  23.9 us (30%)
  Pallas kernels  18.4 us (23%)
    ppermute x6, starting transfers between devices, hop(): return lax.ppermute(value, ('cfg', 'seq'), pairs)  18.4 us
    ppermute x15, starting transfers between devices, exchanged(): return lax.ppermute(value, axis, pairs)  14.4 us
    ppermute x15, waiting for transfers between devices, exchanged(): return lax.ppermute(value, axis, pairs)  14 us
    ppermute x6, waiting for transfers between devices, hop(): return lax.ppermute(value, ('cfg', 'seq'), pairs)  9.83 us
    pallas_call x2, Pallas kernels, feed(): pl.pallas_call(functools.partial(feed_kernel, turn, len(att)), out_shape=...  5.92 us
    ppermute x2, starting transfers between devices, across(): return lax.ppermute(value, ('cfg', 'blk'), pairs)  4.52 us
    pallas_call x1, Pallas kernels, load(): pl.pallas_call(load_kernel, out_shape=[pltpu.VMEM(array.shape, BF16) for...  4.07 us
    pallas_call x1, Pallas kernels, attention_by_head(): pl.pallas_call(attend_kernel, out_shape=[shape_of((slots, 128))] * 4, in_...  2.08 us
  transfers between devices with their start and end apart: 23, of which 9 were waited for; matrix products, arithmetic and copies ran while one was open for 1% of the time, Pallas kernels for 20%

profile of v9, /device:TPU:0, one launch (start us, length us, event | category | flops | bytes accessed | tf_op | source)
XLA Modules:
  0.0 80.5 jit_solution(10060397602555265137)
XLA Ops:
  0.0 2.9 %collective-permute-start.3 = (bf16[384,1536]{1,0:T(8,128)(2,1)}, bf16[384,1536]{1,0:T(8,128)(2,1)S(1)}, u32[]{:S(2)}, u32[]{:S(2)}) collective-permute-start(bf16[384,1536]{1,0:T(8,128)(2,1)} %own.1), channel_id=1, source_target_pairs={{0,1},{1,0},{2,3},{3,2},{16,18},{17,19},{18,16},{19,17},{4,5},{5,4... | collective-permute-start | bytes 3538952 | tf_op jit(solution)/shard_map/ppermute | solution.py:188
  2.9 1.3 %pack.1 = (bf16[1168,128]{1,0:T(8,128)(2,1)S(1)}, bf16[1168,128]{1,0:T(8,128)(2,1)S(1)}, bf16[1168,128]{1,0:T(8,128)(2,1)S(1)}, bf16[1168,128]{1,0:T(8,128)(2,1)S(1)}) custom-call(bf16[384,384]{1,0:T(8,128)(2,1)} %bitcast.7, bf16[384,384]{1,0:T(8,128)(2,1)} %bitcast.8, bf16[384,384]{1,0:T(8,128)(2,1)} %bitcast.9, s32[3,128]{1,0:T(4,128)} %bitcast.12), custom_call_target="tpu_custom_call" | custom-call | tf_op jit(solution)/shard_map/pack/pallas_call | solution.py:266
  4.2 4.5 %collective-permute-start = (bf16[1168,128]{1,0:T(8,128)(2,1)S(1)}, bf16[1168,128]{1,0:T(8,128)(2,1)S(1)}, u32[]{:S(2)}, u32[]{:S(2)}) collective-permute-start(bf16[1168,128]{1,0:T(8,128)(2,1)S(1)} %get-tuple-element.29), channel_id=1, source_target_pairs={{0,8},{8,0},{12,4},{16,24},{20,28},{28,20},{1,9},{9,1},{13,5},{17,... | collective-permute-start | bytes 897032 | tf_op jit(solution)/shard_map/ppermute | solution.py:53
  8.7 1.3 %collective-permute-start.1 = (bf16[1168,128]{1,0:T(8,128)(2,1)S(1)}, bf16[1168,128]{1,0:T(8,128)(2,1)S(1)}, u32[]{:S(2)}, u32[]{:S(2)}) collective-permute-start(bf16[1168,128]{1,0:T(8,128)(2,1)S(1)} %get-tuple-element.30), channel_id=1, source_target_pairs={{4,8},{8,4},{12,0},{16,28},{20,24},{24,20},{5,9},{9,5},{13,1},{17,... | collective-permute-start | bytes 897032 | tf_op jit(solution)/shard_map/ppermute | solution.py:53
  10.0 3.4 %collective-permute-start.2 = (bf16[1168,128]{1,0:T(8,128)(2,1)S(1)}, bf16[1168,128]{1,0:T(8,128)(2,1)S(1)}, u32[]{:S(2)}, u32[]{:S(2)}) collective-permute-start(bf16[1168,128]{1,0:T(8,128)(2,1)S(1)} %get-tuple-element.31), channel_id=1, source_target_pairs={{0,4},{4,0},{12,8},{16,20},{24,28},{28,24},{1,5},{5,1},{13,9},{17,... | collective-permute-start | bytes 897032 | tf_op jit(solution)/shard_map/ppermute | solution.py:53
  13.5 0.1 constant_dynamic-slice_fusion
  13.5 0.2 convert_reduce_fusion
  13.7 4.1 %load.1 = (bf16[1536,1536]{1,0:T(8,128)(2,1)S(1)}, bf16[1536,1536]{1,0:T(8,128)(2,1)S(1)}, bf16[384,1536]{1,0:T(8,128)(2,1)S(1)}) custom-call(bf16[1536,1536]{1,0:T(8,128)(2,1)} %refs_0_.1, bf16[1536,1536]{1,0:T(8,128)(2,1)} %refs_1_.1, bf16[384,1536]{1,0:T(8,128)(2,1)} %bitcast.13, bf16[1168,128]{1,0:T(8,128)(2,1)S(1)} %get-tuple-element.28.refs_3_.refs_0_), custom_call_target="tpu_custom_call" | custom-call | flops 17179869184 | bytes 16777216 | tf_op jit(solution)/shard_map/load/pallas_call | solution.py:172
  17.8 0.1 compare_select_fusion
  17.9 0.1 cut.1.refs_6_
  18.1 1.6 %collective-permute-start.9 = (bf16[192,1536]{1,0:T(8,128)(2,1)S(1)}, bf16[192,1536]{1,0:T(8,128)(2,1)S(1)}, u32[]{:S(2)}, u32[]{:S(2)}) collective-permute-start(bf16[192,1536]{1,0:T(8,128)(2,1)S(1)} %cut.1.refs_6_), channel_id=1, source_target_pairs={{0,2},{1,3},{2,0},{3,1},{16,17},{17,16},{18,19},{19,18},{4,6},{5,7... | collective-permute-start | bytes 1769480 | tf_op jit(solution)/shard_map/ppermute | solution.py:188
  19.7 6.4 %collective-permute-done.refs_1_ = bf16[1168,128]{1,0:T(8,128)(2,1)S(1)} collective-permute-done((bf16[1168,128]{1,0:T(8,128)(2,1)S(1)}, bf16[1168,128]{1,0:T(8,128)(2,1)S(1)}, u32[]{:S(2)}, u32[]{:S(2)}) %collective-permute-start) | collective-permute-done | bytes 299040 | tf_op jit(solution)/shard_map/ppermute | solution.py:53
  26.1 0.1 broadcast_in_dim.9.refs_4_.refs_6_.refs_9_.clip_ref
  26.2 0.1 broadcast_in_dim.11.refs_7_.scale_ref
  26.3 2.1 %attend.1 = (bf16[384,128]{1,0:T(8,128)(2,1)S(1)}, bf16[384,128]{1,0:T(8,128)(2,1)S(1)}, bf16[384,128]{1,0:T(8,128)(2,1)S(1)}, bf16[384,128]{1,0:T(8,128)(2,1)S(1)}) custom-call(bf16[1168,128]{1,0:T(8,128)(2,1)S(1)} %get-tuple-element.28.refs_3_.refs_0_, bf16[1168,128]{1,0:T(8,128)(2,1)S(1)} %collective-permute-done.refs_1_, ...), custom_call_target="tpu_custom_call" | custom-call | flops 4294967296 | bytes 2097152 | tf_op jit(solution)/shard_map/attend/pallas_call | solution.py:281
  28.4 4.8 %collective-permute-start.4 = (bf16[384,128]{1,0:T(8,128)(2,1)S(1)}, bf16[384,128]{1,0:T(8,128)(2,1)S(1)}, u32[]{:S(2)}, u32[]{:S(2)}) collective-permute-start(bf16[384,128]{1,0:T(8,128)(2,1)S(1)} %get-tuple-element.36), channel_id=1, source_target_pairs={{8,0},{0,8},{4,12},{24,16},{28,20},{20,28},{9,1},{1,9},{5,13},{25,... | collective-permute-start | bytes 294920 | tf_op jit(solution)/shard_map/ppermute | solution.py:53
  33.2 1.3 %collective-permute-start.5 = (bf16[384,128]{1,0:T(8,128)(2,1)S(1)}, bf16[384,128]{1,0:T(8,128)(2,1)S(1)}, u32[]{:S(2)}, u32[]{:S(2)}) collective-permute-start(bf16[384,128]{1,0:T(8,128)(2,1)S(1)} %get-tuple-element.37), channel_id=1, source_target_pairs={{8,4},{4,8},{0,12},{28,16},{24,20},{20,24},{9,5},{5,9},{1,13},{29,... | collective-permute-start | bytes 294920 | tf_op jit(solution)/shard_map/ppermute | solution.py:53
  34.5 3.2 %collective-permute-start.6 = (bf16[384,128]{1,0:T(8,128)(2,1)S(1)}, bf16[384,128]{1,0:T(8,128)(2,1)S(1)}, u32[]{:S(2)}, u32[]{:S(2)}) collective-permute-start(bf16[384,128]{1,0:T(8,128)(2,1)S(1)} %get-tuple-element.38), channel_id=1, source_target_pairs={{4,0},{0,4},{8,12},{20,16},{28,24},{24,28},{5,1},{1,5},{9,13},{21,... | collective-permute-start | bytes 294920 | tf_op jit(solution)/shard_map/ppermute | solution.py:53
  37.7 3.4 %collective-permute-done.6.back3 = bf16[384,128]{1,0:T(8,128)(2,1)S(1)} collective-permute-done((bf16[384,128]{1,0:T(8,128)(2,1)S(1)}, bf16[384,128]{1,0:T(8,128)(2,1)S(1)}, u32[]{:S(2)}, u32[]{:S(2)}) %collective-permute-start.6) | collective-permute-done | bytes 98336 | tf_op jit(solution)/shard_map/ppermute | solution.py:53
  41.1 0.3 regroup.1
  41.4 0.1 collective-permute-start.10
  41.5 1.3 %collective-permute-start.13 = (bf16[192,384]{1,0:T(8,128)(2,1)S(1)}, bf16[192,384]{1,0:T(8,128)(2,1)S(1)}, u32[]{:S(2)}, u32[]{:S(2)}) collective-permute-start(bf16[192,384]{1,0:T(8,128)(2,1)S(1)} %get-tuple-element.40.after.refs_0_), channel_id=1, source_target_pairs={{0,1},{1,0},{2,3},{3,2},{4,5},{5,4},{6,7},{7,6},{8,9},{9,8},{10,11... | collective-permute-start | bytes 442376 | tf_op jit(solution)/shard_map/ppermute | solution.py:492
  42.8 0.9 %collective-permute-start.14 = (bf16[192,384]{1,0:T(8,128)(2,1)S(1)}, bf16[192,384]{1,0:T(8,128)(2,1)S(1)}, u32[]{:S(2)}, u32[]{:S(2)}) collective-permute-start(bf16[192,384]{1,0:T(8,128)(2,1)S(1)} %get-tuple-element.40.after.refs_0_), channel_id=1, source_target_pairs={{0,2},{1,3},{2,0},{3,1},{4,6},{5,7},{6,4},{7,5},{8,10},{9,11},{10,... | collective-permute-start | bytes 442376 | tf_op jit(solution)/shard_map/ppermute | solution.py:492
  43.7 1.4 %collective-permute-start.15 = (bf16[192,384]{1,0:T(8,128)(2,1)S(1)}, bf16[192,384]{1,0:T(8,128)(2,1)S(1)}, u32[]{:S(2)}, u32[]{:S(2)}) collective-permute-start(bf16[192,384]{1,0:T(8,128)(2,1)S(1)} %get-tuple-element.40.after.refs_0_), channel_id=1, source_target_pairs={{0,3},{1,2},{2,1},{3,0},{4,7},{5,6},{6,5},{7,4},{8,11},{9,10},{10,... | collective-permute-start | bytes 442376 | tf_op jit(solution)/shard_map/ppermute | solution.py:492
  45.0 1.2 %collective-permute-start.11 = (bf16[192,384]{1,0:T(8,128)(2,1)S(1)}, bf16[192,384]{1,0:T(8,128)(2,1)S(1)}, u32[]{:S(2)}, u32[]{:S(2)}) collective-permute-start(bf16[192,384]{1,0:T(8,128)(2,1)S(1)} %get-tuple-element.39.refs_0_), channel_id=1, source_target_pairs={{0,1},{1,0},{2,3},{3,2},{4,5},{5,4},{6,7},{7,6},{8,9},{9,8},{10,11... | collective-permute-start | bytes 442376 | tf_op jit(solution)/shard_map/ppermute | solution.py:492
  46.3 0.9 %collective-permute-start.12 = (bf16[192,384]{1,0:T(8,128)(2,1)S(1)}, bf16[192,384]{1,0:T(8,128)(2,1)S(1)}, u32[]{:S(2)}, u32[]{:S(2)}) collective-permute-start(bf16[192,384]{1,0:T(8,128)(2,1)S(1)} %get-tuple-element.39.refs_0_), channel_id=1, source_target_pairs={{0,2},{1,3},{2,0},{3,1},{4,6},{5,7},{6,4},{7,5},{8,10},{9,11},{10,... | collective-permute-start | bytes 442376 | tf_op jit(solution)/shard_map/ppermute | solution.py:492
  47.2 1.3 %join.1.refs_3_.refs_1_.refs_4_ = bf16[1536,1536]{1,0:T(8,128)(2,1)S(1)} custom-call(bf16[384,1536]{1,0:T(8,128)(2,1)} %own.1, bf16[384,1536]{1,0:T(8,128)(2,1)S(1)} %collective-permute-done.3.got.near, bf16[384,1536]{1,0:T(8,128)(2,1)S(1)} %collective-permute-done.8.near_swap, bf16[192,1536]{1,0:T(8,128)(2,1)S(1)} %gate.1.far, ...), custom_call_target="tpu_custom_call" | custom-call | tf_op jit(solution)/shard_map/join/pallas_call | solution.py:253
  48.5 1.4 %collective-permute-start.7 = (bf16[192,384]{1,0:T(8,128)(2,1)S(1)}, bf16[192,384]{1,0:T(8,128)(2,1)S(1)}, u32[]{:S(2)}, u32[]{:S(2)}) collective-permute-start(bf16[192,384]{1,0:T(8,128)(2,1)S(1)} %get-tuple-element.39.refs_0_), channel_id=1, source_target_pairs={{0,3},{1,2},{2,1},{3,0},{4,7},{5,6},{6,5},{7,4},{8,11},{9,10},{10,... | collective-permute-start | bytes 442376 | tf_op jit(solution)/shard_map/ppermute | solution.py:492
  49.9 2.7 %collective-permute-done.14.refs_2_ = bf16[192,384]{1,0:T(8,128)(2,1)S(1)} collective-permute-done((bf16[192,384]{1,0:T(8,128)(2,1)S(1)}, bf16[192,384]{1,0:T(8,128)(2,1)S(1)}, u32[]{:S(2)}, u32[]{:S(2)}) %collective-permute-start.14) | collective-permute-done | bytes 147488 | tf_op jit(solution)/shard_map/ppermute | solution.py:492
  52.6 3.7 %feed.3 = bf16[192,1536]{1,0:T(8,128)(2,1)S(1)} custom-call(bf16[192,384]{1,0:T(8,128)(2,1)S(1)} %get-tuple-element.40.after.refs_0_, bf16[192,384]{1,0:T(8,128)(2,1)S(1)} %collective-permute-done.13.refs_1_, bf16[192,384]{1,0:T(8,128)(2,1)S(1)} %collective-permute-done.14.refs_2_, bf16[192,384]{1,0:T(8,128)(2,1)S(1)} %collective-permute-done.15.refs_3_, ...), custom_call_target="tpu_custom_call" | custom-call | flops 68719476736 | bytes 16777216 | tf_op jit(solution)/shard_map/feed/pallas_call | solution.py:440
  56.4 0.1 collective-permute-start.16
  56.5 1.7 %collective-permute-done.12.refs_2_ = bf16[192,384]{1,0:T(8,128)(2,1)S(1)} collective-permute-done((bf16[192,384]{1,0:T(8,128)(2,1)S(1)}, bf16[192,384]{1,0:T(8,128)(2,1)S(1)}, u32[]{:S(2)}, u32[]{:S(2)}) %collective-permute-start.12) | collective-permute-done | bytes 147488 | tf_op jit(solution)/shard_map/ppermute | solution.py:492
  58.2 0.9 %project.1.refs_7_ = f32[192,1536]{1,0:T(8,128)S(1)} custom-call(bf16[192,384]{1,0:T(8,128)(2,1)S(1)} %get-tuple-element.39.refs_0_, bf16[192,384]{1,0:T(8,128)(2,1)S(1)} %collective-permute-done.11.refs_1_, bf16[192,384]{1,0:T(8,128)(2,1)S(1)} %collective-permute-done.12.refs_2_, bf16[1536,1536]{1,0:T(8,128)(2,1)S(1)} %join.1.refs_3_.refs_1_.refs_4_), custom_call_target="tpu_custom_call" | custom-call | flops 4294967296 | bytes 4194304 | tf_op jit(solution)/shard_map/project/pallas_call | solution.py:379
  59.1 2.2 %feed.2 = (bf16[192,1536]{1,0:T(8,128)(2,1)S(1)}, f32[192,1536]{1,0:T(8,128)S(1)}) custom-call(bf16[192,384]{1,0:T(8,128)(2,1)S(1)} %collective-permute-done.7.refs_0_, bf16[1536,1536]{1,0:T(8,128)(2,1)S(1)} %join.1.refs_3_.refs_1_.refs_4_, bf16[1536,1536]{1,0:T(8,128)(2,1)S(1)} %get-tuple-element.32.refs_8_.refs_2_.refs_5_, ...), custom_call_target="tpu_custom_call" | custom-call | flops 68719476736 | bytes 16777216 | tf_op jit(solution)/shard_map/feed/pallas_call | solution.py:440
  61.4 1.4 %guide.1 = (f32[192,384]{1,0:T(8,128)S(1)}, bf16[192,384]{1,0:T(8,128)(2,1)S(1)}, bf16[192,384]{1,0:T(8,128)(2,1)S(1)}, bf16[192,384]{1,0:T(8,128)(2,1)S(1)}) custom-call(bf16[192,1536]{1,0:T(8,128)(2,1)S(1)} %get-tuple-element.41.hidden, f32[192,1536]{1,0:T(8,128)S(1)} %get-tuple-element.42.mixed, ...), custom_call_target="tpu_custom_call" | custom-call | tf_op jit(solution)/shard_map/guide/pallas_call | solution.py:541
  62.7 0.9 %collective-permute-start.17 = (bf16[192,384]{1,0:T(8,128)(2,1)S(1)}, bf16[192,384]{1,0:T(8,128)(2,1)S(1)}, u32[]{:S(2)}, u32[]{:S(2)}) collective-permute-start(bf16[192,384]{1,0:T(8,128)(2,1)S(1)} %get-tuple-element.44), channel_id=1, source_target_pairs={{0,1},{1,0},{2,3},{3,2},{4,5},{5,4},{6,7},{7,6},{8,9},{9,8},{10,11... | collective-permute-start | bytes 442376 | tf_op jit(solution)/shard_map/ppermute | solution.py:492
  63.6 0.2 collective-permute-start.18
  63.8 2.5 %collective-permute-start.19 = (bf16[192,384]{1,0:T(8,128)(2,1)S(1)}, bf16[192,384]{1,0:T(8,128)(2,1)S(1)}, u32[]{:S(2)}, u32[]{:S(2)}) collective-permute-start(bf16[192,384]{1,0:T(8,128)(2,1)S(1)} %get-tuple-element.46), channel_id=1, source_target_pairs={{0,3},{1,2},{2,1},{3,0},{4,7},{5,6},{6,5},{7,4},{8,11},{9,10},{10,... | collective-permute-start | bytes 442376 | tf_op jit(solution)/shard_map/ppermute | solution.py:492
  66.3 2.6 %collective-permute-done.17.got1 = bf16[192,384]{1,0:T(8,128)(2,1)S(1)} collective-permute-done((bf16[192,384]{1,0:T(8,128)(2,1)S(1)}, bf16[192,384]{1,0:T(8,128)(2,1)S(1)}, u32[]{:S(2)}, u32[]{:S(2)}) %collective-permute-start.17) | collective-permute-done | bytes 147488 | tf_op jit(solution)/shard_map/ppermute | solution.py:492
  68.9 2.3 %collective-permute-done.18.got2 = bf16[192,384]{1,0:T(8,128)(2,1)S(1)} collective-permute-done((bf16[192,384]{1,0:T(8,128)(2,1)S(1)}, bf16[192,384]{1,0:T(8,128)(2,1)S(1)}, u32[]{:S(2)}, u32[]{:S(2)}) %collective-permute-start.18) | collective-permute-done | bytes 147488 | tf_op jit(solution)/shard_map/ppermute | solution.py:492
  71.2 0.3 place.1
  71.5 1.2 %collective-permute-start.20 = (bf16[96,384]{1,0:T(8,128)(2,1)S(1)}, bf16[96,384]{1,0:T(8,128)(2,1)S(1)}, u32[]{:S(2)}, u32[]{:S(2)}) collective-permute-start(bf16[96,384]{1,0:T(8,128)(2,1)S(1)} %get-tuple-element.48), channel_id=1, source_target_pairs={{0,8},{4,12},{8,0},{12,4},{1,9},{5,13},{9,1},{13,5},{2,10},{6,14},... | collective-permute-start | bytes 221192 | tf_op jit(solution)/shard_map/ppermute | solution.py:492
  72.7 2.0 %collective-permute-start.21 = (bf16[96,384]{1,0:T(8,128)(2,1)S(1)}, bf16[96,384]{1,0:T(8,128)(2,1)S(1)}, u32[]{:S(2)}, u32[]{:S(2)}) collective-permute-start(bf16[96,384]{1,0:T(8,128)(2,1)S(1)} %get-tuple-element.49), channel_id=1, source_target_pairs={{0,12},{4,8},{8,4},{12,0},{1,13},{5,9},{9,5},{13,1},{2,14},{6,10},... | collective-permute-start | bytes 221192 | tf_op jit(solution)/shard_map/ppermute | solution.py:492
  74.7 0.4 collective-permute-start.22
  75.1 2.6 %collective-permute-done.20.refs_1_ = bf16[96,384]{1,0:T(8,128)(2,1)S(1)} collective-permute-done((bf16[96,384]{1,0:T(8,128)(2,1)S(1)}, bf16[96,384]{1,0:T(8,128)(2,1)S(1)}, u32[]{:S(2)}, u32[]{:S(2)}) %collective-permute-start.20) | collective-permute-done | bytes 73760 | tf_op jit(solution)/shard_map/ppermute | solution.py:492
  77.6 1.4 %collective-permute-done.21.refs_2_ = bf16[96,384]{1,0:T(8,128)(2,1)S(1)} collective-permute-done((bf16[96,384]{1,0:T(8,128)(2,1)S(1)}, bf16[96,384]{1,0:T(8,128)(2,1)S(1)}, u32[]{:S(2)}, u32[]{:S(2)}) %collective-permute-start.21) | collective-permute-done | bytes 73760 | tf_op jit(solution)/shard_map/ppermute | solution.py:492
  79.0 0.7 collective-permute-done.22.refs_3_
  79.7 0.8 arrange.1
  (29 shorter events, 0.1 us)
Async XLA Ops:
  0.0 13.5 %copy-start = (s32[384,1]{0,1:T(1,128)S(1)}, s32[384,1]{0,1:T(1,128)}, u32[]{:S(2)}) copy-start(s32[384,1]{0,1:T(1,128)} %param.21) | copy-start | bytes 4612
  0.0 17.9 %collective-permute-start.3 = (bf16[384,1536]{1,0:T(8,128)(2,1)}, bf16[384,1536]{1,0:T(8,128)(2,1)S(1)}, u32[]{:S(2)}, u32[]{:S(2)}) collective-permute-start(bf16[384,1536]{1,0:T(8,128)(2,1)} %own.1), channel_id=1, source_target_pairs={{0,1},{1,0},{2,3},{3,2},{16,18},{17,19},{18,16},{19,17},{4,5},{5,4... | collective-permute-start | bytes 3538952 | tf_op jit(solution)/shard_map/ppermute | solution.py:188
  4.2 21.9 %collective-permute-start = (bf16[1168,128]{1,0:T(8,128)(2,1)S(1)}, bf16[1168,128]{1,0:T(8,128)(2,1)S(1)}, u32[]{:S(2)}, u32[]{:S(2)}) collective-permute-start(bf16[1168,128]{1,0:T(8,128)(2,1)S(1)} %get-tuple-element.29), channel_id=1, source_target_pairs={{0,8},{8,0},{12,4},{16,24},{20,28},{28,20},{1,9},{9,1},{13,5},{17,... | collective-permute-start | bytes 897032 | tf_op jit(solution)/shard_map/ppermute | solution.py:53
  8.7 17.4 %collective-permute-start.1 = (bf16[1168,128]{1,0:T(8,128)(2,1)S(1)}, bf16[1168,128]{1,0:T(8,128)(2,1)S(1)}, u32[]{:S(2)}, u32[]{:S(2)}) collective-permute-start(bf16[1168,128]{1,0:T(8,128)(2,1)S(1)} %get-tuple-element.30), channel_id=1, source_target_pairs={{4,8},{8,4},{12,0},{16,28},{20,24},{24,20},{5,9},{9,5},{13,1},{17,... | collective-permute-start | bytes 897032 | tf_op jit(solution)/shard_map/ppermute | solution.py:53
  10.0 16.1 %collective-permute-start.2 = (bf16[1168,128]{1,0:T(8,128)(2,1)S(1)}, bf16[1168,128]{1,0:T(8,128)(2,1)S(1)}, u32[]{:S(2)}, u32[]{:S(2)}) collective-permute-start(bf16[1168,128]{1,0:T(8,128)(2,1)S(1)} %get-tuple-element.31), channel_id=1, source_target_pairs={{0,4},{4,0},{12,8},{16,20},{24,28},{28,24},{1,5},{5,1},{13,9},{17,... | collective-permute-start | bytes 897032 | tf_op jit(solution)/shard_map/ppermute | solution.py:53
  13.7 4.1 %copy-start.4 = (s32[384]{0:T(512)S(1)}, s32[384]{0:T(512)}, u32[]{:S(2)}) copy-start(s32[384]{0:T(512)} %param.20) | copy-start | bytes 4612
  17.8 8.4 %copy-start.5 = (f32[3]{0:T(128)S(1)}, f32[3]{0:T(128)}, u32[]{:S(2)}) copy-start(f32[3]{0:T(128)} %param.19) | copy-start | bytes 40
  18.1 23.3 %collective-permute-start.9 = (bf16[192,1536]{1,0:T(8,128)(2,1)S(1)}, bf16[192,1536]{1,0:T(8,128)(2,1)S(1)}, u32[]{:S(2)}, u32[]{:S(2)}) collective-permute-start(bf16[192,1536]{1,0:T(8,128)(2,1)S(1)} %cut.1.refs_6_), channel_id=1, source_target_pairs={{0,2},{1,3},{2,0},{3,1},{16,17},{17,16},{18,19},{19,18},{4,6},{5,7... | collective-permute-start | bytes 1769480 | tf_op jit(solution)/shard_map/ppermute | solution.py:188
  19.6 26.6 %collective-permute-start.8 = (bf16[384,1536]{1,0:T(8,128)(2,1)S(1)}, bf16[384,1536]{1,0:T(8,128)(2,1)S(1)}, u32[]{:S(2)}, u32[]{:S(2)}) collective-permute-start(bf16[384,1536]{1,0:T(8,128)(2,1)S(1)} %collective-permute-done.3.got.near), channel_id=1, source_target_pairs={{0,16},{16,0},{1,17},{17,1},{2,18},{18,2},{3,19},{19,3},{4,20},{20... | collective-permute-start | bytes 3538952 | tf_op jit(solution)/shard_map/ppermute | solution.py:492
  19.7 8.7 %copy-start.1 = (bf16[384,192]{1,0:T(8,128)(2,1)}, bf16[384,192]{1,0:T(8,128)(2,1)S(1)}, u32[]{:S(2)}) copy-start(bf16[384,192]{1,0:T(8,128)(2,1)S(1)} %fusion.refs_5_.placing) | copy-start | bytes 442372
  28.4 9.2 %collective-permute-start.4 = (bf16[384,128]{1,0:T(8,128)(2,1)S(1)}, bf16[384,128]{1,0:T(8,128)(2,1)S(1)}, u32[]{:S(2)}, u32[]{:S(2)}) collective-permute-start(bf16[384,128]{1,0:T(8,128)(2,1)S(1)} %get-tuple-element.36), channel_id=1, source_target_pairs={{8,0},{0,8},{4,12},{24,16},{28,20},{20,28},{9,1},{1,9},{5,13},{25,... | collective-permute-start | bytes 294920 | tf_op jit(solution)/shard_map/ppermute | solution.py:53
  33.2 4.5 %collective-permute-start.5 = (bf16[384,128]{1,0:T(8,128)(2,1)S(1)}, bf16[384,128]{1,0:T(8,128)(2,1)S(1)}, u32[]{:S(2)}, u32[]{:S(2)}) collective-permute-start(bf16[384,128]{1,0:T(8,128)(2,1)S(1)} %get-tuple-element.37), channel_id=1, source_target_pairs={{8,4},{4,8},{0,12},{28,16},{24,20},{20,24},{9,5},{5,9},{1,13},{29,... | collective-permute-start | bytes 294920 | tf_op jit(solution)/shard_map/ppermute | solution.py:53
  34.5 6.6 %collective-permute-start.6 = (bf16[384,128]{1,0:T(8,128)(2,1)S(1)}, bf16[384,128]{1,0:T(8,128)(2,1)S(1)}, u32[]{:S(2)}, u32[]{:S(2)}) collective-permute-start(bf16[384,128]{1,0:T(8,128)(2,1)S(1)} %get-tuple-element.38), channel_id=1, source_target_pairs={{4,0},{0,4},{8,12},{20,16},{28,24},{24,28},{5,1},{1,5},{9,13},{21,... | collective-permute-start | bytes 294920 | tf_op jit(solution)/shard_map/ppermute | solution.py:53
  41.4 3.6 %collective-permute-start.10 = (bf16[192,1536]{1,0:T(8,128)(2,1)S(1)}, bf16[192,1536]{1,0:T(8,128)(2,1)S(1)}, u32[]{:S(2)}, u32[]{:S(2)}) collective-permute-start(bf16[192,1536]{1,0:T(8,128)(2,1)S(1)} %gate.1.far), channel_id=1, source_target_pairs={{0,16},{16,0},{1,17},{17,1},{2,18},{18,2},{3,19},{19,3},{4,20},{20... | collective-permute-start | bytes 1769480 | tf_op jit(solution)/shard_map/ppermute | solution.py:492
  41.5 7.0 %collective-permute-start.13 = (bf16[192,384]{1,0:T(8,128)(2,1)S(1)}, bf16[192,384]{1,0:T(8,128)(2,1)S(1)}, u32[]{:S(2)}, u32[]{:S(2)}) collective-permute-start(bf16[192,384]{1,0:T(8,128)(2,1)S(1)} %get-tuple-element.40.after.refs_0_), channel_id=1, source_target_pairs={{0,1},{1,0},{2,3},{3,2},{4,5},{5,4},{6,7},{7,6},{8,9},{9,8},{10,11... | collective-permute-start | bytes 442376 | tf_op jit(solution)/shard_map/ppermute | solution.py:492
  42.8 9.9 %collective-permute-start.14 = (bf16[192,384]{1,0:T(8,128)(2,1)S(1)}, bf16[192,384]{1,0:T(8,128)(2,1)S(1)}, u32[]{:S(2)}, u32[]{:S(2)}) collective-permute-start(bf16[192,384]{1,0:T(8,128)(2,1)S(1)} %get-tuple-element.40.after.refs_0_), channel_id=1, source_target_pairs={{0,2},{1,3},{2,0},{3,1},{4,6},{5,7},{6,4},{7,5},{8,10},{9,11},{10,... | collective-permute-start | bytes 442376 | tf_op jit(solution)/shard_map/ppermute | solution.py:492
  43.7 9.0 %collective-permute-start.15 = (bf16[192,384]{1,0:T(8,128)(2,1)S(1)}, bf16[192,384]{1,0:T(8,128)(2,1)S(1)}, u32[]{:S(2)}, u32[]{:S(2)}) collective-permute-start(bf16[192,384]{1,0:T(8,128)(2,1)S(1)} %get-tuple-element.40.after.refs_0_), channel_id=1, source_target_pairs={{0,3},{1,2},{2,1},{3,0},{4,7},{5,6},{6,5},{7,4},{8,11},{9,10},{10,... | collective-permute-start | bytes 442376 | tf_op jit(solution)/shard_map/ppermute | solution.py:492
  45.0 7.6 %copy-start.3 = (f32[3,4,1536]{2,1,0:T(4,128)S(1)}, f32[3,4,1536]{2,1,0:T(4,128)}, u32[]{:S(2)}) copy-start(f32[3,4,1536]{2,1,0:T(4,128)} %mod.1) | copy-start | bytes 221188
  45.0 11.4 %collective-permute-start.11 = (bf16[192,384]{1,0:T(8,128)(2,1)S(1)}, bf16[192,384]{1,0:T(8,128)(2,1)S(1)}, u32[]{:S(2)}, u32[]{:S(2)}) collective-permute-start(bf16[192,384]{1,0:T(8,128)(2,1)S(1)} %get-tuple-element.39.refs_0_), channel_id=1, source_target_pairs={{0,1},{1,0},{2,3},{3,2},{4,5},{5,4},{6,7},{7,6},{8,9},{9,8},{10,11... | collective-permute-start | bytes 442376 | tf_op jit(solution)/shard_map/ppermute | solution.py:492
  46.3 11.9 %collective-permute-start.12 = (bf16[192,384]{1,0:T(8,128)(2,1)S(1)}, bf16[192,384]{1,0:T(8,128)(2,1)S(1)}, u32[]{:S(2)}, u32[]{:S(2)}) collective-permute-start(bf16[192,384]{1,0:T(8,128)(2,1)S(1)} %get-tuple-element.39.refs_0_), channel_id=1, source_target_pairs={{0,2},{1,3},{2,0},{3,1},{4,6},{5,7},{6,4},{7,5},{8,10},{9,11},{10,... | collective-permute-start | bytes 442376 | tf_op jit(solution)/shard_map/ppermute | solution.py:492
  48.5 10.6 %collective-permute-start.7 = (bf16[192,384]{1,0:T(8,128)(2,1)S(1)}, bf16[192,384]{1,0:T(8,128)(2,1)S(1)}, u32[]{:S(2)}, u32[]{:S(2)}) collective-permute-start(bf16[192,384]{1,0:T(8,128)(2,1)S(1)} %get-tuple-element.39.refs_0_), channel_id=1, source_target_pairs={{0,3},{1,2},{2,1},{3,0},{4,7},{5,6},{6,5},{7,4},{8,11},{9,10},{10,... | collective-permute-start | bytes 442376 | tf_op jit(solution)/shard_map/ppermute | solution.py:492
  56.4 4.9 %collective-permute-start.16 = (bf16[192,1536]{1,0:T(8,128)(2,1)S(1)}, bf16[192,1536]{1,0:T(8,128)(2,1)S(1)}, u32[]{:S(2)}, u32[]{:S(2)}) collective-permute-start(bf16[192,1536]{1,0:T(8,128)(2,1)S(1)} %feed.3), channel_id=1, source_target_pairs={{0,16},{16,0},{1,17},{17,1},{2,18},{18,2},{3,19},{19,3},{4,20},{20... | collective-permute-start | bytes 1769480 | tf_op jit(solution)/shard_map/ppermute | solution.py:492
  61.3 9.9 %copy-start.2 = (bf16[384,192]{1,0:T(8,128)(2,1)S(1)}, bf16[384,192]{1,0:T(8,128)(2,1)}, u32[]{:S(2)}) copy-start(bf16[384,192]{1,0:T(8,128)(2,1)} %copy-done.1) | copy-start | bytes 442372
  62.7 6.2 %collective-permute-start.17 = (bf16[192,384]{1,0:T(8,128)(2,1)S(1)}, bf16[192,384]{1,0:T(8,128)(2,1)S(1)}, u32[]{:S(2)}, u32[]{:S(2)}) collective-permute-start(bf16[192,384]{1,0:T(8,128)(2,1)S(1)} %get-tuple-element.44), channel_id=1, source_target_pairs={{0,1},{1,0},{2,3},{3,2},{4,5},{5,4},{6,7},{7,6},{8,9},{9,8},{10,11... | collective-permute-start | bytes 442376 | tf_op jit(solution)/shard_map/ppermute | solution.py:492
  63.6 7.7 %collective-permute-start.18 = (bf16[192,384]{1,0:T(8,128)(2,1)S(1)}, bf16[192,384]{1,0:T(8,128)(2,1)S(1)}, u32[]{:S(2)}, u32[]{:S(2)}) collective-permute-start(bf16[192,384]{1,0:T(8,128)(2,1)S(1)} %get-tuple-element.45), channel_id=1, source_target_pairs={{0,2},{1,3},{2,0},{3,1},{4,6},{5,7},{6,4},{7,5},{8,10},{9,11},{10,... | collective-permute-start | bytes 442376 | tf_op jit(solution)/shard_map/ppermute | solution.py:492
  63.8 7.5 %collective-permute-start.19 = (bf16[192,384]{1,0:T(8,128)(2,1)S(1)}, bf16[192,384]{1,0:T(8,128)(2,1)S(1)}, u32[]{:S(2)}, u32[]{:S(2)}) collective-permute-start(bf16[192,384]{1,0:T(8,128)(2,1)S(1)} %get-tuple-element.46), channel_id=1, source_target_pairs={{0,3},{1,2},{2,1},{3,0},{4,7},{5,6},{6,5},{7,4},{8,11},{9,10},{10,... | collective-permute-start | bytes 442376 | tf_op jit(solution)/shard_map/ppermute | solution.py:492
  71.5 6.1 %collective-permute-start.20 = (bf16[96,384]{1,0:T(8,128)(2,1)S(1)}, bf16[96,384]{1,0:T(8,128)(2,1)S(1)}, u32[]{:S(2)}, u32[]{:S(2)}) collective-permute-start(bf16[96,384]{1,0:T(8,128)(2,1)S(1)} %get-tuple-element.48), channel_id=1, source_target_pairs={{0,8},{4,12},{8,0},{12,4},{1,9},{5,13},{9,1},{13,5},{2,10},{6,14},... | collective-permute-start | bytes 221192 | tf_op jit(solution)/shard_map/ppermute | solution.py:492
  72.7 6.3 %collective-permute-start.21 = (bf16[96,384]{1,0:T(8,128)(2,1)S(1)}, bf16[96,384]{1,0:T(8,128)(2,1)S(1)}, u32[]{:S(2)}, u32[]{:S(2)}) collective-permute-start(bf16[96,384]{1,0:T(8,128)(2,1)S(1)} %get-tuple-element.49), channel_id=1, source_target_pairs={{0,12},{4,8},{8,4},{12,0},{1,13},{5,9},{9,5},{13,1},{2,14},{6,10},... | collective-permute-start | bytes 221192 | tf_op jit(solution)/shard_map/ppermute | solution.py:492
  74.7 5.1 %collective-permute-start.22 = (bf16[96,384]{1,0:T(8,128)(2,1)S(1)}, bf16[96,384]{1,0:T(8,128)(2,1)S(1)}, u32[]{:S(2)}, u32[]{:S(2)}) collective-permute-start(bf16[96,384]{1,0:T(8,128)(2,1)S(1)} %get-tuple-element.50), channel_id=1, source_target_pairs={{0,4},{4,0},{8,12},{12,8},{1,5},{5,1},{9,13},{13,9},{2,6},{6,2},{1... | collective-permute-start | bytes 221192 | tf_op jit(solution)/shard_map/ppermute | solution.py:492

commit v10 on v9

--- a/solution.py
+++ b/solution.py
@@ -482,7 +482,7 @@
     out = refs[4]
     place = lax.axis_index("seq")
     count = refs[0].shape[0]
-    for step, source in zip(STEPS, refs):
+    for step, source in zip((0, 3, 2, 1), refs):
         origin = jnp.bitwise_xor(place, step)
         out[pl.ds(pl.multiple_of(origin * count, count), count), :] = source[...]
 
@@ -566,7 +566,7 @@
         )
         return arrived.reshape(1, seq_count * capacity, width)
     home = [
-        exchanged(placed[step], "seq", step) for step in STEPS[1:]
+        exchanged(placed[step], "seq", step) for step in (3, 2, 1)
     ]
     arranged = pl.pallas_call(
         arrange_kernel,

time: 80.8 us -> 80.4 us (level)
  waiting for transfers between devices: 23.9 us -> 22.6 us
  starting transfers between devices: 37.3 us -> 38.2 us
    ppermute x15, waiting for transfers between devices: 14 us -> 12.7 us  [exchanged(): return lax.ppermute(value, axis, pairs)]
    ppermute x15, starting transfers between devices: 14.4 us -> 15.3 us  [exchanged(): return lax.ppermute(value, axis, pairs)]
  transfers between devices with their start and end apart: 23 -> 23, of which waited for: 9 -> 8; matrix products, arithmetic and copies ran while one was open for 1% -> 1% of each run, Pallas kernels for 20% -> 20%
where the time goes in v10:
time: 80.4 us; the launch traced here: 80.1 us
  starting transfers between devices  38.2 us (48%)
  waiting for transfers between devices  22.6 us (28%)
  Pallas kernels  18.4 us (23%)
    ppermute x6, starting transfers between devices, hop(): return lax.ppermute(value, ('cfg', 'seq'), pairs)  18.4 us
    ppermute x15, starting transfers between devices, exchanged(): return lax.ppermute(value, axis, pairs)  15.3 us
    ppermute x15, waiting for transfers between devices, exchanged(): return lax.ppermute(value, axis, pairs)  12.7 us
    ppermute x6, waiting for transfers between devices, hop(): return lax.ppermute(value, ('cfg', 'seq'), pairs)  9.83 us
    pallas_call x2, Pallas kernels, feed(): pl.pallas_call(functools.partial(feed_kernel, turn, len(att)), out_shape=...  5.92 us
    ppermute x2, starting transfers between devices, across(): return lax.ppermute(value, ('cfg', 'blk'), pairs)  4.52 us
    pallas_call x1, Pallas kernels, load(): pl.pallas_call(load_kernel, out_shape=[pltpu.VMEM(array.shape, BF16) for...  4.07 us
    pallas_call x1, Pallas kernels, attention_by_head(): pl.pallas_call(attend_kernel, out_shape=[shape_of((slots, 128))] * 4, in_...  2.08 us
  transfers between devices with their start and end apart: 23, of which 8 were waited for; matrix products, arithmetic and copies ran while one was open for 1% of the time, Pallas kernels for 20%

profile of v10, /device:TPU:0, one launch (start us, length us, event | category | flops | bytes accessed | tf_op | source)
XLA Modules:
  0.0 80.1 jit_solution(5362823119660925616)
XLA Ops:
  0.0 2.9 %collective-permute-start.3 = (bf16[384,1536]{1,0:T(8,128)(2,1)}, bf16[384,1536]{1,0:T(8,128)(2,1)S(1)}, u32[]{:S(2)}, u32[]{:S(2)}) collective-permute-start(bf16[384,1536]{1,0:T(8,128)(2,1)} %own.1), channel_id=1, source_target_pairs={{0,1},{1,0},{2,3},{3,2},{16,18},{17,19},{18,16},{19,17},{4,5},{5,4... | collective-permute-start | bytes 3538952 | tf_op jit(solution)/shard_map/ppermute | solution.py:188
  2.9 1.3 %pack.1 = (bf16[1168,128]{1,0:T(8,128)(2,1)S(1)}, bf16[1168,128]{1,0:T(8,128)(2,1)S(1)}, bf16[1168,128]{1,0:T(8,128)(2,1)S(1)}, bf16[1168,128]{1,0:T(8,128)(2,1)S(1)}) custom-call(bf16[384,384]{1,0:T(8,128)(2,1)} %bitcast.7, bf16[384,384]{1,0:T(8,128)(2,1)} %bitcast.8, bf16[384,384]{1,0:T(8,128)(2,1)} %bitcast.9, s32[3,128]{1,0:T(4,128)} %bitcast.12), custom_call_target="tpu_custom_call" | custom-call | tf_op jit(solution)/shard_map/pack/pallas_call | solution.py:266
  4.2 4.5 %collective-permute-start = (bf16[1168,128]{1,0:T(8,128)(2,1)S(1)}, bf16[1168,128]{1,0:T(8,128)(2,1)S(1)}, u32[]{:S(2)}, u32[]{:S(2)}) collective-permute-start(bf16[1168,128]{1,0:T(8,128)(2,1)S(1)} %get-tuple-element.29), channel_id=1, source_target_pairs={{0,8},{8,0},{12,4},{16,24},{20,28},{28,20},{1,9},{9,1},{13,5},{17,... | collective-permute-start | bytes 897032 | tf_op jit(solution)/shard_map/ppermute | solution.py:53
  8.7 1.3 %collective-permute-start.1 = (bf16[1168,128]{1,0:T(8,128)(2,1)S(1)}, bf16[1168,128]{1,0:T(8,128)(2,1)S(1)}, u32[]{:S(2)}, u32[]{:S(2)}) collective-permute-start(bf16[1168,128]{1,0:T(8,128)(2,1)S(1)} %get-tuple-element.30), channel_id=1, source_target_pairs={{4,8},{8,4},{12,0},{16,28},{20,24},{24,20},{5,9},{9,5},{13,1},{17,... | collective-permute-start | bytes 897032 | tf_op jit(solution)/shard_map/ppermute | solution.py:53
  10.0 3.4 %collective-permute-start.2 = (bf16[1168,128]{1,0:T(8,128)(2,1)S(1)}, bf16[1168,128]{1,0:T(8,128)(2,1)S(1)}, u32[]{:S(2)}, u32[]{:S(2)}) collective-permute-start(bf16[1168,128]{1,0:T(8,128)(2,1)S(1)} %get-tuple-element.31), channel_id=1, source_target_pairs={{0,4},{4,0},{12,8},{16,20},{24,28},{28,24},{1,5},{5,1},{13,9},{17,... | collective-permute-start | bytes 897032 | tf_op jit(solution)/shard_map/ppermute | solution.py:53
  13.5 0.1 constant_dynamic-slice_fusion
  13.5 0.2 convert_reduce_fusion
  13.7 0.0 copy-start.4
  13.7 4.1 %load.1 = (bf16[1536,1536]{1,0:T(8,128)(2,1)S(1)}, bf16[1536,1536]{1,0:T(8,128)(2,1)S(1)}, bf16[384,1536]{1,0:T(8,128)(2,1)S(1)}) custom-call(bf16[1536,1536]{1,0:T(8,128)(2,1)} %refs_0_.1, bf16[1536,1536]{1,0:T(8,128)(2,1)} %refs_1_.1, bf16[384,1536]{1,0:T(8,128)(2,1)} %bitcast.13, bf16[1168,128]{1,0:T(8,128)(2,1)S(1)} %get-tuple-element.28.refs_3_.refs_0_), custom_call_target="tpu_custom_call" | custom-call | flops 17179869184 | bytes 16777216 | tf_op jit(solution)/shard_map/load/pallas_call | solution.py:172
  17.8 0.1 compare_select_fusion
  17.9 0.1 cut.1.refs_6_
  18.1 1.6 %collective-permute-start.9 = (bf16[192,1536]{1,0:T(8,128)(2,1)S(1)}, bf16[192,1536]{1,0:T(8,128)(2,1)S(1)}, u32[]{:S(2)}, u32[]{:S(2)}) collective-permute-start(bf16[192,1536]{1,0:T(8,128)(2,1)S(1)} %cut.1.refs_6_), channel_id=1, source_target_pairs={{0,2},{1,3},{2,0},{3,1},{16,17},{17,16},{18,19},{19,18},{4,6},{5,7... | collective-permute-start | bytes 1769480 | tf_op jit(solution)/shard_map/ppermute | solution.py:188
  19.7 6.4 %collective-permute-done.refs_1_ = bf16[1168,128]{1,0:T(8,128)(2,1)S(1)} collective-permute-done((bf16[1168,128]{1,0:T(8,128)(2,1)S(1)}, bf16[1168,128]{1,0:T(8,128)(2,1)S(1)}, u32[]{:S(2)}, u32[]{:S(2)}) %collective-permute-start) | collective-permute-done | bytes 299040 | tf_op jit(solution)/shard_map/ppermute | solution.py:53
  26.1 0.1 broadcast_in_dim.9.refs_4_.refs_6_.refs_9_.clip_ref
  26.2 0.1 broadcast_in_dim.11.refs_7_.scale_ref
  26.3 2.1 %attend.1 = (bf16[384,128]{1,0:T(8,128)(2,1)S(1)}, bf16[384,128]{1,0:T(8,128)(2,1)S(1)}, bf16[384,128]{1,0:T(8,128)(2,1)S(1)}, bf16[384,128]{1,0:T(8,128)(2,1)S(1)}) custom-call(bf16[1168,128]{1,0:T(8,128)(2,1)S(1)} %get-tuple-element.28.refs_3_.refs_0_, bf16[1168,128]{1,0:T(8,128)(2,1)S(1)} %collective-permute-done.refs_1_, ...), custom_call_target="tpu_custom_call" | custom-call | flops 4294967296 | bytes 2097152 | tf_op jit(solution)/shard_map/attend/pallas_call | solution.py:281
  28.4 4.8 %collective-permute-start.4 = (bf16[384,128]{1,0:T(8,128)(2,1)S(1)}, bf16[384,128]{1,0:T(8,128)(2,1)S(1)}, u32[]{:S(2)}, u32[]{:S(2)}) collective-permute-start(bf16[384,128]{1,0:T(8,128)(2,1)S(1)} %get-tuple-element.36), channel_id=1, source_target_pairs={{8,0},{0,8},{4,12},{24,16},{28,20},{20,28},{9,1},{1,9},{5,13},{25,... | collective-permute-start | bytes 294920 | tf_op jit(solution)/shard_map/ppermute | solution.py:53
  33.2 1.3 %collective-permute-start.5 = (bf16[384,128]{1,0:T(8,128)(2,1)S(1)}, bf16[384,128]{1,0:T(8,128)(2,1)S(1)}, u32[]{:S(2)}, u32[]{:S(2)}) collective-permute-start(bf16[384,128]{1,0:T(8,128)(2,1)S(1)} %get-tuple-element.37), channel_id=1, source_target_pairs={{8,4},{4,8},{0,12},{28,16},{24,20},{20,24},{9,5},{5,9},{1,13},{29,... | collective-permute-start | bytes 294920 | tf_op jit(solution)/shard_map/ppermute | solution.py:53
  34.5 3.2 %collective-permute-start.6 = (bf16[384,128]{1,0:T(8,128)(2,1)S(1)}, bf16[384,128]{1,0:T(8,128)(2,1)S(1)}, u32[]{:S(2)}, u32[]{:S(2)}) collective-permute-start(bf16[384,128]{1,0:T(8,128)(2,1)S(1)} %get-tuple-element.38), channel_id=1, source_target_pairs={{4,0},{0,4},{8,12},{20,16},{28,24},{24,28},{5,1},{1,5},{9,13},{21,... | collective-permute-start | bytes 294920 | tf_op jit(solution)/shard_map/ppermute | solution.py:53
  37.7 3.4 %collective-permute-done.6.back3 = bf16[384,128]{1,0:T(8,128)(2,1)S(1)} collective-permute-done((bf16[384,128]{1,0:T(8,128)(2,1)S(1)}, bf16[384,128]{1,0:T(8,128)(2,1)S(1)}, u32[]{:S(2)}, u32[]{:S(2)}) %collective-permute-start.6) | collective-permute-done | bytes 98336 | tf_op jit(solution)/shard_map/ppermute | solution.py:53
  41.1 0.3 regroup.1
  41.4 0.1 collective-permute-start.10
  41.5 1.3 %collective-permute-start.13 = (bf16[192,384]{1,0:T(8,128)(2,1)S(1)}, bf16[192,384]{1,0:T(8,128)(2,1)S(1)}, u32[]{:S(2)}, u32[]{:S(2)}) collective-permute-start(bf16[192,384]{1,0:T(8,128)(2,1)S(1)} %get-tuple-element.40.after.refs_0_), channel_id=1, source_target_pairs={{0,1},{1,0},{2,3},{3,2},{4,5},{5,4},{6,7},{7,6},{8,9},{9,8},{10,11... | collective-permute-start | bytes 442376 | tf_op jit(solution)/shard_map/ppermute | solution.py:492
  42.8 0.9 %collective-permute-start.14 = (bf16[192,384]{1,0:T(8,128)(2,1)S(1)}, bf16[192,384]{1,0:T(8,128)(2,1)S(1)}, u32[]{:S(2)}, u32[]{:S(2)}) collective-permute-start(bf16[192,384]{1,0:T(8,128)(2,1)S(1)} %get-tuple-element.40.after.refs_0_), channel_id=1, source_target_pairs={{0,2},{1,3},{2,0},{3,1},{4,6},{5,7},{6,4},{7,5},{8,10},{9,11},{10,... | collective-permute-start | bytes 442376 | tf_op jit(solution)/shard_map/ppermute | solution.py:492
  43.7 1.4 %collective-permute-start.15 = (bf16[192,384]{1,0:T(8,128)(2,1)S(1)}, bf16[192,384]{1,0:T(8,128)(2,1)S(1)}, u32[]{:S(2)}, u32[]{:S(2)}) collective-permute-start(bf16[192,384]{1,0:T(8,128)(2,1)S(1)} %get-tuple-element.40.after.refs_0_), channel_id=1, source_target_pairs={{0,3},{1,2},{2,1},{3,0},{4,7},{5,6},{6,5},{7,4},{8,11},{9,10},{10,... | collective-permute-start | bytes 442376 | tf_op jit(solution)/shard_map/ppermute | solution.py:492
  45.0 1.2 %collective-permute-start.11 = (bf16[192,384]{1,0:T(8,128)(2,1)S(1)}, bf16[192,384]{1,0:T(8,128)(2,1)S(1)}, u32[]{:S(2)}, u32[]{:S(2)}) collective-permute-start(bf16[192,384]{1,0:T(8,128)(2,1)S(1)} %get-tuple-element.39.refs_0_), channel_id=1, source_target_pairs={{0,1},{1,0},{2,3},{3,2},{4,5},{5,4},{6,7},{7,6},{8,9},{9,8},{10,11... | collective-permute-start | bytes 442376 | tf_op jit(solution)/shard_map/ppermute | solution.py:492
  46.3 0.9 %collective-permute-start.12 = (bf16[192,384]{1,0:T(8,128)(2,1)S(1)}, bf16[192,384]{1,0:T(8,128)(2,1)S(1)}, u32[]{:S(2)}, u32[]{:S(2)}) collective-permute-start(bf16[192,384]{1,0:T(8,128)(2,1)S(1)} %get-tuple-element.39.refs_0_), channel_id=1, source_target_pairs={{0,2},{1,3},{2,0},{3,1},{4,6},{5,7},{6,4},{7,5},{8,10},{9,11},{10,... | collective-permute-start | bytes 442376 | tf_op jit(solution)/shard_map/ppermute | solution.py:492
  47.2 1.3 %join.1.refs_3_.refs_1_.refs_4_ = bf16[1536,1536]{1,0:T(8,128)(2,1)S(1)} custom-call(bf16[384,1536]{1,0:T(8,128)(2,1)} %own.1, bf16[384,1536]{1,0:T(8,128)(2,1)S(1)} %collective-permute-done.3.got.near, bf16[384,1536]{1,0:T(8,128)(2,1)S(1)} %collective-permute-done.8.near_swap, bf16[192,1536]{1,0:T(8,128)(2,1)S(1)} %gate.1.far, ...), custom_call_target="tpu_custom_call" | custom-call | tf_op jit(solution)/shard_map/join/pallas_call | solution.py:253
  48.5 1.4 %collective-permute-start.7 = (bf16[192,384]{1,0:T(8,128)(2,1)S(1)}, bf16[192,384]{1,0:T(8,128)(2,1)S(1)}, u32[]{:S(2)}, u32[]{:S(2)}) collective-permute-start(bf16[192,384]{1,0:T(8,128)(2,1)S(1)} %get-tuple-element.39.refs_0_), channel_id=1, source_target_pairs={{0,3},{1,2},{2,1},{3,0},{4,7},{5,6},{6,5},{7,4},{8,11},{9,10},{10,... | collective-permute-start | bytes 442376 | tf_op jit(solution)/shard_map/ppermute | solution.py:492
  49.9 2.7 %collective-permute-done.14.refs_2_ = bf16[192,384]{1,0:T(8,128)(2,1)S(1)} collective-permute-done((bf16[192,384]{1,0:T(8,128)(2,1)S(1)}, bf16[192,384]{1,0:T(8,128)(2,1)S(1)}, u32[]{:S(2)}, u32[]{:S(2)}) %collective-permute-start.14) | collective-permute-done | bytes 147488 | tf_op jit(solution)/shard_map/ppermute | solution.py:492
  52.6 3.7 %feed.3 = bf16[192,1536]{1,0:T(8,128)(2,1)S(1)} custom-call(bf16[192,384]{1,0:T(8,128)(2,1)S(1)} %get-tuple-element.40.after.refs_0_, bf16[192,384]{1,0:T(8,128)(2,1)S(1)} %collective-permute-done.13.refs_1_, bf16[192,384]{1,0:T(8,128)(2,1)S(1)} %collective-permute-done.14.refs_2_, bf16[192,384]{1,0:T(8,128)(2,1)S(1)} %collective-permute-done.15.refs_3_, ...), custom_call_target="tpu_custom_call" | custom-call | flops 68719476736 | bytes 16777216 | tf_op jit(solution)/shard_map/feed/pallas_call | solution.py:440
  56.4 0.1 collective-permute-start.16
  56.5 1.7 %collective-permute-done.12.refs_2_ = bf16[192,384]{1,0:T(8,128)(2,1)S(1)} collective-permute-done((bf16[192,384]{1,0:T(8,128)(2,1)S(1)}, bf16[192,384]{1,0:T(8,128)(2,1)S(1)}, u32[]{:S(2)}, u32[]{:S(2)}) %collective-permute-start.12) | collective-permute-done | bytes 147488 | tf_op jit(solution)/shard_map/ppermute | solution.py:492
  58.2 0.9 %project.1.refs_7_ = f32[192,1536]{1,0:T(8,128)S(1)} custom-call(bf16[192,384]{1,0:T(8,128)(2,1)S(1)} %get-tuple-element.39.refs_0_, bf16[192,384]{1,0:T(8,128)(2,1)S(1)} %collective-permute-done.11.refs_1_, bf16[192,384]{1,0:T(8,128)(2,1)S(1)} %collective-permute-done.12.refs_2_, bf16[1536,1536]{1,0:T(8,128)(2,1)S(1)} %join.1.refs_3_.refs_1_.refs_4_), custom_call_target="tpu_custom_call" | custom-call | flops 4294967296 | bytes 4194304 | tf_op jit(solution)/shard_map/project/pallas_call | solution.py:379
  59.1 2.2 %feed.2 = (bf16[192,1536]{1,0:T(8,128)(2,1)S(1)}, f32[192,1536]{1,0:T(8,128)S(1)}) custom-call(bf16[192,384]{1,0:T(8,128)(2,1)S(1)} %collective-permute-done.7.refs_0_, bf16[1536,1536]{1,0:T(8,128)(2,1)S(1)} %join.1.refs_3_.refs_1_.refs_4_, bf16[1536,1536]{1,0:T(8,128)(2,1)S(1)} %get-tuple-element.32.refs_8_.refs_2_.refs_5_, ...), custom_call_target="tpu_custom_call" | custom-call | flops 68719476736 | bytes 16777216 | tf_op jit(solution)/shard_map/feed/pallas_call | solution.py:440
  61.4 1.4 %guide.1 = (f32[192,384]{1,0:T(8,128)S(1)}, bf16[192,384]{1,0:T(8,128)(2,1)S(1)}, bf16[192,384]{1,0:T(8,128)(2,1)S(1)}, bf16[192,384]{1,0:T(8,128)(2,1)S(1)}) custom-call(bf16[192,1536]{1,0:T(8,128)(2,1)S(1)} %get-tuple-element.41.hidden, f32[192,1536]{1,0:T(8,128)S(1)} %get-tuple-element.42.mixed, ...), custom_call_target="tpu_custom_call" | custom-call | tf_op jit(solution)/shard_map/guide/pallas_call | solution.py:541
  62.7 0.9 %collective-permute-start.17 = (bf16[192,384]{1,0:T(8,128)(2,1)S(1)}, bf16[192,384]{1,0:T(8,128)(2,1)S(1)}, u32[]{:S(2)}, u32[]{:S(2)}) collective-permute-start(bf16[192,384]{1,0:T(8,128)(2,1)S(1)} %get-tuple-element.44), channel_id=1, source_target_pairs={{0,1},{1,0},{2,3},{3,2},{4,5},{5,4},{6,7},{7,6},{8,9},{9,8},{10,11... | collective-permute-start | bytes 442376 | tf_op jit(solution)/shard_map/ppermute | solution.py:492
  63.6 0.2 collective-permute-start.18
  63.8 2.5 %collective-permute-start.19 = (bf16[192,384]{1,0:T(8,128)(2,1)S(1)}, bf16[192,384]{1,0:T(8,128)(2,1)S(1)}, u32[]{:S(2)}, u32[]{:S(2)}) collective-permute-start(bf16[192,384]{1,0:T(8,128)(2,1)S(1)} %get-tuple-element.46), channel_id=1, source_target_pairs={{0,3},{1,2},{2,1},{3,0},{4,7},{5,6},{6,5},{7,4},{8,11},{9,10},{10,... | collective-permute-start | bytes 442376 | tf_op jit(solution)/shard_map/ppermute | solution.py:492
  66.3 2.6 %collective-permute-done.17.got1 = bf16[192,384]{1,0:T(8,128)(2,1)S(1)} collective-permute-done((bf16[192,384]{1,0:T(8,128)(2,1)S(1)}, bf16[192,384]{1,0:T(8,128)(2,1)S(1)}, u32[]{:S(2)}, u32[]{:S(2)}) %collective-permute-start.17) | collective-permute-done | bytes 147488 | tf_op jit(solution)/shard_map/ppermute | solution.py:492
  68.9 2.3 %collective-permute-done.18.got2 = bf16[192,384]{1,0:T(8,128)(2,1)S(1)} collective-permute-done((bf16[192,384]{1,0:T(8,128)(2,1)S(1)}, bf16[192,384]{1,0:T(8,128)(2,1)S(1)}, u32[]{:S(2)}, u32[]{:S(2)}) %collective-permute-start.18) | collective-permute-done | bytes 147488 | tf_op jit(solution)/shard_map/ppermute | solution.py:492
  71.2 0.3 place.1
  71.5 1.9 %collective-permute-start.20 = (bf16[96,384]{1,0:T(8,128)(2,1)S(1)}, bf16[96,384]{1,0:T(8,128)(2,1)S(1)}, u32[]{:S(2)}, u32[]{:S(2)}) collective-permute-start(bf16[96,384]{1,0:T(8,128)(2,1)S(1)} %get-tuple-element.48), channel_id=1, source_target_pairs={{0,12},{4,8},{8,4},{12,0},{1,13},{5,9},{9,5},{13,1},{2,14},{6,10},... | collective-permute-start | bytes 221192 | tf_op jit(solution)/shard_map/ppermute | solution.py:492
  73.4 0.4 collective-permute-start.21
  73.8 2.2 %collective-permute-start.22 = (bf16[96,384]{1,0:T(8,128)(2,1)S(1)}, bf16[96,384]{1,0:T(8,128)(2,1)S(1)}, u32[]{:S(2)}, u32[]{:S(2)}) collective-permute-start(bf16[96,384]{1,0:T(8,128)(2,1)S(1)} %get-tuple-element.50), channel_id=1, source_target_pairs={{0,4},{4,0},{8,12},{12,8},{1,5},{5,1},{9,13},{13,9},{2,6},{6,2},{1... | collective-permute-start | bytes 221192 | tf_op jit(solution)/shard_map/ppermute | solution.py:492
  76.0 1.8 %collective-permute-done.20.refs_1_ = bf16[96,384]{1,0:T(8,128)(2,1)S(1)} collective-permute-done((bf16[96,384]{1,0:T(8,128)(2,1)S(1)}, bf16[96,384]{1,0:T(8,128)(2,1)S(1)}, u32[]{:S(2)}, u32[]{:S(2)}) %collective-permute-start.20) | collective-permute-done | bytes 73760 | tf_op jit(solution)/shard_map/ppermute | solution.py:492
  77.8 1.6 %collective-permute-done.21.refs_2_ = bf16[96,384]{1,0:T(8,128)(2,1)S(1)} collective-permute-done((bf16[96,384]{1,0:T(8,128)(2,1)S(1)}, bf16[96,384]{1,0:T(8,128)(2,1)S(1)}, u32[]{:S(2)}, u32[]{:S(2)}) %collective-permute-start.21) | collective-permute-done | bytes 73760 | tf_op jit(solution)/shard_map/ppermute | solution.py:492
  79.3 0.8 arrange.1
  (29 shorter events, 0.1 us)
Async XLA Ops:
  0.0 13.5 %copy-start = (s32[384,1]{0,1:T(1,128)S(1)}, s32[384,1]{0,1:T(1,128)}, u32[]{:S(2)}) copy-start(s32[384,1]{0,1:T(1,128)} %param.21) | copy-start | bytes 4612
  0.0 17.9 %collective-permute-start.3 = (bf16[384,1536]{1,0:T(8,128)(2,1)}, bf16[384,1536]{1,0:T(8,128)(2,1)S(1)}, u32[]{:S(2)}, u32[]{:S(2)}) collective-permute-start(bf16[384,1536]{1,0:T(8,128)(2,1)} %own.1), channel_id=1, source_target_pairs={{0,1},{1,0},{2,3},{3,2},{16,18},{17,19},{18,16},{19,17},{4,5},{5,4... | collective-permute-start | bytes 3538952 | tf_op jit(solution)/shard_map/ppermute | solution.py:188
  4.2 21.9 %collective-permute-start = (bf16[1168,128]{1,0:T(8,128)(2,1)S(1)}, bf16[1168,128]{1,0:T(8,128)(2,1)S(1)}, u32[]{:S(2)}, u32[]{:S(2)}) collective-permute-start(bf16[1168,128]{1,0:T(8,128)(2,1)S(1)} %get-tuple-element.29), channel_id=1, source_target_pairs={{0,8},{8,0},{12,4},{16,24},{20,28},{28,20},{1,9},{9,1},{13,5},{17,... | collective-permute-start | bytes 897032 | tf_op jit(solution)/shard_map/ppermute | solution.py:53
  8.7 17.4 %collective-permute-start.1 = (bf16[1168,128]{1,0:T(8,128)(2,1)S(1)}, bf16[1168,128]{1,0:T(8,128)(2,1)S(1)}, u32[]{:S(2)}, u32[]{:S(2)}) collective-permute-start(bf16[1168,128]{1,0:T(8,128)(2,1)S(1)} %get-tuple-element.30), channel_id=1, source_target_pairs={{4,8},{8,4},{12,0},{16,28},{20,24},{24,20},{5,9},{9,5},{13,1},{17,... | collective-permute-start | bytes 897032 | tf_op jit(solution)/shard_map/ppermute | solution.py:53
  10.0 16.1 %collective-permute-start.2 = (bf16[1168,128]{1,0:T(8,128)(2,1)S(1)}, bf16[1168,128]{1,0:T(8,128)(2,1)S(1)}, u32[]{:S(2)}, u32[]{:S(2)}) collective-permute-start(bf16[1168,128]{1,0:T(8,128)(2,1)S(1)} %get-tuple-element.31), channel_id=1, source_target_pairs={{0,4},{4,0},{12,8},{16,20},{24,28},{28,24},{1,5},{5,1},{13,9},{17,... | collective-permute-start | bytes 897032 | tf_op jit(solution)/shard_map/ppermute | solution.py:53
  13.7 4.1 %copy-start.4 = (s32[384]{0:T(512)S(1)}, s32[384]{0:T(512)}, u32[]{:S(2)}) copy-start(s32[384]{0:T(512)} %param.20) | copy-start | bytes 4612
  17.8 8.4 %copy-start.5 = (f32[3]{0:T(128)S(1)}, f32[3]{0:T(128)}, u32[]{:S(2)}) copy-start(f32[3]{0:T(128)} %param.19) | copy-start | bytes 40
  18.1 23.3 %collective-permute-start.9 = (bf16[192,1536]{1,0:T(8,128)(2,1)S(1)}, bf16[192,1536]{1,0:T(8,128)(2,1)S(1)}, u32[]{:S(2)}, u32[]{:S(2)}) collective-permute-start(bf16[192,1536]{1,0:T(8,128)(2,1)S(1)} %cut.1.refs_6_), channel_id=1, source_target_pairs={{0,2},{1,3},{2,0},{3,1},{16,17},{17,16},{18,19},{19,18},{4,6},{5,7... | collective-permute-start | bytes 1769480 | tf_op jit(solution)/shard_map/ppermute | solution.py:188
  19.6 26.6 %collective-permute-start.8 = (bf16[384,1536]{1,0:T(8,128)(2,1)S(1)}, bf16[384,1536]{1,0:T(8,128)(2,1)S(1)}, u32[]{:S(2)}, u32[]{:S(2)}) collective-permute-start(bf16[384,1536]{1,0:T(8,128)(2,1)S(1)} %collective-permute-done.3.got.near), channel_id=1, source_target_pairs={{0,16},{16,0},{1,17},{17,1},{2,18},{18,2},{3,19},{19,3},{4,20},{20... | collective-permute-start | bytes 3538952 | tf_op jit(solution)/shard_map/ppermute | solution.py:492
  19.7 8.7 %copy-start.1 = (bf16[384,192]{1,0:T(8,128)(2,1)}, bf16[384,192]{1,0:T(8,128)(2,1)S(1)}, u32[]{:S(2)}) copy-start(bf16[384,192]{1,0:T(8,128)(2,1)S(1)} %fusion.refs_5_.placing) | copy-start | bytes 442372
  28.4 9.2 %collective-permute-start.4 = (bf16[384,128]{1,0:T(8,128)(2,1)S(1)}, bf16[384,128]{1,0:T(8,128)(2,1)S(1)}, u32[]{:S(2)}, u32[]{:S(2)}) collective-permute-start(bf16[384,128]{1,0:T(8,128)(2,1)S(1)} %get-tuple-element.36), channel_id=1, source_target_pairs={{8,0},{0,8},{4,12},{24,16},{28,20},{20,28},{9,1},{1,9},{5,13},{25,... | collective-permute-start | bytes 294920 | tf_op jit(solution)/shard_map/ppermute | solution.py:53
  33.2 4.5 %collective-permute-start.5 = (bf16[384,128]{1,0:T(8,128)(2,1)S(1)}, bf16[384,128]{1,0:T(8,128)(2,1)S(1)}, u32[]{:S(2)}, u32[]{:S(2)}) collective-permute-start(bf16[384,128]{1,0:T(8,128)(2,1)S(1)} %get-tuple-element.37), channel_id=1, source_target_pairs={{8,4},{4,8},{0,12},{28,16},{24,20},{20,24},{9,5},{5,9},{1,13},{29,... | collective-permute-start | bytes 294920 | tf_op jit(solution)/shard_map/ppermute | solution.py:53
  34.5 6.6 %collective-permute-start.6 = (bf16[384,128]{1,0:T(8,128)(2,1)S(1)}, bf16[384,128]{1,0:T(8,128)(2,1)S(1)}, u32[]{:S(2)}, u32[]{:S(2)}) collective-permute-start(bf16[384,128]{1,0:T(8,128)(2,1)S(1)} %get-tuple-element.38), channel_id=1, source_target_pairs={{4,0},{0,4},{8,12},{20,16},{28,24},{24,28},{5,1},{1,5},{9,13},{21,... | collective-permute-start | bytes 294920 | tf_op jit(solution)/shard_map/ppermute | solution.py:53
  41.4 3.6 %collective-permute-start.10 = (bf16[192,1536]{1,0:T(8,128)(2,1)S(1)}, bf16[192,1536]{1,0:T(8,128)(2,1)S(1)}, u32[]{:S(2)}, u32[]{:S(2)}) collective-permute-start(bf16[192,1536]{1,0:T(8,128)(2,1)S(1)} %gate.1.far), channel_id=1, source_target_pairs={{0,16},{16,0},{1,17},{17,1},{2,18},{18,2},{3,19},{19,3},{4,20},{20... | collective-permute-start | bytes 1769480 | tf_op jit(solution)/shard_map/ppermute | solution.py:492
  41.5 7.0 %collective-permute-start.13 = (bf16[192,384]{1,0:T(8,128)(2,1)S(1)}, bf16[192,384]{1,0:T(8,128)(2,1)S(1)}, u32[]{:S(2)}, u32[]{:S(2)}) collective-permute-start(bf16[192,384]{1,0:T(8,128)(2,1)S(1)} %get-tuple-element.40.after.refs_0_), channel_id=1, source_target_pairs={{0,1},{1,0},{2,3},{3,2},{4,5},{5,4},{6,7},{7,6},{8,9},{9,8},{10,11... | collective-permute-start | bytes 442376 | tf_op jit(solution)/shard_map/ppermute | solution.py:492
  42.8 9.9 %collective-permute-start.14 = (bf16[192,384]{1,0:T(8,128)(2,1)S(1)}, bf16[192,384]{1,0:T(8,128)(2,1)S(1)}, u32[]{:S(2)}, u32[]{:S(2)}) collective-permute-start(bf16[192,384]{1,0:T(8,128)(2,1)S(1)} %get-tuple-element.40.after.refs_0_), channel_id=1, source_target_pairs={{0,2},{1,3},{2,0},{3,1},{4,6},{5,7},{6,4},{7,5},{8,10},{9,11},{10,... | collective-permute-start | bytes 442376 | tf_op jit(solution)/shard_map/ppermute | solution.py:492
  43.7 9.0 %collective-permute-start.15 = (bf16[192,384]{1,0:T(8,128)(2,1)S(1)}, bf16[192,384]{1,0:T(8,128)(2,1)S(1)}, u32[]{:S(2)}, u32[]{:S(2)}) collective-permute-start(bf16[192,384]{1,0:T(8,128)(2,1)S(1)} %get-tuple-element.40.after.refs_0_), channel_id=1, source_target_pairs={{0,3},{1,2},{2,1},{3,0},{4,7},{5,6},{6,5},{7,4},{8,11},{9,10},{10,... | collective-permute-start | bytes 442376 | tf_op jit(solution)/shard_map/ppermute | solution.py:492
  45.0 7.6 %copy-start.3 = (f32[3,4,1536]{2,1,0:T(4,128)S(1)}, f32[3,4,1536]{2,1,0:T(4,128)}, u32[]{:S(2)}) copy-start(f32[3,4,1536]{2,1,0:T(4,128)} %mod.1) | copy-start | bytes 221188
  45.0 11.4 %collective-permute-start.11 = (bf16[192,384]{1,0:T(8,128)(2,1)S(1)}, bf16[192,384]{1,0:T(8,128)(2,1)S(1)}, u32[]{:S(2)}, u32[]{:S(2)}) collective-permute-start(bf16[192,384]{1,0:T(8,128)(2,1)S(1)} %get-tuple-element.39.refs_0_), channel_id=1, source_target_pairs={{0,1},{1,0},{2,3},{3,2},{4,5},{5,4},{6,7},{7,6},{8,9},{9,8},{10,11... | collective-permute-start | bytes 442376 | tf_op jit(solution)/shard_map/ppermute | solution.py:492
  46.3 11.9 %collective-permute-start.12 = (bf16[192,384]{1,0:T(8,128)(2,1)S(1)}, bf16[192,384]{1,0:T(8,128)(2,1)S(1)}, u32[]{:S(2)}, u32[]{:S(2)}) collective-permute-start(bf16[192,384]{1,0:T(8,128)(2,1)S(1)} %get-tuple-element.39.refs_0_), channel_id=1, source_target_pairs={{0,2},{1,3},{2,0},{3,1},{4,6},{5,7},{6,4},{7,5},{8,10},{9,11},{10,... | collective-permute-start | bytes 442376 | tf_op jit(solution)/shard_map/ppermute | solution.py:492
  48.5 10.6 %collective-permute-start.7 = (bf16[192,384]{1,0:T(8,128)(2,1)S(1)}, bf16[192,384]{1,0:T(8,128)(2,1)S(1)}, u32[]{:S(2)}, u32[]{:S(2)}) collective-permute-start(bf16[192,384]{1,0:T(8,128)(2,1)S(1)} %get-tuple-element.39.refs_0_), channel_id=1, source_target_pairs={{0,3},{1,2},{2,1},{3,0},{4,7},{5,6},{6,5},{7,4},{8,11},{9,10},{10,... | collective-permute-start | bytes 442376 | tf_op jit(solution)/shard_map/ppermute | solution.py:492
  56.4 4.9 %collective-permute-start.16 = (bf16[192,1536]{1,0:T(8,128)(2,1)S(1)}, bf16[192,1536]{1,0:T(8,128)(2,1)S(1)}, u32[]{:S(2)}, u32[]{:S(2)}) collective-permute-start(bf16[192,1536]{1,0:T(8,128)(2,1)S(1)} %feed.3), channel_id=1, source_target_pairs={{0,16},{16,0},{1,17},{17,1},{2,18},{18,2},{3,19},{19,3},{4,20},{20... | collective-permute-start | bytes 1769480 | tf_op jit(solution)/shard_map/ppermute | solution.py:492
  61.3 9.9 %copy-start.2 = (bf16[384,192]{1,0:T(8,128)(2,1)S(1)}, bf16[384,192]{1,0:T(8,128)(2,1)}, u32[]{:S(2)}) copy-start(bf16[384,192]{1,0:T(8,128)(2,1)} %copy-done.1) | copy-start | bytes 442372
  62.7 6.2 %collective-permute-start.17 = (bf16[192,384]{1,0:T(8,128)(2,1)S(1)}, bf16[192,384]{1,0:T(8,128)(2,1)S(1)}, u32[]{:S(2)}, u32[]{:S(2)}) collective-permute-start(bf16[192,384]{1,0:T(8,128)(2,1)S(1)} %get-tuple-element.44), channel_id=1, source_target_pairs={{0,1},{1,0},{2,3},{3,2},{4,5},{5,4},{6,7},{7,6},{8,9},{9,8},{10,11... | collective-permute-start | bytes 442376 | tf_op jit(solution)/shard_map/ppermute | solution.py:492
  63.6 7.7 %collective-permute-start.18 = (bf16[192,384]{1,0:T(8,128)(2,1)S(1)}, bf16[192,384]{1,0:T(8,128)(2,1)S(1)}, u32[]{:S(2)}, u32[]{:S(2)}) collective-permute-start(bf16[192,384]{1,0:T(8,128)(2,1)S(1)} %get-tuple-element.45), channel_id=1, source_target_pairs={{0,2},{1,3},{2,0},{3,1},{4,6},{5,7},{6,4},{7,5},{8,10},{9,11},{10,... | collective-permute-start | bytes 442376 | tf_op jit(solution)/shard_map/ppermute | solution.py:492
  63.8 7.5 %collective-permute-start.19 = (bf16[192,384]{1,0:T(8,128)(2,1)S(1)}, bf16[192,384]{1,0:T(8,128)(2,1)S(1)}, u32[]{:S(2)}, u32[]{:S(2)}) collective-permute-start(bf16[192,384]{1,0:T(8,128)(2,1)S(1)} %get-tuple-element.46), channel_id=1, source_target_pairs={{0,3},{1,2},{2,1},{3,0},{4,7},{5,6},{6,5},{7,4},{8,11},{9,10},{10,... | collective-permute-start | bytes 442376 | tf_op jit(solution)/shard_map/ppermute | solution.py:492
  71.5 6.2 %collective-permute-start.20 = (bf16[96,384]{1,0:T(8,128)(2,1)S(1)}, bf16[96,384]{1,0:T(8,128)(2,1)S(1)}, u32[]{:S(2)}, u32[]{:S(2)}) collective-permute-start(bf16[96,384]{1,0:T(8,128)(2,1)S(1)} %get-tuple-element.48), channel_id=1, source_target_pairs={{0,12},{4,8},{8,4},{12,0},{1,13},{5,9},{9,5},{13,1},{2,14},{6,10},... | collective-permute-start | bytes 221192 | tf_op jit(solution)/shard_map/ppermute | solution.py:492
  73.4 5.9 %collective-permute-start.21 = (bf16[96,384]{1,0:T(8,128)(2,1)S(1)}, bf16[96,384]{1,0:T(8,128)(2,1)S(1)}, u32[]{:S(2)}, u32[]{:S(2)}) collective-permute-start(bf16[96,384]{1,0:T(8,128)(2,1)S(1)} %get-tuple-element.49), channel_id=1, source_target_pairs={{0,8},{4,12},{8,0},{12,4},{1,9},{5,13},{9,1},{13,5},{2,10},{6,14},... | collective-permute-start | bytes 221192 | tf_op jit(solution)/shard_map/ppermute | solution.py:492
  73.8 5.6 %collective-permute-start.22 = (bf16[96,384]{1,0:T(8,128)(2,1)S(1)}, bf16[96,384]{1,0:T(8,128)(2,1)S(1)}, u32[]{:S(2)}, u32[]{:S(2)}) collective-permute-start(bf16[96,384]{1,0:T(8,128)(2,1)S(1)} %get-tuple-element.50), channel_id=1, source_target_pairs={{0,4},{4,0},{8,12},{12,8},{1,5},{5,1},{9,13},{13,9},{2,6},{6,2},{1... | collective-permute-start | bytes 221192 | tf_op jit(solution)/shard_map/ppermute | solution.py:492

commit v11 on v10

--- a/solution.py
+++ b/solution.py
@@ -365,7 +365,7 @@
 
 
 def project_kernel(*refs):
-    att, w_out, out = refs[:3], refs[3], refs[4]
+    att, w_out, out = (refs[0], refs[2], refs[1]), refs[3], refs[4]
     rows_in = jnp.concatenate([piece[...] for piece in att], axis=1)
     depth = rows_in.shape[1]
     for start in range(0, D, 512):
@@ -384,7 +384,7 @@
         compiler_params=params(16),
         cost_estimate=cost(2**32, 2**22),
         name="project",
-    )(*att, kept(w_out))
+    )(att[0], att[2], att[1], kept(w_out))
 
 
 def feed_kernel(turn, count, *refs):

time: 80.4 us -> 80.4 us (level)
  no operation moved by 1% of the time
where the time goes in v11:
time: 80.4 us; the launch traced here: 80.1 us
  starting transfers between devices  38.2 us (48%)
  waiting for transfers between devices  22.6 us (28%)
  Pallas kernels  18.4 us (23%)
    ppermute x6, starting transfers between devices, hop(): return lax.ppermute(value, ('cfg', 'seq'), pairs)  18.4 us
    ppermute x15, starting transfers between devices, exchanged(): return lax.ppermute(value, axis, pairs)  15.3 us
    ppermute x15, waiting for transfers between devices, exchanged(): return lax.ppermute(value, axis, pairs)  12.7 us
    ppermute x6, waiting for transfers between devices, hop(): return lax.ppermute(value, ('cfg', 'seq'), pairs)  9.83 us
    pallas_call x2, Pallas kernels, feed(): pl.pallas_call(functools.partial(feed_kernel, turn, len(att)), out_shape=...  5.93 us
    ppermute x2, starting transfers between devices, across(): return lax.ppermute(value, ('cfg', 'blk'), pairs)  4.52 us
    pallas_call x1, Pallas kernels, load(): pl.pallas_call(load_kernel, out_shape=[pltpu.VMEM(array.shape, BF16) for...  4.07 us
    pallas_call x1, Pallas kernels, attention_by_head(): pl.pallas_call(attend_kernel, out_shape=[shape_of((slots, 128))] * 4, in_...  2.08 us
  transfers between devices with their start and end apart: 23, of which 8 were waited for; matrix products, arithmetic and copies ran while one was open for 1% of the time, Pallas kernels for 20%

profile of v11, /device:TPU:0, one launch (start us, length us, event | category | flops | bytes accessed | tf_op | source)
XLA Modules:
  0.0 80.1 jit_solution(17605158315001630462)
XLA Ops:
  0.0 2.9 %collective-permute-start.3 = (bf16[384,1536]{1,0:T(8,128)(2,1)}, bf16[384,1536]{1,0:T(8,128)(2,1)S(1)}, u32[]{:S(2)}, u32[]{:S(2)}) collective-permute-start(bf16[384,1536]{1,0:T(8,128)(2,1)} %own.1), channel_id=1, source_target_pairs={{0,1},{1,0},{2,3},{3,2},{16,18},{17,19},{18,16},{19,17},{4,5},{5,4... | collective-permute-start | bytes 3538952 | tf_op jit(solution)/shard_map/ppermute | solution.py:188
  2.9 1.3 %pack.1 = (bf16[1168,128]{1,0:T(8,128)(2,1)S(1)}, bf16[1168,128]{1,0:T(8,128)(2,1)S(1)}, bf16[1168,128]{1,0:T(8,128)(2,1)S(1)}, bf16[1168,128]{1,0:T(8,128)(2,1)S(1)}) custom-call(bf16[384,384]{1,0:T(8,128)(2,1)} %bitcast.7, bf16[384,384]{1,0:T(8,128)(2,1)} %bitcast.8, bf16[384,384]{1,0:T(8,128)(2,1)} %bitcast.9, s32[3,128]{1,0:T(4,128)} %bitcast.12), custom_call_target="tpu_custom_call" | custom-call | tf_op jit(solution)/shard_map/pack/pallas_call | solution.py:266
  4.2 4.5 %collective-permute-start = (bf16[1168,128]{1,0:T(8,128)(2,1)S(1)}, bf16[1168,128]{1,0:T(8,128)(2,1)S(1)}, u32[]{:S(2)}, u32[]{:S(2)}) collective-permute-start(bf16[1168,128]{1,0:T(8,128)(2,1)S(1)} %get-tuple-element.29), channel_id=1, source_target_pairs={{0,8},{8,0},{12,4},{16,24},{20,28},{28,20},{1,9},{9,1},{13,5},{17,... | collective-permute-start | bytes 897032 | tf_op jit(solution)/shard_map/ppermute | solution.py:53
  8.7 1.3 %collective-permute-start.1 = (bf16[1168,128]{1,0:T(8,128)(2,1)S(1)}, bf16[1168,128]{1,0:T(8,128)(2,1)S(1)}, u32[]{:S(2)}, u32[]{:S(2)}) collective-permute-start(bf16[1168,128]{1,0:T(8,128)(2,1)S(1)} %get-tuple-element.30), channel_id=1, source_target_pairs={{4,8},{8,4},{12,0},{16,28},{20,24},{24,20},{5,9},{9,5},{13,1},{17,... | collective-permute-start | bytes 897032 | tf_op jit(solution)/shard_map/ppermute | solution.py:53
  10.0 3.4 %collective-permute-start.2 = (bf16[1168,128]{1,0:T(8,128)(2,1)S(1)}, bf16[1168,128]{1,0:T(8,128)(2,1)S(1)}, u32[]{:S(2)}, u32[]{:S(2)}) collective-permute-start(bf16[1168,128]{1,0:T(8,128)(2,1)S(1)} %get-tuple-element.31), channel_id=1, source_target_pairs={{0,4},{4,0},{12,8},{16,20},{24,28},{28,24},{1,5},{5,1},{13,9},{17,... | collective-permute-start | bytes 897032 | tf_op jit(solution)/shard_map/ppermute | solution.py:53
  13.5 0.1 constant_dynamic-slice_fusion
  13.5 0.2 convert_reduce_fusion
  13.7 0.0 copy-start.4
  13.7 4.1 %load.1 = (bf16[1536,1536]{1,0:T(8,128)(2,1)S(1)}, bf16[1536,1536]{1,0:T(8,128)(2,1)S(1)}, bf16[384,1536]{1,0:T(8,128)(2,1)S(1)}) custom-call(bf16[1536,1536]{1,0:T(8,128)(2,1)} %refs_0_.1, bf16[1536,1536]{1,0:T(8,128)(2,1)} %refs_1_.1, bf16[384,1536]{1,0:T(8,128)(2,1)} %bitcast.13, bf16[1168,128]{1,0:T(8,128)(2,1)S(1)} %get-tuple-element.28.refs_3_.refs_0_), custom_call_target="tpu_custom_call" | custom-call | flops 17179869184 | bytes 16777216 | tf_op jit(solution)/shard_map/load/pallas_call | solution.py:172
  17.8 0.1 compare_select_fusion
  17.9 0.1 cut.1.refs_6_
  18.1 1.6 %collective-permute-start.9 = (bf16[192,1536]{1,0:T(8,128)(2,1)S(1)}, bf16[192,1536]{1,0:T(8,128)(2,1)S(1)}, u32[]{:S(2)}, u32[]{:S(2)}) collective-permute-start(bf16[192,1536]{1,0:T(8,128)(2,1)S(1)} %cut.1.refs_6_), channel_id=1, source_target_pairs={{0,2},{1,3},{2,0},{3,1},{16,17},{17,16},{18,19},{19,18},{4,6},{5,7... | collective-permute-start | bytes 1769480 | tf_op jit(solution)/shard_map/ppermute | solution.py:188
  19.7 6.4 %collective-permute-done.refs_1_ = bf16[1168,128]{1,0:T(8,128)(2,1)S(1)} collective-permute-done((bf16[1168,128]{1,0:T(8,128)(2,1)S(1)}, bf16[1168,128]{1,0:T(8,128)(2,1)S(1)}, u32[]{:S(2)}, u32[]{:S(2)}) %collective-permute-start) | collective-permute-done | bytes 299040 | tf_op jit(solution)/shard_map/ppermute | solution.py:53
  26.1 0.1 broadcast_in_dim.9.refs_4_.refs_6_.refs_9_.clip_ref
  26.2 0.1 broadcast_in_dim.11.refs_7_.scale_ref
  26.3 2.1 %attend.1 = (bf16[384,128]{1,0:T(8,128)(2,1)S(1)}, bf16[384,128]{1,0:T(8,128)(2,1)S(1)}, bf16[384,128]{1,0:T(8,128)(2,1)S(1)}, bf16[384,128]{1,0:T(8,128)(2,1)S(1)}) custom-call(bf16[1168,128]{1,0:T(8,128)(2,1)S(1)} %get-tuple-element.28.refs_3_.refs_0_, bf16[1168,128]{1,0:T(8,128)(2,1)S(1)} %collective-permute-done.refs_1_, ...), custom_call_target="tpu_custom_call" | custom-call | flops 4294967296 | bytes 2097152 | tf_op jit(solution)/shard_map/attend/pallas_call | solution.py:281
  28.4 4.8 %collective-permute-start.4 = (bf16[384,128]{1,0:T(8,128)(2,1)S(1)}, bf16[384,128]{1,0:T(8,128)(2,1)S(1)}, u32[]{:S(2)}, u32[]{:S(2)}) collective-permute-start(bf16[384,128]{1,0:T(8,128)(2,1)S(1)} %get-tuple-element.36), channel_id=1, source_target_pairs={{8,0},{0,8},{4,12},{24,16},{28,20},{20,28},{9,1},{1,9},{5,13},{25,... | collective-permute-start | bytes 294920 | tf_op jit(solution)/shard_map/ppermute | solution.py:53
  33.2 1.3 %collective-permute-start.5 = (bf16[384,128]{1,0:T(8,128)(2,1)S(1)}, bf16[384,128]{1,0:T(8,128)(2,1)S(1)}, u32[]{:S(2)}, u32[]{:S(2)}) collective-permute-start(bf16[384,128]{1,0:T(8,128)(2,1)S(1)} %get-tuple-element.37), channel_id=1, source_target_pairs={{8,4},{4,8},{0,12},{28,16},{24,20},{20,24},{9,5},{5,9},{1,13},{29,... | collective-permute-start | bytes 294920 | tf_op jit(solution)/shard_map/ppermute | solution.py:53
  34.5 3.2 %collective-permute-start.6 = (bf16[384,128]{1,0:T(8,128)(2,1)S(1)}, bf16[384,128]{1,0:T(8,128)(2,1)S(1)}, u32[]{:S(2)}, u32[]{:S(2)}) collective-permute-start(bf16[384,128]{1,0:T(8,128)(2,1)S(1)} %get-tuple-element.38), channel_id=1, source_target_pairs={{4,0},{0,4},{8,12},{20,16},{28,24},{24,28},{5,1},{1,5},{9,13},{21,... | collective-permute-start | bytes 294920 | tf_op jit(solution)/shard_map/ppermute | solution.py:53
  37.7 3.4 %collective-permute-done.6.back3 = bf16[384,128]{1,0:T(8,128)(2,1)S(1)} collective-permute-done((bf16[384,128]{1,0:T(8,128)(2,1)S(1)}, bf16[384,128]{1,0:T(8,128)(2,1)S(1)}, u32[]{:S(2)}, u32[]{:S(2)}) %collective-permute-start.6) | collective-permute-done | bytes 98336 | tf_op jit(solution)/shard_map/ppermute | solution.py:53
  41.1 0.3 regroup.1
  41.4 0.1 collective-permute-start.10
  41.5 1.3 %collective-permute-start.13 = (bf16[192,384]{1,0:T(8,128)(2,1)S(1)}, bf16[192,384]{1,0:T(8,128)(2,1)S(1)}, u32[]{:S(2)}, u32[]{:S(2)}) collective-permute-start(bf16[192,384]{1,0:T(8,128)(2,1)S(1)} %get-tuple-element.40.after.refs_0_), channel_id=1, source_target_pairs={{0,1},{1,0},{2,3},{3,2},{4,5},{5,4},{6,7},{7,6},{8,9},{9,8},{10,11... | collective-permute-start | bytes 442376 | tf_op jit(solution)/shard_map/ppermute | solution.py:492
  42.8 0.9 %collective-permute-start.14 = (bf16[192,384]{1,0:T(8,128)(2,1)S(1)}, bf16[192,384]{1,0:T(8,128)(2,1)S(1)}, u32[]{:S(2)}, u32[]{:S(2)}) collective-permute-start(bf16[192,384]{1,0:T(8,128)(2,1)S(1)} %get-tuple-element.40.after.refs_0_), channel_id=1, source_target_pairs={{0,2},{1,3},{2,0},{3,1},{4,6},{5,7},{6,4},{7,5},{8,10},{9,11},{10,... | collective-permute-start | bytes 442376 | tf_op jit(solution)/shard_map/ppermute | solution.py:492
  43.7 1.4 %collective-permute-start.15 = (bf16[192,384]{1,0:T(8,128)(2,1)S(1)}, bf16[192,384]{1,0:T(8,128)(2,1)S(1)}, u32[]{:S(2)}, u32[]{:S(2)}) collective-permute-start(bf16[192,384]{1,0:T(8,128)(2,1)S(1)} %get-tuple-element.40.after.refs_0_), channel_id=1, source_target_pairs={{0,3},{1,2},{2,1},{3,0},{4,7},{5,6},{6,5},{7,4},{8,11},{9,10},{10,... | collective-permute-start | bytes 442376 | tf_op jit(solution)/shard_map/ppermute | solution.py:492
  45.0 0.7 collective-permute-start.11
  45.7 1.5 %collective-permute-start.12 = (bf16[192,384]{1,0:T(8,128)(2,1)S(1)}, bf16[192,384]{1,0:T(8,128)(2,1)S(1)}, u32[]{:S(2)}, u32[]{:S(2)}) collective-permute-start(bf16[192,384]{1,0:T(8,128)(2,1)S(1)} %get-tuple-element.39.refs_0_), channel_id=1, source_target_pairs={{0,1},{1,0},{2,3},{3,2},{4,5},{5,4},{6,7},{7,6},{8,9},{9,8},{10,11... | collective-permute-start | bytes 442376 | tf_op jit(solution)/shard_map/ppermute | solution.py:492
  47.2 1.3 %join.1.refs_3_.refs_1_.refs_4_ = bf16[1536,1536]{1,0:T(8,128)(2,1)S(1)} custom-call(bf16[384,1536]{1,0:T(8,128)(2,1)} %own.1, bf16[384,1536]{1,0:T(8,128)(2,1)S(1)} %collective-permute-done.3.got.near, bf16[384,1536]{1,0:T(8,128)(2,1)S(1)} %collective-permute-done.8.near_swap, bf16[192,1536]{1,0:T(8,128)(2,1)S(1)} %gate.1.far, ...), custom_call_target="tpu_custom_call" | custom-call | tf_op jit(solution)/shard_map/join/pallas_call | solution.py:253
  48.5 1.4 %collective-permute-start.7 = (bf16[192,384]{1,0:T(8,128)(2,1)S(1)}, bf16[192,384]{1,0:T(8,128)(2,1)S(1)}, u32[]{:S(2)}, u32[]{:S(2)}) collective-permute-start(bf16[192,384]{1,0:T(8,128)(2,1)S(1)} %get-tuple-element.39.refs_0_), channel_id=1, source_target_pairs={{0,3},{1,2},{2,1},{3,0},{4,7},{5,6},{6,5},{7,4},{8,11},{9,10},{10,... | collective-permute-start | bytes 442376 | tf_op jit(solution)/shard_map/ppermute | solution.py:492
  49.9 2.7 %collective-permute-done.14.refs_2_ = bf16[192,384]{1,0:T(8,128)(2,1)S(1)} collective-permute-done((bf16[192,384]{1,0:T(8,128)(2,1)S(1)}, bf16[192,384]{1,0:T(8,128)(2,1)S(1)}, u32[]{:S(2)}, u32[]{:S(2)}) %collective-permute-start.14) | collective-permute-done | bytes 147488 | tf_op jit(solution)/shard_map/ppermute | solution.py:492
  52.6 3.7 %feed.3 = bf16[192,1536]{1,0:T(8,128)(2,1)S(1)} custom-call(bf16[192,384]{1,0:T(8,128)(2,1)S(1)} %get-tuple-element.40.after.refs_0_, bf16[192,384]{1,0:T(8,128)(2,1)S(1)} %collective-permute-done.13.refs_1_, bf16[192,384]{1,0:T(8,128)(2,1)S(1)} %collective-permute-done.14.refs_2_, bf16[192,384]{1,0:T(8,128)(2,1)S(1)} %collective-permute-done.15.refs_3_, ...), custom_call_target="tpu_custom_call" | custom-call | flops 68719476736 | bytes 16777216 | tf_op jit(solution)/shard_map/feed/pallas_call | solution.py:440
  56.4 0.1 collective-permute-start.16
  56.5 1.7 %collective-permute-done.11.refs_1_ = bf16[192,384]{1,0:T(8,128)(2,1)S(1)} collective-permute-done((bf16[192,384]{1,0:T(8,128)(2,1)S(1)}, bf16[192,384]{1,0:T(8,128)(2,1)S(1)}, u32[]{:S(2)}, u32[]{:S(2)}) %collective-permute-start.11) | collective-permute-done | bytes 147488 | tf_op jit(solution)/shard_map/ppermute | solution.py:492
  58.2 0.9 %project.1.refs_7_ = f32[192,1536]{1,0:T(8,128)S(1)} custom-call(bf16[192,384]{1,0:T(8,128)(2,1)S(1)} %get-tuple-element.39.refs_0_, bf16[192,384]{1,0:T(8,128)(2,1)S(1)} %collective-permute-done.11.refs_1_, bf16[192,384]{1,0:T(8,128)(2,1)S(1)} %collective-permute-done.12.refs_2_, bf16[1536,1536]{1,0:T(8,128)(2,1)S(1)} %join.1.refs_3_.refs_1_.refs_4_), custom_call_target="tpu_custom_call" | custom-call | flops 4294967296 | bytes 4194304 | tf_op jit(solution)/shard_map/project/pallas_call | solution.py:379
  59.1 2.2 %feed.2 = (bf16[192,1536]{1,0:T(8,128)(2,1)S(1)}, f32[192,1536]{1,0:T(8,128)S(1)}) custom-call(bf16[192,384]{1,0:T(8,128)(2,1)S(1)} %collective-permute-done.7.refs_0_, bf16[1536,1536]{1,0:T(8,128)(2,1)S(1)} %join.1.refs_3_.refs_1_.refs_4_, bf16[1536,1536]{1,0:T(8,128)(2,1)S(1)} %get-tuple-element.32.refs_8_.refs_2_.refs_5_, ...), custom_call_target="tpu_custom_call" | custom-call | flops 68719476736 | bytes 16777216 | tf_op jit(solution)/shard_map/feed/pallas_call | solution.py:440
  61.4 1.4 %guide.1 = (f32[192,384]{1,0:T(8,128)S(1)}, bf16[192,384]{1,0:T(8,128)(2,1)S(1)}, bf16[192,384]{1,0:T(8,128)(2,1)S(1)}, bf16[192,384]{1,0:T(8,128)(2,1)S(1)}) custom-call(bf16[192,1536]{1,0:T(8,128)(2,1)S(1)} %get-tuple-element.41.hidden, f32[192,1536]{1,0:T(8,128)S(1)} %get-tuple-element.42.mixed, ...), custom_call_target="tpu_custom_call" | custom-call | tf_op jit(solution)/shard_map/guide/pallas_call | solution.py:541
  62.7 0.9 %collective-permute-start.17 = (bf16[192,384]{1,0:T(8,128)(2,1)S(1)}, bf16[192,384]{1,0:T(8,128)(2,1)S(1)}, u32[]{:S(2)}, u32[]{:S(2)}) collective-permute-start(bf16[192,384]{1,0:T(8,128)(2,1)S(1)} %get-tuple-element.44), channel_id=1, source_target_pairs={{0,1},{1,0},{2,3},{3,2},{4,5},{5,4},{6,7},{7,6},{8,9},{9,8},{10,11... | collective-permute-start | bytes 442376 | tf_op jit(solution)/shard_map/ppermute | solution.py:492
  63.6 0.2 collective-permute-start.18
  63.8 2.5 %collective-permute-start.19 = (bf16[192,384]{1,0:T(8,128)(2,1)S(1)}, bf16[192,384]{1,0:T(8,128)(2,1)S(1)}, u32[]{:S(2)}, u32[]{:S(2)}) collective-permute-start(bf16[192,384]{1,0:T(8,128)(2,1)S(1)} %get-tuple-element.46), channel_id=1, source_target_pairs={{0,3},{1,2},{2,1},{3,0},{4,7},{5,6},{6,5},{7,4},{8,11},{9,10},{10,... | collective-permute-start | bytes 442376 | tf_op jit(solution)/shard_map/ppermute | solution.py:492
  66.3 2.7 %collective-permute-done.17.got1 = bf16[192,384]{1,0:T(8,128)(2,1)S(1)} collective-permute-done((bf16[192,384]{1,0:T(8,128)(2,1)S(1)}, bf16[192,384]{1,0:T(8,128)(2,1)S(1)}, u32[]{:S(2)}, u32[]{:S(2)}) %collective-permute-start.17) | collective-permute-done | bytes 147488 | tf_op jit(solution)/shard_map/ppermute | solution.py:492
  69.0 2.2 %collective-permute-done.18.got2 = bf16[192,384]{1,0:T(8,128)(2,1)S(1)} collective-permute-done((bf16[192,384]{1,0:T(8,128)(2,1)S(1)}, bf16[192,384]{1,0:T(8,128)(2,1)S(1)}, u32[]{:S(2)}, u32[]{:S(2)}) %collective-permute-start.18) | collective-permute-done | bytes 147488 | tf_op jit(solution)/shard_map/ppermute | solution.py:492
  71.2 0.3 place.1
  71.5 2.1 %collective-permute-start.20 = (bf16[96,384]{1,0:T(8,128)(2,1)S(1)}, bf16[96,384]{1,0:T(8,128)(2,1)S(1)}, u32[]{:S(2)}, u32[]{:S(2)}) collective-permute-start(bf16[96,384]{1,0:T(8,128)(2,1)S(1)} %get-tuple-element.48), channel_id=1, source_target_pairs={{0,12},{4,8},{8,4},{12,0},{1,13},{5,9},{9,5},{13,1},{2,14},{6,10},... | collective-permute-start | bytes 221192 | tf_op jit(solution)/shard_map/ppermute | solution.py:492
  73.6 0.3 collective-permute-start.21
  74.0 2.0 %collective-permute-start.22 = (bf16[96,384]{1,0:T(8,128)(2,1)S(1)}, bf16[96,384]{1,0:T(8,128)(2,1)S(1)}, u32[]{:S(2)}, u32[]{:S(2)}) collective-permute-start(bf16[96,384]{1,0:T(8,128)(2,1)S(1)} %get-tuple-element.50), channel_id=1, source_target_pairs={{0,4},{4,0},{8,12},{12,8},{1,5},{5,1},{9,13},{13,9},{2,6},{6,2},{1... | collective-permute-start | bytes 221192 | tf_op jit(solution)/shard_map/ppermute | solution.py:492
  76.0 1.8 %collective-permute-done.20.refs_1_ = bf16[96,384]{1,0:T(8,128)(2,1)S(1)} collective-permute-done((bf16[96,384]{1,0:T(8,128)(2,1)S(1)}, bf16[96,384]{1,0:T(8,128)(2,1)S(1)}, u32[]{:S(2)}, u32[]{:S(2)}) %collective-permute-start.20) | collective-permute-done | bytes 73760 | tf_op jit(solution)/shard_map/ppermute | solution.py:492
  77.8 1.6 %collective-permute-done.21.refs_2_ = bf16[96,384]{1,0:T(8,128)(2,1)S(1)} collective-permute-done((bf16[96,384]{1,0:T(8,128)(2,1)S(1)}, bf16[96,384]{1,0:T(8,128)(2,1)S(1)}, u32[]{:S(2)}, u32[]{:S(2)}) %collective-permute-start.21) | collective-permute-done | bytes 73760 | tf_op jit(solution)/shard_map/ppermute | solution.py:492
  79.3 0.8 arrange.1
  (29 shorter events, 0.1 us)
Async XLA Ops:
  0.0 13.5 %copy-start = (s32[384,1]{0,1:T(1,128)S(1)}, s32[384,1]{0,1:T(1,128)}, u32[]{:S(2)}) copy-start(s32[384,1]{0,1:T(1,128)} %param.21) | copy-start | bytes 4612
  0.0 17.9 %collective-permute-start.3 = (bf16[384,1536]{1,0:T(8,128)(2,1)}, bf16[384,1536]{1,0:T(8,128)(2,1)S(1)}, u32[]{:S(2)}, u32[]{:S(2)}) collective-permute-start(bf16[384,1536]{1,0:T(8,128)(2,1)} %own.1), channel_id=1, source_target_pairs={{0,1},{1,0},{2,3},{3,2},{16,18},{17,19},{18,16},{19,17},{4,5},{5,4... | collective-permute-start | bytes 3538952 | tf_op jit(solution)/shard_map/ppermute | solution.py:188
  4.2 21.9 %collective-permute-start = (bf16[1168,128]{1,0:T(8,128)(2,1)S(1)}, bf16[1168,128]{1,0:T(8,128)(2,1)S(1)}, u32[]{:S(2)}, u32[]{:S(2)}) collective-permute-start(bf16[1168,128]{1,0:T(8,128)(2,1)S(1)} %get-tuple-element.29), channel_id=1, source_target_pairs={{0,8},{8,0},{12,4},{16,24},{20,28},{28,20},{1,9},{9,1},{13,5},{17,... | collective-permute-start | bytes 897032 | tf_op jit(solution)/shard_map/ppermute | solution.py:53
  8.7 17.4 %collective-permute-start.1 = (bf16[1168,128]{1,0:T(8,128)(2,1)S(1)}, bf16[1168,128]{1,0:T(8,128)(2,1)S(1)}, u32[]{:S(2)}, u32[]{:S(2)}) collective-permute-start(bf16[1168,128]{1,0:T(8,128)(2,1)S(1)} %get-tuple-element.30), channel_id=1, source_target_pairs={{4,8},{8,4},{12,0},{16,28},{20,24},{24,20},{5,9},{9,5},{13,1},{17,... | collective-permute-start | bytes 897032 | tf_op jit(solution)/shard_map/ppermute | solution.py:53
  10.0 16.1 %collective-permute-start.2 = (bf16[1168,128]{1,0:T(8,128)(2,1)S(1)}, bf16[1168,128]{1,0:T(8,128)(2,1)S(1)}, u32[]{:S(2)}, u32[]{:S(2)}) collective-permute-start(bf16[1168,128]{1,0:T(8,128)(2,1)S(1)} %get-tuple-element.31), channel_id=1, source_target_pairs={{0,4},{4,0},{12,8},{16,20},{24,28},{28,24},{1,5},{5,1},{13,9},{17,... | collective-permute-start | bytes 897032 | tf_op jit(solution)/shard_map/ppermute | solution.py:53
  13.7 4.1 %copy-start.4 = (s32[384]{0:T(512)S(1)}, s32[384]{0:T(512)}, u32[]{:S(2)}) copy-start(s32[384]{0:T(512)} %param.20) | copy-start | bytes 4612
  17.8 8.4 %copy-start.5 = (f32[3]{0:T(128)S(1)}, f32[3]{0:T(128)}, u32[]{:S(2)}) copy-start(f32[3]{0:T(128)} %param.19) | copy-start | bytes 40
  18.1 23.3 %collective-permute-start.9 = (bf16[192,1536]{1,0:T(8,128)(2,1)S(1)}, bf16[192,1536]{1,0:T(8,128)(2,1)S(1)}, u32[]{:S(2)}, u32[]{:S(2)}) collective-permute-start(bf16[192,1536]{1,0:T(8,128)(2,1)S(1)} %cut.1.refs_6_), channel_id=1, source_target_pairs={{0,2},{1,3},{2,0},{3,1},{16,17},{17,16},{18,19},{19,18},{4,6},{5,7... | collective-permute-start | bytes 1769480 | tf_op jit(solution)/shard_map/ppermute | solution.py:188
  19.6 26.1 %collective-permute-start.8 = (bf16[384,1536]{1,0:T(8,128)(2,1)S(1)}, bf16[384,1536]{1,0:T(8,128)(2,1)S(1)}, u32[]{:S(2)}, u32[]{:S(2)}) collective-permute-start(bf16[384,1536]{1,0:T(8,128)(2,1)S(1)} %collective-permute-done.3.got.near), channel_id=1, source_target_pairs={{0,16},{16,0},{1,17},{17,1},{2,18},{18,2},{3,19},{19,3},{4,20},{20... | collective-permute-start | bytes 3538952 | tf_op jit(solution)/shard_map/ppermute | solution.py:492
  19.7 8.7 %copy-start.1 = (bf16[384,192]{1,0:T(8,128)(2,1)}, bf16[384,192]{1,0:T(8,128)(2,1)S(1)}, u32[]{:S(2)}) copy-start(bf16[384,192]{1,0:T(8,128)(2,1)S(1)} %fusion.refs_5_.placing) | copy-start | bytes 442372
  28.4 9.2 %collective-permute-start.4 = (bf16[384,128]{1,0:T(8,128)(2,1)S(1)}, bf16[384,128]{1,0:T(8,128)(2,1)S(1)}, u32[]{:S(2)}, u32[]{:S(2)}) collective-permute-start(bf16[384,128]{1,0:T(8,128)(2,1)S(1)} %get-tuple-element.36), channel_id=1, source_target_pairs={{8,0},{0,8},{4,12},{24,16},{28,20},{20,28},{9,1},{1,9},{5,13},{25,... | collective-permute-start | bytes 294920 | tf_op jit(solution)/shard_map/ppermute | solution.py:53
  33.2 4.5 %collective-permute-start.5 = (bf16[384,128]{1,0:T(8,128)(2,1)S(1)}, bf16[384,128]{1,0:T(8,128)(2,1)S(1)}, u32[]{:S(2)}, u32[]{:S(2)}) collective-permute-start(bf16[384,128]{1,0:T(8,128)(2,1)S(1)} %get-tuple-element.37), channel_id=1, source_target_pairs={{8,4},{4,8},{0,12},{28,16},{24,20},{20,24},{9,5},{5,9},{1,13},{29,... | collective-permute-start | bytes 294920 | tf_op jit(solution)/shard_map/ppermute | solution.py:53
  34.5 6.6 %collective-permute-start.6 = (bf16[384,128]{1,0:T(8,128)(2,1)S(1)}, bf16[384,128]{1,0:T(8,128)(2,1)S(1)}, u32[]{:S(2)}, u32[]{:S(2)}) collective-permute-start(bf16[384,128]{1,0:T(8,128)(2,1)S(1)} %get-tuple-element.38), channel_id=1, source_target_pairs={{4,0},{0,4},{8,12},{20,16},{28,24},{24,28},{5,1},{1,5},{9,13},{21,... | collective-permute-start | bytes 294920 | tf_op jit(solution)/shard_map/ppermute | solution.py:53
  41.4 3.6 %collective-permute-start.10 = (bf16[192,1536]{1,0:T(8,128)(2,1)S(1)}, bf16[192,1536]{1,0:T(8,128)(2,1)S(1)}, u32[]{:S(2)}, u32[]{:S(2)}) collective-permute-start(bf16[192,1536]{1,0:T(8,128)(2,1)S(1)} %gate.1.far), channel_id=1, source_target_pairs={{0,16},{16,0},{1,17},{17,1},{2,18},{18,2},{3,19},{19,3},{4,20},{20... | collective-permute-start | bytes 1769480 | tf_op jit(solution)/shard_map/ppermute | solution.py:492
  41.5 7.0 %collective-permute-start.13 = (bf16[192,384]{1,0:T(8,128)(2,1)S(1)}, bf16[192,384]{1,0:T(8,128)(2,1)S(1)}, u32[]{:S(2)}, u32[]{:S(2)}) collective-permute-start(bf16[192,384]{1,0:T(8,128)(2,1)S(1)} %get-tuple-element.40.after.refs_0_), channel_id=1, source_target_pairs={{0,1},{1,0},{2,3},{3,2},{4,5},{5,4},{6,7},{7,6},{8,9},{9,8},{10,11... | collective-permute-start | bytes 442376 | tf_op jit(solution)/shard_map/ppermute | solution.py:492
  42.8 9.9 %collective-permute-start.14 = (bf16[192,384]{1,0:T(8,128)(2,1)S(1)}, bf16[192,384]{1,0:T(8,128)(2,1)S(1)}, u32[]{:S(2)}, u32[]{:S(2)}) collective-permute-start(bf16[192,384]{1,0:T(8,128)(2,1)S(1)} %get-tuple-element.40.after.refs_0_), channel_id=1, source_target_pairs={{0,2},{1,3},{2,0},{3,1},{4,6},{5,7},{6,4},{7,5},{8,10},{9,11},{10,... | collective-permute-start | bytes 442376 | tf_op jit(solution)/shard_map/ppermute | solution.py:492
  43.7 9.0 %collective-permute-start.15 = (bf16[192,384]{1,0:T(8,128)(2,1)S(1)}, bf16[192,384]{1,0:T(8,128)(2,1)S(1)}, u32[]{:S(2)}, u32[]{:S(2)}) collective-permute-start(bf16[192,384]{1,0:T(8,128)(2,1)S(1)} %get-tuple-element.40.after.refs_0_), channel_id=1, source_target_pairs={{0,3},{1,2},{2,1},{3,0},{4,7},{5,6},{6,5},{7,4},{8,11},{9,10},{10,... | collective-permute-start | bytes 442376 | tf_op jit(solution)/shard_map/ppermute | solution.py:492
  45.0 7.6 %copy-start.3 = (f32[3,4,1536]{2,1,0:T(4,128)S(1)}, f32[3,4,1536]{2,1,0:T(4,128)}, u32[]{:S(2)}) copy-start(f32[3,4,1536]{2,1,0:T(4,128)} %mod.1) | copy-start | bytes 221188
  45.0 13.1 %collective-permute-start.11 = (bf16[192,384]{1,0:T(8,128)(2,1)S(1)}, bf16[192,384]{1,0:T(8,128)(2,1)S(1)}, u32[]{:S(2)}, u32[]{:S(2)}) collective-permute-start(bf16[192,384]{1,0:T(8,128)(2,1)S(1)} %get-tuple-element.39.refs_0_), channel_id=1, source_target_pairs={{0,2},{1,3},{2,0},{3,1},{4,6},{5,7},{6,4},{7,5},{8,10},{9,11},{10,... | collective-permute-start | bytes 442376 | tf_op jit(solution)/shard_map/ppermute | solution.py:492
  45.7 12.5 %collective-permute-start.12 = (bf16[192,384]{1,0:T(8,128)(2,1)S(1)}, bf16[192,384]{1,0:T(8,128)(2,1)S(1)}, u32[]{:S(2)}, u32[]{:S(2)}) collective-permute-start(bf16[192,384]{1,0:T(8,128)(2,1)S(1)} %get-tuple-element.39.refs_0_), channel_id=1, source_target_pairs={{0,1},{1,0},{2,3},{3,2},{4,5},{5,4},{6,7},{7,6},{8,9},{9,8},{10,11... | collective-permute-start | bytes 442376 | tf_op jit(solution)/shard_map/ppermute | solution.py:492
  48.5 10.6 %collective-permute-start.7 = (bf16[192,384]{1,0:T(8,128)(2,1)S(1)}, bf16[192,384]{1,0:T(8,128)(2,1)S(1)}, u32[]{:S(2)}, u32[]{:S(2)}) collective-permute-start(bf16[192,384]{1,0:T(8,128)(2,1)S(1)} %get-tuple-element.39.refs_0_), channel_id=1, source_target_pairs={{0,3},{1,2},{2,1},{3,0},{4,7},{5,6},{6,5},{7,4},{8,11},{9,10},{10,... | collective-permute-start | bytes 442376 | tf_op jit(solution)/shard_map/ppermute | solution.py:492
  56.4 4.9 %collective-permute-start.16 = (bf16[192,1536]{1,0:T(8,128)(2,1)S(1)}, bf16[192,1536]{1,0:T(8,128)(2,1)S(1)}, u32[]{:S(2)}, u32[]{:S(2)}) collective-permute-start(bf16[192,1536]{1,0:T(8,128)(2,1)S(1)} %feed.3), channel_id=1, source_target_pairs={{0,16},{16,0},{1,17},{17,1},{2,18},{18,2},{3,19},{19,3},{4,20},{20... | collective-permute-start | bytes 1769480 | tf_op jit(solution)/shard_map/ppermute | solution.py:492
  61.3 9.9 %copy-start.2 = (bf16[384,192]{1,0:T(8,128)(2,1)S(1)}, bf16[384,192]{1,0:T(8,128)(2,1)}, u32[]{:S(2)}) copy-start(bf16[384,192]{1,0:T(8,128)(2,1)} %copy-done.1) | copy-start | bytes 442372
  62.7 6.3 %collective-permute-start.17 = (bf16[192,384]{1,0:T(8,128)(2,1)S(1)}, bf16[192,384]{1,0:T(8,128)(2,1)S(1)}, u32[]{:S(2)}, u32[]{:S(2)}) collective-permute-start(bf16[192,384]{1,0:T(8,128)(2,1)S(1)} %get-tuple-element.44), channel_id=1, source_target_pairs={{0,1},{1,0},{2,3},{3,2},{4,5},{5,4},{6,7},{7,6},{8,9},{9,8},{10,11... | collective-permute-start | bytes 442376 | tf_op jit(solution)/shard_map/ppermute | solution.py:492
  63.6 7.6 %collective-permute-start.18 = (bf16[192,384]{1,0:T(8,128)(2,1)S(1)}, bf16[192,384]{1,0:T(8,128)(2,1)S(1)}, u32[]{:S(2)}, u32[]{:S(2)}) collective-permute-start(bf16[192,384]{1,0:T(8,128)(2,1)S(1)} %get-tuple-element.45), channel_id=1, source_target_pairs={{0,2},{1,3},{2,0},{3,1},{4,6},{5,7},{6,4},{7,5},{8,10},{9,11},{10,... | collective-permute-start | bytes 442376 | tf_op jit(solution)/shard_map/ppermute | solution.py:492
  63.8 7.5 %collective-permute-start.19 = (bf16[192,384]{1,0:T(8,128)(2,1)S(1)}, bf16[192,384]{1,0:T(8,128)(2,1)S(1)}, u32[]{:S(2)}, u32[]{:S(2)}) collective-permute-start(bf16[192,384]{1,0:T(8,128)(2,1)S(1)} %get-tuple-element.46), channel_id=1, source_target_pairs={{0,3},{1,2},{2,1},{3,0},{4,7},{5,6},{6,5},{7,4},{8,11},{9,10},{10,... | collective-permute-start | bytes 442376 | tf_op jit(solution)/shard_map/ppermute | solution.py:492
  71.5 6.2 %collective-permute-start.20 = (bf16[96,384]{1,0:T(8,128)(2,1)S(1)}, bf16[96,384]{1,0:T(8,128)(2,1)S(1)}, u32[]{:S(2)}, u32[]{:S(2)}) collective-permute-start(bf16[96,384]{1,0:T(8,128)(2,1)S(1)} %get-tuple-element.48), channel_id=1, source_target_pairs={{0,12},{4,8},{8,4},{12,0},{1,13},{5,9},{9,5},{13,1},{2,14},{6,10},... | collective-permute-start | bytes 221192 | tf_op jit(solution)/shard_map/ppermute | solution.py:492
  73.6 5.7 %collective-permute-start.21 = (bf16[96,384]{1,0:T(8,128)(2,1)S(1)}, bf16[96,384]{1,0:T(8,128)(2,1)S(1)}, u32[]{:S(2)}, u32[]{:S(2)}) collective-permute-start(bf16[96,384]{1,0:T(8,128)(2,1)S(1)} %get-tuple-element.49), channel_id=1, source_target_pairs={{0,8},{4,12},{8,0},{12,4},{1,9},{5,13},{9,1},{13,5},{2,10},{6,14},... | collective-permute-start | bytes 221192 | tf_op jit(solution)/shard_map/ppermute | solution.py:492
  74.0 5.4 %collective-permute-start.22 = (bf16[96,384]{1,0:T(8,128)(2,1)S(1)}, bf16[96,384]{1,0:T(8,128)(2,1)S(1)}, u32[]{:S(2)}, u32[]{:S(2)}) collective-permute-start(bf16[96,384]{1,0:T(8,128)(2,1)S(1)} %get-tuple-element.50), channel_id=1, source_target_pairs={{0,4},{4,0},{8,12},{12,8},{1,5},{5,1},{9,13},{13,9},{2,6},{6,2},{1... | collective-permute-start | bytes 221192 | tf_op jit(solution)/shard_map/ppermute | solution.py:492
